TPU v7x, 128 devices: a whole 4x4x4 slice. The times are simulated.
128 devices in a mesh: fsdp: 16 (over y, x), tp: 8 (over z, core).
Axes of the slice: x: 4, y: 4, z: 4, core: 2. Of those that a mesh axis runs over, the one named last changes fastest.
Arguments:
- momentum: bfloat16 [8192, 28672], P('fsdp', 'tp'), may hold values from -300 to 300
- gradient: bfloat16 [8192, 28672], P('fsdp', 'tp'), may hold values from -300 to 300
- seed_value: int32 [1], replicated, may hold values from 0 to 999999
Outputs:
- new_momentum: bfloat16 [8192, 28672], P('fsdp', 'tp')
- update: bfloat16 [8192, 28672], P('fsdp', 'tp')
All inputs are finite; a program needn't handle non-finite values.
Results may differ from a plain program's by a relative error of at most 0.012.
Values may be sent and summed in bfloat16 or wider, within the bound.
No kernel may reach another device: no remote copies, remote signals or barrier semaphores. Data moves between devices by JAX's collectives and lax.ppermute only.
A program may use at most 128 MiB of HBM per device.

v0:
```python
import math

import jax
import jax.numpy as jnp
from jax import lax
from jax.sharding import PartitionSpec as P

D = 8192
F = 28672
RANK = 512


def start_factor(seed_value, first_row, row_count):
    row_ids = (first_row + jnp.arange(row_count, dtype=jnp.int32))[:, None]
    col_ids = jnp.arange(RANK, dtype=jnp.int32)[None, :]
    hashed = (row_ids * 40503 + col_ids * 9973 + seed_value[0]) % 65521
    second = (hashed % 32768 * (hashed % 32768) + 7) % 65521
    third = (second % 32768 * (second % 32768) + hashed) % 65521
    uniform_part = third.astype(jnp.float32) / 65521.0 - 0.5
    return (uniform_part * math.sqrt(12.0 / F)).astype(jnp.bfloat16)


def per_device(momentum, gradient, seed_value):
    local_cols = momentum.shape[1]
    blended = (momentum.astype(jnp.float32) + gradient.astype(jnp.float32)).astype(jnp.bfloat16)
    start_rows = start_factor(seed_value, lax.axis_index("tp") * local_cols, local_cols)
    partial_left = jnp.dot(blended, start_rows, preferred_element_type=jnp.float32)
    projected = lax.psum(partial_left, "tp")
    gram_part = jnp.dot(projected.T, projected, precision=lax.Precision.HIGHEST)
    gram_whole = lax.psum(gram_part, "fsdp")
    lower_factor = jnp.linalg.cholesky(gram_whole)
    ortho_left = jax.scipy.linalg.solve_triangular(lower_factor, projected.T, lower=True).T.astype(
        jnp.bfloat16
    )
    contract_rows = (((0,), (0,)), ((), ()))
    partial_right = lax.dot_general(
        blended, ortho_left, contract_rows, preferred_element_type=jnp.float32
    )
    right_factor = lax.psum(partial_right, "fsdp")
    square_sums = lax.psum(jnp.sum(right_factor * right_factor, axis=0), "tp")
    next_factor = (right_factor * lax.rsqrt(square_sums + 1e-06)[None, :]).astype(jnp.bfloat16)
    right_rounded = right_factor.astype(jnp.bfloat16)
    contract_cols = (((1,), (1,)), ((), ()))
    feedback = lax.dot_general(
        ortho_left, right_rounded, contract_cols, preferred_element_type=jnp.float32
    )
    new_momentum = (blended.astype(jnp.float32) - 0.05 * feedback).astype(jnp.bfloat16)
    direction = lax.dot_general(
        ortho_left, next_factor, contract_cols, preferred_element_type=jnp.float32
    )
    update = (math.sqrt(D * F / RANK) * direction).astype(jnp.bfloat16)
    return (new_momentum, update)


def solution(mesh):
    return jax.shard_map(
        per_device,
        mesh=mesh,
        in_specs=(P("fsdp", "tp"), P("fsdp", "tp"), P()),
        out_specs=(P("fsdp", "tp"), P("fsdp", "tp")),
        check_vma=False,
    )
```

profile of v0, /device:TPU:1, one launch (start us, length us, event | category | flops | bytes accessed | tf_op | source)
XLA Modules:
  0.0 509.3 jit_solution(14262774875700640523)
XLA Ops:
  7.2 0.0 all-reduce.5.cloned.1.call-start
  7.9 25.9 %fusion.16 = f32[512,512]{1,0:T(8,128)} fusion(s32[]{:T(128)} %bitcast.58, s32[512]{0:T(512)S(1)} %iota_multiply_fusion, s32[3584]{0:T(1024)S(1)} %add_multiply_fusion, bf16[512,3584]{1,0:T(8,128)(2,1)} %param.4, bf16[512,3584]{1,0:T(8,128)(2,1)} %param.3), kind=kOutput, calls=%fused_computation.33 | convolution fusion | flops 1979973632 | bytes 8404996 | tf_op jit(solution)/shard_map/dot_general | solution.py:27
  33.8 0.0 all-reduce.5.cloned.1.call-update
  33.9 0.0 all-reduce.7.cloned.1.call-start
  33.9 63.9 %all-reduce.5.cloned.1.call-done = f32[512,512]{1,0:T(8,128)} async-done(((f32[512,512]{1,0:T(8,128)}), f32[512,512]{1,0:T(8,128)}) %all-reduce.5.cloned.1.call-update) | async-done | bytes 1048592 | tf_op jit(solution)/shard_map/psum | solution.py:28
  97.8 4.4 fusion.73
  102.2 0.0 all-reduce.7.cloned.1.call-update
  102.3 0.6 all-reduce.9.cloned.1.call-start
  102.9 86.1 %all-reduce.7.cloned.1.call-done = f32[512,512]{0,1:T(8,128)} async-done(((f32[512,512]{0,1:T(8,128)}), f32[512,512]{0,1:T(8,128)}) %all-reduce.7.cloned.1.call-update) | async-done | bytes 1048592 | tf_op jit(solution)/shard_map/psum | solution.py:30
  188.9 1.6 copy.6
  190.5 1.4 fusion.31
  191.9 11.7 %cholesky.104 = f32[128,128]{1,0:T(8,128)S(1)} custom-call(f32[128,128]{1,0:T(8,128)S(1)} %cholesky.266), custom_call_target="Cholesky" | custom-call | tf_op jit(solution)/shard_map/jit(cholesky)/cholesky | solution.py:31
  203.7 9.8 %custom-call.31 = f32[1,128,128]{1,2,0:T(8,128)S(1)} custom-call(f32[1,128,128]{2,1,0:T(8,128)S(1)} %get-tuple-element.29), custom_call_target="InvertDiagBlocksLowerTriangular" | custom-call | tf_op jit(solution)/shard_map/jit(cholesky)/cholesky | solution.py:31
  213.5 0.1 cholesky.224
  213.6 0.3 constant_dynamic-update-slice_fusion.3
  213.9 0.3 convolution_subtract_fusion.3
  214.3 11.7 %cholesky.217 = f32[128,128]{1,0:T(8,128)S(1)} custom-call(f32[128,128]{1,0:T(8,128)S(1)} %cholesky.270), custom_call_target="Cholesky" | custom-call | tf_op jit(solution)/shard_map/jit(cholesky)/cholesky | solution.py:31
  226.0 10.0 %custom-call.32 = f32[1,128,128]{1,2,0:T(8,128)S(1)} custom-call(f32[1,128,128]{2,1,0:T(8,128)S(1)} %get-tuple-element.26), custom_call_target="InvertDiagBlocksLowerTriangular" | custom-call | tf_op jit(solution)/shard_map/jit(cholesky)/cholesky | solution.py:31
  236.0 0.3 convolution_dynamic-update-slice_fusion
  236.3 0.4 convolution_subtract_fusion.4
  236.7 11.7 %cholesky.238 = f32[128,128]{1,0:T(8,128)S(1)} custom-call(f32[128,128]{1,0:T(8,128)S(1)} %cholesky.275), custom_call_target="Cholesky" | custom-call | tf_op jit(solution)/shard_map/jit(cholesky)/cholesky | solution.py:31
  248.4 0.7 compare_reduce_fusion.1
  249.1 9.8 %custom-call.33 = f32[1,128,128]{1,2,0:T(8,128)S(1)} custom-call(f32[1,128,128]{2,1,0:T(8,128)S(1)} %get-tuple-element.23), custom_call_target="InvertDiagBlocksLowerTriangular" | custom-call | tf_op jit(solution)/shard_map/jit(cholesky)/cholesky | solution.py:31
  259.0 0.2 convolution_dynamic-update-slice_fusion.1
  259.2 0.4 convolution_subtract_fusion.5
  259.6 11.7 %cholesky.255 = f32[128,128]{1,0:T(8,128)S(1)} custom-call(f32[128,128]{1,0:T(8,128)S(1)} %convolution_subtract_fusion.5), custom_call_target="Cholesky" | custom-call | tf_op jit(solution)/shard_map/jit(cholesky)/cholesky | solution.py:31
  271.3 0.6 compare_reduce_fusion
  271.9 0.7 compare_reduce_fusion.2
  275.1 0.3 select_select_fusion
  275.5 10.9 %while.1 = (s32[]{:T(128)}, f32[512,512]{1,0:T(8,128)S(1)}, s32[4,2]{0,1:T(2,128)S(1)}, f32[4,128,128]{2,1,0:T(8,128)}, s32[]{:T(128)}) while((s32[]{:T(128)}, f32[512,512]{1,0:T(8,128)S(1)}, s32[4,2]{0,1:T(2,128)S(1)}, f32[4,128,128]{2,1,0:T(8,128)}, s32[]{:T(128)}) %tuple.34), condition=%wide.while_cond, body=%wide.while_body.sunk | while | flops 2 | bytes 132205 | solution.py:32
  275.5 0.1 constant_dynamic-slice_fusion.2
  275.6 0.6 fusion.82
  276.2 2.1 bitcast_dynamic-update-slice_fusion.2
  278.2 0.1 constant_dynamic-slice_fusion.2
  278.3 0.6 fusion.82
  278.9 2.1 bitcast_dynamic-update-slice_fusion.2
  281.0 0.1 constant_dynamic-slice_fusion.2
  281.0 0.6 fusion.82
  281.6 2.1 bitcast_dynamic-update-slice_fusion.2
  283.7 0.1 constant_dynamic-slice_fusion.2
  283.8 0.6 fusion.82
  284.4 2.1 bitcast_dynamic-update-slice_fusion.2
  286.4 40.1 %custom-call.34 = f32[4,128,128]{1,2,0:T(8,128)S(1)} custom-call(f32[4,128,128]{2,1,0:T(8,128)} %get-tuple-element.9), custom_call_target="InvertDiagBlocksLowerTriangular" | custom-call | tf_op jit(solution)/shard_map/jit(_solve_triangular)/triangular_solve | solution.py:32
  326.6 0.0 copy-start.4
  326.6 0.0 copy-start
  326.6 0.0 copy-done.1
  326.6 0.4 fusion.72
  327.0 0.6 convolution_subtract_fusion.1
  327.6 0.4 fusion.71
  328.1 0.0 copy-done.4
  328.1 1.0 convolution_subtract_fusion
  329.1 1.3 fusion.70
  330.3 0.0 copy-start.2
  330.3 1.5 convolution_subtract_fusion.2
  331.8 1.3 convolution_convert_fusion
  333.1 0.0 copy-done
  333.1 7.3 %fusion.68 = f32[3584,512]{1,0:T(8,128)} fusion(bf16[128,512]{1,0:T(8,128)(2,1)S(1)} %convolution_convert_fusion, bf16[128,512]{1,0:T(8,128)(2,1)S(1)} %get-tuple-element.32, bf16[128,512]{1,0:T(8,128)(2,1)S(1)} %get-tuple-element.34, bf16[128,512]{1,0:T(8,128)(2,1)S(1)} %get-tuple-element.36, bf16[512,3584]{1,0:T(8,128)(2,1)S(1)} %copy-done, ...), kind=kOutput, calls=%fused_computation.122 | convolution fusion | flops 1888485376 | bytes 15204352 | tf_op jit(solution)/shard_map/dot_general | solution.py:36
  340.4 0.0 all-reduce.9.cloned.1.call-update
  340.4 132.1 %all-reduce.9.cloned.1.call-done = f32[3584,512]{1,0:T(8,128)} async-done(((f32[3584,512]{1,0:T(8,128)}), f32[3584,512]{1,0:T(8,128)}) %all-reduce.9.cloned.1.call-update) | async-done | bytes 7340048 | tf_op jit(solution)/shard_map/psum | solution.py:39
  472.5 3.8 multiply_reduce_fusion
  476.3 12.8 %psum.31 = f32[512]{0:T(512)S(1)} all-reduce(f32[512]{0:T(512)S(1)} %multiply_reduce_fusion), channel_id=1, replica_groups=mesh['fsdp'=16,'tp'=8] {'tp'}, use_global_device_ids=true, to_apply=%region_12.13 | all-reduce | flops 512 | bytes 4096 | tf_op jit(solution)/shard_map/psum | solution.py:40
  489.1 9.4 %subtract_convert_fusion = bf16[512,3584]{1,0:T(8,128)(2,1)} fusion(f32[3584,512]{1,0:T(8,128)} %all-reduce.9.cloned.1.call-done, bf16[128,512]{1,0:T(8,128)(2,1)S(1)} %convolution_convert_fusion, bf16[128,512]{1,0:T(8,128)(2,1)} %copy-done.2, bf16[128,512]{1,0:T(8,128)(2,1)S(1)} %get-tuple-element.34, bf16[128,512]{1,0:T(8,128)(2,1)S(1)} %get-tuple-element.36, ...), kind=kOutput, calls=%fused_computation.27 | convolution fusion | flops 1897660416 | bytes 18874368 | tf_op jit(solution)/shard_map/dot_general | solution.py:44
  498.5 0.0 copy-done.3
  498.5 4.0 multiply_convert_fusion
  (21 shorter events, 0.2 us)
Async XLA Ops:
  7.2 90.7 %all-reduce.5.cloned.1.call-start = ((), (), s32[]{:S(2)}) async-start(), calls=%async_computation | async-start | bytes 2097152 | tf_op jit(solution)/shard_map/psum | solution.py:28
  33.9 155.0 %all-reduce.7.cloned.1.call-start = ((), (), s32[]{:S(2)}) async-start(), calls=%async_computation.1 | async-start | bytes 2097152 | tf_op jit(solution)/shard_map/psum | solution.py:30
  102.2 224.4 %copy-start.1 = (f32[512,512]{1,0:T(8,128)S(1)}, f32[512,512]{1,0:T(8,128)}, u32[]{:S(2)}) copy-start(f32[512,512]{1,0:T(8,128)} %all-reduce.5.cloned.1.call-done) | copy-start | bytes 3145732
  102.3 370.2 %all-reduce.9.cloned.1.call-start = ((), (), s32[]{:S(2)}) async-start(), calls=%async_computation.2 | async-start | bytes 14680064 | tf_op jit(solution)/shard_map/psum | solution.py:39
  326.6 1.5 copy-start.4
  326.6 6.5 %copy-start = (bf16[512,3584]{1,0:T(8,128)(2,1)S(1)}, bf16[512,3584]{1,0:T(8,128)(2,1)}, u32[]{:S(2)}) copy-start(bf16[512,3584]{1,0:T(8,128)(2,1)} %param.4) | copy-start | bytes 11010052
  330.3 10.0 %copy-start.2 = (bf16[128,512]{1,0:T(8,128)(2,1)}, bf16[128,512]{1,0:T(8,128)(2,1)S(1)}, u32[]{:S(2)}) copy-start(bf16[128,512]{1,0:T(8,128)(2,1)S(1)} %get-tuple-element.32) | copy-start | bytes 393220
  472.5 26.0 %slice-start = ((s8[7340032]{0:T(1024)(128)(4,1)}), s8[3145728]{0:T(1024)(128)(4,1)S(1)}, s32[]{:S(2)}) async-start(s8[7340032]{0:T(1024)(128)(4,1)} %bitcast.59), calls=%async_computation.3 | async-start | bytes 6291456
  489.1 9.4 %slice-start.1 = ((s8[7340032]{0:T(1024)(128)(4,1)}), s8[4194304]{0:T(1024)(128)(4,1)S(1)}, s32[]{:S(2)}) async-start(s8[7340032]{0:T(1024)(128)(4,1)} %bitcast.59), calls=%async_computation.4 | async-start | bytes 8388608
  489.1 9.4 %copy-start.3 = (bf16[128,512]{1,0:T(8,128)(2,1)S(1)}, bf16[128,512]{1,0:T(8,128)(2,1)}, u32[]{:S(2)}) copy-start(bf16[128,512]{1,0:T(8,128)(2,1)} %copy-done.2) | copy-start | bytes 393220
Sparse Core Ops, SparseCore 0:
  34.0 63.8 all-reduce.4
  102.4 86.4 all-reduce.6
  340.5 131.9 all-reduce.8
where the time goes:
time: 515 us; the launch traced here: 509 us
  waiting for transfers between devices  282 us (55%)
  other arithmetic  124 us (24%)
  matrix products  59.3 us (12%)
  between operations  17.5 us (3%)
  blocking collectives  12.8 us (2%)
  local copies, waits for them, and re-layouts  12.6 us (2%)
    psum x1, waiting for transfers between devices, per_device(): right_factor = lax.psum(partial_right, 'fsdp')  132 us
    psum x1, waiting for transfers between devices, per_device(): gram_whole = lax.psum(gram_part, 'fsdp')  86.1 us
    another operation x14, other arithmetic, per_device(): lower_factor = jnp.linalg.cholesky(gram_whole)  78.6 us
    psum x1, waiting for transfers between devices, per_device(): projected = lax.psum(partial_left, 'tp')  63.9 us
    another operation x3, other arithmetic, per_device(): jax.scipy.linalg.solve_triangular(lower_factor, projected.T, lower=True)  40.5 us
    dot_general x1, matrix products, per_device(): jnp.dot(blended, start_rows, preferred_element_type=jnp.float32)  25.9 us
    psum x1, blocking collectives, per_device(): square_sums = lax.psum(jnp.sum(right_factor * right_factor, axis=0), 'tp')  12.8 us
    another operation x12, local copies, waits for them, and re-layouts  10.9 us
  transfers between devices with their start and end apart: 3, of which 3 were waited for; matrix products, arithmetic and copies ran while one was open for 0% of the time, Pallas kernels for 0%

commit v1 on v0

v1 whole, which is shorter than its diff:
```python
import functools
import math

import jax
import jax.numpy as jnp
from jax import lax
from jax.experimental import pallas as pl
from jax.experimental.pallas import tpu as pltpu
from jax.sharding import PartitionSpec as P

D = 8192
F = 28672
RANK = 512
HALF = RANK // 2
PRIME = 65521
NB = 128
PANEL = 16
VMEM_LIMIT = 48 * 1024 * 1024
F32, BF16 = jnp.float32, jnp.bfloat16
AXES = ("fsdp", "tp")
WIRE = jnp.float32


def flat(y, x, z, core):
    return (y * 4 + x) * 8 + z * 2 + core


def everyone():
    return [(y, x, z, c) for y in range(4) for x in range(4) for z in range(4) for c in range(2)]


def shift(along_first, step):
    pairs = []
    for y, x, z, c in everyone():
        if (c == 0) == along_first:
            to = (y, (x + step) % 4, z, c)
        else:
            to = ((y + step) % 4, x, z, c)
        pairs.append((flat(y, x, z, c), flat(*to)))
    return pairs


def send_first(a, step):
    return lax.ppermute(a, AXES, shift(True, step))


def send_second(a, step):
    return lax.ppermute(a, AXES, shift(False, step))


def swap_cores(a):
    return lax.ppermute(a, "tp", [(i, i ^ 1) for i in range(8)])


Z_GROUPS = [[c, 2 + c, 4 + c, 6 + c] for c in range(2)]
SECOND_GROUPS = [[flat(y, x, z, 0) for y in range(4)] for x in range(4) for z in range(4)] + [
    [flat(y, x, z, 1) for x in range(4)] for y in range(4) for z in range(4)
]
FIRST_Z_GROUPS = [[flat(y, x, z, 0) for x in range(4) for z in range(4)] for y in range(4)] + [
    [flat(y, x, z, 1) for y in range(4) for z in range(4)] for x in range(4)
]


def exchange(a, axis, groups=None):
    return lax.all_to_all(a, axis, 0, 0, axis_index_groups=groups, tiled=True)


def vmem_spec():
    return pl.BlockSpec(memory_space=pltpu.VMEM)


def smem_spec():
    return pl.BlockSpec(memory_space=pltpu.SMEM)


def params():
    return pltpu.CompilerParams(vmem_limit_bytes=VMEM_LIMIT)


def dot(a, b, ca, cb, precision=None):
    return lax.dot_general(
        a, b, (((ca,), (cb,)), ((), ())), precision=precision, preferred_element_type=F32
    )


def exact(a, b, ca, cb):
    return dot(a, b, ca, cb, lax.Precision.HIGHEST)


def fold(v):
    return (v & 65535) + 15 * (v >> 16)


def reduce_mod(v):
    v = fold(fold(v))
    return jnp.where(v >= PRIME, v - PRIME, v)


def start_rows(first_row, count, seed):
    rows = first_row + lax.broadcasted_iota(jnp.int32, (count, 1), 0)
    cols = lax.broadcasted_iota(jnp.int32, (1, RANK), 1)
    hashed = reduce_mod(rows * 40503 + seed) + reduce_mod(cols * 9973)
    hashed = jnp.where(hashed >= PRIME, hashed - PRIME, hashed)
    low = hashed & 32767
    low = reduce_mod(low * low + 7) & 32767
    third = reduce_mod(low * low + hashed).astype(F32)
    scale = math.sqrt(12.0 / F)
    return (third * (scale / PRIME) - 0.5 * scale).astype(BF16)


TILE = 512


def left_kernel(meta_ref, m_ref, g_ref, b_ref, keep_ref, send_ref, acc):
    t = pl.program_id(0)
    core, tp, seed = meta_ref[0], meta_ref[1], meta_ref[2]
    b = (m_ref[...].astype(F32) + g_ref[...].astype(F32)).astype(BF16)
    b_ref[...] = b
    part = dot(b, start_rows(tp * 3584 + t * TILE, TILE, seed), 1, 0)

    @pl.when(t == 0)
    def _():
        acc[...] = part

    @pl.when(t > 0)
    def _():
        acc[...] += part

    @pl.when(t == pl.num_programs(0) - 1)
    def _():
        keep_ref[...] = acc[pl.ds(core * HALF, HALF), :]
        send_ref[...] = acc[pl.ds((1 - core) * HALF, HALF), :]


def left_partial(meta, momentum, gradient):
    rows, cols = momentum.shape
    half = jax.ShapeDtypeStruct((HALF, RANK), F32)
    whole = pl.BlockSpec((HALF, RANK), lambda t: (0, 0))
    tile = pl.BlockSpec((rows, TILE), lambda t: (0, t))
    return pl.pallas_call(
        left_kernel,
        grid=(cols // TILE,),
        out_shape=(jax.ShapeDtypeStruct((rows, cols), BF16), half, half),
        in_specs=[smem_spec(), tile, tile],
        out_specs=(tile, whole, whole),
        scratch_shapes=[pltpu.VMEM((rows, RANK), F32)],
        compiler_params=params(),
        name="left_partial",
    )(meta, momentum, gradient)


def gram_kernel(meta_ref, mine_ref, other_ref, out_ref):
    cols = pl.ds(pl.multiple_of(meta_ref[0] * HALF, HALF), HALF)
    out_ref[...] = exact(mine_ref[...], mine_ref[:, cols], 0, 0) + exact(
        other_ref[...], other_ref[:, cols], 0, 0
    )


def gram_half(meta, mine, other):
    return pl.pallas_call(
        gram_kernel,
        out_shape=jax.ShapeDtypeStruct((RANK, HALF), F32),
        in_specs=[smem_spec(), vmem_spec(), vmem_spec()],
        out_specs=vmem_spec(),
        compiler_params=params(),
        name="gram_half",
    )(meta, mine, other)


def right_kernel(offsets, meta_ref, b_ref, mine_ref, other_ref, *rest):
    outs, (hi, lo) = rest[:-2], rest[-2:]
    r = pl.program_id(0)

    @pl.when(r == 0)
    def _():
        core = meta_ref[0]
        for ref, place in ((mine_ref, core), (other_ref, 1 - core)):
            rows = pl.ds(pl.multiple_of(place * HALF, HALF), HALF)
            top = ref[...].astype(BF16)
            hi[rows, :] = top
            lo[rows, :] = (ref[...] - top.astype(F32)).astype(BF16)

    w = dot(b_ref[...], hi[...], 0, 0) + dot(b_ref[...], lo[...], 0, 0)
    w = w.astype(WIRE)
    for k in range(len(offsets)):

        @pl.when(r == k)
        def _():
            outs[2 * k][...] = w[:, :HALF]
            outs[2 * k + 1][...] = w[:, HALF:]


def right_partial(meta, blended, mine, other, offsets):
    rows, cols = blended.shape
    block = cols // 4
    n = len(offsets)

    def place(r, meta_ref):
        off = offsets[0]
        for k in range(1, n):
            off = jnp.where(r == k, offsets[k], off)
        return (0, (meta_ref[3] + off) % 4)

    whole = pl.BlockSpec((HALF, RANK), lambda r, meta_ref: (0, 0))
    out = pl.BlockSpec((block, HALF), lambda r, meta_ref: (0, 0))
    return pl.pallas_call(
        functools.partial(right_kernel, offsets),
        grid_spec=pltpu.PrefetchScalarGridSpec(
            num_scalar_prefetch=1,
            grid=(n,),
            in_specs=[pl.BlockSpec((rows, block), place), whole, whole],
            out_specs=[out] * (2 * n),
            scratch_shapes=[pltpu.VMEM((RANK, RANK), BF16)] * 2,
        ),
        out_shape=[jax.ShapeDtypeStruct((block, HALF), WIRE)] * (2 * n),
        compiler_params=params(),
        name="right_partial",
    )(meta, blended, mine, other)


def add_kernel(a_ref, b_ref, c_ref, d_ref, x_ref, y_ref):
    x_ref[...] = (a_ref[...].astype(F32) + b_ref[...].astype(F32)).astype(x_ref.dtype)
    y_ref[...] = (c_ref[...].astype(F32) + d_ref[...].astype(F32)).astype(y_ref.dtype)


def add_pairs(a, b, c, d):
    shape = jax.ShapeDtypeStruct(a.shape, a.dtype)
    return pl.pallas_call(
        add_kernel,
        out_shape=(shape, shape),
        in_specs=[vmem_spec()] * 4,
        out_specs=(vmem_spec(),) * 2,
        compiler_params=params(),
        name="add_pairs",
    )(a, b, c, d)


def split_kernel(meta_ref, *refs):
    ins, outs = refs[:6], refs[6:]
    quarter = ins[0].shape[0] // 4
    for k, off in enumerate((2, 1, 3, 0)):
        rows = pl.ds(pl.multiple_of((meta_ref[4] + off) % 4 * quarter, quarter), quarter)
        for h in range(2):
            total = sum(ref[rows, :].astype(F32) for ref in ins[3 * h : 3 * h + 3])
            outs[2 * k + h][...] = total.astype(outs[2 * k + h].dtype)


def add_and_split(meta, terms):
    rows = terms[0].shape[0] // 4
    return pl.pallas_call(
        split_kernel,
        out_shape=[jax.ShapeDtypeStruct((rows, HALF), WIRE)] * 8,
        in_specs=[smem_spec()] + [vmem_spec()] * 6,
        out_specs=[vmem_spec()] * 8,
        compiler_params=params(),
        name="add_and_split",
    )(meta, *terms)


def invert_block(ae):
    rows = lax.broadcasted_iota(jnp.int32, (PANEL, NB), 0)
    for k0 in range(0, NB, PANEL):
        left = ae[k0 : k0 + PANEL, :NB]
        right = ae[k0 : k0 + PANEL, NB:]
        columns = [
            jnp.broadcast_to(left[:, k0 + c : k0 + c + 1], (PANEL, NB)) for c in range(PANEL)
        ]
        pivots = jnp.zeros((PANEL, NB), F32)
        for k in range(PANEL):
            pivot = columns[k][k : k + 1, :]
            pivots = jnp.where(rows == k, pivot, pivots)
            if k < PANEL - 1:
                factor = jnp.where(rows > k, columns[k] * (1.0 / pivot), 0.0)
                for c in range(k + 1, PANEL):
                    columns[c] = columns[c] - factor * columns[c][k : k + 1, :]
                left = left - factor * left[k : k + 1, :]
                right = right - factor * right[k : k + 1, :]
        scale = lax.rsqrt(pivots)
        left, right = left * scale, right * scale
        ae[k0 : k0 + PANEL, NB:] = right
        below = k0 + PANEL
        if below < NB:
            ae[below:, :NB] = ae[below:, :NB] - exact(left, left, 0, 0)[below:]
            ae[below:, NB:] = ae[below:, NB:] - exact(left, right, 0, 0)[below:]


def inverse_kernel(meta_ref, mine_ref, other_ref, out_ref, a, ae):
    core = meta_ref[0]
    a[:, pl.ds(pl.multiple_of(core * HALF, HALF), HALF)] = mine_ref[...]
    a[:, pl.ds(pl.multiple_of((1 - core) * HALF, HALF), HALF)] = other_ref[...]
    big = lambda d: lax.broadcasted_iota(jnp.int32, (RANK, RANK), d)
    small = lambda d: lax.broadcasted_iota(jnp.int32, (NB, NB), d)
    out_ref[...] = jnp.where(big(0) == big(1), 1.0, 0.0)
    for lo in range(0, RANK, NB):
        hi = lo + NB
        ae[:, :NB] = a[lo:hi, lo:hi]
        ae[:, NB:] = jnp.where(small(0) == small(1), 1.0, 0.0)
        invert_block(ae)
        inverse = jnp.where(small(0) >= small(1), ae[:, NB:], 0.0)
        done = exact(inverse, out_ref[lo:hi, :hi], 1, 0)
        out_ref[lo:hi, :hi] = done
        if hi < RANK:
            below = exact(a[hi:, lo:hi], inverse, 1, 1)
            a[hi:, hi:] = a[hi:, hi:] - exact(below, below, 1, 1)
            out_ref[hi:, :hi] = out_ref[hi:, :hi] - exact(below, done, 1, 0)


def inverse_factor(meta, mine, other):
    return pl.pallas_call(
        inverse_kernel,
        out_shape=jax.ShapeDtypeStruct((RANK, RANK), F32),
        in_specs=[smem_spec(), vmem_spec(), vmem_spec()],
        out_specs=vmem_spec(),
        scratch_shapes=[pltpu.VMEM((RANK, RANK), F32), pltpu.VMEM((NB, 2 * NB), F32)],
        compiler_params=params(),
        name="inverse_factor",
    )(meta, mine, other)


def solve_kernel(a0, a1, a2, b0, b1, b2, inv_ref, out_ref):
    left = a0[...].astype(F32) + a1[...].astype(F32) + a2[...].astype(F32)
    right = b0[...].astype(F32) + b1[...].astype(F32) + b2[...].astype(F32)
    out_ref[...] = (
        exact(left, inv_ref[:, :HALF], 1, 1) + exact(right, inv_ref[:, HALF:], 1, 1)
    ).astype(BF16)


def solve_rows(terms, inverse):
    return pl.pallas_call(
        solve_kernel,
        out_shape=jax.ShapeDtypeStruct((terms[0].shape[0], RANK), BF16),
        in_specs=[vmem_spec()] * 7,
        out_specs=vmem_spec(),
        compiler_params=params(),
        name="solve_rows",
    )(*terms, inverse)


def ortho_kernel(meta_ref, mine_ref, other_ref, inv_ref, out_ref):
    core = meta_ref[0]
    for ref, place in ((mine_ref, core), (other_ref, 1 - core)):
        rows = pl.ds(pl.multiple_of(place * HALF, HALF), HALF)
        out_ref[rows, :] = exact(ref[...], inv_ref[...], 1, 1).astype(BF16)


def ortho_left(meta, mine, other, inverse):
    return pl.pallas_call(
        ortho_kernel,
        out_shape=jax.ShapeDtypeStruct((RANK, RANK), BF16),
        in_specs=[smem_spec()] + [vmem_spec()] * 3,
        out_specs=vmem_spec(),
        compiler_params=params(),
        name="ortho_left",
    )(meta, mine, other, inverse)


def apply_kernel(parts, meta_ref, b_ref, q_ref, sums_ref, *refs):
    rights, (m_ref, u_ref, scaled) = refs[:parts], refs[-3:]
    scale = lax.rsqrt(sums_ref[0:1, :] + 1e-6) * math.sqrt(D * F / RANK)
    scaled[...] = (q_ref[...].astype(F32) * scale).astype(BF16)
    width = RANK // parts
    feedback = direction = 0.0
    for k, right in enumerate(rights):
        cols = slice(k * width, (k + 1) * width)
        feedback += dot(q_ref[:, cols], right[...], 1, 1)
        direction += dot(scaled[:, cols], right[...], 1, 1)
    m_ref[...] = (b_ref[...].astype(F32) - 0.05 * feedback).astype(BF16)
    u_ref[...] = direction.astype(BF16)


def apply_block(meta, blended, q, sums, rights, offset, outs):
    rows, cols = blended.shape
    block = cols // 4
    here = pl.BlockSpec((rows, block), lambda i, meta_ref: (0, (meta_ref[3] + offset) % 4))
    whole = lambda a: pl.BlockSpec(a.shape, lambda i, meta_ref: (0, 0))
    n = len(rights)
    shape = jax.ShapeDtypeStruct((rows, cols), BF16)
    kept = [pl.BlockSpec(memory_space=pl.ANY)] * len(outs)
    return pl.pallas_call(
        functools.partial(apply_kernel, n),
        grid_spec=pltpu.PrefetchScalarGridSpec(
            num_scalar_prefetch=1,
            grid=(1,),
            in_specs=[here, whole(q), whole(sums)] + [whole(r) for r in rights] + kept,
            out_specs=[here, here],
            scratch_shapes=[pltpu.VMEM((rows, RANK), BF16)],
        ),
        out_shape=[shape, shape],
        input_output_aliases={4 + n + k: k for k in range(len(outs))},
        compiler_params=params(),
        name="apply_block",
    )(meta, blended, q, sums, *rights, *outs)


def sums_kernel(r_ref, out_ref):
    r = r_ref[...].astype(F32)
    out_ref[...] = jnp.broadcast_to(jnp.sum(r * r, axis=0, keepdims=True), out_ref.shape)


def block_sums(r):
    return pl.pallas_call(
        sums_kernel,
        out_shape=jax.ShapeDtypeStruct((16, RANK), F32),
        in_specs=[vmem_spec()],
        out_specs=vmem_spec(),
        compiler_params=params(),
        name="block_sums",
    )(r)


def per_device(momentum, gradient, seed_value):
    fsdp, tp = lax.axis_index("fsdp"), lax.axis_index("tp")
    core, x, y = tp % 2, fsdp % 4, fsdp // 4
    first, second = jnp.where(core == 0, x, y), jnp.where(core == 0, y, x)
    meta = jnp.stack([core, tp, seed_value[0], first, second]).astype(jnp.int32)

    blended, keep, send = left_partial(meta, momentum, gradient)
    half = keep + swap_cores(send)
    pieces = exchange(half, "tp", Z_GROUPS)
    piece = jnp.sum(pieces.reshape(4, HALF // 4, RANK), axis=0)
    mine = exchange(jnp.tile(piece, (4, 1)), "tp", Z_GROUPS)
    other = swap_cores(mine)

    gram = gram_half(meta, mine, other)

    far_a, far_b = right_partial(meta, blended, mine, other, (2,))
    from_low_a = send_first(far_a, 1)
    from_high_b = send_first(far_b, -1)
    next_a, next_b, prev_a, prev_b, own_a, own_b = right_partial(
        meta, blended, mine, other, (1, 3, 0)
    )
    own_b_low = send_first(next_b, 1)
    own_a_high = send_first(prev_a, -1)
    next_a, prev_b = add_pairs(next_a, from_low_a, prev_b, from_high_b)
    own_a_low = send_first(next_a, 1)
    own_b_high = send_first(prev_b, -1)
    cut = add_and_split(meta, (own_a, own_a_low, own_a_high, own_b, own_b_low, own_b_high))
    far_a, far_b, next_a, next_b, prev_a, prev_b, own_a, own_b = cut
    from_low_a = send_second(far_a, 1)
    from_high_b = send_second(far_b, -1)
    own_b_low = send_second(next_b, 1)
    own_a_high = send_second(prev_a, -1)
    next_a, prev_b = add_pairs(next_a, from_low_a, prev_b, from_high_b)
    own_a_low = send_second(next_a, 1)
    own_b_high = send_second(prev_b, -1)

    gram = exchange(gram, "fsdp")
    gram = jnp.sum(gram.reshape(16, RANK // 16, HALF), axis=0)
    gram = exchange(jnp.tile(gram, (16, 1)), "fsdp")
    inverse = inverse_factor(meta, gram, swap_cores(gram))

    block = solve_rows((own_a, own_a_low, own_a_high, own_b, own_b_low, own_b_high), inverse)
    right = exchange(jnp.tile(block, (4, 1)), AXES, SECOND_GROUPS)
    right_low = send_first(right, 1)
    right_high = send_first(right, -1)
    q = ortho_left(meta, mine, other, inverse)
    sums = exchange(block_sums(right), AXES, FIRST_Z_GROUPS)
    sums = jnp.sum(sums, axis=0, keepdims=True)
    sums = jnp.broadcast_to(sums + swap_cores(sums), (8, RANK))
    far_a = send_first(right_low[:, :HALF], 1)
    far_b = send_first(right_high[:, HALF:], -1)
    outs = apply_block(meta, blended, q, sums, [right], 0, [])
    outs = apply_block(meta, blended, q, sums, [right_low], 3, outs)
    outs = apply_block(meta, blended, q, sums, [right_high], 1, outs)
    outs = apply_block(meta, blended, q, sums, [far_a, far_b], 2, outs)
    return tuple(outs)


def solution(mesh):
    return jax.shard_map(
        per_device,
        mesh=mesh,
        in_specs=(P("fsdp", "tp"), P("fsdp", "tp"), P()),
        out_specs=(P("fsdp", "tp"), P("fsdp", "tp")),
        check_vma=False,
    )
```

time: 515 us -> 208 us (0.40); the launches traced: 509 us -> 207 us
  waiting for transfers between devices: 282 us -> 17.7 us
  other arithmetic: 124 us -> 1.24 us
  Pallas kernels: 0 us -> 70.3 us
  matrix products: 59.3 us -> 0 us
  blocking collectives: 12.8 us -> 66.4 us
  starting transfers between devices: 0.65 us -> 41.1 us
  between operations: 17.5 us -> 1.52 us
    psum x3 -> x0, waiting for transfers between devices: 282 us -> none  [the longest x1 132 us: per_device(): right_factor = lax.psum(partial_right, 'fsdp')]
    another operation x17 -> x0, other arithmetic: 119 us -> none  [the longest x14 78.6 us: per_device(): lower_factor = jnp.linalg.cholesky(gram_whole)]
    pallas_call x0 -> x15, Pallas kernels: none -> 70.3 us  [the longest x1 21.8 us: inverse_factor(): pl.pallas_call(inverse_kernel, out_shape=jax.ShapeDtypeStruct((RANK, RANK...]
    all_to_all x0 -> x5, blocking collectives: none -> 66.4 us  [exchange(): return lax.all_to_all(a, axis, 0, 0, axis_index_groups=groups, tiled=True)]
    dot_general x5 -> x0, matrix products: 51 us -> none  [the longest x1 25.9 us: per_device(): jnp.dot(blended, start_rows, preferred_element_type=jnp.float32)]
    ppermute x0 -> x20, starting transfers between devices: none -> 35.6 us  [the longest x4 16.6 us: swap_cores(): return lax.ppermute(a, 'tp', [(i, i ^ 1) for i in range(8)])]
    ppermute x0 -> x20, waiting for transfers between devices: none -> 17.7 us  [the longest x10 11.1 us: send_first(): return lax.ppermute(a, AXES, shift(True, step))]
    psum x1 -> x0, blocking collectives: 12.8 us -> none  [per_device(): square_sums = lax.psum(jnp.sum(right_factor * right_factor, axis=0), 'tp')]
  transfers between devices with their start and end apart: 3 -> 21, of which waited for: 3 -> 5; matrix products, arithmetic and copies ran while one was open for 0% -> 1% of each run, Pallas kernels for 0% -> 22%
where the time goes in v1:
time: 208 us; the launch traced here: 207 us
  Pallas kernels  70.3 us (34%)
  blocking collectives  66.4 us (32%)
  starting transfers between devices  41.1 us (20%)
  waiting for transfers between devices  17.7 us (9%)
  local copies, waits for them, and re-layouts  9.12 us (4%)
    all_to_all x5, blocking collectives, exchange(): return lax.all_to_all(a, axis, 0, 0, axis_index_groups=groups, tiled=True)  66.4 us
    pallas_call x1, Pallas kernels, inverse_factor(): pl.pallas_call(inverse_kernel, out_shape=jax.ShapeDtypeStruct((RANK, RANK...  21.8 us
    ppermute x4, starting transfers between devices, swap_cores(): return lax.ppermute(a, 'tp', [(i, i ^ 1) for i in range(8)])  16.6 us
    pallas_call x1, Pallas kernels, left_partial(): pl.pallas_call(left_kernel, grid=(cols // TILE,), out_shape=(jax.ShapeDty...  14.8 us
    ppermute x10, starting transfers between devices, send_first(): return lax.ppermute(a, AXES, shift(True, step))  13.3 us
    pallas_call x4, Pallas kernels, apply_block(): pl.pallas_call(functools.partial(apply_kernel, n), grid_spec=pltpu.Prefet...  12.2 us
    pallas_call x2, Pallas kernels, right_partial(): pl.pallas_call(functools.partial(right_kernel, offsets), grid_spec=pltpu....  11.7 us
    ppermute x10, waiting for transfers between devices, send_first(): return lax.ppermute(a, AXES, shift(True, step))  11.1 us
  transfers between devices with their start and end apart: 21, of which 5 were waited for; matrix products, arithmetic and copies ran while one was open for 1% of the time, Pallas kernels for 22%

profile of v1, /device:TPU:1, one launch (start us, length us, event | category | flops | bytes accessed | tf_op | source)
XLA Modules:
  0.0 207.5 jit_solution(18069769613082350932)
XLA Ops:
  1.3 0.1 stack.19.meta_ref
  1.4 14.8 %left_partial.1 = (bf16[512,3584]{1,0:T(8,128)(2,1)S(1)}, f32[256,512]{1,0:T(8,128)S(1)}, f32[256,512]{1,0:T(8,128)S(1)}) custom-call(s32[5]{0:T(128)S(1)} %stack.19.meta_ref, bf16[512,3584]{1,0:T(8,128)(2,1)} %m_ref.1, bf16[512,3584]{1,0:T(8,128)(2,1)} %g_ref.1), custom_call_target="tpu_custom_call" | custom-call | tf_op jit(solution)/shard_map/left_partial/pallas_call | solution.py:140
  16.2 0.0 copy-start
  16.2 1.8 copy-done
  18.0 1.4 collective-permute-start
  19.4 1.5 collective-permute-done
  21.0 0.1 add.16
  21.1 13.5 %all_to_all.51 = f32[4,64,512]{2,1,0:T(8,128)S(1)} all-to-all(f32[4,64,512]{2,1,0:T(8,128)S(1)} %bitcast.24), channel_id=1, replica_groups={{0,2,4,6},{1,3,5,7},{8,10,12,14},{9,11,13,15},{16,18,20,22},{17,19,21,2..., dimensions={0} | all-to-all | bytes 1048576 | tf_op jit(solution)/shard_map/all_to_all | solution.py:65
  34.6 0.1 tile.6
  34.7 10.1 %all_to_all.52 = f32[4,64,512]{2,1,0:T(8,128)S(1)} all-to-all(f32[4,64,512]{2,1,0:T(8,128)S(1)} %tile.6), channel_id=1, replica_groups={{0,2,4,6},{1,3,5,7},{8,10,12,14},{9,11,13,15},{16,18,20,22},{17,19,21,2..., dimensions={0} | all-to-all | bytes 1048576 | tf_op jit(solution)/shard_map/all_to_all | solution.py:65
  44.8 2.7 %collective-permute-start.1 = (f32[256,512]{1,0:T(8,128)S(1)}, f32[256,512]{1,0:T(8,128)S(1)}, u32[]{:S(2)}, u32[]{:S(2)}) collective-permute-start(f32[256,512]{1,0:T(8,128)S(1)} %bitcast.12), channel_id=1, source_target_pairs={{0,1},{1,0},{2,3},{3,2},{4,5},{5,4},{6,7},{7,6},{8,9},{9,8},{10,11... | collective-permute-start | bytes 1572872 | tf_op jit(solution)/shard_map/ppermute | solution.py:52
  47.5 1.5 collective-permute-done.1.other_ref
  49.1 4.4 %right_partial.3 = (f32[896,256]{1,0:T(8,128)}, f32[896,256]{1,0:T(8,128)}) custom-call(s32[5]{0:T(128)S(1)} %stack.19.meta_ref, bf16[512,3584]{1,0:T(8,128)(2,1)} %copy-done, f32[256,512]{1,0:T(8,128)S(1)} %bitcast.13, f32[256,512]{1,0:T(8,128)S(1)} %collective-permute-done.1.other_ref), custom_call_target="tpu_custom_call" | custom-call | tf_op jit(solution)/shard_map/right_partial/pallas_call | solution.py:206
  53.5 1.3 collective-permute-start.3
  54.7 1.4 collective-permute-start.4
  56.2 2.6 %gram_half.1 = f32[512,256]{1,0:T(8,128)} custom-call(s32[5]{0:T(128)S(1)} %stack.19.meta_ref, f32[256,512]{1,0:T(8,128)S(1)} %bitcast.14, f32[256,512]{1,0:T(8,128)S(1)} %collective-permute-done.1.other_ref), custom_call_target="tpu_custom_call" | custom-call | tf_op jit(solution)/shard_map/gram_half/pallas_call | solution.py:160
  58.8 5.5 %all-to-all-start.2 = ((f32[16,32,256]{2,1,0:T(8,128)}), f32[16,32,256]{2,1,0:T(8,128)}, u32[]{:S(2)}, u32[]{:S(2)}) async-start(f32[16,32,256]{2,1,0:T(8,128)} %bitcast.6), calls=%async_computation.2 | async-start | bytes 1048576 | tf_op jit(solution)/shard_map/all_to_all | solution.py:65
  64.3 7.3 %right_partial.2 = (f32[896,256]{1,0:T(8,128)S(1)}, f32[896,256]{1,0:T(8,128)}, f32[896,256]{1,0:T(8,128)}, f32[896,256]{1,0:T(8,128)S(1)}, f32[896,256]{1,0:T(8,128)S(1)}, /*index=5*/f32[896,256]{1,0:T(8,128)}) custom-call(s32[5]{0:T(128)S(1)} %stack.19.meta_ref, bf16[512,3584]{1,0:T(8,128)(2,1)} %copy-done, f32[256,512]{1,0:T(8,128)S(1)} %bitcast.15, ...), custom_call_target="tpu_custom_call" | custom-call | tf_op jit(solution)/shard_map/right_partial/pallas_call | solution.py:206
  71.7 2.5 %collective-permute-start.6 = (f32[896,256]{1,0:T(8,128)}, f32[896,256]{1,0:T(8,128)}, u32[]{:S(2)}, u32[]{:S(2)}) collective-permute-start(f32[896,256]{1,0:T(8,128)} %get-tuple-element.40), channel_id=1, source_target_pairs={{0,24},{1,97},{2,26},{3,99},{4,28},{5,101},{6,30},{7,103},{8,0},{9... | collective-permute-start | bytes 2752520 | tf_op jit(solution)/shard_map/ppermute | solution.py:44
  74.2 0.0 collective-permute-done.4.d_ref
  74.2 1.4 add_pairs.2
  75.6 0.2 collective-permute-start.5
  75.9 2.4 %collective-permute-start.8 = (f32[896,256]{1,0:T(8,128)}, f32[896,256]{1,0:T(8,128)}, u32[]{:S(2)}, u32[]{:S(2)}) collective-permute-start(f32[896,256]{1,0:T(8,128)} %get-tuple-element.43), channel_id=1, source_target_pairs={{0,24},{1,97},{2,26},{3,99},{4,28},{5,101},{6,30},{7,103},{8,0},{9... | collective-permute-start | bytes 2752520 | tf_op jit(solution)/shard_map/ppermute | solution.py:44
  78.3 0.0 all-to-all-done.2
  78.3 1.1 reduce_sum.28
  79.5 22.0 %all_to_all.53 = f32[16,32,256]{2,1,0:T(8,128)S(1)} all-to-all(f32[16,32,256]{2,1,0:T(8,128)S(1)} %tile.7), channel_id=1, replica_groups=mesh['fsdp'=16,'tp'=8] {'fsdp'}, dimensions={0} | all-to-all | bytes 1048576 | tf_op jit(solution)/shard_map/all_to_all | solution.py:65
  101.5 6.4 %collective-permute-start.2 = (f32[512,256]{1,0:T(8,128)S(1)}, f32[512,256]{1,0:T(8,128)S(1)}, u32[]{:S(2)}, u32[]{:S(2)}) collective-permute-start(f32[512,256]{1,0:T(8,128)S(1)} %bitcast.21), channel_id=1, source_target_pairs={{0,1},{1,0},{2,3},{3,2},{4,5},{5,4},{6,7},{7,6},{8,9},{9,8},{10,11... | collective-permute-start | bytes 1572872 | tf_op jit(solution)/shard_map/ppermute | solution.py:52
  107.9 0.0 collective-permute-done.6.refs_2_
  107.9 0.0 collective-permute-done.7.refs_4_
  108.0 0.0 collective-permute-done.8.refs_5_
  108.0 1.2 copy-done.7
  109.1 1.2 copy-done.8
  110.3 2.0 add_and_split.1
  112.3 0.2 collective-permute-start.10
  112.5 1.4 collective-permute-start.9
  113.9 1.3 collective-permute-start.12
  115.2 0.1 collective-permute-start.13
  115.3 2.2 %collective-permute-done.10.d_ref = f32[224,256]{1,0:T(8,128)S(1)} collective-permute-done((f32[224,256]{1,0:T(8,128)S(1)}, f32[224,256]{1,0:T(8,128)S(1)}, u32[]{:S(2)}, u32[]{:S(2)}) %collective-permute-start.10) | collective-permute-done | bytes 229408 | tf_op jit(solution)/shard_map/ppermute | solution.py:48
  117.6 1.3 collective-permute-done.9.b_ref
  119.0 0.2 collective-permute-start.11
  119.2 2.5 %collective-permute-start.14 = (f32[224,256]{1,0:T(8,128)S(1)}, f32[224,256]{1,0:T(8,128)S(1)}, u32[]{:S(2)}, u32[]{:S(2)}) collective-permute-start(f32[224,256]{1,0:T(8,128)S(1)} %get-tuple-element.53), channel_id=1, source_target_pairs={{0,96},{1,25},{2,98},{3,27},{4,100},{5,29},{6,102},{7,31},{8,104},... | collective-permute-start | bytes 688136 | tf_op jit(solution)/shard_map/ppermute | solution.py:48
  121.7 0.0 collective-permute-done.2.other_ref
  121.7 21.8 %inverse_factor.1.inv_ref = f32[512,512]{1,0:T(8,128)S(1)} custom-call(s32[5]{0:T(128)S(1)} %stack.19.meta_ref, f32[512,256]{1,0:T(8,128)S(1)} %bitcast.22, f32[512,256]{1,0:T(8,128)S(1)} %collective-permute-done.2.other_ref), custom_call_target="tpu_custom_call" | custom-call | tf_op jit(solution)/shard_map/inverse_factor/pallas_call | solution.py:309
  143.5 0.0 collective-permute-done.13.b1
  143.5 0.0 collective-permute-done.11.a1
  143.6 1.2 solve_rows.1
  144.7 0.1 tile.8
  144.8 11.8 %all_to_all.54 = bf16[4,224,512]{2,1,0:T(8,128)(2,1)S(1)} all-to-all(bf16[4,224,512]{2,1,0:T(8,128)(2,1)S(1)} %tile.8), channel_id=1, replica_groups={{0,32,64,96},{2,34,66,98},{4,36,68,100},{6,38,70,102},{8,40,72,104},{10..., dimensions={0} | all-to-all | bytes 1835008 | tf_op jit(solution)/shard_map/all_to_all | solution.py:65
  156.6 2.7 %collective-permute-start.18 = (bf16[896,512]{1,0:T(8,128)(2,1)S(1)}, bf16[896,512]{1,0:T(8,128)(2,1)S(1)}, u32[]{:S(2)}, u32[]{:S(2)}) collective-permute-start(bf16[896,512]{1,0:T(8,128)(2,1)S(1)} %bitcast.18), channel_id=1, source_target_pairs={{0,24},{1,97},{2,26},{3,99},{4,28},{5,101},{6,30},{7,103},{8,0},{9... | collective-permute-start | bytes 2752520 | tf_op jit(solution)/shard_map/ppermute | solution.py:44
  159.2 11.1 %collective-permute-done.16.refs_0_ = bf16[896,512]{1,0:T(8,128)(2,1)S(1)} collective-permute-done((bf16[896,512]{1,0:T(8,128)(2,1)S(1)}, bf16[896,512]{1,0:T(8,128)(2,1)S(1)}, u32[]{:S(2)}, u32[]{:S(2)}) %collective-permute-start.16) | collective-permute-done | bytes 917536 | tf_op jit(solution)/shard_map/ppermute | solution.py:44
  170.3 0.9 slice.8
  171.2 0.8 slice.9
  172.0 0.9 copy-done.2
  172.9 2.7 %collective-permute-start.19 = (bf16[896,256]{1,0:T(8,128)(2,1)}, bf16[896,256]{1,0:T(8,128)(2,1)}, u32[]{:S(2)}, u32[]{:S(2)}) collective-permute-start(bf16[896,256]{1,0:T(8,128)(2,1)} %slice.9), channel_id=1, source_target_pairs={{0,24},{1,97},{2,26},{3,99},{4,28},{5,101},{6,30},{7,103},{8,0},{9... | collective-permute-start | bytes 1376264 | tf_op jit(solution)/shard_map/ppermute | solution.py:44
  175.6 0.1 block_sums.1
  175.7 9.0 %all_to_all.55 = f32[16,1,512]{2,1,0:T(1,128)S(1)} all-to-all(f32[16,1,512]{2,1,0:T(1,128)S(1)} %copy.11), channel_id=1, replica_groups={{0,2,4,6,8,10,12,14,16,18,20,22,24,26,28,30},{32,34,36,38,40,42,44,46,4..., dimensions={0} | all-to-all | bytes 65536 | tf_op jit(solution)/shard_map/all_to_all | solution.py:65
  184.8 6.0 %collective-permute-start.15 = (f32[1,512]{1,0:T(1,128)S(1)}, f32[1,512]{1,0:T(1,128)S(1)}, u32[]{:S(2)}, u32[]{:S(2)}) collective-permute-start(f32[1,512]{1,0:T(1,128)S(1)} %bitcast.25), channel_id=1, source_target_pairs={{0,1},{1,0},{2,3},{3,2},{4,5},{5,4},{6,7},{7,6},{8,9},{9,8},{10,11... | collective-permute-start | bytes 6152 | tf_op jit(solution)/shard_map/ppermute | solution.py:52
  190.8 2.4 %ortho_left.1.q_ref = bf16[512,512]{1,0:T(8,128)(2,1)S(1)} custom-call(s32[5]{0:T(128)S(1)} %stack.19.meta_ref, f32[256,512]{1,0:T(8,128)S(1)} %bitcast.16, f32[256,512]{1,0:T(8,128)S(1)} %collective-permute-done.1.other_ref, f32[512,512]{1,0:T(8,128)S(1)} %inverse_factor.1.inv_ref), custom_call_target="tpu_custom_call" | custom-call | tf_op jit(solution)/shard_map/ortho_left/pallas_call | solution.py:347
  193.2 0.0 copy-start.1
  193.3 2.0 copy-done.1
  195.3 2.8 %apply_block.4 = (bf16[512,3584]{1,0:T(8,128)(2,1)}, bf16[512,3584]{1,0:T(8,128)(2,1)}) custom-call(s32[5]{0:T(128)S(1)} %stack.19.meta_ref, bf16[512,3584]{1,0:T(8,128)(2,1)S(1)} %copy-done.1, bf16[512,512]{1,0:T(8,128)(2,1)S(1)} %ortho_left.1.q_ref, f32[8,512]{1,0:T(8,128)S(1)} %broadcast_in_dim.12.sums_ref, bf16[896,512]{1,0:T(8,128)(2,1)S(1)} %bitcast.20), custom_call_target="tpu_custom_call" | custom-call | tf_op jit(solution)/shard_map/apply_block/pallas_call | solution.py:379
  198.1 2.8 %apply_block.5 = (bf16[512,3584]{1,0:T(8,128)(2,1)}, bf16[512,3584]{1,0:T(8,128)(2,1)}) custom-call(s32[5]{0:T(128)S(1)} %stack.19.meta_ref, bf16[512,3584]{1,0:T(8,128)(2,1)S(1)} %copy-done.1, bf16[512,512]{1,0:T(8,128)(2,1)S(1)} %ortho_left.1.q_ref, f32[8,512]{1,0:T(8,128)S(1)} %broadcast_in_dim.12.sums_ref, ...), custom_call_target="tpu_custom_call", output_to_operand_aliasing={{0}: (5, {}), {1}: (6, {})} | custom-call | tf_op jit(solution)/shard_map/apply_block/pallas_call | solution.py:379
  200.9 2.8 %apply_block.6 = (bf16[512,3584]{1,0:T(8,128)(2,1)}, bf16[512,3584]{1,0:T(8,128)(2,1)}) custom-call(s32[5]{0:T(128)S(1)} %stack.19.meta_ref, bf16[512,3584]{1,0:T(8,128)(2,1)S(1)} %copy-done.1, bf16[512,512]{1,0:T(8,128)(2,1)S(1)} %ortho_left.1.q_ref, f32[8,512]{1,0:T(8,128)S(1)} %broadcast_in_dim.12.sums_ref, ...), custom_call_target="tpu_custom_call", output_to_operand_aliasing={{0}: (5, {}), {1}: (6, {})} | custom-call | tf_op jit(solution)/shard_map/apply_block/pallas_call | solution.py:379
  203.7 3.8 %apply_block.7 = (bf16[512,3584]{1,0:T(8,128)(2,1)}, bf16[512,3584]{1,0:T(8,128)(2,1)}) custom-call(s32[5]{0:T(128)S(1)} %stack.19.meta_ref, bf16[512,3584]{1,0:T(8,128)(2,1)S(1)} %copy-done.1, bf16[512,512]{1,0:T(8,128)(2,1)S(1)} %ortho_left.1.q_ref, f32[8,512]{1,0:T(8,128)S(1)} %broadcast_in_dim.12.sums_ref, ...), custom_call_target="tpu_custom_call", output_to_operand_aliasing={{0}: (6, {}), {1}: (7, {})} | custom-call | tf_op jit(solution)/shard_map/apply_block/pallas_call | solution.py:379
  (29 shorter events, 0.3 us)
Async XLA Ops:
  16.2 1.8 copy-start
  18.0 3.0 %collective-permute-start = (f32[256,512]{1,0:T(8,128)S(1)}, f32[256,512]{1,0:T(8,128)S(1)}, u32[]{:S(2)}, u32[]{:S(2)}) collective-permute-start(f32[256,512]{1,0:T(8,128)S(1)} %get-tuple-element.33), channel_id=1, source_target_pairs={{0,1},{1,0},{2,3},{3,2},{4,5},{5,4},{6,7},{7,6},{8,9},{9,8},{10,11... | collective-permute-start | bytes 1572872 | tf_op jit(solution)/shard_map/ppermute | solution.py:52
  44.8 4.3 %collective-permute-start.1 = (f32[256,512]{1,0:T(8,128)S(1)}, f32[256,512]{1,0:T(8,128)S(1)}, u32[]{:S(2)}, u32[]{:S(2)}) collective-permute-start(f32[256,512]{1,0:T(8,128)S(1)} %bitcast.12), channel_id=1, source_target_pairs={{0,1},{1,0},{2,3},{3,2},{4,5},{5,4},{6,7},{7,6},{8,9},{9,8},{10,11... | collective-permute-start | bytes 1572872 | tf_op jit(solution)/shard_map/ppermute | solution.py:52
  53.5 20.8 %collective-permute-start.3 = (f32[896,256]{1,0:T(8,128)}, f32[896,256]{1,0:T(8,128)S(1)}, u32[]{:S(2)}, u32[]{:S(2)}) collective-permute-start(f32[896,256]{1,0:T(8,128)} %get-tuple-element.36), channel_id=1, source_target_pairs={{0,8},{1,33},{2,10},{3,35},{4,12},{5,37},{6,14},{7,39},{8,16},{9,4... | collective-permute-start | bytes 2752520 | tf_op jit(solution)/shard_map/ppermute | solution.py:44
  54.7 19.5 %collective-permute-start.4 = (f32[896,256]{1,0:T(8,128)}, f32[896,256]{1,0:T(8,128)S(1)}, u32[]{:S(2)}, u32[]{:S(2)}) collective-permute-start(f32[896,256]{1,0:T(8,128)} %get-tuple-element.38), channel_id=1, source_target_pairs={{0,24},{1,97},{2,26},{3,99},{4,28},{5,101},{6,30},{7,103},{8,0},{9... | collective-permute-start | bytes 2752520 | tf_op jit(solution)/shard_map/ppermute | solution.py:44
  58.8 19.5 %all-to-all-start.2 = ((f32[16,32,256]{2,1,0:T(8,128)}), f32[16,32,256]{2,1,0:T(8,128)}, u32[]{:S(2)}, u32[]{:S(2)}) async-start(f32[16,32,256]{2,1,0:T(8,128)} %bitcast.6), calls=%async_computation.2 | async-start | bytes 1048576 | tf_op jit(solution)/shard_map/all_to_all | solution.py:65
  71.7 4.0 %copy-start.6 = (f32[896,256]{1,0:T(8,128)}, f32[896,256]{1,0:T(8,128)S(1)}, u32[]{:S(2)}) copy-start(f32[896,256]{1,0:T(8,128)S(1)} %get-tuple-element.34.refs_0_) | copy-start | bytes 2752516
  71.7 36.3 %collective-permute-start.6 = (f32[896,256]{1,0:T(8,128)}, f32[896,256]{1,0:T(8,128)}, u32[]{:S(2)}, u32[]{:S(2)}) collective-permute-start(f32[896,256]{1,0:T(8,128)} %get-tuple-element.40), channel_id=1, source_target_pairs={{0,24},{1,97},{2,26},{3,99},{4,28},{5,101},{6,30},{7,103},{8,0},{9... | collective-permute-start | bytes 2752520 | tf_op jit(solution)/shard_map/ppermute | solution.py:44
  74.2 33.7 %collective-permute-start.7 = (f32[896,256]{1,0:T(8,128)}, f32[896,256]{1,0:T(8,128)}, u32[]{:S(2)}, u32[]{:S(2)}) collective-permute-start(f32[896,256]{1,0:T(8,128)} %get-tuple-element.42), channel_id=1, source_target_pairs={{0,8},{1,33},{2,10},{3,35},{4,12},{5,37},{6,14},{7,39},{8,16},{9,4... | collective-permute-start | bytes 2752520 | tf_op jit(solution)/shard_map/ppermute | solution.py:44
  75.6 32.3 %collective-permute-start.5 = (f32[896,256]{1,0:T(8,128)}, f32[896,256]{1,0:T(8,128)S(1)}, u32[]{:S(2)}, u32[]{:S(2)}) collective-permute-start(f32[896,256]{1,0:T(8,128)} %get-tuple-element.39), channel_id=1, source_target_pairs={{0,8},{1,33},{2,10},{3,35},{4,12},{5,37},{6,14},{7,39},{8,16},{9,4... | collective-permute-start | bytes 2752520 | tf_op jit(solution)/shard_map/ppermute | solution.py:44
  75.9 32.1 %collective-permute-start.8 = (f32[896,256]{1,0:T(8,128)}, f32[896,256]{1,0:T(8,128)}, u32[]{:S(2)}, u32[]{:S(2)}) collective-permute-start(f32[896,256]{1,0:T(8,128)} %get-tuple-element.43), channel_id=1, source_target_pairs={{0,24},{1,97},{2,26},{3,99},{4,28},{5,101},{6,30},{7,103},{8,0},{9... | collective-permute-start | bytes 2752520 | tf_op jit(solution)/shard_map/ppermute | solution.py:44
  101.5 20.2 %collective-permute-start.2 = (f32[512,256]{1,0:T(8,128)S(1)}, f32[512,256]{1,0:T(8,128)S(1)}, u32[]{:S(2)}, u32[]{:S(2)}) collective-permute-start(f32[512,256]{1,0:T(8,128)S(1)} %bitcast.21), channel_id=1, source_target_pairs={{0,1},{1,0},{2,3},{3,2},{4,5},{5,4},{6,7},{7,6},{8,9},{9,8},{10,11... | collective-permute-start | bytes 1572872 | tf_op jit(solution)/shard_map/ppermute | solution.py:52
  108.0 1.2 copy-start.7
  109.1 1.2 copy-start.8
  112.3 5.2 %collective-permute-start.10 = (f32[224,256]{1,0:T(8,128)S(1)}, f32[224,256]{1,0:T(8,128)S(1)}, u32[]{:S(2)}, u32[]{:S(2)}) collective-permute-start(f32[224,256]{1,0:T(8,128)S(1)} %get-tuple-element.48), channel_id=1, source_target_pairs={{0,96},{1,25},{2,98},{3,27},{4,100},{5,29},{6,102},{7,31},{8,104},... | collective-permute-start | bytes 688136 | tf_op jit(solution)/shard_map/ppermute | solution.py:48
  112.5 6.4 %collective-permute-start.9 = (f32[224,256]{1,0:T(8,128)S(1)}, f32[224,256]{1,0:T(8,128)S(1)}, u32[]{:S(2)}, u32[]{:S(2)}) collective-permute-start(f32[224,256]{1,0:T(8,128)S(1)} %get-tuple-element.46), channel_id=1, source_target_pairs={{0,32},{1,9},{2,34},{3,11},{4,36},{5,13},{6,38},{7,15},{8,40},{9,1... | collective-permute-start | bytes 688136 | tf_op jit(solution)/shard_map/ppermute | solution.py:48
  113.9 29.6 %collective-permute-start.12 = (f32[224,256]{1,0:T(8,128)S(1)}, f32[224,256]{1,0:T(8,128)S(1)}, u32[]{:S(2)}, u32[]{:S(2)}) collective-permute-start(f32[224,256]{1,0:T(8,128)S(1)} %get-tuple-element.50), channel_id=1, source_target_pairs={{0,96},{1,25},{2,98},{3,27},{4,100},{5,29},{6,102},{7,31},{8,104},... | collective-permute-start | bytes 688136 | tf_op jit(solution)/shard_map/ppermute | solution.py:48
  115.2 28.3 %collective-permute-start.13 = (f32[224,256]{1,0:T(8,128)S(1)}, f32[224,256]{1,0:T(8,128)S(1)}, u32[]{:S(2)}, u32[]{:S(2)}) collective-permute-start(f32[224,256]{1,0:T(8,128)S(1)} %get-tuple-element.52), channel_id=1, source_target_pairs={{0,32},{1,9},{2,34},{3,11},{4,36},{5,13},{6,38},{7,15},{8,40},{9,1... | collective-permute-start | bytes 688136 | tf_op jit(solution)/shard_map/ppermute | solution.py:48
  119.0 24.6 %collective-permute-start.11 = (f32[224,256]{1,0:T(8,128)S(1)}, f32[224,256]{1,0:T(8,128)S(1)}, u32[]{:S(2)}, u32[]{:S(2)}) collective-permute-start(f32[224,256]{1,0:T(8,128)S(1)} %get-tuple-element.49), channel_id=1, source_target_pairs={{0,32},{1,9},{2,34},{3,11},{4,36},{5,13},{6,38},{7,15},{8,40},{9,1... | collective-permute-start | bytes 688136 | tf_op jit(solution)/shard_map/ppermute | solution.py:48
  119.2 24.4 %collective-permute-start.14 = (f32[224,256]{1,0:T(8,128)S(1)}, f32[224,256]{1,0:T(8,128)S(1)}, u32[]{:S(2)}, u32[]{:S(2)}) collective-permute-start(f32[224,256]{1,0:T(8,128)S(1)} %get-tuple-element.53), channel_id=1, source_target_pairs={{0,96},{1,25},{2,98},{3,27},{4,100},{5,29},{6,102},{7,31},{8,104},... | collective-permute-start | bytes 688136 | tf_op jit(solution)/shard_map/ppermute | solution.py:48
  156.6 13.8 %collective-permute-start.16 = (bf16[896,512]{1,0:T(8,128)(2,1)S(1)}, bf16[896,512]{1,0:T(8,128)(2,1)S(1)}, u32[]{:S(2)}, u32[]{:S(2)}) collective-permute-start(bf16[896,512]{1,0:T(8,128)(2,1)S(1)} %bitcast.17), channel_id=1, source_target_pairs={{0,8},{1,33},{2,10},{3,35},{4,12},{5,37},{6,14},{7,39},{8,16},{9,4... | collective-permute-start | bytes 2752520 | tf_op jit(solution)/shard_map/ppermute | solution.py:44
  156.6 14.6 %collective-permute-start.18 = (bf16[896,512]{1,0:T(8,128)(2,1)S(1)}, bf16[896,512]{1,0:T(8,128)(2,1)S(1)}, u32[]{:S(2)}, u32[]{:S(2)}) collective-permute-start(bf16[896,512]{1,0:T(8,128)(2,1)S(1)} %bitcast.18), channel_id=1, source_target_pairs={{0,24},{1,97},{2,26},{3,99},{4,28},{5,101},{6,30},{7,103},{8,0},{9... | collective-permute-start | bytes 2752520 | tf_op jit(solution)/shard_map/ppermute | solution.py:44
  170.3 1.7 copy-start.4
  171.2 32.5 %collective-permute-start.17 = (bf16[896,256]{1,0:T(8,128)(2,1)}, bf16[896,256]{1,0:T(8,128)(2,1)S(1)}, u32[]{:S(2)}, u32[]{:S(2)}) collective-permute-start(bf16[896,256]{1,0:T(8,128)(2,1)} %slice.8), channel_id=1, source_target_pairs={{0,8},{1,33},{2,10},{3,35},{4,12},{5,37},{6,14},{7,39},{8,16},{9,4... | collective-permute-start | bytes 1376264 | tf_op jit(solution)/shard_map/ppermute | solution.py:44
  172.0 0.9 copy-start.2
  172.9 30.7 %collective-permute-start.19 = (bf16[896,256]{1,0:T(8,128)(2,1)}, bf16[896,256]{1,0:T(8,128)(2,1)}, u32[]{:S(2)}, u32[]{:S(2)}) collective-permute-start(bf16[896,256]{1,0:T(8,128)(2,1)} %slice.9), channel_id=1, source_target_pairs={{0,24},{1,97},{2,26},{3,99},{4,28},{5,101},{6,30},{7,103},{8,0},{9... | collective-permute-start | bytes 1376264 | tf_op jit(solution)/shard_map/ppermute | solution.py:44
  184.8 13.3 %copy-start.5 = (bf16[896,512]{1,0:T(8,128)(2,1)S(1)}, bf16[896,512]{1,0:T(8,128)(2,1)}, u32[]{:S(2)}) copy-start(bf16[896,512]{1,0:T(8,128)(2,1)} %copy-done.4) | copy-start | bytes 2752516
  184.8 8.4 %collective-permute-start.15 = (f32[1,512]{1,0:T(1,128)S(1)}, f32[1,512]{1,0:T(1,128)S(1)}, u32[]{:S(2)}, u32[]{:S(2)}) collective-permute-start(f32[1,512]{1,0:T(1,128)S(1)} %bitcast.25), channel_id=1, source_target_pairs={{0,1},{1,0},{2,3},{3,2},{4,5},{5,4},{6,7},{7,6},{8,9},{9,8},{10,11... | collective-permute-start | bytes 6152 | tf_op jit(solution)/shard_map/ppermute | solution.py:52
  193.2 2.0 copy-start.1
  198.1 2.8 %copy-start.3 = (bf16[896,512]{1,0:T(8,128)(2,1)S(1)}, bf16[896,512]{1,0:T(8,128)(2,1)}, u32[]{:S(2)}) copy-start(bf16[896,512]{1,0:T(8,128)(2,1)} %copy-done.2) | copy-start | bytes 2752516

commit v2 on v1

v2 whole, which is shorter than its diff:
```python
import functools
import math

import jax
import jax.numpy as jnp
from jax import lax
from jax.experimental import pallas as pl
from jax.experimental.pallas import tpu as pltpu
from jax.sharding import PartitionSpec as P

D = 8192
F = 28672
RANK = 512
HALF = RANK // 2
PRIME = 65521
NB = 128
PANEL = 16
VMEM_LIMIT = 48 * 1024 * 1024
VMEM_MOST = 61 * 1024 * 1024
F32, BF16 = jnp.float32, jnp.bfloat16
AXES = ("fsdp", "tp")
LOSS_MAX = 2.0


def flat(y, x, z, core):
    return (y * 4 + x) * 8 + z * 2 + core


def everyone():
    return [(y, x, z, c) for y in range(4) for x in range(4) for z in range(4) for c in range(2)]


def shift(along_first, step):
    pairs = []
    for y, x, z, c in everyone():
        if (c == 0) == along_first:
            to = (y, (x + step) % 4, z, c)
        else:
            to = ((y + step) % 4, x, z, c)
        pairs.append((flat(y, x, z, c), flat(*to)))
    return pairs


def send_first(a, step):
    return lax.ppermute(a, AXES, shift(True, step))


def send_second(a, step):
    return lax.ppermute(a, AXES, shift(False, step))


def swap_cores(a):
    return lax.ppermute(a, "tp", [(i, i ^ 1) for i in range(8)])


Z_GROUPS = [[c, 2 + c, 4 + c, 6 + c] for c in range(2)]
SECOND_GROUPS = [[flat(y, x, z, 0) for y in range(4)] for x in range(4) for z in range(4)] + [
    [flat(y, x, z, 1) for x in range(4)] for y in range(4) for z in range(4)
]
FIRST_GROUPS = [[flat(y, x, z, 0) for x in range(4)] for y in range(4) for z in range(4)] + [
    [flat(y, x, z, 1) for y in range(4)] for x in range(4) for z in range(4)
]
FIRST_Z_GROUPS = [[flat(y, x, z, 0) for x in range(4) for z in range(4)] for y in range(4)] + [
    [flat(y, x, z, 1) for y in range(4) for z in range(4)] for x in range(4)
]


def exchange(a, axis, groups=None):
    return lax.all_to_all(a, axis, 0, 0, axis_index_groups=groups, tiled=True)


def vmem_spec():
    return pl.BlockSpec(memory_space=pltpu.VMEM)


def smem_spec():
    return pl.BlockSpec(memory_space=pltpu.SMEM)


def params(limit=VMEM_LIMIT):
    return pltpu.CompilerParams(vmem_limit_bytes=limit)


def scatter(a, groups):
    return lax.psum_scatter(
        a, AXES, scatter_dimension=0, axis_index_groups=groups, tiled=True
    )


def sum_kernel(n, a_ref, out_ref):
    rows = a_ref.shape[0] // n
    total = a_ref[:rows, :]
    for k in range(1, n):
        total = total + a_ref[k * rows : (k + 1) * rows, :]
    for k in range(n):
        out_ref[k * rows : (k + 1) * rows, :] = total


def sum_parts(a, n):
    return pl.pallas_call(
        functools.partial(sum_kernel, n),
        out_shape=jax.ShapeDtypeStruct(a.shape, a.dtype),
        in_specs=[vmem_spec()],
        out_specs=vmem_spec(),
        compiler_params=params(),
        name="sum_parts",
    )(a)


def dot(a, b, ca, cb, precision=None):
    return lax.dot_general(
        a, b, (((ca,), (cb,)), ((), ())), precision=precision, preferred_element_type=F32
    )


def exact(a, b, ca, cb):
    return dot(a, b, ca, cb, lax.Precision.HIGHEST)


def fold(v):
    return (v & 65535) + 15 * (v >> 16)


def reduce_mod(v):
    v = fold(fold(v))
    return jnp.where(v >= PRIME, v - PRIME, v)


def start_rows(first_row, count, seed):
    rows = first_row + lax.broadcasted_iota(jnp.int32, (count, 1), 0)
    cols = lax.broadcasted_iota(jnp.int32, (1, RANK), 1)
    hashed = reduce_mod(rows * 40503 + seed) + reduce_mod(cols * 9973)
    hashed = jnp.where(hashed >= PRIME, hashed - PRIME, hashed)
    low = hashed & 32767
    low = reduce_mod(low * low + 7) & 32767
    third = reduce_mod(low * low + hashed).astype(F32)
    scale = math.sqrt(12.0 / F)
    return (third * (scale / PRIME) - 0.5 * scale).astype(BF16)


TILE = 512


def left_kernel(meta_ref, m_ref, g_ref, b_ref, keep_ref, send_ref, acc):
    t = pl.program_id(0)
    core, tp, seed = meta_ref[0], meta_ref[1], meta_ref[2]
    b = (m_ref[...].astype(F32) + g_ref[...].astype(F32)).astype(BF16)
    b_ref[...] = b
    part = dot(b, start_rows(tp * 3584 + t * TILE, TILE, seed), 1, 0)

    @pl.when(t == 0)
    def _():
        acc[...] = part

    @pl.when(t > 0)
    def _():
        acc[...] += part

    @pl.when(t == pl.num_programs(0) - 1)
    def _():
        keep_ref[...] = acc[pl.ds(core * HALF, HALF), :]
        send_ref[...] = acc[pl.ds((1 - core) * HALF, HALF), :]


def left_partial(meta, momentum, gradient):
    rows, cols = momentum.shape
    half = jax.ShapeDtypeStruct((HALF, RANK), F32)
    whole = pl.BlockSpec((HALF, RANK), lambda t: (0, 0))
    tile = pl.BlockSpec((rows, TILE), lambda t: (0, t))
    return pl.pallas_call(
        left_kernel,
        grid=(cols // TILE,),
        out_shape=(jax.ShapeDtypeStruct((rows, cols), BF16), half, half),
        in_specs=[smem_spec(), tile, tile],
        out_specs=(tile, whole, whole),
        scratch_shapes=[pltpu.VMEM((rows, RANK), F32)],
        compiler_params=params(VMEM_MOST),
        name="left_partial",
    )(meta, momentum, gradient)


GRAM_SHARE = (((0, 512, 0, 128), (128, 256, 128, 256)), ((256, 512, 128, 384), (384, 512, 384, 512)))


def gram_blocks(core):
    return [
        (i, j)
        for r0, r1, c0, c1 in GRAM_SHARE[core]
        for i in range(r0, r1, NB)
        for j in range(c0, c1, NB)
    ]


def gram_kernel(meta_ref, mine_ref, other_ref, out_ref):
    for core in range(2):

        @pl.when(meta_ref[0] == core)
        def _():
            k = 0
            for r0, r1, c0, c1 in GRAM_SHARE[core]:
                g = exact(mine_ref[:, r0:r1], mine_ref[:, c0:c1], 0, 0) + exact(
                    other_ref[:, r0:r1], other_ref[:, c0:c1], 0, 0
                )
                for i in range(0, r1 - r0, NB):
                    for j in range(0, c1 - c0, NB):
                        out_ref[k * NB : (k + 1) * NB, :] = g[i : i + NB, j : j + NB]
                        k += 1


def gram_share(meta, mine, other):
    return pl.pallas_call(
        gram_kernel,
        out_shape=jax.ShapeDtypeStruct((5 * NB, NB), F32),
        in_specs=[smem_spec(), vmem_spec(), vmem_spec()],
        out_specs=vmem_spec(),
        compiler_params=params(),
        name="gram_share",
    )(meta, mine, other)


def right_kernel(terms, meta_ref, b_ref, mine_ref, other_ref, out_ref, split):
    @pl.when(pl.program_id(0) == 0)
    def _():
        core = meta_ref[0]
        for ref, place in ((mine_ref, core), (other_ref, 1 - core)):
            rows = pl.ds(pl.multiple_of(place * HALF, HALF), HALF)
            rest = ref[...]
            for k in range(terms):
                term = rest.astype(BF16)
                split[rows, k * RANK : (k + 1) * RANK] = term
                rest = rest - term.astype(F32)

    w = dot(b_ref[...], split[...], 0, 0)
    out_ref[...] = sum(w[:, k * RANK : (k + 1) * RANK] for k in range(terms)).astype(out_ref.dtype)


def right_partial(meta, blended, mine, other, terms, wire):
    rows, cols = blended.shape
    block = cols // 4
    whole = pl.BlockSpec((HALF, RANK), lambda r: (0, 0))
    return pl.pallas_call(
        functools.partial(right_kernel, terms),
        grid=(4,),
        in_specs=[smem_spec(), pl.BlockSpec((rows, block), lambda r: (0, r)), whole, whole],
        out_specs=pl.BlockSpec((block, RANK), lambda r: (r, 0)),
        scratch_shapes=[pltpu.VMEM((RANK, terms * RANK), BF16)],
        out_shape=jax.ShapeDtypeStruct((cols, RANK), wire),
        compiler_params=params(VMEM_MOST),
        name="right_partial",
    )(meta, blended, mine, other)


def invert_block(ae):
    rows = lax.broadcasted_iota(jnp.int32, (PANEL, NB), 0)
    for k0 in range(0, NB, PANEL):
        left = ae[k0 : k0 + PANEL, :NB]
        right = ae[k0 : k0 + PANEL, NB:]
        columns = [
            jnp.broadcast_to(left[:, k0 + c : k0 + c + 1], (PANEL, NB)) for c in range(PANEL)
        ]
        pivots = jnp.zeros((PANEL, NB), F32)
        for k in range(PANEL):
            pivot = columns[k][k : k + 1, :]
            pivots = jnp.where(rows == k, pivot, pivots)
            if k < PANEL - 1:
                factor = jnp.where(rows > k, columns[k] * (1.0 / pivot), 0.0)
                for c in range(k + 1, PANEL):
                    columns[c] = columns[c] - factor * columns[c][k : k + 1, :]
                left = left - factor * left[k : k + 1, :]
                right = right - factor * right[k : k + 1, :]
        scale = lax.rsqrt(pivots)
        left, right = left * scale, right * scale
        ae[k0 : k0 + PANEL, NB:] = right
        below = k0 + PANEL
        if below < NB:
            ae[below:, :NB] = ae[below:, :NB] - exact(left, left, 0, 0)[below:]
            ae[below:, NB:] = ae[below:, NB:] - exact(left, right, 0, 0)[below:]


def inverse_kernel(meta_ref, mine_ref, other_ref, out_ref, loss_ref, a, ae, diagonal):
    for core in range(2):
        for share, ref in ((core, mine_ref), (1 - core, other_ref)):

            @pl.when(meta_ref[0] == core)
            def _():
                for k, (i, j) in enumerate(gram_blocks(share)):
                    a[i : i + NB, j : j + NB] = ref[k * NB : (k + 1) * NB, :]

    big = lambda d: lax.broadcasted_iota(jnp.int32, (RANK, RANK), d)
    small = lambda d: lax.broadcasted_iota(jnp.int32, (NB, NB), d)
    out_ref[...] = jnp.where(big(0) == big(1), 1.0, 0.0)
    for lo in range(0, RANK, NB):
        hi = lo + NB
        on = jnp.where(small(0) == small(1), a[lo:hi, lo:hi], 0.0)
        diagonal[:, lo:hi] = jnp.sum(on, axis=0, keepdims=True)
    for lo in range(0, RANK, NB):
        hi = lo + NB
        ae[:, :NB] = a[lo:hi, lo:hi]
        ae[:, NB:] = jnp.where(small(0) == small(1), 1.0, 0.0)
        invert_block(ae)
        inverse = jnp.where(small(0) >= small(1), ae[:, NB:], 0.0)
        done = exact(inverse, out_ref[lo:hi, :hi], 1, 0)
        out_ref[lo:hi, :hi] = done
        if hi < RANK:
            below = exact(a[hi:, lo:hi], inverse, 1, 1)
            a[hi:, hi:] = a[hi:, hi:] - exact(below, below, 1, 1)
            out_ref[hi:, :hi] = out_ref[hi:, :hi] - exact(below, done, 1, 0)
    out = out_ref[...]
    loss = jnp.max(jnp.sum(out * out * diagonal[...], axis=1, keepdims=True), axis=0, keepdims=True)
    loss_ref[...] = jnp.broadcast_to(loss, loss_ref.shape)


def inverse_factor(meta, mine, other):
    return pl.pallas_call(
        inverse_kernel,
        out_shape=(
            jax.ShapeDtypeStruct((RANK, RANK), F32),
            jax.ShapeDtypeStruct((8, NB), F32),
        ),
        in_specs=[smem_spec(), vmem_spec(), vmem_spec()],
        out_specs=(vmem_spec(), vmem_spec()),
        scratch_shapes=[
            pltpu.VMEM((RANK, RANK), F32),
            pltpu.VMEM((NB, 2 * NB), F32),
            pltpu.VMEM((1, RANK), F32),
        ],
        compiler_params=params(),
        cost_estimate=pl.CostEstimate(flops=0, bytes_accessed=70_000_000, transcendentals=0),
        name="inverse_factor",
    )(meta, mine, other)


def solve_kernel(w_ref, inv_ref, out_ref):
    out_ref[...] = exact(w_ref[...].astype(F32), inv_ref[...], 1, 1).astype(BF16)


def solve_rows(w, inverse):
    return pl.pallas_call(
        solve_kernel,
        out_shape=jax.ShapeDtypeStruct(w.shape, BF16),
        in_specs=[vmem_spec()] * 2,
        out_specs=vmem_spec(),
        compiler_params=params(),
        name="solve_rows",
    )(w, inverse)


def ortho_kernel(meta_ref, mine_ref, other_ref, inv_ref, out_ref):
    core = meta_ref[0]
    for ref, place in ((mine_ref, core), (other_ref, 1 - core)):
        rows = pl.ds(pl.multiple_of(place * HALF, HALF), HALF)
        out_ref[rows, :] = exact(ref[...], inv_ref[...], 1, 1).astype(BF16)


def ortho_left(meta, mine, other, inverse):
    return pl.pallas_call(
        ortho_kernel,
        out_shape=jax.ShapeDtypeStruct((RANK, RANK), BF16),
        in_specs=[smem_spec()] + [vmem_spec()] * 3,
        out_specs=vmem_spec(),
        compiler_params=params(),
        name="ortho_left",
    )(meta, mine, other, inverse)


def apply_kernel(parts, meta_ref, b_ref, q_ref, sums_ref, *refs):
    rights, (m_ref, u_ref) = refs[:parts], refs[-2:]
    scale = lax.rsqrt(sums_ref[0:1, :] + 1e-6) * math.sqrt(D * F / RANK)
    scaled = (q_ref[...].astype(F32) * scale).astype(BF16)
    width = RANK // parts
    feedback = direction = 0.0
    for k, right in enumerate(rights):
        cols = slice(k * width, (k + 1) * width)
        feedback += dot(q_ref[:, cols], right[...], 1, 1)
        direction += dot(scaled[:, cols], right[...], 1, 1)
    m_ref[...] = (b_ref[...].astype(F32) - 0.05 * feedback).astype(BF16)
    u_ref[...] = direction.astype(BF16)


def apply_block(meta, blended, q, sums, rights, offset, outs):
    rows, cols = blended.shape
    tiles = 2
    here = pl.BlockSpec(
        (rows // tiles, cols // 4), lambda i, meta_ref: (i, (meta_ref[3] + offset) % 4)
    )
    whole = lambda a: pl.BlockSpec(a.shape, lambda i, meta_ref: (0, 0))
    n = len(rights)
    shape = jax.ShapeDtypeStruct((rows, cols), BF16)
    kept = [pl.BlockSpec(memory_space=pl.ANY)] * len(outs)
    return pl.pallas_call(
        functools.partial(apply_kernel, n),
        grid_spec=pltpu.PrefetchScalarGridSpec(
            num_scalar_prefetch=1,
            grid=(tiles,),
            in_specs=[
                here,
                pl.BlockSpec((rows // tiles, RANK), lambda i, meta_ref: (i, 0)),
                whole(sums),
            ]
            + [whole(r) for r in rights]
            + kept,
            out_specs=[here, here],
        ),
        out_shape=[shape, shape],
        input_output_aliases={4 + n + k: k for k in range(len(outs))},
        compiler_params=params(),
        name="apply_block",
    )(meta, blended, q, sums, *rights, *outs)


def sums_kernel(r_ref, out_ref):
    r = r_ref[...].astype(F32)
    out_ref[...] = jnp.broadcast_to(jnp.sum(r * r, axis=0, keepdims=True), out_ref.shape)


def block_sums(r):
    return pl.pallas_call(
        sums_kernel,
        out_shape=jax.ShapeDtypeStruct((16, RANK), F32),
        in_specs=[vmem_spec()],
        out_specs=vmem_spec(),
        compiler_params=params(),
        name="block_sums",
    )(r)


def per_device(momentum, gradient, seed_value):
    fsdp, tp = lax.axis_index("fsdp"), lax.axis_index("tp")
    core, x, y = tp % 2, fsdp % 4, fsdp // 4
    first, second = jnp.where(core == 0, x, y), jnp.where(core == 0, y, x)
    meta = jnp.stack([core, tp, seed_value[0], first, second]).astype(jnp.int32)

    blended, keep, send = left_partial(meta, momentum, gradient)
    half = keep + swap_cores(send)
    mine = exchange(sum_parts(exchange(half, "tp", Z_GROUPS), 4), "tp", Z_GROUPS)
    other = swap_cores(mine)

    w = right_partial(meta, blended, mine, other, 1, BF16)
    mine, other, w = lax.optimization_barrier((mine, other, w))
    w = scatter(w, FIRST_GROUPS)
    gram = exchange(gram_share(meta, mine, other), "fsdp")
    gram = exchange(sum_parts(gram, 16), "fsdp")
    w, gram, gram_other = lax.optimization_barrier((w, gram, swap_cores(gram)))
    w = scatter(w, SECOND_GROUPS)
    inverse, loss = inverse_factor(meta, gram, gram_other)
    w, inverse, loss = lax.optimization_barrier((w, inverse, loss))

    def careful():
        wide = right_partial(meta, blended, mine, other, 2, F32)
        return solve_rows(scatter(scatter(wide, FIRST_GROUPS), SECOND_GROUPS), inverse)

    block = lax.cond(loss[0, 0] <= LOSS_MAX**2, lambda: solve_rows(w, inverse), careful)
    right = exchange(jnp.tile(block, (4, 1)), AXES, SECOND_GROUPS)
    right_low = send_first(right, 1)
    right_high = send_first(right, -1)
    sums = sum_parts(exchange(block_sums(right), AXES, FIRST_Z_GROUPS), 16)
    sums = sums + swap_cores(sums)
    right_low, right_high, sums = lax.optimization_barrier((right_low, right_high, sums))
    far_a = send_first(right_low[:, :HALF], 1)
    far_b = send_first(right_high[:, HALF:], -1)
    q = ortho_left(meta, mine, other, inverse)
    outs = apply_block(meta, blended, q, sums, [right], 0, [])
    outs = apply_block(meta, blended, q, sums, [right_low], 3, outs)
    outs = apply_block(meta, blended, q, sums, [right_high], 1, outs)
    outs = apply_block(meta, blended, q, sums, [far_a, far_b], 2, outs)
    return tuple(outs)


def solution(mesh):
    return jax.shard_map(
        per_device,
        mesh=mesh,
        in_specs=(P("fsdp", "tp"), P("fsdp", "tp"), P()),
        out_specs=(P("fsdp", "tp"), P("fsdp", "tp")),
        check_vma=False,
    )
```

time: 208 us -> 257 us (1.24)
  waiting for transfers between devices: 17.7 us -> 71.8 us
  starting transfers between devices: 41.1 us -> 17.8 us
  between operations: 1.52 us -> 15.2 us
  blocking collectives: 66.4 us -> 79.8 us
  local copies, waits for them, and re-layouts: 9.12 us -> 1.79 us
    reduce_scatter x0 -> x4, waiting for transfers between devices: none -> 66.3 us  [scatter(): lax.psum_scatter(a, AXES, scatter_dimension=0, axis_index_groups=groups,...]
    all_to_all x5 -> x6, blocking collectives: 66.4 us -> 79.8 us  [exchange(): return lax.all_to_all(a, axis, 0, 0, axis_index_groups=groups, tiled=True)]
    ppermute x10 -> x4, waiting for transfers between devices: 11.1 us -> 0.01 us  [send_first(): return lax.ppermute(a, AXES, shift(True, step))]
    ppermute x10 -> x4, starting transfers between devices: 13.3 us -> 5.49 us  [send_first(): return lax.ppermute(a, AXES, shift(True, step))]
    unnamed x18 -> x3, local copies, waits for them, and re-layouts: 7.16 us -> 0.01 us
    ppermute x6 -> x0, starting transfers between devices: 5.75 us -> none  [send_second(): return lax.ppermute(a, AXES, shift(False, step))]
    all_to_all x1 -> x0, starting transfers between devices: 5.54 us -> none  [exchange(): return lax.all_to_all(a, axis, 0, 0, axis_index_groups=groups, tiled=True)]
    ppermute x4, starting transfers between devices: 16.6 us -> 12.1 us  [swap_cores(): return lax.ppermute(a, 'tp', [(i, i ^ 1) for i in range(8)])]
  transfers between devices with their start and end apart: 21 -> 12, of which waited for: 5 -> 6; matrix products, arithmetic and copies ran while one was open for 1% -> 0% of each run, Pallas kernels for 22% -> 14%
where the time goes in v2:
time: 257 us; the launch traced here: 256 us
  blocking collectives  79.8 us (31%)
  waiting for transfers between devices  71.8 us (28%)
  Pallas kernels  68.6 us (27%)
  starting transfers between devices  17.8 us (7%)
  between operations  15.2 us (6%)
    all_to_all x6, blocking collectives, exchange(): return lax.all_to_all(a, axis, 0, 0, axis_index_groups=groups, tiled=True)  79.8 us
    reduce_scatter x4, waiting for transfers between devices, scatter(): lax.psum_scatter(a, AXES, scatter_dimension=0, axis_index_groups=groups,...  66.3 us
    pallas_call x1, Pallas kernels, inverse_factor(): pl.pallas_call(inverse_kernel, out_shape=(jax.ShapeDtypeStruct((RANK, RAN...  22 us
    pallas_call x1, Pallas kernels, left_partial(): pl.pallas_call(left_kernel, grid=(cols // TILE,), out_shape=(jax.ShapeDty...  15.7 us
    pallas_call x2, Pallas kernels, right_partial(): pl.pallas_call(functools.partial(right_kernel, terms), grid=(4,), in_spec...  13.8 us
    ppermute x4, starting transfers between devices, swap_cores(): return lax.ppermute(a, 'tp', [(i, i ^ 1) for i in range(8)])  12.1 us
    pallas_call x4, Pallas kernels, apply_block(): pl.pallas_call(functools.partial(apply_kernel, n), grid_spec=pltpu.Prefet...  11.9 us
    ppermute x4, starting transfers between devices, send_first(): return lax.ppermute(a, AXES, shift(True, step))  5.49 us
  transfers between devices with their start and end apart: 12, of which 6 were waited for; matrix products, arithmetic and copies ran while one was open for 0% of the time, Pallas kernels for 14%

profile of v2, /device:TPU:1, one launch (start us, length us, event | category | flops | bytes accessed | tf_op | source)
XLA Modules:
  0.0 256.1 jit_solution(13833516564711186881)
XLA Ops:
  7.2 0.0 reduce-scatter.9.cloned.1.call-start
  7.9 0.1 stack.19.meta_ref
  8.0 15.7 %left_partial.1 = (bf16[512,3584]{1,0:T(8,128)(2,1)}, f32[256,512]{1,0:T(8,128)}, f32[256,512]{1,0:T(8,128)}) custom-call(s32[5]{0:T(128)S(1)} %stack.19.meta_ref, bf16[512,3584]{1,0:T(8,128)(2,1)} %m_ref.1, bf16[512,3584]{1,0:T(8,128)(2,1)} %g_ref.1), custom_call_target="tpu_custom_call" | custom-call | tf_op jit(solution)/shard_map/left_partial/pallas_call | solution.py:170
  23.7 1.4 collective-permute-start
  25.1 1.7 collective-permute-done
  26.9 1.1 add.24
  28.0 13.5 %all_to_all.64 = f32[4,64,512]{2,1,0:T(8,128)S(1)} all-to-all(f32[4,64,512]{2,1,0:T(8,128)S(1)} %bitcast.36), channel_id=1, replica_groups={{0,2,4,6},{1,3,5,7},{8,10,12,14},{9,11,13,15},{16,18,20,22},{17,19,21,2..., dimensions={0} | all-to-all | bytes 1048576 | tf_op jit(solution)/shard_map/all_to_all | solution.py:69
  41.6 10.1 %all_to_all.65 = f32[4,64,512]{2,1,0:T(8,128)S(1)} all-to-all(f32[4,64,512]{2,1,0:T(8,128)S(1)} %bitcast.23), channel_id=1, replica_groups={{0,2,4,6},{1,3,5,7},{8,10,12,14},{9,11,13,15},{16,18,20,22},{17,19,21,2..., dimensions={0} | all-to-all | bytes 1048576 | tf_op jit(solution)/shard_map/all_to_all | solution.py:69
  51.7 2.7 %collective-permute-start.1 = (f32[256,512]{1,0:T(8,128)S(1)}, f32[256,512]{1,0:T(8,128)S(1)}, u32[]{:S(2)}, u32[]{:S(2)}) collective-permute-start(f32[256,512]{1,0:T(8,128)S(1)} %bitcast.31), channel_id=1, source_target_pairs={{0,1},{1,0},{2,3},{3,2},{4,5},{5,4},{6,7},{7,6},{8,9},{9,8},{10,11... | collective-permute-start | bytes 1572872 | tf_op jit(solution)/shard_map/ppermute | solution.py:53
  54.4 1.5 collective-permute-done.1.other_ref
  55.9 5.8 %right_partial.3 = bf16[3584,512]{1,0:T(8,128)(2,1)} custom-call(s32[5]{0:T(128)S(1)} %stack.19.meta_ref, bf16[512,3584]{1,0:T(8,128)(2,1)} %get-tuple-element.49.b_ref, f32[256,512]{1,0:T(8,128)S(1)} %bitcast.32, f32[256,512]{1,0:T(8,128)S(1)} %collective-permute-done.1.other_ref), custom_call_target="tpu_custom_call" | custom-call | tf_op jit(solution)/shard_map/right_partial/pallas_call | solution.py:241
  61.7 0.0 reduce-scatter.9.cloned.1.call-update
  61.7 0.0 reduce-scatter.11.cloned.1.call-start
  61.8 1.4 gram_share.1
  63.2 16.9 %all_to_all.66 = f32[16,40,128]{2,1,0:T(8,128)S(1)} all-to-all(f32[16,40,128]{2,1,0:T(8,128)S(1)} %bitcast.24), channel_id=1, replica_groups=mesh['fsdp'=16,'tp'=8] {'fsdp'}, dimensions={0} | all-to-all | bytes 655360 | tf_op jit(solution)/shard_map/all_to_all | solution.py:69
  80.2 12.9 %all_to_all.67 = f32[16,40,128]{2,1,0:T(8,128)S(1)} all-to-all(f32[16,40,128]{2,1,0:T(8,128)S(1)} %bitcast.28), channel_id=1, replica_groups=mesh['fsdp'=16,'tp'=8] {'fsdp'}, dimensions={0} | all-to-all | bytes 655360 | tf_op jit(solution)/shard_map/all_to_all | solution.py:69
  93.1 3.3 %collective-permute-start.2 = (f32[640,128]{1,0:T(8,128)S(1)}, f32[640,128]{1,0:T(8,128)S(1)}, u32[]{:S(2)}, u32[]{:S(2)}) collective-permute-start(f32[640,128]{1,0:T(8,128)S(1)} %bitcast.25), channel_id=1, source_target_pairs={{0,1},{1,0},{2,3},{3,2},{4,5},{5,4},{6,7},{7,6},{8,9},{9,8},{10,11... | collective-permute-start | bytes 983048 | tf_op jit(solution)/shard_map/ppermute | solution.py:53
  96.4 1.3 collective-permute-done.2.other_ref
  97.7 0.0 reduce-scatter.9.cloned.1.call-done
  97.7 0.0 reduce-scatter.11.cloned.1.call-update
  97.7 22.0 %inverse_factor.1 = (f32[512,512]{1,0:T(8,128)S(1)}, f32[8,128]{1,0:T(8,128)S(1)}) custom-call(s32[5]{0:T(128)S(1)} %stack.19.meta_ref, f32[640,128]{1,0:T(8,128)S(1)} %bitcast.26, f32[640,128]{1,0:T(8,128)S(1)} %collective-permute-done.2.other_ref), custom_call_target="tpu_custom_call" | custom-call | bytes 70000000 | tf_op jit(solution)/shard_map/inverse_factor/pallas_call | solution.py:314
  119.7 0.0 reduce-scatter.11.cloned.1.call-done
  119.8 0.5 slice.9
  120.9 76.6 %conditional.1 = (bf16[224,512]{1,0:T(8,128)(2,1)S(1)}) conditional(s32[]{:T(128)} %bitcast.12, (s32[5]{0:T(128)S(1)}, bf16[512,3584]{1,0:T(8,128)(2,1)}, f32[256,512]{1,0:T(8,128)S(1)}, f32[256,512]{1,0:T(8,128)S(1)}, f32[512,512]{1,0:T(8,128)S(1)}) %tuple.33, (bf16[224,512]{1,0:T(8,128)(2,1)}, f32[512,512]{1,0:T(8,128)S(1)}) %tuple.21), branch_computations={%region_2.5_spmd, %region_5.6_spmd} | conditional | bytes 36241524 | solution.py:452
  120.9 0.0 reduce-scatter.5.cloned.1.call-start
  121.0 8.0 %right_partial.2 = f32[3584,512]{1,0:T(8,128)} custom-call(s32[5]{0:T(128)S(1)} %get-tuple-element.14.meta_ref, bf16[512,3584]{1,0:T(8,128)(2,1)} %get-tuple-element.18.b_ref, f32[256,512]{1,0:T(8,128)S(1)} %get-tuple-element.19.mine_ref, f32[256,512]{1,0:T(8,128)S(1)} %get-tuple-element.20.other_ref), custom_call_target="tpu_custom_call" | custom-call | tf_op jit(solution)/shard_map/cond/branch_0_fun/right_partial/pallas_call | solution.py:241
  129.0 0.0 reduce-scatter.5.cloned.1.call-update
  129.0 0.0 reduce-scatter.7.cloned.1.call-start
  129.1 42.0 %reduce-scatter.5.cloned.1.call-done = f32[896,512]{1,0:T(8,128)} async-done(((f32[3584,512]{1,0:T(8,128)}), f32[896,512]{1,0:T(8,128)}) %reduce-scatter.5.cloned.1.call-update) | async-done | bytes 1835024 | tf_op jit(solution)/shard_map/cond/branch_0_fun/reduce_scatter | solution.py:85
  171.0 0.0 reduce-scatter.7.cloned.1.call-update
  171.1 24.3 %reduce-scatter.7.cloned.1.call-done.w_ref = f32[224,512]{1,0:T(8,128)} async-done(((f32[896,512]{1,0:T(8,128)}), f32[224,512]{1,0:T(8,128)}) %reduce-scatter.7.cloned.1.call-update) | async-done | bytes 458768 | tf_op jit(solution)/shard_map/cond/branch_0_fun/reduce_scatter | solution.py:85
  195.4 0.0 copy-start
  195.4 1.0 copy-done
  196.4 1.1 solve_rows.2
  197.5 0.1 tile.2
  197.6 0.0 copy-start.1
  197.6 12.1 %all_to_all.68 = bf16[4,224,512]{2,1,0:T(8,128)(2,1)S(1)} all-to-all(bf16[4,224,512]{2,1,0:T(8,128)(2,1)S(1)} %tile.2), channel_id=1, replica_groups={{0,32,64,96},{2,34,66,98},{4,36,68,100},{6,38,70,102},{8,40,72,104},{10..., dimensions={0} | all-to-all | bytes 1835008 | tf_op jit(solution)/shard_map/all_to_all | solution.py:69
  209.7 0.3 collective-permute-start.3
  210.0 2.4 collective-permute-start.4
  212.4 0.1 block_sums.1
  212.5 14.2 %all_to_all.69 = f32[16,1,512]{2,1,0:T(1,128)S(1)} all-to-all(f32[16,1,512]{2,1,0:T(1,128)S(1)} %copy.11), channel_id=1, replica_groups={{0,2,4,6,8,10,12,14,16,18,20,22,24,26,28,30},{32,34,36,38,40,42,44,46,4..., dimensions={0} | all-to-all | bytes 65536 | tf_op jit(solution)/shard_map/all_to_all | solution.py:69
  226.7 4.7 %collective-permute-start.5 = (f32[16,512]{1,0:T(8,128)S(1)}, f32[16,512]{1,0:T(8,128)S(1)}, u32[]{:S(2)}, u32[]{:S(2)}) collective-permute-start(f32[16,512]{1,0:T(8,128)S(1)} %sum_parts.5), channel_id=1, source_target_pairs={{0,1},{1,0},{2,3},{3,2},{4,5},{5,4},{6,7},{7,6},{8,9},{9,8},{10,11... | collective-permute-start | bytes 98312 | tf_op jit(solution)/shard_map/ppermute | solution.py:53
  231.4 0.9 collective-permute-done.5
  232.2 0.0 collective-permute-done.3.refs_0_
  232.3 0.0 collective-permute-done.4.refs_0_
  232.3 0.3 collective-permute-start.6
  232.7 2.5 collective-permute-start.7
  235.2 2.5 ortho_left.1.q_ref
  237.6 0.0 copy-done.1
  237.7 3.0 %apply_block.4 = (bf16[512,3584]{1,0:T(8,128)(2,1)}, bf16[512,3584]{1,0:T(8,128)(2,1)}) custom-call(s32[5]{0:T(128)S(1)} %stack.19.meta_ref, bf16[512,3584]{1,0:T(8,128)(2,1)S(1)} %copy-done.1, bf16[512,512]{1,0:T(8,128)(2,1)S(1)} %ortho_left.1.q_ref, f32[16,512]{1,0:T(8,128)S(1)} %add.25.sums_ref, bf16[896,512]{1,0:T(8,128)(2,1)S(1)} %bitcast.21), custom_call_target="tpu_custom_call" | custom-call | tf_op jit(solution)/shard_map/apply_block/pallas_call | solution.py:390
  240.6 3.0 %apply_block.5 = (bf16[512,3584]{1,0:T(8,128)(2,1)}, bf16[512,3584]{1,0:T(8,128)(2,1)}) custom-call(s32[5]{0:T(128)S(1)} %stack.19.meta_ref, bf16[512,3584]{1,0:T(8,128)(2,1)S(1)} %copy-done.1, bf16[512,512]{1,0:T(8,128)(2,1)S(1)} %ortho_left.1.q_ref, f32[16,512]{1,0:T(8,128)S(1)} %add.25.sums_ref, ...), custom_call_target="tpu_custom_call", output_to_operand_aliasing={{0}: (5, {}), {1}: (6, {})} | custom-call | tf_op jit(solution)/shard_map/apply_block/pallas_call | solution.py:390
  243.6 3.0 %apply_block.6 = (bf16[512,3584]{1,0:T(8,128)(2,1)}, bf16[512,3584]{1,0:T(8,128)(2,1)}) custom-call(s32[5]{0:T(128)S(1)} %stack.19.meta_ref, bf16[512,3584]{1,0:T(8,128)(2,1)S(1)} %copy-done.1, bf16[512,512]{1,0:T(8,128)(2,1)S(1)} %ortho_left.1.q_ref, f32[16,512]{1,0:T(8,128)S(1)} %add.25.sums_ref, ...), custom_call_target="tpu_custom_call", output_to_operand_aliasing={{0}: (5, {}), {1}: (6, {})} | custom-call | tf_op jit(solution)/shard_map/apply_block/pallas_call | solution.py:390
  246.5 0.0 collective-permute-done.6.refs_0_
  246.5 0.0 collective-permute-done.7.refs_1_
  246.5 3.0 %apply_block.7 = (bf16[512,3584]{1,0:T(8,128)(2,1)}, bf16[512,3584]{1,0:T(8,128)(2,1)}) custom-call(s32[5]{0:T(128)S(1)} %stack.19.meta_ref, bf16[512,3584]{1,0:T(8,128)(2,1)S(1)} %copy-done.1, bf16[512,512]{1,0:T(8,128)(2,1)S(1)} %ortho_left.1.q_ref, f32[16,512]{1,0:T(8,128)S(1)} %add.25.sums_ref, ...), custom_call_target="tpu_custom_call", output_to_operand_aliasing={{0}: (6, {}), {1}: (7, {})} | custom-call | tf_op jit(solution)/shard_map/apply_block/pallas_call | solution.py:390
  (8 shorter events, 0.2 us)
Async XLA Ops:
  7.2 90.5 %reduce-scatter.9.cloned.1.call-start = ((), (), s32[]{:S(2)}) async-start(), calls=%async_computation.12 | async-start | bytes 4587520 | tf_op jit(solution)/shard_map/reduce_scatter | solution.py:85
  23.7 3.2 %collective-permute-start = (f32[256,512]{1,0:T(8,128)}, f32[256,512]{1,0:T(8,128)S(1)}, u32[]{:S(2)}, u32[]{:S(2)}) collective-permute-start(f32[256,512]{1,0:T(8,128)} %get-tuple-element.51), channel_id=1, source_target_pairs={{0,1},{1,0},{2,3},{3,2},{4,5},{5,4},{6,7},{7,6},{8,9},{9,8},{10,11... | collective-permute-start | bytes 1572872 | tf_op jit(solution)/shard_map/ppermute | solution.py:53
  51.7 4.3 %collective-permute-start.1 = (f32[256,512]{1,0:T(8,128)S(1)}, f32[256,512]{1,0:T(8,128)S(1)}, u32[]{:S(2)}, u32[]{:S(2)}) collective-permute-start(f32[256,512]{1,0:T(8,128)S(1)} %bitcast.31), channel_id=1, source_target_pairs={{0,1},{1,0},{2,3},{3,2},{4,5},{5,4},{6,7},{7,6},{8,9},{9,8},{10,11... | collective-permute-start | bytes 1572872 | tf_op jit(solution)/shard_map/ppermute | solution.py:53
  61.7 58.0 %reduce-scatter.11.cloned.1.call-start = ((), (), s32[]{:S(2)}) async-start(), calls=%async_computation.13 | async-start | bytes 1146880 | tf_op jit(solution)/shard_map/reduce_scatter | solution.py:85
  93.1 4.5 %collective-permute-start.2 = (f32[640,128]{1,0:T(8,128)S(1)}, f32[640,128]{1,0:T(8,128)S(1)}, u32[]{:S(2)}, u32[]{:S(2)}) collective-permute-start(f32[640,128]{1,0:T(8,128)S(1)} %bitcast.25), channel_id=1, source_target_pairs={{0,1},{1,0},{2,3},{3,2},{4,5},{5,4},{6,7},{7,6},{8,9},{9,8},{10,11... | collective-permute-start | bytes 983048 | tf_op jit(solution)/shard_map/ppermute | solution.py:53
  120.9 50.1 %reduce-scatter.5.cloned.1.call-start = ((), (), s32[]{:S(2)}) async-start(), calls=%async_computation.10 | async-start | bytes 9175040 | tf_op jit(solution)/shard_map/cond/branch_0_fun/reduce_scatter | solution.py:85
  129.0 66.3 %reduce-scatter.7.cloned.1.call-start = ((), (), s32[]{:S(2)}) async-start(), calls=%async_computation.11 | async-start | bytes 2293760 | tf_op jit(solution)/shard_map/cond/branch_0_fun/reduce_scatter | solution.py:85
  195.4 1.0 copy-start
  197.6 40.1 %copy-start.1 = (bf16[512,3584]{1,0:T(8,128)(2,1)S(1)}, bf16[512,3584]{1,0:T(8,128)(2,1)}, u32[]{:S(2)}) copy-start(bf16[512,3584]{1,0:T(8,128)(2,1)} %get-tuple-element.49.b_ref) | copy-start | bytes 11010052
  209.7 22.6 %collective-permute-start.3 = (bf16[896,512]{1,0:T(8,128)(2,1)S(1)}, bf16[896,512]{1,0:T(8,128)(2,1)S(1)}, u32[]{:S(2)}, u32[]{:S(2)}) collective-permute-start(bf16[896,512]{1,0:T(8,128)(2,1)S(1)} %bitcast.18), channel_id=1, source_target_pairs={{0,8},{1,33},{2,10},{3,35},{4,12},{5,37},{6,14},{7,39},{8,16},{9,4... | collective-permute-start | bytes 2752520 | tf_op jit(solution)/shard_map/ppermute | solution.py:45
  210.0 22.2 %collective-permute-start.4 = (bf16[896,512]{1,0:T(8,128)(2,1)S(1)}, bf16[896,512]{1,0:T(8,128)(2,1)S(1)}, u32[]{:S(2)}, u32[]{:S(2)}) collective-permute-start(bf16[896,512]{1,0:T(8,128)(2,1)S(1)} %bitcast.19), channel_id=1, source_target_pairs={{0,24},{1,97},{2,26},{3,99},{4,28},{5,101},{6,30},{7,103},{8,0},{9... | collective-permute-start | bytes 2752520 | tf_op jit(solution)/shard_map/ppermute | solution.py:45
  226.7 5.5 %collective-permute-start.5 = (f32[16,512]{1,0:T(8,128)S(1)}, f32[16,512]{1,0:T(8,128)S(1)}, u32[]{:S(2)}, u32[]{:S(2)}) collective-permute-start(f32[16,512]{1,0:T(8,128)S(1)} %sum_parts.5), channel_id=1, source_target_pairs={{0,1},{1,0},{2,3},{3,2},{4,5},{5,4},{6,7},{7,6},{8,9},{9,8},{10,11... | collective-permute-start | bytes 98312 | tf_op jit(solution)/shard_map/ppermute | solution.py:53
  232.3 14.2 %collective-permute-start.6 = (bf16[896,256]{1,0:T(8,128)(2,1)S(1)}, bf16[896,256]{1,0:T(8,128)(2,1)S(1)}, u32[]{:S(2)}, u32[]{:S(2)}) collective-permute-start(bf16[896,256]{1,0:T(8,128)(2,1)S(1)} %slice.10), channel_id=1, source_target_pairs={{0,8},{1,33},{2,10},{3,35},{4,12},{5,37},{6,14},{7,39},{8,16},{9,4... | collective-permute-start | bytes 1376264 | tf_op jit(solution)/shard_map/ppermute | solution.py:45
  232.7 13.9 %collective-permute-start.7 = (bf16[896,256]{1,0:T(8,128)(2,1)S(1)}, bf16[896,256]{1,0:T(8,128)(2,1)S(1)}, u32[]{:S(2)}, u32[]{:S(2)}) collective-permute-start(bf16[896,256]{1,0:T(8,128)(2,1)S(1)} %slice.11), channel_id=1, source_target_pairs={{0,24},{1,97},{2,26},{3,99},{4,28},{5,101},{6,30},{7,103},{8,0},{9... | collective-permute-start | bytes 1376264 | tf_op jit(solution)/shard_map/ppermute | solution.py:45
Sparse Core Ops, SparseCore 0:
  61.9 34.0 reduce-scatter.8
  98.4 18.1 reduce-scatter.10
  129.2 41.8 reduce-scatter.4
  173.3 22.0 reduce-scatter.6

commit v3 on v2

--- a/solution.py
+++ b/solution.py
@@ -14,7 +14,8 @@
 HALF = RANK // 2
 PRIME = 65521
 NB = 128
-PANEL = 16
+PANEL = 64
+STRIP = 16
 VMEM_LIMIT = 48 * 1024 * 1024
 VMEM_MOST = 61 * 1024 * 1024
 F32, BF16 = jnp.float32, jnp.bfloat16
@@ -118,48 +119,79 @@
 
 
 def fold(v):
-    return (v & 65535) + 15 * (v >> 16)
-
-
-def reduce_mod(v):
-    v = fold(fold(v))
+    return v - (v >> 16) * PRIME
+
+
+def wrap(v):
     return jnp.where(v >= PRIME, v - PRIME, v)
 
 
-def start_rows(first_row, count, seed):
-    rows = first_row + lax.broadcasted_iota(jnp.int32, (count, 1), 0)
-    cols = lax.broadcasted_iota(jnp.int32, (1, RANK), 1)
-    hashed = reduce_mod(rows * 40503 + seed) + reduce_mod(cols * 9973)
-    hashed = jnp.where(hashed >= PRIME, hashed - PRIME, hashed)
-    low = hashed & 32767
-    low = reduce_mod(low * low + 7) & 32767
-    third = reduce_mod(low * low + hashed).astype(F32)
+def start_value(a):
+    low = a & 32767
+    low = wrap(fold(fold(low * low + 7))) & 32767
+    third = fold(low * low + a).astype(F32)
+    third = third - jnp.floor(third * (1.0 / PRIME) + 0.5 / PRIME) * PRIME
     scale = math.sqrt(12.0 / F)
-    return (third * (scale / PRIME) - 0.5 * scale).astype(BF16)
-
-
-TILE = 512
-
-
-def left_kernel(meta_ref, m_ref, g_ref, b_ref, keep_ref, send_ref, acc):
+    return third * (scale / PRIME) - 0.5 * scale
+
+
+INVERSE = pow(9973, -1, PRIME)
+ROW = INVERSE * 40503 % PRIME
+TABLE = 520
+UNROLL = 8
+TILE = 1792
+
+
+def build_table(table):
+    rows = lax.broadcasted_iota(jnp.int32, (8, 128), 0)
+    cols = lax.broadcasted_iota(jnp.int32, (8, 128), 1)
+    base = wrap(fold(fold(cols * 9973 + rows * 40503)))
+
+    def step(i, offset):
+        for k in range(UNROLL):
+            table[i * UNROLL + k] = start_value(wrap(base + offset))
+            offset = wrap(offset + 9973 * 128 % PRIME)
+        return offset
+
+    lax.fori_loop(0, TABLE // UNROLL, step, jnp.int32(0))
+
+
+def left_kernel(meta_ref, m_ref, g_ref, b_ref, keep_ref, send_ref, acc, table, start):
     t = pl.program_id(0)
-    core, tp, seed = meta_ref[0], meta_ref[1], meta_ref[2]
+    core, tp, seed = meta_ref[0], meta_ref[1], lax.rem(meta_ref[2], PRIME)
+
+    @pl.when(t == 0)
+    def _():
+        build_table(table)
+
+    window = lax.rem(lax.rem(INVERSE * (seed >> 8), PRIME) * 256 + INVERSE * (seed & 255), PRIME)
+    window += lax.rem(tp * (ROW * 3584 % PRIME), PRIME) + lax.rem(t * (ROW * TILE % PRIME), PRIME)
+    window = lax.rem(window, PRIME)
+    lanes = lax.broadcasted_iota(jnp.int32, (8, 128), 1)
+    for i in range(0, TILE, 16):
+        groups = []
+        for _ in range(2):
+            part, whole = window & 127, window >> 7
+            turned = [pltpu.roll(table[whole + k], (128 - part) & 127, 1) for k in range(5)]
+            first = lanes < 128 - part
+            groups.append([jnp.where(first, turned[k], turned[k + 1]) for k in range(4)])
+            window = wrap(window + ROW * 8 % PRIME)
+        for k in range(4):
+            rows = jnp.concatenate([groups[0][k], groups[1][k]], axis=0)
+            start[i : i + 16, k * 128 : (k + 1) * 128] = rows.astype(BF16)
     b = (m_ref[...].astype(F32) + g_ref[...].astype(F32)).astype(BF16)
     b_ref[...] = b
-    part = dot(b, start_rows(tp * 3584 + t * TILE, TILE, seed), 1, 0)
+    part = dot(b, start[...], 1, 0)
 
     @pl.when(t == 0)
     def _():
         acc[...] = part
 
-    @pl.when(t > 0)
+    @pl.when(t == pl.num_programs(0) - 1)
     def _():
         acc[...] += part
-
-    @pl.when(t == pl.num_programs(0) - 1)
-    def _():
-        keep_ref[...] = acc[pl.ds(core * HALF, HALF), :]
-        send_ref[...] = acc[pl.ds((1 - core) * HALF, HALF), :]
+        keep_ref[...] = acc[pl.ds(pl.multiple_of(core * HALF, HALF), HALF), :]
+        send_ref[...] = acc[pl.ds(pl.multiple_of((1 - core) * HALF, HALF), HALF), :]
 
 
 def left_partial(meta, momentum, gradient):
@@ -169,11 +201,15 @@
     tile = pl.BlockSpec((rows, TILE), lambda t: (0, t))
     return pl.pallas_call(
         left_kernel,
-        grid=(cols // TILE,),
+        grid=(2,),
         out_shape=(jax.ShapeDtypeStruct((rows, cols), BF16), half, half),
         in_specs=[smem_spec(), tile, tile],
         out_specs=(tile, whole, whole),
-        scratch_shapes=[pltpu.VMEM((rows, RANK), F32)],
+        scratch_shapes=[
+            pltpu.VMEM((rows, RANK), F32),
+            pltpu.VMEM((TABLE, 8, 128), F32),
+            pltpu.VMEM((TILE, RANK), BF16),
+        ],
         compiler_params=params(VMEM_MOST),
         name="left_partial",
     )(meta, momentum, gradient)
@@ -251,30 +287,31 @@
 
 
 def invert_block(ae):
-    rows = lax.broadcasted_iota(jnp.int32, (PANEL, NB), 0)
-    for k0 in range(0, NB, PANEL):
-        left = ae[k0 : k0 + PANEL, :NB]
-        right = ae[k0 : k0 + PANEL, NB:]
-        columns = [
-            jnp.broadcast_to(left[:, k0 + c : k0 + c + 1], (PANEL, NB)) for c in range(PANEL)
-        ]
-        pivots = jnp.zeros((PANEL, NB), F32)
-        for k in range(PANEL):
-            pivot = columns[k][k : k + 1, :]
-            pivots = jnp.where(rows == k, pivot, pivots)
-            if k < PANEL - 1:
+    for top in range(0, NB, PANEL):
+        end = top + PANEL
+        for k0 in range(top, end, STRIP):
+            n = end - k0
+            rows = lax.broadcasted_iota(jnp.int32, (n, NB), 0)
+            left, right = ae[k0:end, :NB], ae[k0:end, NB:]
+            columns = [jnp.broadcast_to(left[:, k0 + c : k0 + c + 1], (n, NB)) for c in range(STRIP)]
+            scales = []
+            for k in range(STRIP):
+                pivot = columns[k][k : k + 1, :]
+                scales.append(lax.rsqrt(pivot))
                 factor = jnp.where(rows > k, columns[k] * (1.0 / pivot), 0.0)
-                for c in range(k + 1, PANEL):
+                for c in range(k + 1, STRIP):
                     columns[c] = columns[c] - factor * columns[c][k : k + 1, :]
                 left = left - factor * left[k : k + 1, :]
                 right = right - factor * right[k : k + 1, :]
-        scale = lax.rsqrt(pivots)
-        left, right = left * scale, right * scale
-        ae[k0 : k0 + PANEL, NB:] = right
-        below = k0 + PANEL
-        if below < NB:
-            ae[below:, :NB] = ae[below:, :NB] - exact(left, left, 0, 0)[below:]
-            ae[below:, NB:] = ae[below:, NB:] - exact(left, right, 0, 0)[below:]
+            scale = jnp.concatenate(scales, axis=0)
+            ae[k0 : k0 + STRIP, :NB] = left[:STRIP] * scale
+            ae[k0 : k0 + STRIP, NB:] = right[:STRIP] * scale
+            if n > STRIP:
+                ae[k0 + STRIP : end, :NB] = left[STRIP:]
+                ae[k0 + STRIP : end, NB:] = right[STRIP:]
+        if end < NB:
+            done = ae[top:end, :]
+            ae[end:, :] = ae[end:, :] - exact(done[:, :NB], done, 0, 0)[end:]
 
 
 def inverse_kernel(meta_ref, mine_ref, other_ref, out_ref, loss_ref, a, ae, diagonal):
@@ -306,8 +343,7 @@
             a[hi:, hi:] = a[hi:, hi:] - exact(below, below, 1, 1)
             out_ref[hi:, :hi] = out_ref[hi:, :hi] - exact(below, done, 1, 0)
     out = out_ref[...]
-    loss = jnp.max(jnp.sum(out * out * diagonal[...], axis=1, keepdims=True), axis=0, keepdims=True)
-    loss_ref[...] = jnp.broadcast_to(loss, loss_ref.shape)
+    loss_ref[0, 0] = jnp.max(jnp.sum(out * out * diagonal[...], axis=1, keepdims=True))
 
 
 def inverse_factor(meta, mine, other):
@@ -315,10 +351,10 @@
         inverse_kernel,
         out_shape=(
             jax.ShapeDtypeStruct((RANK, RANK), F32),
-            jax.ShapeDtypeStruct((8, NB), F32),
+            jax.ShapeDtypeStruct((1, 1), F32),
         ),
         in_specs=[smem_spec(), vmem_spec(), vmem_spec()],
-        out_specs=(vmem_spec(), vmem_spec()),
+        out_specs=(vmem_spec(), smem_spec()),
         scratch_shapes=[
             pltpu.VMEM((RANK, RANK), F32),
             pltpu.VMEM((NB, 2 * NB), F32),
@@ -330,8 +366,18 @@
     )(meta, mine, other)
 
 
+def two_terms(a):
+    top = a.astype(BF16)
+    return top, (a - top.astype(F32)).astype(BF16)
+
+
 def solve_kernel(w_ref, inv_ref, out_ref):
-    out_ref[...] = exact(w_ref[...].astype(F32), inv_ref[...], 1, 1).astype(BF16)
+    if w_ref.dtype == BF16:
+        top, rest = two_terms(inv_ref[...])
+        out = dot(w_ref[...], top, 1, 1) + dot(w_ref[...], rest, 1, 1)
+    else:
+        out = exact(w_ref[...], inv_ref[...], 1, 1)
+    out_ref[...] = out.astype(BF16)
 
 
 def solve_rows(w, inverse):
@@ -345,67 +391,93 @@
     )(w, inverse)
 
 
-def ortho_kernel(meta_ref, mine_ref, other_ref, inv_ref, out_ref):
-    core = meta_ref[0]
-    for ref, place in ((mine_ref, core), (other_ref, 1 - core)):
-        rows = pl.ds(pl.multiple_of(place * HALF, HALF), HALF)
-        out_ref[rows, :] = exact(ref[...], inv_ref[...], 1, 1).astype(BF16)
-
-
-def ortho_left(meta, mine, other, inverse):
-    return pl.pallas_call(
-        ortho_kernel,
-        out_shape=jax.ShapeDtypeStruct((RANK, RANK), BF16),
-        in_specs=[smem_spec()] + [vmem_spec()] * 3,
-        out_specs=vmem_spec(),
-        compiler_params=params(),
-        name="ortho_left",
-    )(meta, mine, other, inverse)
-
-
-def apply_kernel(parts, meta_ref, b_ref, q_ref, sums_ref, *refs):
-    rights, (m_ref, u_ref) = refs[:parts], refs[-2:]
-    scale = lax.rsqrt(sums_ref[0:1, :] + 1e-6) * math.sqrt(D * F / RANK)
-    scaled = (q_ref[...].astype(F32) * scale).astype(BF16)
-    width = RANK // parts
-    feedback = direction = 0.0
-    for k, right in enumerate(rights):
-        cols = slice(k * width, (k + 1) * width)
-        feedback += dot(q_ref[:, cols], right[...], 1, 1)
-        direction += dot(scaled[:, cols], right[...], 1, 1)
+def apply_both(b, q, scaled, right):
+    feedback = dot(q, right, 1, 1)
+    return (b.astype(F32) - 0.05 * feedback).astype(BF16), dot(scaled, right, 1, 1).astype(BF16)
+
+
+def apply_kernel(meta_ref, b_ref, mine_ref, other_ref, inv_ref, sums_ref, *refs):
+    rights, (m_ref, u_ref, q_ref, scaled_ref) = refs[:3], refs[3:]
+    i = pl.program_id(0)
+
+    @pl.when(i == 0)
+    def _():
+        scale = lax.rsqrt(sums_ref[0:1, :] + 1e-6) * math.sqrt(D * F / RANK)
+        top, rest = two_terms(inv_ref[...])
+        for ref, place in ((mine_ref, meta_ref[0]), (other_ref, 1 - meta_ref[0])):
+            rows = pl.ds(pl.multiple_of(place * HALF, HALF), HALF)
+            p_top, p_rest = two_terms(ref[...])
+            q = dot(p_top, top, 1, 1) + (dot(p_top, rest, 1, 1) + dot(p_rest, top, 1, 1))
+            q = q.astype(BF16)
+            q_ref[rows, :] = q
+            scaled_ref[rows, :] = (q.astype(F32) * scale).astype(BF16)
+
+    for k in range(3):
+
+        @pl.when(i == k)
+        def _():
+            m_ref[...], u_ref[...] = apply_both(
+                b_ref[...], q_ref[...], scaled_ref[...], rights[k][...]
+            )
+
+
+def apply_three(meta, blended, mine, other, inverse, sums, rights):
+    rows, cols = blended.shape
+
+    def place(i, meta_ref):
+        offset = jnp.where(i == 0, 0, jnp.where(i == 1, 3, 1))
+        return (0, (meta_ref[3] + offset) % 4)
+
+    here = pl.BlockSpec((rows, cols // 4), place)
+    whole = lambda a: pl.BlockSpec(a.shape, lambda i, meta_ref: (0, 0))
+    shape = jax.ShapeDtypeStruct((rows, cols), BF16)
+    square = jax.ShapeDtypeStruct((rows, RANK), BF16)
+    rest = [mine, other, inverse, sums] + rights
+    return pl.pallas_call(
+        apply_kernel,
+        grid_spec=pltpu.PrefetchScalarGridSpec(
+            num_scalar_prefetch=1,
+            grid=(3,),
+            in_specs=[here] + [whole(a) for a in rest],
+            out_specs=[here, here, whole(square), whole(square)],
+        ),
+        out_shape=[shape, shape, square, square],
+        compiler_params=params(),
+        name="apply_three",
+    )(meta, blended, *rest)
+
+
+def last_kernel(meta_ref, b_ref, q_ref, scaled_ref, a_ref, c_ref, m_in, u_in, m_ref, u_ref):
+    q, scaled = q_ref[...], scaled_ref[...]
+    feedback = dot(q[:, :HALF], a_ref[...], 1, 1) + dot(q[:, HALF:], c_ref[...], 1, 1)
+    direction = dot(scaled[:, :HALF], a_ref[...], 1, 1) + dot(scaled[:, HALF:], c_ref[...], 1, 1)
     m_ref[...] = (b_ref[...].astype(F32) - 0.05 * feedback).astype(BF16)
     u_ref[...] = direction.astype(BF16)
 
 
-def apply_block(meta, blended, q, sums, rights, offset, outs):
+def apply_last(meta, blended, q, scaled, rights, outs):
     rows, cols = blended.shape
     tiles = 2
     here = pl.BlockSpec(
-        (rows // tiles, cols // 4), lambda i, meta_ref: (i, (meta_ref[3] + offset) % 4)
+        (rows // tiles, cols // 4), lambda i, meta_ref: (i, (meta_ref[3] + 2) % 4)
     )
-    whole = lambda a: pl.BlockSpec(a.shape, lambda i, meta_ref: (0, 0))
-    n = len(rights)
+    part = pl.BlockSpec((rows // tiles, RANK), lambda i, meta_ref: (i, 0))
+    whole = pl.BlockSpec((cols // 4, HALF), lambda i, meta_ref: (0, 0))
+    kept = pl.BlockSpec(memory_space=pl.ANY)
     shape = jax.ShapeDtypeStruct((rows, cols), BF16)
-    kept = [pl.BlockSpec(memory_space=pl.ANY)] * len(outs)
-    return pl.pallas_call(
-        functools.partial(apply_kernel, n),
+    return pl.pallas_call(
+        last_kernel,
         grid_spec=pltpu.PrefetchScalarGridSpec(
             num_scalar_prefetch=1,
             grid=(tiles,),
-            in_specs=[
-                here,
-                pl.BlockSpec((rows // tiles, RANK), lambda i, meta_ref: (i, 0)),
-                whole(sums),
-            ]
-            + [whole(r) for r in rights]
-            + kept,
+            in_specs=[here, part, part, whole, whole, kept, kept],
             out_specs=[here, here],
         ),
         out_shape=[shape, shape],
-        input_output_aliases={4 + n + k: k for k in range(len(outs))},
-        compiler_params=params(),
-        name="apply_block",
-    )(meta, blended, q, sums, *rights, *outs)
+        input_output_aliases={6: 0, 7: 1},
+        compiler_params=params(),
+        name="apply_last",
+    )(meta, blended, q, scaled, *rights, *outs)
 
 
 def sums_kernel(r_ref, out_ref):
@@ -449,7 +521,7 @@
         wide = right_partial(meta, blended, mine, other, 2, F32)
         return solve_rows(scatter(scatter(wide, FIRST_GROUPS), SECOND_GROUPS), inverse)
 
-    block = lax.cond(loss[0, 0] <= LOSS_MAX**2, lambda: solve_rows(w, inverse), careful)
+    block = lax.cond(loss.reshape(()) <= LOSS_MAX**2, lambda: solve_rows(w, inverse), careful)
     right = exchange(jnp.tile(block, (4, 1)), AXES, SECOND_GROUPS)
     right_low = send_first(right, 1)
     right_high = send_first(right, -1)
@@ -458,12 +530,10 @@
     right_low, right_high, sums = lax.optimization_barrier((right_low, right_high, sums))
     far_a = send_first(right_low[:, :HALF], 1)
     far_b = send_first(right_high[:, HALF:], -1)
-    q = ortho_left(meta, mine, other, inverse)
-    outs = apply_block(meta, blended, q, sums, [right], 0, [])
-    outs = apply_block(meta, blended, q, sums, [right_low], 3, outs)
-    outs = apply_block(meta, blended, q, sums, [right_high], 1, outs)
-    outs = apply_block(meta, blended, q, sums, [far_a, far_b], 2, outs)
-    return tuple(outs)
+    *outs, q, scaled = apply_three(
+        meta, blended, mine, other, inverse, sums, [right, right_low, right_high]
+    )
+    return tuple(apply_last(meta, blended, q, scaled, [far_a, far_b], outs))
 
 
 def solution(mesh):

time: 257 us -> 248 us (0.965)
  Pallas kernels: 68.6 us -> 54.5 us
  waiting for transfers between devices: 71.8 us -> 77.3 us
    pallas_call x6 -> x3, Pallas kernels: 30.1 us -> 20 us  [the longest x1 10 us: left_partial(): pl.pallas_call(left_kernel, grid=(2,), out_shape=(jax.ShapeDtypeStruct((r...]
    reduce_scatter x4, waiting for transfers between devices: 66.3 us -> 70.6 us  [scatter(): lax.psum_scatter(a, AXES, scatter_dimension=0, axis_index_groups=groups,...]
    pallas_call x1, Pallas kernels: 22 us -> 18 us  [inverse_factor(): pl.pallas_call(inverse_kernel, out_shape=(jax.ShapeDtypeStruct((RANK, RAN...]
  transfers between devices with their start and end apart: 12 -> 12, of which waited for: 6 -> 8; matrix products, arithmetic and copies ran while one was open for 0% -> 0% of each run, Pallas kernels for 14% -> 11%
where the time goes in v3:
time: 248 us; the launch traced here: 247 us
  blocking collectives  81.6 us (33%)
  waiting for transfers between devices  77.3 us (31%)
  Pallas kernels  54.5 us (22%)
  starting transfers between devices  16.3 us (7%)
  between operations  15.2 us (6%)
    all_to_all x6, blocking collectives, exchange(): return lax.all_to_all(a, axis, 0, 0, axis_index_groups=groups, tiled=True)  81.6 us
    reduce_scatter x4, waiting for transfers between devices, scatter(): lax.psum_scatter(a, AXES, scatter_dimension=0, axis_index_groups=groups,...  70.6 us
    pallas_call x1, Pallas kernels, inverse_factor(): pl.pallas_call(inverse_kernel, out_shape=(jax.ShapeDtypeStruct((RANK, RAN...  18 us
    pallas_call x2, Pallas kernels, right_partial(): pl.pallas_call(functools.partial(right_kernel, terms), grid=(4,), in_spec...  13.8 us
    ppermute x4, starting transfers between devices, swap_cores(): return lax.ppermute(a, 'tp', [(i, i ^ 1) for i in range(8)])  12.3 us
    pallas_call x1, Pallas kernels, left_partial(): pl.pallas_call(left_kernel, grid=(2,), out_shape=(jax.ShapeDtypeStruct((r...  10 us
    pallas_call x1, Pallas kernels, apply_three(): pl.pallas_call(apply_kernel, grid_spec=pltpu.PrefetchScalarGridSpec(num_s...  7.03 us
    ppermute x4, waiting for transfers between devices, swap_cores(): return lax.ppermute(a, 'tp', [(i, i ^ 1) for i in range(8)])  5.4 us
  transfers between devices with their start and end apart: 12, of which 8 were waited for; matrix products, arithmetic and copies ran while one was open for 0% of the time, Pallas kernels for 11%

profile of v3, /device:TPU:1, one launch (start us, length us, event | category | flops | bytes accessed | tf_op | source)
XLA Modules:
  0.0 247.3 jit_solution(1135650859909744246)
XLA Ops:
  7.2 0.0 reduce-scatter.9.cloned.1.call-start
  7.9 0.1 stack.19.meta_ref
  8.0 10.0 %left_partial.1 = (bf16[512,3584]{1,0:T(8,128)(2,1)}, f32[256,512]{1,0:T(8,128)}, f32[256,512]{1,0:T(8,128)}) custom-call(s32[5]{0:T(128)S(1)} %stack.19.meta_ref, bf16[512,3584]{1,0:T(8,128)(2,1)} %m_ref.1, bf16[512,3584]{1,0:T(8,128)(2,1)} %g_ref.1), custom_call_target="tpu_custom_call" | custom-call | tf_op jit(solution)/shard_map/left_partial/pallas_call | solution.py:202
  18.0 1.4 collective-permute-start
  19.4 1.7 collective-permute-done
  21.2 1.1 add.24
  22.3 13.5 %all_to_all.64 = f32[4,64,512]{2,1,0:T(8,128)S(1)} all-to-all(f32[4,64,512]{2,1,0:T(8,128)S(1)} %bitcast.36), channel_id=1, replica_groups={{0,2,4,6},{1,3,5,7},{8,10,12,14},{9,11,13,15},{16,18,20,22},{17,19,21,2..., dimensions={0} | all-to-all | bytes 1048576 | tf_op jit(solution)/shard_map/all_to_all | solution.py:70
  35.9 10.1 %all_to_all.65 = f32[4,64,512]{2,1,0:T(8,128)S(1)} all-to-all(f32[4,64,512]{2,1,0:T(8,128)S(1)} %bitcast.23), channel_id=1, replica_groups={{0,2,4,6},{1,3,5,7},{8,10,12,14},{9,11,13,15},{16,18,20,22},{17,19,21,2..., dimensions={0} | all-to-all | bytes 1048576 | tf_op jit(solution)/shard_map/all_to_all | solution.py:70
  46.0 2.7 %collective-permute-start.1 = (f32[256,512]{1,0:T(8,128)S(1)}, f32[256,512]{1,0:T(8,128)S(1)}, u32[]{:S(2)}, u32[]{:S(2)}) collective-permute-start(f32[256,512]{1,0:T(8,128)S(1)} %bitcast.31), channel_id=1, source_target_pairs={{0,1},{1,0},{2,3},{3,2},{4,5},{5,4},{6,7},{7,6},{8,9},{9,8},{10,11... | collective-permute-start | bytes 1572872 | tf_op jit(solution)/shard_map/ppermute | solution.py:54
  48.7 1.5 collective-permute-done.1.other_ref
  50.2 5.8 %right_partial.3 = bf16[3584,512]{1,0:T(8,128)(2,1)} custom-call(s32[5]{0:T(128)S(1)} %stack.19.meta_ref, bf16[512,3584]{1,0:T(8,128)(2,1)} %get-tuple-element.47.b_ref, f32[256,512]{1,0:T(8,128)S(1)} %bitcast.32, f32[256,512]{1,0:T(8,128)S(1)} %collective-permute-done.1.other_ref), custom_call_target="tpu_custom_call" | custom-call | tf_op jit(solution)/shard_map/right_partial/pallas_call | solution.py:277
  56.0 0.0 reduce-scatter.9.cloned.1.call-update
  56.1 0.0 reduce-scatter.11.cloned.1.call-start
  56.1 1.4 gram_share.1
  57.5 16.9 %all_to_all.66 = f32[16,40,128]{2,1,0:T(8,128)S(1)} all-to-all(f32[16,40,128]{2,1,0:T(8,128)S(1)} %bitcast.24), channel_id=1, replica_groups=mesh['fsdp'=16,'tp'=8] {'fsdp'}, dimensions={0} | all-to-all | bytes 655360 | tf_op jit(solution)/shard_map/all_to_all | solution.py:70
  74.5 12.9 %all_to_all.67 = f32[16,40,128]{2,1,0:T(8,128)S(1)} all-to-all(f32[16,40,128]{2,1,0:T(8,128)S(1)} %bitcast.28), channel_id=1, replica_groups=mesh['fsdp'=16,'tp'=8] {'fsdp'}, dimensions={0} | all-to-all | bytes 655360 | tf_op jit(solution)/shard_map/all_to_all | solution.py:70
  87.4 3.3 %collective-permute-start.2 = (f32[640,128]{1,0:T(8,128)S(1)}, f32[640,128]{1,0:T(8,128)S(1)}, u32[]{:S(2)}, u32[]{:S(2)}) collective-permute-start(f32[640,128]{1,0:T(8,128)S(1)} %bitcast.25), channel_id=1, source_target_pairs={{0,1},{1,0},{2,3},{3,2},{4,5},{5,4},{6,7},{7,6},{8,9},{9,8},{10,11... | collective-permute-start | bytes 983048 | tf_op jit(solution)/shard_map/ppermute | solution.py:54
  90.7 1.3 collective-permute-done.2.other_ref
  92.0 0.0 reduce-scatter.9.cloned.1.call-done
  92.0 0.0 reduce-scatter.11.cloned.1.call-update
  92.0 18.0 %inverse_factor.1 = (f32[512,512]{1,0:T(8,128)S(1)}, f32[1,1]{1,0:T(1,128)}) custom-call(s32[5]{0:T(128)S(1)} %stack.19.meta_ref, f32[640,128]{1,0:T(8,128)S(1)} %bitcast.26, f32[640,128]{1,0:T(8,128)S(1)} %collective-permute-done.2.other_ref), custom_call_target="tpu_custom_call" | custom-call | bytes 70000000 | tf_op jit(solution)/shard_map/inverse_factor/pallas_call | solution.py:350
  110.0 1.0 reduce-scatter.11.cloned.1.call-done
  111.6 79.9 %conditional.1 = (bf16[224,512]{1,0:T(8,128)(2,1)S(1)}) conditional(s32[]{:T(128)} %bitcast.12, (s32[5]{0:T(128)S(1)}, bf16[512,3584]{1,0:T(8,128)(2,1)}, f32[256,512]{1,0:T(8,128)S(1)}, f32[256,512]{1,0:T(8,128)S(1)}, f32[512,512]{1,0:T(8,128)S(1)}) %tuple.33, (bf16[224,512]{1,0:T(8,128)(2,1)}, f32[512,512]{1,0:T(8,128)S(1)}) %tuple.21), branch_computations={%region_2.5_spmd, %region_5.6_spmd} | conditional | bytes 36241524 | solution.py:524
  111.6 0.0 reduce-scatter.5.cloned.1.call-start
  111.7 8.0 %right_partial.2 = f32[3584,512]{1,0:T(8,128)} custom-call(s32[5]{0:T(128)S(1)} %get-tuple-element.14.meta_ref, bf16[512,3584]{1,0:T(8,128)(2,1)} %get-tuple-element.18.b_ref, f32[256,512]{1,0:T(8,128)S(1)} %get-tuple-element.19.mine_ref, f32[256,512]{1,0:T(8,128)S(1)} %get-tuple-element.20.other_ref), custom_call_target="tpu_custom_call" | custom-call | tf_op jit(solution)/shard_map/cond/branch_0_fun/right_partial/pallas_call | solution.py:277
  119.7 0.0 reduce-scatter.5.cloned.1.call-update
  119.7 0.0 reduce-scatter.7.cloned.1.call-start
  119.8 45.1 %reduce-scatter.5.cloned.1.call-done = f32[896,512]{1,0:T(8,128)} async-done(((f32[3584,512]{1,0:T(8,128)}), f32[896,512]{1,0:T(8,128)}) %reduce-scatter.5.cloned.1.call-update) | async-done | bytes 1835024 | tf_op jit(solution)/shard_map/cond/branch_0_fun/reduce_scatter | solution.py:86
  164.9 0.0 reduce-scatter.7.cloned.1.call-update
  164.9 24.5 %reduce-scatter.7.cloned.1.call-done.w_ref = f32[224,512]{1,0:T(8,128)} async-done(((f32[896,512]{1,0:T(8,128)}), f32[224,512]{1,0:T(8,128)}) %reduce-scatter.7.cloned.1.call-update) | async-done | bytes 458768 | tf_op jit(solution)/shard_map/cond/branch_0_fun/reduce_scatter | solution.py:86
  189.4 0.0 copy-start
  189.4 1.0 copy-done
  190.4 1.1 solve_rows.2
  191.5 0.0 copy-start.1
  191.6 0.1 tile.2
  191.6 11.9 %all_to_all.68 = bf16[4,224,512]{2,1,0:T(8,128)(2,1)S(1)} all-to-all(bf16[4,224,512]{2,1,0:T(8,128)(2,1)S(1)} %tile.2), channel_id=1, replica_groups={{0,32,64,96},{2,34,66,98},{4,36,68,100},{6,38,70,102},{8,40,72,104},{10..., dimensions={0} | all-to-all | bytes 1835008 | tf_op jit(solution)/shard_map/all_to_all | solution.py:70
  203.6 2.3 collective-permute-start.4
  205.9 0.0 collective-permute-start.3
  205.9 0.1 block_sums.1
  206.0 16.2 %all_to_all.69 = f32[16,1,512]{2,1,0:T(1,128)S(1)} all-to-all(f32[16,1,512]{2,1,0:T(1,128)S(1)} %copy.7), channel_id=1, replica_groups={{0,2,4,6,8,10,12,14,16,18,20,22,24,26,28,30},{32,34,36,38,40,42,44,46,4..., dimensions={0} | all-to-all | bytes 65536 | tf_op jit(solution)/shard_map/all_to_all | solution.py:70
  222.2 4.8 %collective-permute-start.5 = (f32[16,512]{1,0:T(8,128)S(1)}, f32[16,512]{1,0:T(8,128)S(1)}, u32[]{:S(2)}, u32[]{:S(2)}) collective-permute-start(f32[16,512]{1,0:T(8,128)S(1)} %sum_parts.5), channel_id=1, source_target_pairs={{0,1},{1,0},{2,3},{3,2},{4,5},{5,4},{6,7},{7,6},{8,9},{9,8},{10,11... | collective-permute-start | bytes 98312 | tf_op jit(solution)/shard_map/ppermute | solution.py:54
  227.0 0.9 collective-permute-done.5
  227.9 0.0 collective-permute-done.4.refs_2_
  227.9 0.0 collective-permute-done.3.refs_1_
  228.0 1.2 collective-permute-start.7
  229.2 0.3 collective-permute-start.6
  229.5 0.0 copy-done.1
  229.5 7.0 %apply_three.1 = (bf16[512,3584]{1,0:T(8,128)(2,1)}, bf16[512,3584]{1,0:T(8,128)(2,1)}, bf16[512,512]{1,0:T(8,128)(2,1)S(1)}, bf16[512,512]{1,0:T(8,128)(2,1)S(1)}) custom-call(s32[5]{0:T(128)S(1)} %stack.19.meta_ref, bf16[512,3584]{1,0:T(8,128)(2,1)S(1)} %copy-done.1, f32[256,512]{1,0:T(8,128)S(1)} %bitcast.35, ...), custom_call_target="tpu_custom_call" | custom-call | tf_op jit(solution)/shard_map/apply_three/pallas_call | solution.py:436
  236.6 0.0 collective-permute-done.7.c_ref
  236.6 1.2 collective-permute-done.6.a_ref
  237.8 3.0 %apply_last.1 = (bf16[512,3584]{1,0:T(8,128)(2,1)}, bf16[512,3584]{1,0:T(8,128)(2,1)}) custom-call(s32[5]{0:T(128)S(1)} %stack.19.meta_ref, bf16[512,3584]{1,0:T(8,128)(2,1)S(1)} %copy-done.1, bf16[512,512]{1,0:T(8,128)(2,1)S(1)} %get-tuple-element.64.q_ref, ...), custom_call_target="tpu_custom_call", output_to_operand_aliasing={{0}: (6, {}), {1}: (7, {})} | custom-call | tf_op jit(solution)/shard_map/apply_last/pallas_call | solution.py:468
  (8 shorter events, 0.2 us)
Async XLA Ops:
  7.2 84.8 %reduce-scatter.9.cloned.1.call-start = ((), (), s32[]{:S(2)}) async-start(), calls=%async_computation.12 | async-start | bytes 4587520 | tf_op jit(solution)/shard_map/reduce_scatter | solution.py:86
  18.0 3.2 %collective-permute-start = (f32[256,512]{1,0:T(8,128)}, f32[256,512]{1,0:T(8,128)S(1)}, u32[]{:S(2)}, u32[]{:S(2)}) collective-permute-start(f32[256,512]{1,0:T(8,128)} %get-tuple-element.49), channel_id=1, source_target_pairs={{0,1},{1,0},{2,3},{3,2},{4,5},{5,4},{6,7},{7,6},{8,9},{9,8},{10,11... | collective-permute-start | bytes 1572872 | tf_op jit(solution)/shard_map/ppermute | solution.py:54
  46.0 4.3 %collective-permute-start.1 = (f32[256,512]{1,0:T(8,128)S(1)}, f32[256,512]{1,0:T(8,128)S(1)}, u32[]{:S(2)}, u32[]{:S(2)}) collective-permute-start(f32[256,512]{1,0:T(8,128)S(1)} %bitcast.31), channel_id=1, source_target_pairs={{0,1},{1,0},{2,3},{3,2},{4,5},{5,4},{6,7},{7,6},{8,9},{9,8},{10,11... | collective-permute-start | bytes 1572872 | tf_op jit(solution)/shard_map/ppermute | solution.py:54
  56.1 54.9 %reduce-scatter.11.cloned.1.call-start = ((), (), s32[]{:S(2)}) async-start(), calls=%async_computation.13 | async-start | bytes 1146880 | tf_op jit(solution)/shard_map/reduce_scatter | solution.py:86
  87.4 4.6 %collective-permute-start.2 = (f32[640,128]{1,0:T(8,128)S(1)}, f32[640,128]{1,0:T(8,128)S(1)}, u32[]{:S(2)}, u32[]{:S(2)}) collective-permute-start(f32[640,128]{1,0:T(8,128)S(1)} %bitcast.25), channel_id=1, source_target_pairs={{0,1},{1,0},{2,3},{3,2},{4,5},{5,4},{6,7},{7,6},{8,9},{9,8},{10,11... | collective-permute-start | bytes 983048 | tf_op jit(solution)/shard_map/ppermute | solution.py:54
  111.6 53.2 %reduce-scatter.5.cloned.1.call-start = ((), (), s32[]{:S(2)}) async-start(), calls=%async_computation.10 | async-start | bytes 9175040 | tf_op jit(solution)/shard_map/cond/branch_0_fun/reduce_scatter | solution.py:86
  119.7 69.7 %reduce-scatter.7.cloned.1.call-start = ((), (), s32[]{:S(2)}) async-start(), calls=%async_computation.11 | async-start | bytes 2293760 | tf_op jit(solution)/shard_map/cond/branch_0_fun/reduce_scatter | solution.py:86
  189.4 1.0 copy-start
  191.5 38.0 %copy-start.1 = (bf16[512,3584]{1,0:T(8,128)(2,1)S(1)}, bf16[512,3584]{1,0:T(8,128)(2,1)}, u32[]{:S(2)}) copy-start(bf16[512,3584]{1,0:T(8,128)(2,1)} %get-tuple-element.47.b_ref) | copy-start | bytes 11010052
  203.6 24.3 %collective-permute-start.4 = (bf16[896,512]{1,0:T(8,128)(2,1)S(1)}, bf16[896,512]{1,0:T(8,128)(2,1)S(1)}, u32[]{:S(2)}, u32[]{:S(2)}) collective-permute-start(bf16[896,512]{1,0:T(8,128)(2,1)S(1)} %bitcast.18), channel_id=1, source_target_pairs={{0,24},{1,97},{2,26},{3,99},{4,28},{5,101},{6,30},{7,103},{8,0},{9... | collective-permute-start | bytes 2752520 | tf_op jit(solution)/shard_map/ppermute | solution.py:46
  205.9 22.0 %collective-permute-start.3 = (bf16[896,512]{1,0:T(8,128)(2,1)S(1)}, bf16[896,512]{1,0:T(8,128)(2,1)S(1)}, u32[]{:S(2)}, u32[]{:S(2)}) collective-permute-start(bf16[896,512]{1,0:T(8,128)(2,1)S(1)} %bitcast.19), channel_id=1, source_target_pairs={{0,8},{1,33},{2,10},{3,35},{4,12},{5,37},{6,14},{7,39},{8,16},{9,4... | collective-permute-start | bytes 2752520 | tf_op jit(solution)/shard_map/ppermute | solution.py:46
  222.2 5.7 %collective-permute-start.5 = (f32[16,512]{1,0:T(8,128)S(1)}, f32[16,512]{1,0:T(8,128)S(1)}, u32[]{:S(2)}, u32[]{:S(2)}) collective-permute-start(f32[16,512]{1,0:T(8,128)S(1)} %sum_parts.5), channel_id=1, source_target_pairs={{0,1},{1,0},{2,3},{3,2},{4,5},{5,4},{6,7},{7,6},{8,9},{9,8},{10,11... | collective-permute-start | bytes 98312 | tf_op jit(solution)/shard_map/ppermute | solution.py:54
  228.0 8.6 %collective-permute-start.7 = (bf16[896,256]{1,0:T(8,128)(2,1)S(1)}, bf16[896,256]{1,0:T(8,128)(2,1)S(1)}, u32[]{:S(2)}, u32[]{:S(2)}) collective-permute-start(bf16[896,256]{1,0:T(8,128)(2,1)S(1)} %slice.7), channel_id=1, source_target_pairs={{0,24},{1,97},{2,26},{3,99},{4,28},{5,101},{6,30},{7,103},{8,0},{9... | collective-permute-start | bytes 1376264 | tf_op jit(solution)/shard_map/ppermute | solution.py:46
  229.2 8.6 %collective-permute-start.6 = (bf16[896,256]{1,0:T(8,128)(2,1)S(1)}, bf16[896,256]{1,0:T(8,128)(2,1)S(1)}, u32[]{:S(2)}, u32[]{:S(2)}) collective-permute-start(bf16[896,256]{1,0:T(8,128)(2,1)S(1)} %slice.6), channel_id=1, source_target_pairs={{0,8},{1,33},{2,10},{3,35},{4,12},{5,37},{6,14},{7,39},{8,16},{9,4... | collective-permute-start | bytes 1376264 | tf_op jit(solution)/shard_map/ppermute | solution.py:46
Sparse Core Ops, SparseCore 0:
  56.2 34.0 reduce-scatter.8
  92.7 18.1 reduce-scatter.10
  119.8 44.9 reduce-scatter.4
  167.1 22.2 reduce-scatter.6

commit v4 on v3

--- a/solution.py
+++ b/solution.py
@@ -61,9 +61,6 @@
 FIRST_GROUPS = [[flat(y, x, z, 0) for x in range(4)] for y in range(4) for z in range(4)] + [
     [flat(y, x, z, 1) for y in range(4)] for x in range(4) for z in range(4)
 ]
-FIRST_Z_GROUPS = [[flat(y, x, z, 0) for x in range(4) for z in range(4)] for y in range(4)] + [
-    [flat(y, x, z, 1) for y in range(4) for z in range(4)] for x in range(4)
-]
 
 
 def exchange(a, axis, groups=None):
@@ -88,19 +85,20 @@
     )
 
 
-def sum_kernel(n, a_ref, out_ref):
+def sum_kernel(n, copies, a_ref, out_ref):
     rows = a_ref.shape[0] // n
     total = a_ref[:rows, :]
     for k in range(1, n):
         total = total + a_ref[k * rows : (k + 1) * rows, :]
-    for k in range(n):
+    for k in range(copies):
         out_ref[k * rows : (k + 1) * rows, :] = total
 
 
-def sum_parts(a, n):
-    return pl.pallas_call(
-        functools.partial(sum_kernel, n),
-        out_shape=jax.ShapeDtypeStruct(a.shape, a.dtype),
+def sum_parts(a, n, copies):
+    rows, cols = a.shape
+    return pl.pallas_call(
+        functools.partial(sum_kernel, n, copies),
+        out_shape=jax.ShapeDtypeStruct((rows // n * copies, cols), a.dtype),
         in_specs=[vmem_spec()],
         out_specs=vmem_spec(),
         compiler_params=params(),
@@ -215,40 +213,27 @@
     )(meta, momentum, gradient)
 
 
-GRAM_SHARE = (((0, 512, 0, 128), (128, 256, 128, 256)), ((256, 512, 128, 384), (384, 512, 384, 512)))
-
-
-def gram_blocks(core):
-    return [
-        (i, j)
-        for r0, r1, c0, c1 in GRAM_SHARE[core]
-        for i in range(r0, r1, NB)
-        for j in range(c0, c1, NB)
-    ]
-
-
-def gram_kernel(meta_ref, mine_ref, other_ref, out_ref):
-    for core in range(2):
-
-        @pl.when(meta_ref[0] == core)
-        def _():
-            k = 0
-            for r0, r1, c0, c1 in GRAM_SHARE[core]:
-                g = exact(mine_ref[:, r0:r1], mine_ref[:, c0:c1], 0, 0) + exact(
-                    other_ref[:, r0:r1], other_ref[:, c0:c1], 0, 0
-                )
-                for i in range(0, r1 - r0, NB):
-                    for j in range(0, c1 - c0, NB):
-                        out_ref[k * NB : (k + 1) * NB, :] = g[i : i + NB, j : j + NB]
-                        k += 1
+SHARE = NB // 2
+
+
+def gram_kernel(meta_ref, mine_ref, other_ref, out_ref, g):
+    core, z = meta_ref[0], meta_ref[1] // 2
+    cols = pl.ds(pl.multiple_of(z * NB, NB), NB)
+    g[...] = exact(mine_ref[:, cols], mine_ref[...], 0, 0) + exact(
+        other_ref[:, cols], other_ref[...], 0, 0
+    )
+    rows = pl.ds(pl.multiple_of(core * SHARE, SHARE), SHARE)
+    for k in range(4):
+        out_ref[k * SHARE : (k + 1) * SHARE, :] = g[rows, k * NB : (k + 1) * NB]
 
 
 def gram_share(meta, mine, other):
     return pl.pallas_call(
         gram_kernel,
-        out_shape=jax.ShapeDtypeStruct((5 * NB, NB), F32),
+        out_shape=jax.ShapeDtypeStruct((4 * SHARE, NB), F32),
         in_specs=[smem_spec(), vmem_spec(), vmem_spec()],
         out_specs=vmem_spec(),
+        scratch_shapes=[pltpu.VMEM((NB, RANK), F32)],
         compiler_params=params(),
         name="gram_share",
     )(meta, mine, other)
@@ -272,11 +257,11 @@
 
 def right_partial(meta, blended, mine, other, terms, wire):
     rows, cols = blended.shape
-    block = cols // 4
+    block = cols // 2
     whole = pl.BlockSpec((HALF, RANK), lambda r: (0, 0))
     return pl.pallas_call(
         functools.partial(right_kernel, terms),
-        grid=(4,),
+        grid=(2,),
         in_specs=[smem_spec(), pl.BlockSpec((rows, block), lambda r: (0, r)), whole, whole],
         out_specs=pl.BlockSpec((block, RANK), lambda r: (r, 0)),
         scratch_shapes=[pltpu.VMEM((RANK, terms * RANK), BF16)],
@@ -315,14 +300,12 @@
 
 
 def inverse_kernel(meta_ref, mine_ref, other_ref, out_ref, loss_ref, a, ae, diagonal):
-    for core in range(2):
-        for share, ref in ((core, mine_ref), (1 - core, other_ref)):
-
-            @pl.when(meta_ref[0] == core)
-            def _():
-                for k, (i, j) in enumerate(gram_blocks(share)):
-                    a[i : i + NB, j : j + NB] = ref[k * NB : (k + 1) * NB, :]
-
+    for ref, core in ((mine_ref, meta_ref[0]), (other_ref, 1 - meta_ref[0])):
+        for z in range(4):
+            rows = pl.ds(pl.multiple_of(z * NB + core * SHARE, SHARE), SHARE)
+            for k in range(z + 1):
+                place = (z * 4 + k) * SHARE
+                a[rows, k * NB : (k + 1) * NB] = ref[place : place + SHARE, :]
     big = lambda d: lax.broadcasted_iota(jnp.int32, (RANK, RANK), d)
     small = lambda d: lax.broadcasted_iota(jnp.int32, (NB, NB), d)
     out_ref[...] = jnp.where(big(0) == big(1), 1.0, 0.0)
@@ -396,13 +379,14 @@
     return (b.astype(F32) - 0.05 * feedback).astype(BF16), dot(scaled, right, 1, 1).astype(BF16)
 
 
-def apply_kernel(meta_ref, b_ref, mine_ref, other_ref, inv_ref, sums_ref, *refs):
+def apply_kernel(meta_ref, b_ref, mine_ref, other_ref, inv_ref, sums_ref, swapped_ref, *refs):
     rights, (m_ref, u_ref, q_ref, scaled_ref) = refs[:3], refs[3:]
-    i = pl.program_id(0)
-
-    @pl.when(i == 0)
+    i, j = pl.program_id(0), pl.program_id(1)
+
+    @pl.when((i == 0) & (j == 0))
     def _():
-        scale = lax.rsqrt(sums_ref[0:1, :] + 1e-6) * math.sqrt(D * F / RANK)
+        sums = sums_ref[0:1, :] + swapped_ref[0:1, :]
+        scale = lax.rsqrt(sums + 1e-6) * math.sqrt(D * F / RANK)
         top, rest = two_terms(inv_ref[...])
         for ref, place in ((mine_ref, meta_ref[0]), (other_ref, 1 - meta_ref[0])):
             rows = pl.ds(pl.multiple_of(place * HALF, HALF), HALF)
@@ -412,32 +396,36 @@
             q_ref[rows, :] = q
             scaled_ref[rows, :] = (q.astype(F32) * scale).astype(BF16)
 
+    tile = m_ref.shape[0]
+    rows = pl.ds(pl.multiple_of(j * tile, tile), tile)
     for k in range(3):
 
         @pl.when(i == k)
         def _():
             m_ref[...], u_ref[...] = apply_both(
-                b_ref[...], q_ref[...], scaled_ref[...], rights[k][...]
+                b_ref[...], q_ref[rows, :], scaled_ref[rows, :], rights[k][...]
             )
 
 
 def apply_three(meta, blended, mine, other, inverse, sums, rights):
     rows, cols = blended.shape
 
-    def place(i, meta_ref):
+    tiles = 2
+
+    def place(i, j, meta_ref):
         offset = jnp.where(i == 0, 0, jnp.where(i == 1, 3, 1))
-        return (0, (meta_ref[3] + offset) % 4)
-
-    here = pl.BlockSpec((rows, cols // 4), place)
-    whole = lambda a: pl.BlockSpec(a.shape, lambda i, meta_ref: (0, 0))
+        return (j, (meta_ref[3] + offset) % 4)
+
+    here = pl.BlockSpec((rows // tiles, cols // 4), place)
+    whole = lambda a: pl.BlockSpec(a.shape, lambda i, j, meta_ref: (0, 0))
     shape = jax.ShapeDtypeStruct((rows, cols), BF16)
     square = jax.ShapeDtypeStruct((rows, RANK), BF16)
-    rest = [mine, other, inverse, sums] + rights
+    rest = [mine, other, inverse] + sums + rights
     return pl.pallas_call(
         apply_kernel,
         grid_spec=pltpu.PrefetchScalarGridSpec(
             num_scalar_prefetch=1,
-            grid=(3,),
+            grid=(3, tiles),
             in_specs=[here] + [whole(a) for a in rest],
             out_specs=[here, here, whole(square), whole(square)],
         ),
@@ -488,7 +476,7 @@
 def block_sums(r):
     return pl.pallas_call(
         sums_kernel,
-        out_shape=jax.ShapeDtypeStruct((16, RANK), F32),
+        out_shape=jax.ShapeDtypeStruct((32, RANK), F32),
         in_specs=[vmem_spec()],
         out_specs=vmem_spec(),
         compiler_params=params(),
@@ -504,14 +492,15 @@
 
     blended, keep, send = left_partial(meta, momentum, gradient)
     half = keep + swap_cores(send)
-    mine = exchange(sum_parts(exchange(half, "tp", Z_GROUPS), 4), "tp", Z_GROUPS)
+    mine = exchange(sum_parts(exchange(half, "tp", Z_GROUPS), 4, 4), "tp", Z_GROUPS)
     other = swap_cores(mine)
 
     w = right_partial(meta, blended, mine, other, 1, BF16)
     mine, other, w = lax.optimization_barrier((mine, other, w))
     w = scatter(w, FIRST_GROUPS)
     gram = exchange(gram_share(meta, mine, other), "fsdp")
-    gram = exchange(sum_parts(gram, 16), "fsdp")
+    gram = exchange(sum_parts(gram, 16, 16), "fsdp")
+    gram = exchange(jnp.tile(gram, (4, 1)), "tp", Z_GROUPS)
     w, gram, gram_other = lax.optimization_barrier((w, gram, swap_cores(gram)))
     w = scatter(w, SECOND_GROUPS)
     inverse, loss = inverse_factor(meta, gram, gram_other)
@@ -525,11 +514,13 @@
     right = exchange(jnp.tile(block, (4, 1)), AXES, SECOND_GROUPS)
     right_low = send_first(right, 1)
     right_high = send_first(right, -1)
-    sums = sum_parts(exchange(block_sums(right), AXES, FIRST_Z_GROUPS), 16)
-    sums = sums + swap_cores(sums)
-    right_low, right_high, sums = lax.optimization_barrier((right_low, right_high, sums))
+    sums = sum_parts(exchange(block_sums(right), "tp", Z_GROUPS), 4, 1)
+    parts = [sums] + [send_first(sums, k) for k in (1, 2, 3)]
+    right_low, right_high, *parts = lax.optimization_barrier((right_low, right_high, *parts))
     far_a = send_first(right_low[:, :HALF], 1)
     far_b = send_first(right_high[:, HALF:], -1)
+    sums = sum(parts)
+    sums = [sums, swap_cores(sums)]
     *outs, q, scaled = apply_three(
         meta, blended, mine, other, inverse, sums, [right, right_low, right_high]
     )

time: 248 us -> 249 us (level)
  starting transfers between devices: 16.3 us -> 23 us
  blocking collectives: 81.6 us -> 78.2 us
    reduce_scatter x4, waiting for transfers between devices: 70.6 us -> 66.8 us  [scatter(): lax.psum_scatter(a, AXES, scatter_dimension=0, axis_index_groups=groups,...]
    all_to_all x6 -> x7, blocking collectives: 81.6 us -> 78.2 us  [exchange(): return lax.all_to_all(a, axis, 0, 0, axis_index_groups=groups, tiled=True)]
    ppermute x4 -> x7, starting transfers between devices: 3.83 us -> 7.26 us  [send_first(): return lax.ppermute(a, AXES, shift(True, step))]
    ppermute x4, starting transfers between devices: 12.3 us -> 15.6 us  [swap_cores(): return lax.ppermute(a, 'tp', [(i, i ^ 1) for i in range(8)])]
  transfers between devices with their start and end apart: 12 -> 15, of which waited for: 8 -> 8; matrix products, arithmetic and copies ran while one was open for 0% -> 0% of each run, Pallas kernels for 11% -> 11%
where the time goes in v4:
time: 249 us
  blocking collectives  78.2 us (31%)
  waiting for transfers between devices  75.9 us (30%)
  Pallas kernels  53.8 us (22%)
  starting transfers between devices  23 us (9%)
  between operations  15.2 us (6%)
    all_to_all x7, blocking collectives, exchange(): return lax.all_to_all(a, axis, 0, 0, axis_index_groups=groups, tiled=True)  78.2 us
    reduce_scatter x4, waiting for transfers between devices, scatter(): lax.psum_scatter(a, AXES, scatter_dimension=0, axis_index_groups=groups,...  66.8 us
    pallas_call x1, Pallas kernels, inverse_factor(): pl.pallas_call(inverse_kernel, out_shape=(jax.ShapeDtypeStruct((RANK, RAN...  17.8 us
    ppermute x4, starting transfers between devices, swap_cores(): return lax.ppermute(a, 'tp', [(i, i ^ 1) for i in range(8)])  15.6 us
    pallas_call x2, Pallas kernels, right_partial(): pl.pallas_call(functools.partial(right_kernel, terms), grid=(2,), in_spec...  12.9 us
    pallas_call x1, Pallas kernels, left_partial(): pl.pallas_call(left_kernel, grid=(2,), out_shape=(jax.ShapeDtypeStruct((r...  10 us
    pallas_call x1, Pallas kernels, apply_three(): pl.pallas_call(apply_kernel, grid_spec=pltpu.PrefetchScalarGridSpec(num_s...  7.65 us
    ppermute x7, starting transfers between devices, send_first(): return lax.ppermute(a, AXES, shift(True, step))  7.26 us
  transfers between devices with their start and end apart: 15, of which 8 were waited for; matrix products, arithmetic and copies ran while one was open for 0% of the time, Pallas kernels for 11%

profile of v4, /device:TPU:1, one launch (start us, length us, event | category | flops | bytes accessed | tf_op | source)
XLA Modules:
  0.0 248.6 jit_solution(1389839836303075704)
XLA Ops:
  7.2 0.0 reduce-scatter.9.cloned.1.call-start
  7.9 0.1 stack.19.meta_ref
  8.0 10.0 %left_partial.1 = (bf16[512,3584]{1,0:T(8,128)(2,1)}, f32[256,512]{1,0:T(8,128)}, f32[256,512]{1,0:T(8,128)}) custom-call(s32[5]{0:T(128)S(1)} %stack.19.meta_ref, bf16[512,3584]{1,0:T(8,128)(2,1)} %m_ref.1, bf16[512,3584]{1,0:T(8,128)(2,1)} %g_ref.1), custom_call_target="tpu_custom_call" | custom-call | tf_op jit(solution)/shard_map/left_partial/pallas_call | solution.py:200
  18.0 1.4 collective-permute-start
  19.4 1.7 collective-permute-done
  21.2 1.1 add.30
  22.3 13.5 %all_to_all.70 = f32[4,64,512]{2,1,0:T(8,128)S(1)} all-to-all(f32[4,64,512]{2,1,0:T(8,128)S(1)} %bitcast.35), channel_id=1, replica_groups={{0,2,4,6},{1,3,5,7},{8,10,12,14},{9,11,13,15},{16,18,20,22},{17,19,21,2..., dimensions={0} | all-to-all | bytes 1048576 | tf_op jit(solution)/shard_map/all_to_all | solution.py:67
  35.9 10.1 %all_to_all.71 = f32[4,64,512]{2,1,0:T(8,128)S(1)} all-to-all(f32[4,64,512]{2,1,0:T(8,128)S(1)} %bitcast.24), channel_id=1, replica_groups={{0,2,4,6},{1,3,5,7},{8,10,12,14},{9,11,13,15},{16,18,20,22},{17,19,21,2..., dimensions={0} | all-to-all | bytes 1048576 | tf_op jit(solution)/shard_map/all_to_all | solution.py:67
  46.0 2.7 %collective-permute-start.1 = (f32[256,512]{1,0:T(8,128)S(1)}, f32[256,512]{1,0:T(8,128)S(1)}, u32[]{:S(2)}, u32[]{:S(2)}) collective-permute-start(f32[256,512]{1,0:T(8,128)S(1)} %bitcast.30), channel_id=1, source_target_pairs={{0,1},{1,0},{2,3},{3,2},{4,5},{5,4},{6,7},{7,6},{8,9},{9,8},{10,11... | collective-permute-start | bytes 1572872 | tf_op jit(solution)/shard_map/ppermute | solution.py:54
  48.7 1.5 collective-permute-done.1.other_ref
  50.2 5.1 %right_partial.3 = bf16[3584,512]{1,0:T(8,128)(2,1)} custom-call(s32[5]{0:T(128)S(1)} %stack.19.meta_ref, bf16[512,3584]{1,0:T(8,128)(2,1)} %get-tuple-element.50.b_ref, f32[256,512]{1,0:T(8,128)S(1)} %bitcast.31, f32[256,512]{1,0:T(8,128)S(1)} %collective-permute-done.1.other_ref), custom_call_target="tpu_custom_call" | custom-call | tf_op jit(solution)/shard_map/right_partial/pallas_call | solution.py:262
  55.3 0.0 reduce-scatter.9.cloned.1.call-update
  55.4 0.0 reduce-scatter.11.cloned.1.call-start
  55.4 1.2 gram_share.1
  56.7 14.5 %all_to_all.72 = f32[16,16,128]{2,1,0:T(8,128)S(1)} all-to-all(f32[16,16,128]{2,1,0:T(8,128)S(1)} %bitcast.25), channel_id=1, replica_groups=mesh['fsdp'=16,'tp'=8] {'fsdp'}, dimensions={0} | all-to-all | bytes 262144 | tf_op jit(solution)/shard_map/all_to_all | solution.py:67
  71.2 10.2 %all_to_all.73 = f32[16,16,128]{2,1,0:T(8,128)S(1)} all-to-all(f32[16,16,128]{2,1,0:T(8,128)S(1)} %bitcast.27), channel_id=1, replica_groups=mesh['fsdp'=16,'tp'=8] {'fsdp'}, dimensions={0} | all-to-all | bytes 262144 | tf_op jit(solution)/shard_map/all_to_all | solution.py:67
  81.5 9.3 %all_to_all.74 = f32[4,256,128]{2,1,0:T(8,128)S(1)} all-to-all(f32[4,256,128]{2,1,0:T(8,128)S(1)} %tile.7), channel_id=1, replica_groups={{0,2,4,6},{1,3,5,7},{8,10,12,14},{9,11,13,15},{16,18,20,22},{17,19,21,2..., dimensions={0} | all-to-all | bytes 1048576 | tf_op jit(solution)/shard_map/all_to_all | solution.py:67
  90.8 4.0 %collective-permute-start.2 = (f32[1024,128]{1,0:T(8,128)S(1)}, f32[1024,128]{1,0:T(8,128)S(1)}, u32[]{:S(2)}, u32[]{:S(2)}) collective-permute-start(f32[1024,128]{1,0:T(8,128)S(1)} %bitcast.21), channel_id=1, source_target_pairs={{0,1},{1,0},{2,3},{3,2},{4,5},{5,4},{6,7},{7,6},{8,9},{9,8},{10,11... | collective-permute-start | bytes 1572872 | tf_op jit(solution)/shard_map/ppermute | solution.py:54
  94.8 1.5 collective-permute-done.2.other_ref
  96.4 0.0 reduce-scatter.9.cloned.1.call-done
  96.4 0.0 reduce-scatter.11.cloned.1.call-update
  96.4 17.8 %inverse_factor.1 = (f32[512,512]{1,0:T(8,128)S(1)}, f32[1,1]{1,0:T(1,128)}) custom-call(s32[5]{0:T(128)S(1)} %stack.19.meta_ref, f32[1024,128]{1,0:T(8,128)S(1)} %bitcast.22, f32[1024,128]{1,0:T(8,128)S(1)} %collective-permute-done.2.other_ref), custom_call_target="tpu_custom_call" | custom-call | bytes 70000000 | tf_op jit(solution)/shard_map/inverse_factor/pallas_call | solution.py:333
  114.2 0.0 reduce-scatter.11.cloned.1.call-done
  114.9 76.8 %conditional.1 = (bf16[224,512]{1,0:T(8,128)(2,1)S(1)}) conditional(s32[]{:T(128)} %bitcast.13, (s32[5]{0:T(128)S(1)}, bf16[512,3584]{1,0:T(8,128)(2,1)}, f32[256,512]{1,0:T(8,128)S(1)}, f32[256,512]{1,0:T(8,128)S(1)}, f32[512,512]{1,0:T(8,128)S(1)}) %tuple.33, (bf16[224,512]{1,0:T(8,128)(2,1)}, f32[512,512]{1,0:T(8,128)S(1)}) %tuple.21), branch_computations={%region_2.5_spmd, %region_5.6_spmd} | conditional | bytes 36241524 | solution.py:513
  114.9 0.0 reduce-scatter.5.cloned.1.call-start
  114.9 7.8 %right_partial.2 = f32[3584,512]{1,0:T(8,128)} custom-call(s32[5]{0:T(128)S(1)} %get-tuple-element.14.meta_ref, bf16[512,3584]{1,0:T(8,128)(2,1)} %get-tuple-element.18.b_ref, f32[256,512]{1,0:T(8,128)S(1)} %get-tuple-element.19.mine_ref, f32[256,512]{1,0:T(8,128)S(1)} %get-tuple-element.20.other_ref), custom_call_target="tpu_custom_call" | custom-call | tf_op jit(solution)/shard_map/cond/branch_0_fun/right_partial/pallas_call | solution.py:262
  122.7 0.0 reduce-scatter.5.cloned.1.call-update
  122.7 0.0 reduce-scatter.7.cloned.1.call-start
  122.8 42.4 %reduce-scatter.5.cloned.1.call-done = f32[896,512]{1,0:T(8,128)} async-done(((f32[3584,512]{1,0:T(8,128)}), f32[896,512]{1,0:T(8,128)}) %reduce-scatter.5.cloned.1.call-update) | async-done | bytes 1835024 | tf_op jit(solution)/shard_map/cond/branch_0_fun/reduce_scatter | solution.py:83
  165.2 0.0 reduce-scatter.7.cloned.1.call-update
  165.3 24.3 %reduce-scatter.7.cloned.1.call-done.w_ref = f32[224,512]{1,0:T(8,128)} async-done(((f32[896,512]{1,0:T(8,128)}), f32[224,512]{1,0:T(8,128)}) %reduce-scatter.7.cloned.1.call-update) | async-done | bytes 458768 | tf_op jit(solution)/shard_map/cond/branch_0_fun/reduce_scatter | solution.py:83
  189.6 0.0 copy-start
  189.6 1.0 copy-done
  190.6 1.1 solve_rows.2
  191.7 0.0 copy-start.1
  191.7 0.1 tile.8
  191.8 12.1 %all_to_all.75 = bf16[4,224,512]{2,1,0:T(8,128)(2,1)S(1)} all-to-all(bf16[4,224,512]{2,1,0:T(8,128)(2,1)S(1)} %tile.8), channel_id=1, replica_groups={{0,32,64,96},{2,34,66,98},{4,36,68,100},{6,38,70,102},{8,40,72,104},{10..., dimensions={0} | all-to-all | bytes 1835008 | tf_op jit(solution)/shard_map/all_to_all | solution.py:67
  203.9 2.4 collective-permute-start.4
  206.3 0.0 collective-permute-start.3
  206.3 0.1 block_sums.1
  206.3 8.4 %all_to_all.76 = f32[4,8,512]{2,1,0:T(8,128)S(1)} all-to-all(f32[4,8,512]{2,1,0:T(8,128)S(1)} %bitcast.29), channel_id=1, replica_groups={{0,2,4,6},{1,3,5,7},{8,10,12,14},{9,11,13,15},{16,18,20,22},{17,19,21,2..., dimensions={0} | all-to-all | bytes 131072 | tf_op jit(solution)/shard_map/all_to_all | solution.py:67
  214.8 2.7 %collective-permute-start.7 = (f32[8,512]{1,0:T(8,128)S(1)}, f32[8,512]{1,0:T(8,128)S(1)}, u32[]{:S(2)}, u32[]{:S(2)}) collective-permute-start(f32[8,512]{1,0:T(8,128)S(1)} %sum_parts.5), channel_id=1, source_target_pairs={{0,24},{1,97},{2,26},{3,99},{4,28},{5,101},{6,30},{7,103},{8,0},{9... | collective-permute-start | bytes 49160 | tf_op jit(solution)/shard_map/ppermute | solution.py:46
  217.4 0.0 collective-permute-start.6
  217.4 0.7 collective-permute-start.5
  218.1 0.2 collective-permute-done.7
  218.3 3.2 %collective-permute-done.6 = f32[8,512]{1,0:T(8,128)S(1)} collective-permute-done((f32[8,512]{1,0:T(8,128)S(1)}, f32[8,512]{1,0:T(8,128)S(1)}, u32[]{:S(2)}, u32[]{:S(2)}) %collective-permute-start.6) | collective-permute-done | bytes 16416 | tf_op jit(solution)/shard_map/ppermute | solution.py:46
  221.5 0.0 collective-permute-done.5
  221.5 0.0 collective-permute-done.4.refs_2_
  221.5 0.0 collective-permute-done.3.refs_1_
  221.6 0.8 collective-permute-start.10
  222.4 0.7 collective-permute-start.9
  223.2 7.4 %collective-permute-start.8 = (f32[8,512]{1,0:T(8,128)S(1)}, f32[8,512]{1,0:T(8,128)S(1)}, u32[]{:S(2)}, u32[]{:S(2)}) collective-permute-start(f32[8,512]{1,0:T(8,128)S(1)} %add_add_fusion.sums_ref), channel_id=1, source_target_pairs={{0,1},{1,0},{2,3},{3,2},{4,5},{5,4},{6,7},{7,6},{8,9},{9,8},{10,11... | collective-permute-start | bytes 49160 | tf_op jit(solution)/shard_map/ppermute | solution.py:54
  230.6 0.8 collective-permute-done.8.swapped_ref
  231.4 0.0 copy-done.1
  231.4 7.7 %apply_three.1 = (bf16[512,3584]{1,0:T(8,128)(2,1)}, bf16[512,3584]{1,0:T(8,128)(2,1)}, bf16[512,512]{1,0:T(8,128)(2,1)S(1)}, bf16[512,512]{1,0:T(8,128)(2,1)S(1)}) custom-call(s32[5]{0:T(128)S(1)} %stack.19.meta_ref, bf16[512,3584]{1,0:T(8,128)(2,1)S(1)} %copy-done.1, f32[256,512]{1,0:T(8,128)S(1)} %bitcast.34, ...), custom_call_target="tpu_custom_call" | custom-call | tf_op jit(solution)/shard_map/apply_three/pallas_call | solution.py:424
  239.1 0.0 collective-permute-done.10.c_ref
  239.1 0.0 collective-permute-done.9.a_ref
  239.1 3.0 %apply_last.1 = (bf16[512,3584]{1,0:T(8,128)(2,1)}, bf16[512,3584]{1,0:T(8,128)(2,1)}) custom-call(s32[5]{0:T(128)S(1)} %stack.19.meta_ref, bf16[512,3584]{1,0:T(8,128)(2,1)S(1)} %copy-done.1, bf16[512,512]{1,0:T(8,128)(2,1)S(1)} %get-tuple-element.70.q_ref, ...), custom_call_target="tpu_custom_call", output_to_operand_aliasing={{0}: (6, {}), {1}: (7, {})} | custom-call | tf_op jit(solution)/shard_map/apply_last/pallas_call | solution.py:456
  (7 shorter events, 0.2 us)
Async XLA Ops:
  7.2 89.2 %reduce-scatter.9.cloned.1.call-start = ((), (), s32[]{:S(2)}) async-start(), calls=%async_computation.13 | async-start | bytes 4587520 | tf_op jit(solution)/shard_map/reduce_scatter | solution.py:83
  18.0 3.2 %collective-permute-start = (f32[256,512]{1,0:T(8,128)}, f32[256,512]{1,0:T(8,128)S(1)}, u32[]{:S(2)}, u32[]{:S(2)}) collective-permute-start(f32[256,512]{1,0:T(8,128)} %get-tuple-element.52), channel_id=1, source_target_pairs={{0,1},{1,0},{2,3},{3,2},{4,5},{5,4},{6,7},{7,6},{8,9},{9,8},{10,11... | collective-permute-start | bytes 1572872 | tf_op jit(solution)/shard_map/ppermute | solution.py:54
  46.0 4.3 %collective-permute-start.1 = (f32[256,512]{1,0:T(8,128)S(1)}, f32[256,512]{1,0:T(8,128)S(1)}, u32[]{:S(2)}, u32[]{:S(2)}) collective-permute-start(f32[256,512]{1,0:T(8,128)S(1)} %bitcast.30), channel_id=1, source_target_pairs={{0,1},{1,0},{2,3},{3,2},{4,5},{5,4},{6,7},{7,6},{8,9},{9,8},{10,11... | collective-permute-start | bytes 1572872 | tf_op jit(solution)/shard_map/ppermute | solution.py:54
  55.4 58.9 %reduce-scatter.11.cloned.1.call-start = ((), (), s32[]{:S(2)}) async-start(), calls=%async_computation.14 | async-start | bytes 1146880 | tf_op jit(solution)/shard_map/reduce_scatter | solution.py:83
  90.8 5.6 %collective-permute-start.2 = (f32[1024,128]{1,0:T(8,128)S(1)}, f32[1024,128]{1,0:T(8,128)S(1)}, u32[]{:S(2)}, u32[]{:S(2)}) collective-permute-start(f32[1024,128]{1,0:T(8,128)S(1)} %bitcast.21), channel_id=1, source_target_pairs={{0,1},{1,0},{2,3},{3,2},{4,5},{5,4},{6,7},{7,6},{8,9},{9,8},{10,11... | collective-permute-start | bytes 1572872 | tf_op jit(solution)/shard_map/ppermute | solution.py:54
  114.9 50.3 %reduce-scatter.5.cloned.1.call-start = ((), (), s32[]{:S(2)}) async-start(), calls=%async_computation.11 | async-start | bytes 9175040 | tf_op jit(solution)/shard_map/cond/branch_0_fun/reduce_scatter | solution.py:83
  122.7 66.8 %reduce-scatter.7.cloned.1.call-start = ((), (), s32[]{:S(2)}) async-start(), calls=%async_computation.12 | async-start | bytes 2293760 | tf_op jit(solution)/shard_map/cond/branch_0_fun/reduce_scatter | solution.py:83
  189.6 1.0 copy-start
  191.7 39.7 %copy-start.1 = (bf16[512,3584]{1,0:T(8,128)(2,1)S(1)}, bf16[512,3584]{1,0:T(8,128)(2,1)}, u32[]{:S(2)}) copy-start(bf16[512,3584]{1,0:T(8,128)(2,1)} %get-tuple-element.50.b_ref) | copy-start | bytes 11010052
  203.9 17.6 %collective-permute-start.4 = (bf16[896,512]{1,0:T(8,128)(2,1)S(1)}, bf16[896,512]{1,0:T(8,128)(2,1)S(1)}, u32[]{:S(2)}, u32[]{:S(2)}) collective-permute-start(bf16[896,512]{1,0:T(8,128)(2,1)S(1)} %bitcast.17), channel_id=1, source_target_pairs={{0,24},{1,97},{2,26},{3,99},{4,28},{5,101},{6,30},{7,103},{8,0},{9... | collective-permute-start | bytes 2752520 | tf_op jit(solution)/shard_map/ppermute | solution.py:46
  206.3 15.3 %collective-permute-start.3 = (bf16[896,512]{1,0:T(8,128)(2,1)S(1)}, bf16[896,512]{1,0:T(8,128)(2,1)S(1)}, u32[]{:S(2)}, u32[]{:S(2)}) collective-permute-start(bf16[896,512]{1,0:T(8,128)(2,1)S(1)} %bitcast.18), channel_id=1, source_target_pairs={{0,8},{1,33},{2,10},{3,35},{4,12},{5,37},{6,14},{7,39},{8,16},{9,4... | collective-permute-start | bytes 2752520 | tf_op jit(solution)/shard_map/ppermute | solution.py:46
  214.8 3.5 %collective-permute-start.7 = (f32[8,512]{1,0:T(8,128)S(1)}, f32[8,512]{1,0:T(8,128)S(1)}, u32[]{:S(2)}, u32[]{:S(2)}) collective-permute-start(f32[8,512]{1,0:T(8,128)S(1)} %sum_parts.5), channel_id=1, source_target_pairs={{0,24},{1,97},{2,26},{3,99},{4,28},{5,101},{6,30},{7,103},{8,0},{9... | collective-permute-start | bytes 49160 | tf_op jit(solution)/shard_map/ppermute | solution.py:46
  217.4 4.1 %collective-permute-start.6 = (f32[8,512]{1,0:T(8,128)S(1)}, f32[8,512]{1,0:T(8,128)S(1)}, u32[]{:S(2)}, u32[]{:S(2)}) collective-permute-start(f32[8,512]{1,0:T(8,128)S(1)} %sum_parts.5), channel_id=1, source_target_pairs={{0,16},{1,65},{2,18},{3,67},{4,20},{5,69},{6,22},{7,71},{8,24},{9,... | collective-permute-start | bytes 49160 | tf_op jit(solution)/shard_map/ppermute | solution.py:46
  217.4 4.1 %collective-permute-start.5 = (f32[8,512]{1,0:T(8,128)S(1)}, f32[8,512]{1,0:T(8,128)S(1)}, u32[]{:S(2)}, u32[]{:S(2)}) collective-permute-start(f32[8,512]{1,0:T(8,128)S(1)} %sum_parts.5), channel_id=1, source_target_pairs={{0,8},{1,33},{2,10},{3,35},{4,12},{5,37},{6,14},{7,39},{8,16},{9,4... | collective-permute-start | bytes 49160 | tf_op jit(solution)/shard_map/ppermute | solution.py:46
  221.6 17.4 %collective-permute-start.10 = (bf16[896,256]{1,0:T(8,128)(2,1)S(1)}, bf16[896,256]{1,0:T(8,128)(2,1)S(1)}, u32[]{:S(2)}, u32[]{:S(2)}) collective-permute-start(bf16[896,256]{1,0:T(8,128)(2,1)S(1)} %slice.7), channel_id=1, source_target_pairs={{0,24},{1,97},{2,26},{3,99},{4,28},{5,101},{6,30},{7,103},{8,0},{9... | collective-permute-start | bytes 1376264 | tf_op jit(solution)/shard_map/ppermute | solution.py:46
  222.4 16.6 %collective-permute-start.9 = (bf16[896,256]{1,0:T(8,128)(2,1)S(1)}, bf16[896,256]{1,0:T(8,128)(2,1)S(1)}, u32[]{:S(2)}, u32[]{:S(2)}) collective-permute-start(bf16[896,256]{1,0:T(8,128)(2,1)S(1)} %slice.6), channel_id=1, source_target_pairs={{0,8},{1,33},{2,10},{3,35},{4,12},{5,37},{6,14},{7,39},{8,16},{9,4... | collective-permute-start | bytes 1376264 | tf_op jit(solution)/shard_map/ppermute | solution.py:46
  223.2 8.2 %collective-permute-start.8 = (f32[8,512]{1,0:T(8,128)S(1)}, f32[8,512]{1,0:T(8,128)S(1)}, u32[]{:S(2)}, u32[]{:S(2)}) collective-permute-start(f32[8,512]{1,0:T(8,128)S(1)} %add_add_fusion.sums_ref), channel_id=1, source_target_pairs={{0,1},{1,0},{2,3},{3,2},{4,5},{5,4},{6,7},{7,6},{8,9},{9,8},{10,11... | collective-permute-start | bytes 49160 | tf_op jit(solution)/shard_map/ppermute | solution.py:54
Sparse Core Ops, SparseCore 0:
  55.5 30.0 reduce-scatter.8
  96.5 14.9 reduce-scatter.10
  122.9 42.3 reduce-scatter.4
  167.5 22.0 reduce-scatter.6

commit v5 on v3

--- a/solution.py
+++ b/solution.py
@@ -54,6 +54,10 @@
     return lax.ppermute(a, "tp", [(i, i ^ 1) for i in range(8)])
 
 
+def shift_z(a, step):
+    return lax.ppermute(a, "tp", [(i, (i + 2 * step) % 8) for i in range(8)])
+
+
 Z_GROUPS = [[c, 2 + c, 4 + c, 6 + c] for c in range(2)]
 SECOND_GROUPS = [[flat(y, x, z, 0) for y in range(4)] for x in range(4) for z in range(4)] + [
     [flat(y, x, z, 1) for x in range(4)] for y in range(4) for z in range(4)
@@ -61,9 +65,6 @@
 FIRST_GROUPS = [[flat(y, x, z, 0) for x in range(4)] for y in range(4) for z in range(4)] + [
     [flat(y, x, z, 1) for y in range(4)] for x in range(4) for z in range(4)
 ]
-FIRST_Z_GROUPS = [[flat(y, x, z, 0) for x in range(4) for z in range(4)] for y in range(4)] + [
-    [flat(y, x, z, 1) for y in range(4) for z in range(4)] for x in range(4)
-]
 
 
 def exchange(a, axis, groups=None):
@@ -88,19 +89,42 @@
     )
 
 
-def sum_kernel(n, a_ref, out_ref):
+def sum_kernel(n, copies, a_ref, out_ref):
     rows = a_ref.shape[0] // n
     total = a_ref[:rows, :]
     for k in range(1, n):
         total = total + a_ref[k * rows : (k + 1) * rows, :]
-    for k in range(n):
+    for k in range(copies):
         out_ref[k * rows : (k + 1) * rows, :] = total
 
 
-def sum_parts(a, n):
-    return pl.pallas_call(
-        functools.partial(sum_kernel, n),
-        out_shape=jax.ShapeDtypeStruct(a.shape, a.dtype),
+def piece_kernel(a_ref, out_ref, rounded_ref):
+    sum_kernel(4, 1, a_ref, out_ref)
+    for k in range(4):
+        rows = out_ref.shape[0]
+        rounded_ref[k * rows : (k + 1) * rows, :] = out_ref[...].astype(BF16)
+
+
+def sum_piece(a):
+    rows, cols = a.shape
+    return pl.pallas_call(
+        piece_kernel,
+        out_shape=(
+            jax.ShapeDtypeStruct((rows // 4, cols), F32),
+            jax.ShapeDtypeStruct((rows, cols), BF16),
+        ),
+        in_specs=[vmem_spec()],
+        out_specs=(vmem_spec(), vmem_spec()),
+        compiler_params=params(),
+        name="sum_piece",
+    )(a)
+
+
+def sum_parts(a, n, copies):
+    rows, cols = a.shape
+    return pl.pallas_call(
+        functools.partial(sum_kernel, n, copies),
+        out_shape=jax.ShapeDtypeStruct((rows // n * copies, cols), a.dtype),
         in_specs=[vmem_spec()],
         out_specs=vmem_spec(),
         compiler_params=params(),
@@ -116,6 +140,15 @@
 
 def exact(a, b, ca, cb):
     return dot(a, b, ca, cb, lax.Precision.HIGHEST)
+
+
+def two_terms(a):
+    top = a.astype(BF16)
+    return top, (a.astype(F32) - top.astype(F32)).astype(BF16)
+
+
+def product(a, b, ca, cb):
+    return dot(a, b, ca, cb) if a.dtype == BF16 else exact(a, b, ca, cb)
 
 
 def fold(v):
@@ -234,7 +267,7 @@
         def _():
             k = 0
             for r0, r1, c0, c1 in GRAM_SHARE[core]:
-                g = exact(mine_ref[:, r0:r1], mine_ref[:, c0:c1], 0, 0) + exact(
+                g = product(mine_ref[:, r0:r1], mine_ref[:, c0:c1], 0, 0) + product(
                     other_ref[:, r0:r1], other_ref[:, c0:c1], 0, 0
                 )
                 for i in range(0, r1 - r0, NB):
@@ -254,33 +287,33 @@
     )(meta, mine, other)
 
 
-def right_kernel(terms, meta_ref, b_ref, mine_ref, other_ref, out_ref, split):
+def right_kernel(meta_ref, b_ref, mine_ref, other_ref, out_ref, split):
+    terms = split.shape[1] // RANK
+
     @pl.when(pl.program_id(0) == 0)
     def _():
         core = meta_ref[0]
         for ref, place in ((mine_ref, core), (other_ref, 1 - core)):
             rows = pl.ds(pl.multiple_of(place * HALF, HALF), HALF)
-            rest = ref[...]
-            for k in range(terms):
-                term = rest.astype(BF16)
+            for k, term in enumerate(two_terms(ref[...])[:terms]):
                 split[rows, k * RANK : (k + 1) * RANK] = term
-                rest = rest - term.astype(F32)
 
     w = dot(b_ref[...], split[...], 0, 0)
     out_ref[...] = sum(w[:, k * RANK : (k + 1) * RANK] for k in range(terms)).astype(out_ref.dtype)
 
 
-def right_partial(meta, blended, mine, other, terms, wire):
+def right_partial(meta, blended, mine, other, steps):
     rows, cols = blended.shape
-    block = cols // 4
+    block = cols // steps
     whole = pl.BlockSpec((HALF, RANK), lambda r: (0, 0))
-    return pl.pallas_call(
-        functools.partial(right_kernel, terms),
-        grid=(4,),
+    terms = 1 if mine.dtype == BF16 else 2
+    return pl.pallas_call(
+        right_kernel,
+        grid=(steps,),
         in_specs=[smem_spec(), pl.BlockSpec((rows, block), lambda r: (0, r)), whole, whole],
         out_specs=pl.BlockSpec((block, RANK), lambda r: (r, 0)),
         scratch_shapes=[pltpu.VMEM((RANK, terms * RANK), BF16)],
-        out_shape=jax.ShapeDtypeStruct((cols, RANK), wire),
+        out_shape=jax.ShapeDtypeStruct((cols, RANK), mine.dtype),
         compiler_params=params(VMEM_MOST),
         name="right_partial",
     )(meta, blended, mine, other)
@@ -366,29 +399,30 @@
     )(meta, mine, other)
 
 
-def two_terms(a):
-    top = a.astype(BF16)
-    return top, (a - top.astype(F32)).astype(BF16)
-
-
-def solve_kernel(w_ref, inv_ref, out_ref):
+def solve_kernel(meta_ref, w_ref, mine_ref, other_ref, inv_ref, out_ref, q_ref):
     if w_ref.dtype == BF16:
         top, rest = two_terms(inv_ref[...])
-        out = dot(w_ref[...], top, 1, 1) + dot(w_ref[...], rest, 1, 1)
+        solve = lambda a: dot(a, top, 1, 1) + dot(a, rest, 1, 1)
     else:
-        out = exact(w_ref[...], inv_ref[...], 1, 1)
-    out_ref[...] = out.astype(BF16)
-
-
-def solve_rows(w, inverse):
+        solve = lambda a: exact(a, inv_ref[...], 1, 1)
+    out_ref[...] = solve(w_ref[...]).astype(BF16)
+    for ref, place in ((mine_ref, meta_ref[0]), (other_ref, 1 - meta_ref[0])):
+        rows = pl.ds(pl.multiple_of(place * HALF, HALF), HALF)
+        q_ref[rows, :] = solve(ref[...]).astype(BF16)
+
+
+def solve_rows(meta, w, mine, other, inverse):
     return pl.pallas_call(
         solve_kernel,
-        out_shape=jax.ShapeDtypeStruct(w.shape, BF16),
-        in_specs=[vmem_spec()] * 2,
-        out_specs=vmem_spec(),
+        out_shape=(
+            jax.ShapeDtypeStruct(w.shape, BF16),
+            jax.ShapeDtypeStruct((RANK, RANK), BF16),
+        ),
+        in_specs=[smem_spec()] + [vmem_spec()] * 4,
+        out_specs=(vmem_spec(),) * 2,
         compiler_params=params(),
         name="solve_rows",
-    )(w, inverse)
+    )(meta, w, mine, other, inverse)
 
 
 def apply_both(b, q, scaled, right):
@@ -396,52 +430,50 @@
     return (b.astype(F32) - 0.05 * feedback).astype(BF16), dot(scaled, right, 1, 1).astype(BF16)
 
 
-def apply_kernel(meta_ref, b_ref, mine_ref, other_ref, inv_ref, sums_ref, *refs):
-    rights, (m_ref, u_ref, q_ref, scaled_ref) = refs[:3], refs[3:]
-    i = pl.program_id(0)
-
-    @pl.when(i == 0)
+def apply_kernel(meta_ref, b_ref, q_ref, sums_ref, swapped_ref, *refs):
+    rights, (m_ref, u_ref, scaled_ref) = refs[:3], refs[3:]
+    i, j = pl.program_id(0), pl.program_id(1)
+
+    @pl.when((i == 0) & (j == 0))
     def _():
-        scale = lax.rsqrt(sums_ref[0:1, :] + 1e-6) * math.sqrt(D * F / RANK)
-        top, rest = two_terms(inv_ref[...])
-        for ref, place in ((mine_ref, meta_ref[0]), (other_ref, 1 - meta_ref[0])):
-            rows = pl.ds(pl.multiple_of(place * HALF, HALF), HALF)
-            p_top, p_rest = two_terms(ref[...])
-            q = dot(p_top, top, 1, 1) + (dot(p_top, rest, 1, 1) + dot(p_rest, top, 1, 1))
-            q = q.astype(BF16)
-            q_ref[rows, :] = q
-            scaled_ref[rows, :] = (q.astype(F32) * scale).astype(BF16)
-
+        sums = sums_ref[0:1, :] + swapped_ref[0:1, :]
+        scale = lax.rsqrt(sums + 1e-6) * math.sqrt(D * F / RANK)
+        scaled_ref[...] = (q_ref[...].astype(F32) * scale).astype(BF16)
+
+    tile = m_ref.shape[0]
+    rows = pl.ds(pl.multiple_of(j * tile, tile), tile)
     for k in range(3):
 
         @pl.when(i == k)
         def _():
             m_ref[...], u_ref[...] = apply_both(
-                b_ref[...], q_ref[...], scaled_ref[...], rights[k][...]
+                b_ref[...], q_ref[rows, :], scaled_ref[rows, :], rights[k][...]
             )
 
 
-def apply_three(meta, blended, mine, other, inverse, sums, rights):
+def apply_three(meta, blended, q, sums, rights):
     rows, cols = blended.shape
 
-    def place(i, meta_ref):
+    tiles = 2
+
+    def place(i, j, meta_ref):
         offset = jnp.where(i == 0, 0, jnp.where(i == 1, 3, 1))
-        return (0, (meta_ref[3] + offset) % 4)
-
-    here = pl.BlockSpec((rows, cols // 4), place)
-    whole = lambda a: pl.BlockSpec(a.shape, lambda i, meta_ref: (0, 0))
+        return (j, (meta_ref[3] + offset) % 4)
+
+    here = pl.BlockSpec((rows // tiles, cols // 4), place)
+    whole = lambda a: pl.BlockSpec(a.shape, lambda i, j, meta_ref: (0, 0))
     shape = jax.ShapeDtypeStruct((rows, cols), BF16)
     square = jax.ShapeDtypeStruct((rows, RANK), BF16)
-    rest = [mine, other, inverse, sums] + rights
+    rest = [q] + sums + rights
     return pl.pallas_call(
         apply_kernel,
         grid_spec=pltpu.PrefetchScalarGridSpec(
             num_scalar_prefetch=1,
-            grid=(3,),
+            grid=(3, tiles),
             in_specs=[here] + [whole(a) for a in rest],
-            out_specs=[here, here, whole(square), whole(square)],
+            out_specs=[here, here, whole(square)],
         ),
-        out_shape=[shape, shape, square, square],
+        out_shape=[shape, shape, square],
         compiler_params=params(),
         name="apply_three",
     )(meta, blended, *rest)
@@ -488,7 +520,7 @@
 def block_sums(r):
     return pl.pallas_call(
         sums_kernel,
-        out_shape=jax.ShapeDtypeStruct((16, RANK), F32),
+        out_shape=jax.ShapeDtypeStruct((8, RANK), F32),
         in_specs=[vmem_spec()],
         out_specs=vmem_spec(),
         compiler_params=params(),
@@ -504,35 +536,48 @@
 
     blended, keep, send = left_partial(meta, momentum, gradient)
     half = keep + swap_cores(send)
-    mine = exchange(sum_parts(exchange(half, "tp", Z_GROUPS), 4), "tp", Z_GROUPS)
+    piece, rounded = sum_piece(exchange(half, "tp", Z_GROUPS))
+
+    def gram_sum(mine, other):
+        gram = exchange(gram_share(meta, mine, other), "fsdp")
+        gram = exchange(sum_parts(gram, 16, 16), "fsdp")
+        return gram, swap_cores(gram)
+
+    def careful():
+        mine = exchange(jnp.tile(piece, (4, 1)), "tp", Z_GROUPS)
+        other = swap_cores(mine)
+        inverse, _ = inverse_factor(meta, *gram_sum(mine, other))
+        w = right_partial(meta, blended, mine, other, 4)
+        w = scatter(scatter(w, FIRST_GROUPS), SECOND_GROUPS)
+        return solve_rows(meta, w, mine, other, inverse)
+
+    mine = exchange(rounded, "tp", Z_GROUPS)
     other = swap_cores(mine)
-
-    w = right_partial(meta, blended, mine, other, 1, BF16)
+    w = right_partial(meta, blended, mine, other, 2)
     mine, other, w = lax.optimization_barrier((mine, other, w))
     w = scatter(w, FIRST_GROUPS)
-    gram = exchange(gram_share(meta, mine, other), "fsdp")
-    gram = exchange(sum_parts(gram, 16), "fsdp")
-    w, gram, gram_other = lax.optimization_barrier((w, gram, swap_cores(gram)))
+    gram = gram_sum(mine, other)
+    w, *gram = lax.optimization_barrier((w, *gram))
     w = scatter(w, SECOND_GROUPS)
-    inverse, loss = inverse_factor(meta, gram, gram_other)
+    inverse, loss = inverse_factor(meta, *gram)
     w, inverse, loss = lax.optimization_barrier((w, inverse, loss))
-
-    def careful():
-        wide = right_partial(meta, blended, mine, other, 2, F32)
-        return solve_rows(scatter(scatter(wide, FIRST_GROUPS), SECOND_GROUPS), inverse)
-
-    block = lax.cond(loss.reshape(()) <= LOSS_MAX**2, lambda: solve_rows(w, inverse), careful)
+    block, q = lax.cond(
+        loss.reshape(()) <= LOSS_MAX**2,
+        lambda: solve_rows(meta, w, mine, other, inverse),
+        careful,
+    )
     right = exchange(jnp.tile(block, (4, 1)), AXES, SECOND_GROUPS)
     right_low = send_first(right, 1)
     right_high = send_first(right, -1)
-    sums = sum_parts(exchange(block_sums(right), AXES, FIRST_Z_GROUPS), 16)
-    sums = sums + swap_cores(sums)
-    right_low, right_high, sums = lax.optimization_barrier((right_low, right_high, sums))
+    sums = block_sums(right)
+    sums = sums + sum(shift_z(sums, k) for k in (1, 2, 3))
+    parts = [sums] + [send_first(sums, k) for k in (1, 2, 3)]
+    right_low, right_high, *parts = lax.optimization_barrier((right_low, right_high, *parts))
     far_a = send_first(right_low[:, :HALF], 1)
     far_b = send_first(right_high[:, HALF:], -1)
-    *outs, q, scaled = apply_three(
-        meta, blended, mine, other, inverse, sums, [right, right_low, right_high]
-    )
+    sums = sum(parts)
+    sums = [sums, swap_cores(sums)]
+    *outs, scaled = apply_three(meta, blended, q, sums, [right, right_low, right_high])
     return tuple(apply_last(meta, blended, q, scaled, [far_a, far_b], outs))
 
 

time: 248 us -> 284 us (1.15); the launches traced: 247 us -> 280 us
  Pallas kernels: 54.5 us -> 75.5 us
  waiting for transfers between devices: 77.3 us -> 56.5 us
  blocking collectives: 81.6 us -> 99.2 us
  starting transfers between devices: 16.3 us -> 29.4 us
    reduce_scatter x4, waiting for transfers between devices: 70.6 us -> 41.6 us  [scatter(): lax.psum_scatter(a, AXES, scatter_dimension=0, axis_index_groups=groups,...]
    pallas_call x1 -> x2, Pallas kernels: 18 us -> 36.6 us  [inverse_factor(): pl.pallas_call(inverse_kernel, out_shape=(jax.ShapeDtypeStruct((RANK, RAN...]
    all_to_all x6 -> x8, blocking collectives: 81.6 us -> 99.2 us  [exchange(): return lax.all_to_all(a, axis, 0, 0, axis_index_groups=groups, tiled=True)]
    ppermute x4 -> x6, starting transfers between devices: 12.3 us -> 19.7 us  [swap_cores(): return lax.ppermute(a, 'tp', [(i, i ^ 1) for i in range(8)])]
    ppermute x0 -> x3, starting transfers between devices: none -> 3.79 us  [shift_z(): return lax.ppermute(a, 'tp', [(i, (i + 2 * step) % 8) for i in range(8)])]
    ppermute x0 -> x3, waiting for transfers between devices: none -> 3.52 us  [shift_z(): return lax.ppermute(a, 'tp', [(i, (i + 2 * step) % 8) for i in range(8)])]
    ppermute x4 -> x6, waiting for transfers between devices: 5.4 us -> 7.8 us  [swap_cores(): return lax.ppermute(a, 'tp', [(i, i ^ 1) for i in range(8)])]
    ppermute x4 -> x7, starting transfers between devices: 3.83 us -> 5.77 us  [send_first(): return lax.ppermute(a, AXES, shift(True, step))]
  transfers between devices with their start and end apart: 12 -> 20, of which waited for: 8 -> 13; matrix products, arithmetic and copies ran while one was open for 0% -> 0% of each run, Pallas kernels for 11% -> 16%
where the time goes in v5:
time: 284 us; the launch traced here: 280 us
  blocking collectives  99.2 us (35%)
  Pallas kernels  75.5 us (27%)
  waiting for transfers between devices  56.5 us (20%)
  starting transfers between devices  29.4 us (10%)
  between operations  15.3 us (5%)
    all_to_all x8, blocking collectives, exchange(): return lax.all_to_all(a, axis, 0, 0, axis_index_groups=groups, tiled=True)  99.2 us
    reduce_scatter x4, waiting for transfers between devices, scatter(): lax.psum_scatter(a, AXES, scatter_dimension=0, axis_index_groups=groups,...  41.6 us
    pallas_call x2, Pallas kernels, inverse_factor(): pl.pallas_call(inverse_kernel, out_shape=(jax.ShapeDtypeStruct((RANK, RAN...  36.6 us
    ppermute x6, starting transfers between devices, swap_cores(): return lax.ppermute(a, 'tp', [(i, i ^ 1) for i in range(8)])  19.7 us
    pallas_call x2, Pallas kernels, right_partial(): pl.pallas_call(right_kernel, grid=(steps,), in_specs=[smem_spec(), pl.Blo...  13.4 us
    pallas_call x1, Pallas kernels, left_partial(): pl.pallas_call(left_kernel, grid=(2,), out_shape=(jax.ShapeDtypeStruct((r...  10 us
    ppermute x6, waiting for transfers between devices, swap_cores(): return lax.ppermute(a, 'tp', [(i, i ^ 1) for i in range(8)])  7.8 us
    pallas_call x1, Pallas kernels, apply_three(): pl.pallas_call(apply_kernel, grid_spec=pltpu.PrefetchScalarGridSpec(num_s...  6.72 us
  transfers between devices with their start and end apart: 20, of which 13 were waited for; matrix products, arithmetic and copies ran while one was open for 0% of the time, Pallas kernels for 16%

profile of v5, /device:TPU:1, one launch (start us, length us, event | category | flops | bytes accessed | tf_op | source)
XLA Modules:
  0.0 279.5 jit_solution(14233277770923351942)
XLA Ops:
  7.2 0.0 reduce-scatter.9.cloned.1.call-start
  7.9 0.1 stack.19.meta_ref
  8.0 10.0 %left_partial.1 = (bf16[512,3584]{1,0:T(8,128)(2,1)}, f32[256,512]{1,0:T(8,128)}, f32[256,512]{1,0:T(8,128)}) custom-call(s32[5]{0:T(128)S(1)} %stack.19.meta_ref, bf16[512,3584]{1,0:T(8,128)(2,1)} %m_ref.1, bf16[512,3584]{1,0:T(8,128)(2,1)} %g_ref.1), custom_call_target="tpu_custom_call" | custom-call | tf_op jit(solution)/shard_map/left_partial/pallas_call | solution.py:235
  18.0 1.4 collective-permute-start.2
  19.4 1.7 collective-permute-done.2
  21.2 1.1 add.39
  22.3 13.5 %all_to_all.78 = f32[4,64,512]{2,1,0:T(8,128)S(1)} all-to-all(f32[4,64,512]{2,1,0:T(8,128)S(1)} %bitcast.43), channel_id=1, replica_groups={{0,2,4,6},{1,3,5,7},{8,10,12,14},{9,11,13,15},{16,18,20,22},{17,19,21,2..., dimensions={0} | all-to-all | bytes 1048576 | tf_op jit(solution)/shard_map/all_to_all | solution.py:71
  35.9 7.9 %all_to_all.79 = bf16[4,64,512]{2,1,0:T(8,128)(2,1)S(1)} all-to-all(bf16[4,64,512]{2,1,0:T(8,128)(2,1)S(1)} %bitcast.38), channel_id=1, replica_groups={{0,2,4,6},{1,3,5,7},{8,10,12,14},{9,11,13,15},{16,18,20,22},{17,19,21,2..., dimensions={0} | all-to-all | bytes 524288 | tf_op jit(solution)/shard_map/all_to_all | solution.py:71
  43.8 3.0 %collective-permute-start.3 = (bf16[256,512]{1,0:T(8,128)(2,1)S(1)}, bf16[256,512]{1,0:T(8,128)(2,1)S(1)}, u32[]{:S(2)}, u32[]{:S(2)}) collective-permute-start(bf16[256,512]{1,0:T(8,128)(2,1)S(1)} %bitcast.39), channel_id=1, source_target_pairs={{0,1},{1,0},{2,3},{3,2},{4,5},{5,4},{6,7},{7,6},{8,9},{9,8},{10,11... | collective-permute-start | bytes 786440 | tf_op jit(solution)/shard_map/ppermute | solution.py:54
  46.8 1.2 collective-permute-done.3.other_ref
  47.9 5.1 %right_partial.3 = bf16[3584,512]{1,0:T(8,128)(2,1)} custom-call(s32[5]{0:T(128)S(1)} %stack.19.meta_ref, bf16[512,3584]{1,0:T(8,128)(2,1)} %get-tuple-element.54.b_ref, bf16[256,512]{1,0:T(8,128)(2,1)S(1)} %bitcast.40, bf16[256,512]{1,0:T(8,128)(2,1)S(1)} %collective-permute-done.3.other_ref), custom_call_target="tpu_custom_call" | custom-call | tf_op jit(solution)/shard_map/right_partial/pallas_call | solution.py:310
  53.0 0.0 reduce-scatter.9.cloned.1.call-update
  53.0 0.0 reduce-scatter.11.cloned.1.call-start
  53.1 0.9 gram_share.3
  54.0 17.0 %all_to_all.80 = f32[16,40,128]{2,1,0:T(8,128)S(1)} all-to-all(f32[16,40,128]{2,1,0:T(8,128)S(1)} %bitcast.37), channel_id=1, replica_groups=mesh['fsdp'=16,'tp'=8] {'fsdp'}, dimensions={0} | all-to-all | bytes 655360 | tf_op jit(solution)/shard_map/all_to_all | solution.py:71
  71.0 12.9 %all_to_all.81 = f32[16,40,128]{2,1,0:T(8,128)S(1)} all-to-all(f32[16,40,128]{2,1,0:T(8,128)S(1)} %bitcast.34), channel_id=1, replica_groups=mesh['fsdp'=16,'tp'=8] {'fsdp'}, dimensions={0} | all-to-all | bytes 655360 | tf_op jit(solution)/shard_map/all_to_all | solution.py:71
  83.9 3.2 %collective-permute-start.4 = (f32[640,128]{1,0:T(8,128)S(1)}, f32[640,128]{1,0:T(8,128)S(1)}, u32[]{:S(2)}, u32[]{:S(2)}) collective-permute-start(f32[640,128]{1,0:T(8,128)S(1)} %bitcast.29), channel_id=1, source_target_pairs={{0,1},{1,0},{2,3},{3,2},{4,5},{5,4},{6,7},{7,6},{8,9},{9,8},{10,11... | collective-permute-start | bytes 983048 | tf_op jit(solution)/shard_map/ppermute | solution.py:54
  87.1 1.3 collective-permute-done.4.other_ref
  88.3 0.0 reduce-scatter.11.cloned.1.call-update
  88.4 18.3 %inverse_factor.3 = (f32[512,512]{1,0:T(8,128)}, f32[1,1]{1,0:T(1,128)}) custom-call(s32[5]{0:T(128)S(1)} %stack.19.meta_ref, f32[640,128]{1,0:T(8,128)S(1)} %bitcast.30, f32[640,128]{1,0:T(8,128)S(1)} %collective-permute-done.4.other_ref), custom_call_target="tpu_custom_call" | custom-call | bytes 70000000 | tf_op jit(solution)/shard_map/inverse_factor/pallas_call | solution.py:383
  106.7 0.7 reduce-scatter.11.cloned.1.call-done
  108.0 119.7 %conditional.1 = ((bf16[224,512]{1,0:T(8,128)(2,1)S(1)}, bf16[512,512]{1,0:T(8,128)(2,1)S(1)})) conditional(s32[]{:T(128)} %bitcast.17, (f32[64,512]{1,0:T(8,128)S(1)}, s32[5]{0:T(128)S(1)}, bf16[512,3584]{1,0:T(8,128)(2,1)}) %tuple.20, (s32[5]{0:T(128)S(1)}, bf16[224,512]{1,0:T(8,128)(2,1)}, bf16[256,512]{1,0:T(8,128)(2,1)S(1)}, ...), branch_computations={%region_2.5_spmd, %region_5.6_spmd} | conditional | bytes 121052856 | solution.py:564
  108.0 0.0 reduce-scatter.5.cloned.1.call-start
  108.0 0.1 tile.0
  108.1 10.9 %all_to_all.75 = f32[4,64,512]{2,1,0:T(8,128)S(1)} all-to-all(f32[4,64,512]{2,1,0:T(8,128)S(1)} %tile.0), channel_id=1, replica_groups={{0,2,4,6},{1,3,5,7},{8,10,12,14},{9,11,13,15},{16,18,20,22},{17,19,21,2..., dimensions={0} | all-to-all | bytes 1048576 | tf_op jit(solution)/shard_map/cond/branch_0_fun/all_to_all | solution.py:71
  119.0 4.1 %collective-permute-start = (f32[256,512]{1,0:T(8,128)S(1)}, f32[256,512]{1,0:T(8,128)S(1)}, u32[]{:S(2)}, u32[]{:S(2)}) collective-permute-start(f32[256,512]{1,0:T(8,128)S(1)} %bitcast.19), channel_id=1, source_target_pairs={{0,1},{1,0},{2,3},{3,2},{4,5},{5,4},{6,7},{7,6},{8,9},{9,8},{10,11... | collective-permute-start | bytes 1572872 | tf_op jit(solution)/shard_map/cond/branch_0_fun/ppermute | solution.py:54
  123.0 1.5 collective-permute-done.other_ref
  124.6 0.8 copy-done.2
  125.4 8.3 %right_partial.2 = f32[3584,512]{1,0:T(8,128)} custom-call(s32[5]{0:T(128)S(1)} %get-tuple-element.16.meta_ref, bf16[512,3584]{1,0:T(8,128)(2,1)} %get-tuple-element.17.b_ref, f32[256,512]{1,0:T(8,128)} %bitcast.20, f32[256,512]{1,0:T(8,128)} %copy-done.2), custom_call_target="tpu_custom_call" | custom-call | tf_op jit(solution)/shard_map/cond/branch_0_fun/right_partial/pallas_call | solution.py:310
  133.7 0.0 reduce-scatter.5.cloned.1.call-update
  133.7 0.0 reduce-scatter.7.cloned.1.call-start
  133.8 40.9 %reduce-scatter.5.cloned.1.call-done = f32[896,512]{1,0:T(8,128)} async-done(((f32[3584,512]{1,0:T(8,128)}), f32[896,512]{1,0:T(8,128)}) %reduce-scatter.5.cloned.1.call-update) | async-done | bytes 1835024 | tf_op jit(solution)/shard_map/cond/branch_0_fun/reduce_scatter | solution.py:87
  174.6 0.0 reduce-scatter.7.cloned.1.call-update
  174.7 1.4 gram_share.2
  176.1 12.8 %all_to_all.76 = f32[16,40,128]{2,1,0:T(8,128)S(1)} all-to-all(f32[16,40,128]{2,1,0:T(8,128)S(1)} %bitcast.28), channel_id=1, replica_groups=mesh['fsdp'=16,'tp'=8] {'fsdp'}, dimensions={0} | all-to-all | bytes 655360 | tf_op jit(solution)/shard_map/cond/branch_0_fun/all_to_all | solution.py:71
  189.0 12.4 %all_to_all.77 = f32[16,40,128]{2,1,0:T(8,128)S(1)} all-to-all(f32[16,40,128]{2,1,0:T(8,128)S(1)} %bitcast.36), channel_id=1, replica_groups=mesh['fsdp'=16,'tp'=8] {'fsdp'}, dimensions={0} | all-to-all | bytes 655360 | tf_op jit(solution)/shard_map/cond/branch_0_fun/all_to_all | solution.py:71
  201.4 2.1 collective-permute-start.1
  203.5 1.3 collective-permute-done.1.other_ref
  204.8 18.3 %inverse_factor.2 = (f32[512,512]{1,0:T(8,128)S(1)}, f32[1,1]{1,0:T(1,128)}) custom-call(s32[5]{0:T(128)S(1)} %get-tuple-element.16.meta_ref, f32[640,128]{1,0:T(8,128)S(1)} %bitcast.32, f32[640,128]{1,0:T(8,128)S(1)} %collective-permute-done.1.other_ref), custom_call_target="tpu_custom_call" | custom-call | bytes 70000000 | tf_op jit(solution)/shard_map/cond/branch_0_fun/inverse_factor/pallas_call | solution.py:383
  223.1 0.0 reduce-scatter.7.cloned.1.call-done.w_ref
  223.1 1.0 copy-done.4
  224.1 3.4 %solve_rows.2 = (bf16[224,512]{1,0:T(8,128)(2,1)S(1)}, bf16[512,512]{1,0:T(8,128)(2,1)S(1)}) custom-call(s32[5]{0:T(128)S(1)} %get-tuple-element.16.meta_ref, f32[224,512]{1,0:T(8,128)S(1)} %copy-done.4, f32[256,512]{1,0:T(8,128)S(1)} %bitcast.22, f32[256,512]{1,0:T(8,128)S(1)} %copy-done.3, f32[512,512]{1,0:T(8,128)S(1)} %get-tuple-element.19.inv_ref), custom_call_target="tpu_custom_call" | custom-call | tf_op jit(solution)/shard_map/cond/branch_0_fun/solve_rows/pallas_call | solution.py:415
  227.7 0.1 tile.4
  227.7 11.8 %all_to_all.82 = bf16[4,224,512]{2,1,0:T(8,128)(2,1)S(1)} all-to-all(bf16[4,224,512]{2,1,0:T(8,128)(2,1)S(1)} %tile.4), channel_id=1, replica_groups={{0,32,64,96},{2,34,66,98},{4,36,68,100},{6,38,70,102},{8,40,72,104},{10..., dimensions={0} | all-to-all | bytes 1835008 | tf_op jit(solution)/shard_map/all_to_all | solution.py:71
  239.5 1.2 collective-permute-start.6
  240.8 0.2 collective-permute-start.5
  241.0 0.1 block_sums.1
  241.1 2.8 collective-permute-start.9
  243.8 0.4 collective-permute-start.8
  244.2 0.7 collective-permute-start.7
  244.9 3.1 %collective-permute-done.8 = f32[8,512]{1,0:T(8,128)S(1)} collective-permute-done((f32[8,512]{1,0:T(8,128)S(1)}, f32[8,512]{1,0:T(8,128)S(1)}, u32[]{:S(2)}, u32[]{:S(2)}) %collective-permute-start.8) | collective-permute-done | bytes 16416 | tf_op jit(solution)/shard_map/ppermute | solution.py:58
  247.9 0.5 collective-permute-done.7
  248.4 2.1 collective-permute-start.12
  250.5 0.0 collective-permute-start.11
  250.5 0.6 collective-permute-start.10
  251.2 1.1 collective-permute-done.12
  252.2 2.3 collective-permute-done.11
  254.6 0.1 collective-permute-done.10
  254.8 0.7 collective-permute-start.15
  255.5 0.8 collective-permute-start.14
  256.3 5.9 %collective-permute-start.13 = (f32[8,512]{1,0:T(8,128)S(1)}, f32[8,512]{1,0:T(8,128)S(1)}, u32[]{:S(2)}, u32[]{:S(2)}) collective-permute-start(f32[8,512]{1,0:T(8,128)S(1)} %add_add_fusion.sums_ref), channel_id=1, source_target_pairs={{0,1},{1,0},{2,3},{3,2},{4,5},{5,4},{6,7},{7,6},{8,9},{9,8},{10,11... | collective-permute-start | bytes 49160 | tf_op jit(solution)/shard_map/ppermute | solution.py:54
  262.3 0.8 collective-permute-done.13.swapped_ref
  263.1 6.7 %apply_three.1 = (bf16[512,3584]{1,0:T(8,128)(2,1)}, bf16[512,3584]{1,0:T(8,128)(2,1)}, bf16[512,512]{1,0:T(8,128)(2,1)S(1)}) custom-call(s32[5]{0:T(128)S(1)} %stack.19.meta_ref, bf16[512,3584]{1,0:T(8,128)(2,1)S(1)} %copy-done.5, bf16[512,512]{1,0:T(8,128)(2,1)S(1)} %get-tuple-element.70.q_ref, f32[8,512]{1,0:T(8,128)S(1)} %add_add_fusion.sums_ref, ...), custom_call_target="tpu_custom_call" | custom-call | tf_op jit(solution)/shard_map/apply_three/pallas_call | solution.py:468
  269.8 3.0 %apply_last.1 = (bf16[512,3584]{1,0:T(8,128)(2,1)}, bf16[512,3584]{1,0:T(8,128)(2,1)}) custom-call(s32[5]{0:T(128)S(1)} %stack.19.meta_ref, bf16[512,3584]{1,0:T(8,128)(2,1)S(1)} %copy-done.5, bf16[512,512]{1,0:T(8,128)(2,1)S(1)} %get-tuple-element.70.q_ref, ...), custom_call_target="tpu_custom_call", output_to_operand_aliasing={{0}: (6, {}), {1}: (7, {})} | custom-call | tf_op jit(solution)/shard_map/apply_last/pallas_call | solution.py:500
  (23 shorter events, 0.2 us)
Async XLA Ops:
  7.2 81.2 %reduce-scatter.9.cloned.1.call-start = ((), (), s32[]{:S(2)}) async-start(), calls=%async_computation.14 | async-start | bytes 4587520 | tf_op jit(solution)/shard_map/reduce_scatter | solution.py:87
  18.0 3.2 %collective-permute-start.2 = (f32[256,512]{1,0:T(8,128)}, f32[256,512]{1,0:T(8,128)S(1)}, u32[]{:S(2)}, u32[]{:S(2)}) collective-permute-start(f32[256,512]{1,0:T(8,128)} %get-tuple-element.56), channel_id=1, source_target_pairs={{0,1},{1,0},{2,3},{3,2},{4,5},{5,4},{6,7},{7,6},{8,9},{9,8},{10,11... | collective-permute-start | bytes 1572872 | tf_op jit(solution)/shard_map/ppermute | solution.py:54
  43.8 4.1 %collective-permute-start.3 = (bf16[256,512]{1,0:T(8,128)(2,1)S(1)}, bf16[256,512]{1,0:T(8,128)(2,1)S(1)}, u32[]{:S(2)}, u32[]{:S(2)}) collective-permute-start(bf16[256,512]{1,0:T(8,128)(2,1)S(1)} %bitcast.39), channel_id=1, source_target_pairs={{0,1},{1,0},{2,3},{3,2},{4,5},{5,4},{6,7},{7,6},{8,9},{9,8},{10,11... | collective-permute-start | bytes 786440 | tf_op jit(solution)/shard_map/ppermute | solution.py:54
  53.0 54.3 %reduce-scatter.11.cloned.1.call-start = ((), (), s32[]{:S(2)}) async-start(), calls=%async_computation.15 | async-start | bytes 1146880 | tf_op jit(solution)/shard_map/reduce_scatter | solution.py:87
  83.9 4.4 %collective-permute-start.4 = (f32[640,128]{1,0:T(8,128)S(1)}, f32[640,128]{1,0:T(8,128)S(1)}, u32[]{:S(2)}, u32[]{:S(2)}) collective-permute-start(f32[640,128]{1,0:T(8,128)S(1)} %bitcast.29), channel_id=1, source_target_pairs={{0,1},{1,0},{2,3},{3,2},{4,5},{5,4},{6,7},{7,6},{8,9},{9,8},{10,11... | collective-permute-start | bytes 983048 | tf_op jit(solution)/shard_map/ppermute | solution.py:54
  108.0 66.7 %reduce-scatter.5.cloned.1.call-start = ((), (), s32[]{:S(2)}) async-start(), calls=%async_computation.12 | async-start | bytes 9175040 | tf_op jit(solution)/shard_map/cond/branch_0_fun/reduce_scatter | solution.py:87
  119.0 5.6 %copy-start = (f32[4,64,512]{2,1,0:T(8,128)}, f32[4,64,512]{2,1,0:T(8,128)S(1)}, u32[]{:S(2)}) copy-start(f32[4,64,512]{2,1,0:T(8,128)S(1)} %all_to_all.75) | copy-start | bytes 1572868 | tf_op jit(solution)/shard_map/cond
  119.0 5.6 %collective-permute-start = (f32[256,512]{1,0:T(8,128)S(1)}, f32[256,512]{1,0:T(8,128)S(1)}, u32[]{:S(2)}, u32[]{:S(2)}) collective-permute-start(f32[256,512]{1,0:T(8,128)S(1)} %bitcast.19), channel_id=1, source_target_pairs={{0,1},{1,0},{2,3},{3,2},{4,5},{5,4},{6,7},{7,6},{8,9},{9,8},{10,11... | collective-permute-start | bytes 1572872 | tf_op jit(solution)/shard_map/cond/branch_0_fun/ppermute | solution.py:54
  124.6 0.8 copy-start.2
  133.7 41.0 %copy-start.1 = (f32[4,64,512]{2,1,0:T(8,128)S(1)}, f32[4,64,512]{2,1,0:T(8,128)}, u32[]{:S(2)}) copy-start(f32[4,64,512]{2,1,0:T(8,128)} %copy-done) | copy-start | bytes 1572868 | tf_op jit(solution)/shard_map/cond
  133.7 41.0 %copy-start.3 = (f32[256,512]{1,0:T(8,128)S(1)}, f32[256,512]{1,0:T(8,128)}, u32[]{:S(2)}) copy-start(f32[256,512]{1,0:T(8,128)} %copy-done.2) | copy-start | bytes 1572868 | tf_op jit(solution)/shard_map/cond
  133.7 89.3 %reduce-scatter.7.cloned.1.call-start = ((), (), s32[]{:S(2)}) async-start(), calls=%async_computation.13 | async-start | bytes 2293760 | tf_op jit(solution)/shard_map/cond/branch_0_fun/reduce_scatter | solution.py:87
  201.4 3.4 %collective-permute-start.1 = (f32[640,128]{1,0:T(8,128)S(1)}, f32[640,128]{1,0:T(8,128)S(1)}, u32[]{:S(2)}, u32[]{:S(2)}) collective-permute-start(f32[640,128]{1,0:T(8,128)S(1)} %bitcast.31), channel_id=1, source_target_pairs={{0,1},{1,0},{2,3},{3,2},{4,5},{5,4},{6,7},{7,6},{8,9},{9,8},{10,11... | collective-permute-start | bytes 983048 | tf_op jit(solution)/shard_map/cond/branch_0_fun/ppermute | solution.py:54
  223.1 1.0 copy-start.4
  227.6 35.5 %copy-start.5 = (bf16[512,3584]{1,0:T(8,128)(2,1)S(1)}, bf16[512,3584]{1,0:T(8,128)(2,1)}, u32[]{:S(2)}) copy-start(bf16[512,3584]{1,0:T(8,128)(2,1)} %get-tuple-element.54.b_ref) | copy-start | bytes 11010052
  239.5 15.2 %collective-permute-start.6 = (bf16[896,512]{1,0:T(8,128)(2,1)S(1)}, bf16[896,512]{1,0:T(8,128)(2,1)S(1)}, u32[]{:S(2)}, u32[]{:S(2)}) collective-permute-start(bf16[896,512]{1,0:T(8,128)(2,1)S(1)} %bitcast.23), channel_id=1, source_target_pairs={{0,24},{1,97},{2,26},{3,99},{4,28},{5,101},{6,30},{7,103},{8,0},{9... | collective-permute-start | bytes 2752520 | tf_op jit(solution)/shard_map/ppermute | solution.py:46
  240.8 13.9 %collective-permute-start.5 = (bf16[896,512]{1,0:T(8,128)(2,1)S(1)}, bf16[896,512]{1,0:T(8,128)(2,1)S(1)}, u32[]{:S(2)}, u32[]{:S(2)}) collective-permute-start(bf16[896,512]{1,0:T(8,128)(2,1)S(1)} %bitcast.24), channel_id=1, source_target_pairs={{0,8},{1,33},{2,10},{3,35},{4,12},{5,37},{6,14},{7,39},{8,16},{9,4... | collective-permute-start | bytes 2752520 | tf_op jit(solution)/shard_map/ppermute | solution.py:46
  241.1 3.8 %collective-permute-start.9 = (f32[8,512]{1,0:T(8,128)S(1)}, f32[8,512]{1,0:T(8,128)S(1)}, u32[]{:S(2)}, u32[]{:S(2)}) collective-permute-start(f32[8,512]{1,0:T(8,128)S(1)} %block_sums.1), channel_id=1, source_target_pairs={{0,6},{1,7},{2,0},{3,1},{4,2},{5,3},{6,4},{7,5},{8,14},{9,15},{10,... | collective-permute-start | bytes 49160 | tf_op jit(solution)/shard_map/ppermute | solution.py:58
  243.8 4.1 %collective-permute-start.8 = (f32[8,512]{1,0:T(8,128)S(1)}, f32[8,512]{1,0:T(8,128)S(1)}, u32[]{:S(2)}, u32[]{:S(2)}) collective-permute-start(f32[8,512]{1,0:T(8,128)S(1)} %block_sums.1), channel_id=1, source_target_pairs={{0,4},{1,5},{2,6},{3,7},{4,0},{5,1},{6,2},{7,3},{8,12},{9,13},{10,... | collective-permute-start | bytes 49160 | tf_op jit(solution)/shard_map/ppermute | solution.py:58
  244.2 4.2 %collective-permute-start.7 = (f32[8,512]{1,0:T(8,128)S(1)}, f32[8,512]{1,0:T(8,128)S(1)}, u32[]{:S(2)}, u32[]{:S(2)}) collective-permute-start(f32[8,512]{1,0:T(8,128)S(1)} %block_sums.1), channel_id=1, source_target_pairs={{0,2},{1,3},{2,4},{3,5},{4,6},{5,7},{6,0},{7,1},{8,10},{9,11},{10,... | collective-permute-start | bytes 49160 | tf_op jit(solution)/shard_map/ppermute | solution.py:58
  248.4 3.9 %collective-permute-start.12 = (f32[8,512]{1,0:T(8,128)S(1)}, f32[8,512]{1,0:T(8,128)S(1)}, u32[]{:S(2)}, u32[]{:S(2)}) collective-permute-start(f32[8,512]{1,0:T(8,128)S(1)} %add_add_fusion.1), channel_id=1, source_target_pairs={{0,24},{1,97},{2,26},{3,99},{4,28},{5,101},{6,30},{7,103},{8,0},{9... | collective-permute-start | bytes 49160 | tf_op jit(solution)/shard_map/ppermute | solution.py:46
  250.5 4.1 %collective-permute-start.11 = (f32[8,512]{1,0:T(8,128)S(1)}, f32[8,512]{1,0:T(8,128)S(1)}, u32[]{:S(2)}, u32[]{:S(2)}) collective-permute-start(f32[8,512]{1,0:T(8,128)S(1)} %add_add_fusion.1), channel_id=1, source_target_pairs={{0,16},{1,65},{2,18},{3,67},{4,20},{5,69},{6,22},{7,71},{8,24},{9,... | collective-permute-start | bytes 49160 | tf_op jit(solution)/shard_map/ppermute | solution.py:46
  250.5 4.2 %collective-permute-start.10 = (f32[8,512]{1,0:T(8,128)S(1)}, f32[8,512]{1,0:T(8,128)S(1)}, u32[]{:S(2)}, u32[]{:S(2)}) collective-permute-start(f32[8,512]{1,0:T(8,128)S(1)} %add_add_fusion.1), channel_id=1, source_target_pairs={{0,8},{1,33},{2,10},{3,35},{4,12},{5,37},{6,14},{7,39},{8,16},{9,4... | collective-permute-start | bytes 49160 | tf_op jit(solution)/shard_map/ppermute | solution.py:46
  254.8 15.0 %collective-permute-start.15 = (bf16[896,256]{1,0:T(8,128)(2,1)S(1)}, bf16[896,256]{1,0:T(8,128)(2,1)S(1)}, u32[]{:S(2)}, u32[]{:S(2)}) collective-permute-start(bf16[896,256]{1,0:T(8,128)(2,1)S(1)} %slice.7), channel_id=1, source_target_pairs={{0,24},{1,97},{2,26},{3,99},{4,28},{5,101},{6,30},{7,103},{8,0},{9... | collective-permute-start | bytes 1376264 | tf_op jit(solution)/shard_map/ppermute | solution.py:46
  255.5 14.3 %collective-permute-start.14 = (bf16[896,256]{1,0:T(8,128)(2,1)S(1)}, bf16[896,256]{1,0:T(8,128)(2,1)S(1)}, u32[]{:S(2)}, u32[]{:S(2)}) collective-permute-start(bf16[896,256]{1,0:T(8,128)(2,1)S(1)} %slice.6), channel_id=1, source_target_pairs={{0,8},{1,33},{2,10},{3,35},{4,12},{5,37},{6,14},{7,39},{8,16},{9,4... | collective-permute-start | bytes 1376264 | tf_op jit(solution)/shard_map/ppermute | solution.py:46
  256.3 6.8 %collective-permute-start.13 = (f32[8,512]{1,0:T(8,128)S(1)}, f32[8,512]{1,0:T(8,128)S(1)}, u32[]{:S(2)}, u32[]{:S(2)}) collective-permute-start(f32[8,512]{1,0:T(8,128)S(1)} %add_add_fusion.sums_ref), channel_id=1, source_target_pairs={{0,1},{1,0},{2,3},{3,2},{4,5},{5,4},{6,7},{7,6},{8,9},{9,8},{10,11... | collective-permute-start | bytes 49160 | tf_op jit(solution)/shard_map/ppermute | solution.py:54
Sparse Core Ops, SparseCore 0:
  53.2 34.0 reduce-scatter.8
  89.7 17.5 reduce-scatter.10
  133.8 40.7 reduce-scatter.4
  176.9 25.5 reduce-scatter.6

commit v6 on v5

--- a/solution.py
+++ b/solution.py
@@ -201,17 +201,23 @@
     window += lax.rem(tp * (ROW * 3584 % PRIME), PRIME) + lax.rem(t * (ROW * TILE % PRIME), PRIME)
     window = lax.rem(window, PRIME)
     lanes = lax.broadcasted_iota(jnp.int32, (8, 128), 1)
-    for i in range(0, TILE, 16):
-        groups = []
-        for _ in range(2):
-            part, whole = window & 127, window >> 7
-            turned = [pltpu.roll(table[whole + k], (128 - part) & 127, 1) for k in range(5)]
-            first = lanes < 128 - part
-            groups.append([jnp.where(first, turned[k], turned[k + 1]) for k in range(4)])
-            window = wrap(window + ROW * 8 % PRIME)
-        for k in range(4):
-            rows = jnp.concatenate([groups[0][k], groups[1][k]], axis=0)
-            start[i : i + 16, k * 128 : (k + 1) * 128] = rows.astype(BF16)
+
+    def fill(step, window):
+        for i in range(0, 128, 16):
+            groups = []
+            for _ in range(2):
+                part, whole = window & 127, window >> 7
+                turned = [pltpu.roll(table[whole + k], (128 - part) & 127, 1) for k in range(5)]
+                first = lanes < 128 - part
+                groups.append([jnp.where(first, turned[k], turned[k + 1]) for k in range(4)])
+                window = wrap(window + ROW * 8 % PRIME)
+            for k in range(4):
+                rows = jnp.concatenate([groups[0][k], groups[1][k]], axis=0)
+                place = pl.ds(pl.multiple_of(step * 128 + i, 16), 16)
+                start[place, k * 128 : (k + 1) * 128] = rows.astype(BF16)
+        return window
+
+    lax.fori_loop(0, TILE // 128, fill, window)
     b = (m_ref[...].astype(F32) + g_ref[...].astype(F32)).astype(BF16)
     b_ref[...] = b
     part = dot(b, start[...], 1, 0)
@@ -363,18 +369,28 @@
         hi = lo + NB
         on = jnp.where(small(0) == small(1), a[lo:hi, lo:hi], 0.0)
         diagonal[:, lo:hi] = jnp.sum(on, axis=0, keepdims=True)
-    for lo in range(0, RANK, NB):
-        hi = lo + NB
-        ae[:, :NB] = a[lo:hi, lo:hi]
+
+    def block(b, carry):
+        diag = pl.ds(pl.multiple_of(b * NB, NB), NB)
+        ae[:, :NB] = a[diag, diag]
         ae[:, NB:] = jnp.where(small(0) == small(1), 1.0, 0.0)
         invert_block(ae)
-        inverse = jnp.where(small(0) >= small(1), ae[:, NB:], 0.0)
-        done = exact(inverse, out_ref[lo:hi, :hi], 1, 0)
-        out_ref[lo:hi, :hi] = done
-        if hi < RANK:
-            below = exact(a[hi:, lo:hi], inverse, 1, 1)
-            a[hi:, hi:] = a[hi:, hi:] - exact(below, below, 1, 1)
-            out_ref[hi:, :hi] = out_ref[hi:, :hi] - exact(below, done, 1, 0)
+        for k in range(RANK // NB):
+
+            @pl.when(b == k)
+            def _():
+                lo, hi = k * NB, (k + 1) * NB
+                inverse = jnp.where(small(0) >= small(1), ae[:, NB:], 0.0)
+                done = exact(inverse, out_ref[lo:hi, :hi], 1, 0)
+                out_ref[lo:hi, :hi] = done
+                if hi < RANK:
+                    below = exact(a[hi:, lo:hi], inverse, 1, 1)
+                    a[hi:, hi:] = a[hi:, hi:] - exact(below, below, 1, 1)
+                    out_ref[hi:, :hi] = out_ref[hi:, :hi] - exact(below, done, 1, 0)
+
+        return carry
+
+    lax.fori_loop(0, RANK // NB, block, 0)
     out = out_ref[...]
     loss_ref[0, 0] = jnp.max(jnp.sum(out * out * diagonal[...], axis=1, keepdims=True))
 

time: 284 us -> 282 us (level); the launches traced: 280 us -> 282 us
    pallas_call x1, Pallas kernels: 10 us -> 13.2 us  [left_partial(): pl.pallas_call(left_kernel, grid=(2,), out_shape=(jax.ShapeDtypeStruct((r...]
  transfers between devices with their start and end apart: 20 -> 20, of which waited for: 13 -> 12; matrix products, arithmetic and copies ran while one was open for 0% -> 0% of each run, Pallas kernels for 16% -> 16%
where the time goes in v6:
time: 282 us
  blocking collectives  99.3 us (35%)
  Pallas kernels  77.2 us (27%)
  waiting for transfers between devices  57 us (20%)
  starting transfers between devices  29.5 us (10%)
  between operations  15.1 us (5%)
    all_to_all x8, blocking collectives, exchange(): return lax.all_to_all(a, axis, 0, 0, axis_index_groups=groups, tiled=True)  99.3 us
    reduce_scatter x4, waiting for transfers between devices, scatter(): lax.psum_scatter(a, AXES, scatter_dimension=0, axis_index_groups=groups,...  42.2 us
    pallas_call x2, Pallas kernels, inverse_factor(): pl.pallas_call(inverse_kernel, out_shape=(jax.ShapeDtypeStruct((RANK, RAN...  35.1 us
    ppermute x6, starting transfers between devices, swap_cores(): return lax.ppermute(a, 'tp', [(i, i ^ 1) for i in range(8)])  19.6 us
    pallas_call x2, Pallas kernels, right_partial(): pl.pallas_call(right_kernel, grid=(steps,), in_specs=[smem_spec(), pl.Blo...  13.4 us
    pallas_call x1, Pallas kernels, left_partial(): pl.pallas_call(left_kernel, grid=(2,), out_shape=(jax.ShapeDtypeStruct((r...  13.2 us
    ppermute x6, waiting for transfers between devices, swap_cores(): return lax.ppermute(a, 'tp', [(i, i ^ 1) for i in range(8)])  7.8 us
    pallas_call x1, Pallas kernels, apply_three(): pl.pallas_call(apply_kernel, grid_spec=pltpu.PrefetchScalarGridSpec(num_s...  6.72 us
  transfers between devices with their start and end apart: 20, of which 12 were waited for; matrix products, arithmetic and copies ran while one was open for 0% of the time, Pallas kernels for 16%

profile of v6, /device:TPU:1, one launch (start us, length us, event | category | flops | bytes accessed | tf_op | source)
XLA Modules:
  0.0 281.6 jit_solution(423567606301801553)
XLA Ops:
  7.2 0.0 reduce-scatter.9.cloned.1.call-start
  7.9 0.1 stack.19.meta_ref
  8.0 13.2 %left_partial.1 = (bf16[512,3584]{1,0:T(8,128)(2,1)}, f32[256,512]{1,0:T(8,128)}, f32[256,512]{1,0:T(8,128)}) custom-call(s32[5]{0:T(128)S(1)} %stack.19.meta_ref, bf16[512,3584]{1,0:T(8,128)(2,1)} %m_ref.1, bf16[512,3584]{1,0:T(8,128)(2,1)} %g_ref.1), custom_call_target="tpu_custom_call" | custom-call | tf_op jit(solution)/shard_map/left_partial/pallas_call | solution.py:241
  21.2 1.4 collective-permute-start.2
  22.6 1.7 collective-permute-done.2
  24.3 1.1 add.39
  25.5 13.5 %all_to_all.78 = f32[4,64,512]{2,1,0:T(8,128)S(1)} all-to-all(f32[4,64,512]{2,1,0:T(8,128)S(1)} %bitcast.43), channel_id=1, replica_groups={{0,2,4,6},{1,3,5,7},{8,10,12,14},{9,11,13,15},{16,18,20,22},{17,19,21,2..., dimensions={0} | all-to-all | bytes 1048576 | tf_op jit(solution)/shard_map/all_to_all | solution.py:71
  39.0 7.9 %all_to_all.79 = bf16[4,64,512]{2,1,0:T(8,128)(2,1)S(1)} all-to-all(bf16[4,64,512]{2,1,0:T(8,128)(2,1)S(1)} %bitcast.38), channel_id=1, replica_groups={{0,2,4,6},{1,3,5,7},{8,10,12,14},{9,11,13,15},{16,18,20,22},{17,19,21,2..., dimensions={0} | all-to-all | bytes 524288 | tf_op jit(solution)/shard_map/all_to_all | solution.py:71
  47.0 3.0 %collective-permute-start.3 = (bf16[256,512]{1,0:T(8,128)(2,1)S(1)}, bf16[256,512]{1,0:T(8,128)(2,1)S(1)}, u32[]{:S(2)}, u32[]{:S(2)}) collective-permute-start(bf16[256,512]{1,0:T(8,128)(2,1)S(1)} %bitcast.39), channel_id=1, source_target_pairs={{0,1},{1,0},{2,3},{3,2},{4,5},{5,4},{6,7},{7,6},{8,9},{9,8},{10,11... | collective-permute-start | bytes 786440 | tf_op jit(solution)/shard_map/ppermute | solution.py:54
  49.9 1.2 collective-permute-done.3.other_ref
  51.1 5.1 %right_partial.3 = bf16[3584,512]{1,0:T(8,128)(2,1)} custom-call(s32[5]{0:T(128)S(1)} %stack.19.meta_ref, bf16[512,3584]{1,0:T(8,128)(2,1)} %get-tuple-element.54.b_ref, bf16[256,512]{1,0:T(8,128)(2,1)S(1)} %bitcast.40, bf16[256,512]{1,0:T(8,128)(2,1)S(1)} %collective-permute-done.3.other_ref), custom_call_target="tpu_custom_call" | custom-call | tf_op jit(solution)/shard_map/right_partial/pallas_call | solution.py:316
  56.2 0.0 reduce-scatter.9.cloned.1.call-update
  56.2 0.0 reduce-scatter.11.cloned.1.call-start
  56.3 0.9 gram_share.3
  57.1 17.0 %all_to_all.80 = f32[16,40,128]{2,1,0:T(8,128)S(1)} all-to-all(f32[16,40,128]{2,1,0:T(8,128)S(1)} %bitcast.37), channel_id=1, replica_groups=mesh['fsdp'=16,'tp'=8] {'fsdp'}, dimensions={0} | all-to-all | bytes 655360 | tf_op jit(solution)/shard_map/all_to_all | solution.py:71
  74.2 12.9 %all_to_all.81 = f32[16,40,128]{2,1,0:T(8,128)S(1)} all-to-all(f32[16,40,128]{2,1,0:T(8,128)S(1)} %bitcast.34), channel_id=1, replica_groups=mesh['fsdp'=16,'tp'=8] {'fsdp'}, dimensions={0} | all-to-all | bytes 655360 | tf_op jit(solution)/shard_map/all_to_all | solution.py:71
  87.1 3.2 %collective-permute-start.4 = (f32[640,128]{1,0:T(8,128)S(1)}, f32[640,128]{1,0:T(8,128)S(1)}, u32[]{:S(2)}, u32[]{:S(2)}) collective-permute-start(f32[640,128]{1,0:T(8,128)S(1)} %bitcast.29), channel_id=1, source_target_pairs={{0,1},{1,0},{2,3},{3,2},{4,5},{5,4},{6,7},{7,6},{8,9},{9,8},{10,11... | collective-permute-start | bytes 983048 | tf_op jit(solution)/shard_map/ppermute | solution.py:54
  90.2 1.3 collective-permute-done.4.other_ref
  91.5 0.0 reduce-scatter.11.cloned.1.call-update
  91.5 17.7 %inverse_factor.3 = (f32[512,512]{1,0:T(8,128)}, f32[1,1]{1,0:T(1,128)}) custom-call(s32[5]{0:T(128)S(1)} %stack.19.meta_ref, f32[640,128]{1,0:T(8,128)S(1)} %bitcast.30, f32[640,128]{1,0:T(8,128)S(1)} %collective-permute-done.4.other_ref), custom_call_target="tpu_custom_call" | custom-call | bytes 70000000 | tf_op jit(solution)/shard_map/inverse_factor/pallas_call | solution.py:399
  109.2 1.3 reduce-scatter.11.cloned.1.call-done
  111.1 118.9 %conditional.1 = ((bf16[224,512]{1,0:T(8,128)(2,1)S(1)}, bf16[512,512]{1,0:T(8,128)(2,1)S(1)})) conditional(s32[]{:T(128)} %bitcast.17, (f32[64,512]{1,0:T(8,128)S(1)}, s32[5]{0:T(128)S(1)}, bf16[512,3584]{1,0:T(8,128)(2,1)}) %tuple.20, (s32[5]{0:T(128)S(1)}, bf16[224,512]{1,0:T(8,128)(2,1)}, bf16[256,512]{1,0:T(8,128)(2,1)S(1)}, ...), branch_computations={%region_2.5_spmd, %region_5.6_spmd} | conditional | bytes 121052856 | solution.py:580
  111.1 0.0 reduce-scatter.5.cloned.1.call-start
  111.2 0.1 tile.0
  111.2 10.9 %all_to_all.75 = f32[4,64,512]{2,1,0:T(8,128)S(1)} all-to-all(f32[4,64,512]{2,1,0:T(8,128)S(1)} %tile.0), channel_id=1, replica_groups={{0,2,4,6},{1,3,5,7},{8,10,12,14},{9,11,13,15},{16,18,20,22},{17,19,21,2..., dimensions={0} | all-to-all | bytes 1048576 | tf_op jit(solution)/shard_map/cond/branch_0_fun/all_to_all | solution.py:71
  122.1 4.1 %collective-permute-start = (f32[256,512]{1,0:T(8,128)S(1)}, f32[256,512]{1,0:T(8,128)S(1)}, u32[]{:S(2)}, u32[]{:S(2)}) collective-permute-start(f32[256,512]{1,0:T(8,128)S(1)} %bitcast.19), channel_id=1, source_target_pairs={{0,1},{1,0},{2,3},{3,2},{4,5},{5,4},{6,7},{7,6},{8,9},{9,8},{10,11... | collective-permute-start | bytes 1572872 | tf_op jit(solution)/shard_map/cond/branch_0_fun/ppermute | solution.py:54
  126.2 1.5 collective-permute-done.other_ref
  127.7 0.8 copy-done.2
  128.5 8.3 %right_partial.2 = f32[3584,512]{1,0:T(8,128)} custom-call(s32[5]{0:T(128)S(1)} %get-tuple-element.16.meta_ref, bf16[512,3584]{1,0:T(8,128)(2,1)} %get-tuple-element.17.b_ref, f32[256,512]{1,0:T(8,128)} %bitcast.20, f32[256,512]{1,0:T(8,128)} %copy-done.2), custom_call_target="tpu_custom_call" | custom-call | tf_op jit(solution)/shard_map/cond/branch_0_fun/right_partial/pallas_call | solution.py:316
  136.9 0.0 reduce-scatter.5.cloned.1.call-update
  136.9 0.0 reduce-scatter.7.cloned.1.call-start
  136.9 40.9 %reduce-scatter.5.cloned.1.call-done = f32[896,512]{1,0:T(8,128)} async-done(((f32[3584,512]{1,0:T(8,128)}), f32[896,512]{1,0:T(8,128)}) %reduce-scatter.5.cloned.1.call-update) | async-done | bytes 1835024 | tf_op jit(solution)/shard_map/cond/branch_0_fun/reduce_scatter | solution.py:87
  177.8 0.0 reduce-scatter.7.cloned.1.call-update
  177.8 1.4 gram_share.2
  179.3 12.9 %all_to_all.76 = f32[16,40,128]{2,1,0:T(8,128)S(1)} all-to-all(f32[16,40,128]{2,1,0:T(8,128)S(1)} %bitcast.28), channel_id=1, replica_groups=mesh['fsdp'=16,'tp'=8] {'fsdp'}, dimensions={0} | all-to-all | bytes 655360 | tf_op jit(solution)/shard_map/cond/branch_0_fun/all_to_all | solution.py:71
  192.2 12.4 %all_to_all.77 = f32[16,40,128]{2,1,0:T(8,128)S(1)} all-to-all(f32[16,40,128]{2,1,0:T(8,128)S(1)} %bitcast.36), channel_id=1, replica_groups=mesh['fsdp'=16,'tp'=8] {'fsdp'}, dimensions={0} | all-to-all | bytes 655360 | tf_op jit(solution)/shard_map/cond/branch_0_fun/all_to_all | solution.py:71
  204.6 2.1 collective-permute-start.1
  206.7 1.3 collective-permute-done.1.other_ref
  207.9 17.4 %inverse_factor.2 = (f32[512,512]{1,0:T(8,128)S(1)}, f32[1,1]{1,0:T(1,128)}) custom-call(s32[5]{0:T(128)S(1)} %get-tuple-element.16.meta_ref, f32[640,128]{1,0:T(8,128)S(1)} %bitcast.32, f32[640,128]{1,0:T(8,128)S(1)} %collective-permute-done.1.other_ref), custom_call_target="tpu_custom_call" | custom-call | bytes 70000000 | tf_op jit(solution)/shard_map/cond/branch_0_fun/inverse_factor/pallas_call | solution.py:399
  225.4 0.0 reduce-scatter.7.cloned.1.call-done.w_ref
  225.4 1.0 copy-done.4
  226.4 3.3 %solve_rows.2 = (bf16[224,512]{1,0:T(8,128)(2,1)S(1)}, bf16[512,512]{1,0:T(8,128)(2,1)S(1)}) custom-call(s32[5]{0:T(128)S(1)} %get-tuple-element.16.meta_ref, f32[224,512]{1,0:T(8,128)S(1)} %copy-done.4, f32[256,512]{1,0:T(8,128)S(1)} %bitcast.22, f32[256,512]{1,0:T(8,128)S(1)} %copy-done.3, f32[512,512]{1,0:T(8,128)S(1)} %get-tuple-element.19.inv_ref), custom_call_target="tpu_custom_call" | custom-call | tf_op jit(solution)/shard_map/cond/branch_0_fun/solve_rows/pallas_call | solution.py:431
  230.0 0.0 copy-start.5
  230.0 0.1 tile.4
  230.1 11.8 %all_to_all.82 = bf16[4,224,512]{2,1,0:T(8,128)(2,1)S(1)} all-to-all(bf16[4,224,512]{2,1,0:T(8,128)(2,1)S(1)} %tile.4), channel_id=1, replica_groups={{0,32,64,96},{2,34,66,98},{4,36,68,100},{6,38,70,102},{8,40,72,104},{10..., dimensions={0} | all-to-all | bytes 1835008 | tf_op jit(solution)/shard_map/all_to_all | solution.py:71
  241.9 1.2 collective-permute-start.6
  243.1 0.2 collective-permute-start.5
  243.3 0.1 block_sums.1
  243.4 2.7 collective-permute-start.9
  246.1 0.4 collective-permute-start.8
  246.5 0.7 collective-permute-start.7
  247.2 3.0 %collective-permute-done.8 = f32[8,512]{1,0:T(8,128)S(1)} collective-permute-done((f32[8,512]{1,0:T(8,128)S(1)}, f32[8,512]{1,0:T(8,128)S(1)}, u32[]{:S(2)}, u32[]{:S(2)}) %collective-permute-start.8) | collective-permute-done | bytes 16416 | tf_op jit(solution)/shard_map/ppermute | solution.py:58
  250.2 0.5 collective-permute-done.7
  250.7 2.3 collective-permute-start.12
  253.0 0.7 collective-permute-start.10
  253.6 0.9 collective-permute-done.12
  254.6 2.5 collective-permute-done.11
  257.1 0.0 collective-permute-done.10
  257.2 0.8 collective-permute-start.15
  258.0 0.7 collective-permute-start.14
  258.7 5.9 %collective-permute-start.13 = (f32[8,512]{1,0:T(8,128)S(1)}, f32[8,512]{1,0:T(8,128)S(1)}, u32[]{:S(2)}, u32[]{:S(2)}) collective-permute-start(f32[8,512]{1,0:T(8,128)S(1)} %add_add_fusion.sums_ref), channel_id=1, source_target_pairs={{0,1},{1,0},{2,3},{3,2},{4,5},{5,4},{6,7},{7,6},{8,9},{9,8},{10,11... | collective-permute-start | bytes 49160 | tf_op jit(solution)/shard_map/ppermute | solution.py:54
  264.6 0.8 collective-permute-done.13.swapped_ref
  265.4 6.7 %apply_three.1 = (bf16[512,3584]{1,0:T(8,128)(2,1)}, bf16[512,3584]{1,0:T(8,128)(2,1)}, bf16[512,512]{1,0:T(8,128)(2,1)S(1)}) custom-call(s32[5]{0:T(128)S(1)} %stack.19.meta_ref, bf16[512,3584]{1,0:T(8,128)(2,1)S(1)} %copy-done.5, bf16[512,512]{1,0:T(8,128)(2,1)S(1)} %get-tuple-element.70.q_ref, f32[8,512]{1,0:T(8,128)S(1)} %add_add_fusion.sums_ref, ...), custom_call_target="tpu_custom_call" | custom-call | tf_op jit(solution)/shard_map/apply_three/pallas_call | solution.py:484
  272.1 3.0 %apply_last.1 = (bf16[512,3584]{1,0:T(8,128)(2,1)}, bf16[512,3584]{1,0:T(8,128)(2,1)}) custom-call(s32[5]{0:T(128)S(1)} %stack.19.meta_ref, bf16[512,3584]{1,0:T(8,128)(2,1)S(1)} %copy-done.5, bf16[512,512]{1,0:T(8,128)(2,1)S(1)} %get-tuple-element.70.q_ref, ...), custom_call_target="tpu_custom_call", output_to_operand_aliasing={{0}: (6, {}), {1}: (7, {})} | custom-call | tf_op jit(solution)/shard_map/apply_last/pallas_call | solution.py:516
  (23 shorter events, 0.2 us)
Async XLA Ops:
  7.2 84.3 %reduce-scatter.9.cloned.1.call-start = ((), (), s32[]{:S(2)}) async-start(), calls=%async_computation.14 | async-start | bytes 4587520 | tf_op jit(solution)/shard_map/reduce_scatter | solution.py:87
  21.2 3.2 %collective-permute-start.2 = (f32[256,512]{1,0:T(8,128)}, f32[256,512]{1,0:T(8,128)S(1)}, u32[]{:S(2)}, u32[]{:S(2)}) collective-permute-start(f32[256,512]{1,0:T(8,128)} %get-tuple-element.56), channel_id=1, source_target_pairs={{0,1},{1,0},{2,3},{3,2},{4,5},{5,4},{6,7},{7,6},{8,9},{9,8},{10,11... | collective-permute-start | bytes 1572872 | tf_op jit(solution)/shard_map/ppermute | solution.py:54
  47.0 4.1 %collective-permute-start.3 = (bf16[256,512]{1,0:T(8,128)(2,1)S(1)}, bf16[256,512]{1,0:T(8,128)(2,1)S(1)}, u32[]{:S(2)}, u32[]{:S(2)}) collective-permute-start(bf16[256,512]{1,0:T(8,128)(2,1)S(1)} %bitcast.39), channel_id=1, source_target_pairs={{0,1},{1,0},{2,3},{3,2},{4,5},{5,4},{6,7},{7,6},{8,9},{9,8},{10,11... | collective-permute-start | bytes 786440 | tf_op jit(solution)/shard_map/ppermute | solution.py:54
  56.2 54.3 %reduce-scatter.11.cloned.1.call-start = ((), (), s32[]{:S(2)}) async-start(), calls=%async_computation.15 | async-start | bytes 1146880 | tf_op jit(solution)/shard_map/reduce_scatter | solution.py:87
  87.1 4.4 %collective-permute-start.4 = (f32[640,128]{1,0:T(8,128)S(1)}, f32[640,128]{1,0:T(8,128)S(1)}, u32[]{:S(2)}, u32[]{:S(2)}) collective-permute-start(f32[640,128]{1,0:T(8,128)S(1)} %bitcast.29), channel_id=1, source_target_pairs={{0,1},{1,0},{2,3},{3,2},{4,5},{5,4},{6,7},{7,6},{8,9},{9,8},{10,11... | collective-permute-start | bytes 983048 | tf_op jit(solution)/shard_map/ppermute | solution.py:54
  111.1 66.7 %reduce-scatter.5.cloned.1.call-start = ((), (), s32[]{:S(2)}) async-start(), calls=%async_computation.12 | async-start | bytes 9175040 | tf_op jit(solution)/shard_map/cond/branch_0_fun/reduce_scatter | solution.py:87
  122.1 5.6 %copy-start = (f32[4,64,512]{2,1,0:T(8,128)}, f32[4,64,512]{2,1,0:T(8,128)S(1)}, u32[]{:S(2)}) copy-start(f32[4,64,512]{2,1,0:T(8,128)S(1)} %all_to_all.75) | copy-start | bytes 1572868 | tf_op jit(solution)/shard_map/cond
  122.1 5.6 %collective-permute-start = (f32[256,512]{1,0:T(8,128)S(1)}, f32[256,512]{1,0:T(8,128)S(1)}, u32[]{:S(2)}, u32[]{:S(2)}) collective-permute-start(f32[256,512]{1,0:T(8,128)S(1)} %bitcast.19), channel_id=1, source_target_pairs={{0,1},{1,0},{2,3},{3,2},{4,5},{5,4},{6,7},{7,6},{8,9},{9,8},{10,11... | collective-permute-start | bytes 1572872 | tf_op jit(solution)/shard_map/cond/branch_0_fun/ppermute | solution.py:54
  127.7 0.8 copy-start.2
  136.9 41.0 %copy-start.1 = (f32[4,64,512]{2,1,0:T(8,128)S(1)}, f32[4,64,512]{2,1,0:T(8,128)}, u32[]{:S(2)}) copy-start(f32[4,64,512]{2,1,0:T(8,128)} %copy-done) | copy-start | bytes 1572868 | tf_op jit(solution)/shard_map/cond
  136.9 41.0 %copy-start.3 = (f32[256,512]{1,0:T(8,128)S(1)}, f32[256,512]{1,0:T(8,128)}, u32[]{:S(2)}) copy-start(f32[256,512]{1,0:T(8,128)} %copy-done.2) | copy-start | bytes 1572868 | tf_op jit(solution)/shard_map/cond
  136.9 88.5 %reduce-scatter.7.cloned.1.call-start = ((), (), s32[]{:S(2)}) async-start(), calls=%async_computation.13 | async-start | bytes 2293760 | tf_op jit(solution)/shard_map/cond/branch_0_fun/reduce_scatter | solution.py:87
  204.6 3.3 %collective-permute-start.1 = (f32[640,128]{1,0:T(8,128)S(1)}, f32[640,128]{1,0:T(8,128)S(1)}, u32[]{:S(2)}, u32[]{:S(2)}) collective-permute-start(f32[640,128]{1,0:T(8,128)S(1)} %bitcast.31), channel_id=1, source_target_pairs={{0,1},{1,0},{2,3},{3,2},{4,5},{5,4},{6,7},{7,6},{8,9},{9,8},{10,11... | collective-permute-start | bytes 983048 | tf_op jit(solution)/shard_map/cond/branch_0_fun/ppermute | solution.py:54
  225.4 1.0 copy-start.4
  230.0 35.4 %copy-start.5 = (bf16[512,3584]{1,0:T(8,128)(2,1)S(1)}, bf16[512,3584]{1,0:T(8,128)(2,1)}, u32[]{:S(2)}) copy-start(bf16[512,3584]{1,0:T(8,128)(2,1)} %get-tuple-element.54.b_ref) | copy-start | bytes 11010052
  241.9 15.2 %collective-permute-start.6 = (bf16[896,512]{1,0:T(8,128)(2,1)S(1)}, bf16[896,512]{1,0:T(8,128)(2,1)S(1)}, u32[]{:S(2)}, u32[]{:S(2)}) collective-permute-start(bf16[896,512]{1,0:T(8,128)(2,1)S(1)} %bitcast.23), channel_id=1, source_target_pairs={{0,24},{1,97},{2,26},{3,99},{4,28},{5,101},{6,30},{7,103},{8,0},{9... | collective-permute-start | bytes 2752520 | tf_op jit(solution)/shard_map/ppermute | solution.py:46
  243.1 14.0 %collective-permute-start.5 = (bf16[896,512]{1,0:T(8,128)(2,1)S(1)}, bf16[896,512]{1,0:T(8,128)(2,1)S(1)}, u32[]{:S(2)}, u32[]{:S(2)}) collective-permute-start(bf16[896,512]{1,0:T(8,128)(2,1)S(1)} %bitcast.24), channel_id=1, source_target_pairs={{0,8},{1,33},{2,10},{3,35},{4,12},{5,37},{6,14},{7,39},{8,16},{9,4... | collective-permute-start | bytes 2752520 | tf_op jit(solution)/shard_map/ppermute | solution.py:46
  243.4 3.8 %collective-permute-start.9 = (f32[8,512]{1,0:T(8,128)S(1)}, f32[8,512]{1,0:T(8,128)S(1)}, u32[]{:S(2)}, u32[]{:S(2)}) collective-permute-start(f32[8,512]{1,0:T(8,128)S(1)} %block_sums.1), channel_id=1, source_target_pairs={{0,6},{1,7},{2,0},{3,1},{4,2},{5,3},{6,4},{7,5},{8,14},{9,15},{10,... | collective-permute-start | bytes 49160 | tf_op jit(solution)/shard_map/ppermute | solution.py:58
  246.1 4.1 %collective-permute-start.8 = (f32[8,512]{1,0:T(8,128)S(1)}, f32[8,512]{1,0:T(8,128)S(1)}, u32[]{:S(2)}, u32[]{:S(2)}) collective-permute-start(f32[8,512]{1,0:T(8,128)S(1)} %block_sums.1), channel_id=1, source_target_pairs={{0,4},{1,5},{2,6},{3,7},{4,0},{5,1},{6,2},{7,3},{8,12},{9,13},{10,... | collective-permute-start | bytes 49160 | tf_op jit(solution)/shard_map/ppermute | solution.py:58
  246.5 4.2 %collective-permute-start.7 = (f32[8,512]{1,0:T(8,128)S(1)}, f32[8,512]{1,0:T(8,128)S(1)}, u32[]{:S(2)}, u32[]{:S(2)}) collective-permute-start(f32[8,512]{1,0:T(8,128)S(1)} %block_sums.1), channel_id=1, source_target_pairs={{0,2},{1,3},{2,4},{3,5},{4,6},{5,7},{6,0},{7,1},{8,10},{9,11},{10,... | collective-permute-start | bytes 49160 | tf_op jit(solution)/shard_map/ppermute | solution.py:58
  250.7 3.9 %collective-permute-start.12 = (f32[8,512]{1,0:T(8,128)S(1)}, f32[8,512]{1,0:T(8,128)S(1)}, u32[]{:S(2)}, u32[]{:S(2)}) collective-permute-start(f32[8,512]{1,0:T(8,128)S(1)} %add_add_fusion.1), channel_id=1, source_target_pairs={{0,24},{1,97},{2,26},{3,99},{4,28},{5,101},{6,30},{7,103},{8,0},{9... | collective-permute-start | bytes 49160 | tf_op jit(solution)/shard_map/ppermute | solution.py:46
  253.0 4.1 %collective-permute-start.11 = (f32[8,512]{1,0:T(8,128)S(1)}, f32[8,512]{1,0:T(8,128)S(1)}, u32[]{:S(2)}, u32[]{:S(2)}) collective-permute-start(f32[8,512]{1,0:T(8,128)S(1)} %add_add_fusion.1), channel_id=1, source_target_pairs={{0,16},{1,65},{2,18},{3,67},{4,20},{5,69},{6,22},{7,71},{8,24},{9,... | collective-permute-start | bytes 49160 | tf_op jit(solution)/shard_map/ppermute | solution.py:46
  253.0 4.1 %collective-permute-start.10 = (f32[8,512]{1,0:T(8,128)S(1)}, f32[8,512]{1,0:T(8,128)S(1)}, u32[]{:S(2)}, u32[]{:S(2)}) collective-permute-start(f32[8,512]{1,0:T(8,128)S(1)} %add_add_fusion.1), channel_id=1, source_target_pairs={{0,8},{1,33},{2,10},{3,35},{4,12},{5,37},{6,14},{7,39},{8,16},{9,4... | collective-permute-start | bytes 49160 | tf_op jit(solution)/shard_map/ppermute | solution.py:46
  257.2 15.0 %collective-permute-start.15 = (bf16[896,256]{1,0:T(8,128)(2,1)S(1)}, bf16[896,256]{1,0:T(8,128)(2,1)S(1)}, u32[]{:S(2)}, u32[]{:S(2)}) collective-permute-start(bf16[896,256]{1,0:T(8,128)(2,1)S(1)} %slice.7), channel_id=1, source_target_pairs={{0,24},{1,97},{2,26},{3,99},{4,28},{5,101},{6,30},{7,103},{8,0},{9... | collective-permute-start | bytes 1376264 | tf_op jit(solution)/shard_map/ppermute | solution.py:46
  258.0 14.2 %collective-permute-start.14 = (bf16[896,256]{1,0:T(8,128)(2,1)S(1)}, bf16[896,256]{1,0:T(8,128)(2,1)S(1)}, u32[]{:S(2)}, u32[]{:S(2)}) collective-permute-start(bf16[896,256]{1,0:T(8,128)(2,1)S(1)} %slice.6), channel_id=1, source_target_pairs={{0,8},{1,33},{2,10},{3,35},{4,12},{5,37},{6,14},{7,39},{8,16},{9,4... | collective-permute-start | bytes 1376264 | tf_op jit(solution)/shard_map/ppermute | solution.py:46
  258.7 6.7 %collective-permute-start.13 = (f32[8,512]{1,0:T(8,128)S(1)}, f32[8,512]{1,0:T(8,128)S(1)}, u32[]{:S(2)}, u32[]{:S(2)}) collective-permute-start(f32[8,512]{1,0:T(8,128)S(1)} %add_add_fusion.sums_ref), channel_id=1, source_target_pairs={{0,1},{1,0},{2,3},{3,2},{4,5},{5,4},{6,7},{7,6},{8,9},{9,8},{10,11... | collective-permute-start | bytes 49160 | tf_op jit(solution)/shard_map/ppermute | solution.py:54
Sparse Core Ops, SparseCore 0:
  56.3 34.0 reduce-scatter.8
  92.9 17.5 reduce-scatter.10
  137.0 40.7 reduce-scatter.4
  180.1 25.5 reduce-scatter.6

commit v7 on v6

--- a/solution.py
+++ b/solution.py
@@ -201,23 +201,17 @@
     window += lax.rem(tp * (ROW * 3584 % PRIME), PRIME) + lax.rem(t * (ROW * TILE % PRIME), PRIME)
     window = lax.rem(window, PRIME)
     lanes = lax.broadcasted_iota(jnp.int32, (8, 128), 1)
-
-    def fill(step, window):
-        for i in range(0, 128, 16):
-            groups = []
-            for _ in range(2):
-                part, whole = window & 127, window >> 7
-                turned = [pltpu.roll(table[whole + k], (128 - part) & 127, 1) for k in range(5)]
-                first = lanes < 128 - part
-                groups.append([jnp.where(first, turned[k], turned[k + 1]) for k in range(4)])
-                window = wrap(window + ROW * 8 % PRIME)
-            for k in range(4):
-                rows = jnp.concatenate([groups[0][k], groups[1][k]], axis=0)
-                place = pl.ds(pl.multiple_of(step * 128 + i, 16), 16)
-                start[place, k * 128 : (k + 1) * 128] = rows.astype(BF16)
-        return window
-
-    lax.fori_loop(0, TILE // 128, fill, window)
+    for i in range(0, TILE, 16):
+        groups = []
+        for _ in range(2):
+            part, whole = window & 127, window >> 7
+            turned = [pltpu.roll(table[whole + k], (128 - part) & 127, 1) for k in range(5)]
+            first = lanes < 128 - part
+            groups.append([jnp.where(first, turned[k], turned[k + 1]) for k in range(4)])
+            window = wrap(window + ROW * 8 % PRIME)
+        for k in range(4):
+            rows = jnp.concatenate([groups[0][k], groups[1][k]], axis=0)
+            start[i : i + 16, k * 128 : (k + 1) * 128] = rows.astype(BF16)
     b = (m_ref[...].astype(F32) + g_ref[...].astype(F32)).astype(BF16)
     b_ref[...] = b
     part = dot(b, start[...], 1, 0)
@@ -415,30 +409,43 @@
     )(meta, mine, other)
 
 
-def solve_kernel(meta_ref, w_ref, mine_ref, other_ref, inv_ref, out_ref, q_ref):
-    if w_ref.dtype == BF16:
+def solve(a, inv_ref):
+    if a.dtype == BF16:
         top, rest = two_terms(inv_ref[...])
-        solve = lambda a: dot(a, top, 1, 1) + dot(a, rest, 1, 1)
-    else:
-        solve = lambda a: exact(a, inv_ref[...], 1, 1)
-    out_ref[...] = solve(w_ref[...]).astype(BF16)
+        return (dot(a, top, 1, 1) + dot(a, rest, 1, 1)).astype(BF16)
+    return exact(a, inv_ref[...], 1, 1).astype(BF16)
+
+
+def solve_kernel(w_ref, inv_ref, out_ref):
+    out_ref[...] = solve(w_ref[...], inv_ref)
+
+
+def solve_rows(w, inverse):
+    return pl.pallas_call(
+        solve_kernel,
+        out_shape=jax.ShapeDtypeStruct(w.shape, BF16),
+        in_specs=[vmem_spec()] * 2,
+        out_specs=vmem_spec(),
+        compiler_params=params(),
+        name="solve_rows",
+    )(w, inverse)
+
+
+def ortho_kernel(meta_ref, mine_ref, other_ref, inv_ref, out_ref):
     for ref, place in ((mine_ref, meta_ref[0]), (other_ref, 1 - meta_ref[0])):
         rows = pl.ds(pl.multiple_of(place * HALF, HALF), HALF)
-        q_ref[rows, :] = solve(ref[...]).astype(BF16)
-
-
-def solve_rows(meta, w, mine, other, inverse):
-    return pl.pallas_call(
-        solve_kernel,
-        out_shape=(
-            jax.ShapeDtypeStruct(w.shape, BF16),
-            jax.ShapeDtypeStruct((RANK, RANK), BF16),
-        ),
-        in_specs=[smem_spec()] + [vmem_spec()] * 4,
-        out_specs=(vmem_spec(),) * 2,
-        compiler_params=params(),
-        name="solve_rows",
-    )(meta, w, mine, other, inverse)
+        out_ref[rows, :] = solve(ref[...], inv_ref)
+
+
+def ortho_left(meta, mine, other, inverse):
+    return pl.pallas_call(
+        ortho_kernel,
+        out_shape=jax.ShapeDtypeStruct((RANK, RANK), BF16),
+        in_specs=[smem_spec()] + [vmem_spec()] * 3,
+        out_specs=vmem_spec(),
+        compiler_params=params(),
+        name="ortho_left",
+    )(meta, mine, other, inverse)
 
 
 def apply_both(b, q, scaled, right):
@@ -556,16 +563,16 @@
 
     def gram_sum(mine, other):
         gram = exchange(gram_share(meta, mine, other), "fsdp")
-        gram = exchange(sum_parts(gram, 16, 16), "fsdp")
-        return gram, swap_cores(gram)
+        return exchange(sum_parts(gram, 16, 16), "fsdp")
 
     def careful():
         mine = exchange(jnp.tile(piece, (4, 1)), "tp", Z_GROUPS)
         other = swap_cores(mine)
-        inverse, _ = inverse_factor(meta, *gram_sum(mine, other))
+        gram = gram_sum(mine, other)
+        inverse, _ = inverse_factor(meta, gram, swap_cores(gram))
         w = right_partial(meta, blended, mine, other, 4)
         w = scatter(scatter(w, FIRST_GROUPS), SECOND_GROUPS)
-        return solve_rows(meta, w, mine, other, inverse)
+        return solve_rows(w, inverse), ortho_left(meta, mine, other, inverse)
 
     mine = exchange(rounded, "tp", Z_GROUPS)
     other = swap_cores(mine)
@@ -573,14 +580,13 @@
     mine, other, w = lax.optimization_barrier((mine, other, w))
     w = scatter(w, FIRST_GROUPS)
     gram = gram_sum(mine, other)
-    w, *gram = lax.optimization_barrier((w, *gram))
+    w, gram = lax.optimization_barrier((w, gram))
     w = scatter(w, SECOND_GROUPS)
-    inverse, loss = inverse_factor(meta, *gram)
-    w, inverse, loss = lax.optimization_barrier((w, inverse, loss))
+    inverse, loss = inverse_factor(meta, gram, swap_cores(gram))
+    q = ortho_left(meta, mine, other, inverse)
+    w, inverse, loss, q = lax.optimization_barrier((w, inverse, loss, q))
     block, q = lax.cond(
-        loss.reshape(()) <= LOSS_MAX**2,
-        lambda: solve_rows(meta, w, mine, other, inverse),
-        careful,
+        loss.reshape(()) <= LOSS_MAX**2, lambda: (solve_rows(w, inverse), q), careful
     )
     right = exchange(jnp.tile(block, (4, 1)), AXES, SECOND_GROUPS)
     right_low = send_first(right, 1)

time: 282 us -> 281 us (level)
    pallas_call x1, Pallas kernels: 13.2 us -> 10 us  [left_partial(): pl.pallas_call(left_kernel, grid=(2,), out_shape=(jax.ShapeDtypeStruct((r...]
  transfers between devices with their start and end apart: 20 -> 20, of which waited for: 12 -> 12; matrix products, arithmetic and copies ran while one was open for 0% -> 0% of each run, Pallas kernels for 16% -> 17%
where the time goes in v7:
time: 281 us
  blocking collectives  99.5 us (35%)
  Pallas kernels  75.6 us (27%)
  waiting for transfers between devices  57.9 us (21%)
  starting transfers between devices  27.3 us (10%)
  between operations  15.2 us (5%)
  local copies, waits for them, and re-layouts  3.75 us (1%)
    all_to_all x8, blocking collectives, exchange(): return lax.all_to_all(a, axis, 0, 0, axis_index_groups=groups, tiled=True)  99.5 us
    reduce_scatter x4, waiting for transfers between devices, scatter(): lax.psum_scatter(a, AXES, scatter_dimension=0, axis_index_groups=groups,...  43.1 us
    pallas_call x2, Pallas kernels, inverse_factor(): pl.pallas_call(inverse_kernel, out_shape=(jax.ShapeDtypeStruct((RANK, RAN...  35.1 us
    ppermute x6, starting transfers between devices, swap_cores(): return lax.ppermute(a, 'tp', [(i, i ^ 1) for i in range(8)])  17.5 us
    pallas_call x2, Pallas kernels, right_partial(): pl.pallas_call(right_kernel, grid=(steps,), in_specs=[smem_spec(), pl.Blo...  13.5 us
    pallas_call x1, Pallas kernels, left_partial(): pl.pallas_call(left_kernel, grid=(2,), out_shape=(jax.ShapeDtypeStruct((r...  10 us
    ppermute x6, waiting for transfers between devices, swap_cores(): return lax.ppermute(a, 'tp', [(i, i ^ 1) for i in range(8)])  7.8 us
    pallas_call x1, Pallas kernels, apply_three(): pl.pallas_call(apply_kernel, grid_spec=pltpu.PrefetchScalarGridSpec(num_s...  6.73 us
  transfers between devices with their start and end apart: 20, of which 12 were waited for; matrix products, arithmetic and copies ran while one was open for 0% of the time, Pallas kernels for 17%

profile of v7, /device:TPU:1, one launch (start us, length us, event | category | flops | bytes accessed | tf_op | source)
XLA Modules:
  0.0 280.8 jit_solution(6069104839904424185)
XLA Ops:
  7.2 0.0 reduce-scatter.9.cloned.1.call-start
  7.9 0.1 stack.19.meta_ref
  8.0 10.0 %left_partial.1 = (bf16[512,3584]{1,0:T(8,128)(2,1)}, f32[256,512]{1,0:T(8,128)}, f32[256,512]{1,0:T(8,128)}) custom-call(s32[5]{0:T(128)S(1)} %stack.19.meta_ref, bf16[512,3584]{1,0:T(8,128)(2,1)} %m_ref.1, bf16[512,3584]{1,0:T(8,128)(2,1)} %g_ref.1), custom_call_target="tpu_custom_call" | custom-call | tf_op jit(solution)/shard_map/left_partial/pallas_call | solution.py:235
  18.0 1.4 collective-permute-start.2
  19.4 1.7 collective-permute-done.2
  21.2 1.1 add.39
  22.3 13.5 %all_to_all.78 = f32[4,64,512]{2,1,0:T(8,128)S(1)} all-to-all(f32[4,64,512]{2,1,0:T(8,128)S(1)} %bitcast.43), channel_id=1, replica_groups={{0,2,4,6},{1,3,5,7},{8,10,12,14},{9,11,13,15},{16,18,20,22},{17,19,21,2..., dimensions={0} | all-to-all | bytes 1048576 | tf_op jit(solution)/shard_map/all_to_all | solution.py:71
  35.9 7.9 %all_to_all.79 = bf16[4,64,512]{2,1,0:T(8,128)(2,1)S(1)} all-to-all(bf16[4,64,512]{2,1,0:T(8,128)(2,1)S(1)} %bitcast.42), channel_id=1, replica_groups={{0,2,4,6},{1,3,5,7},{8,10,12,14},{9,11,13,15},{16,18,20,22},{17,19,21,2..., dimensions={0} | all-to-all | bytes 524288 | tf_op jit(solution)/shard_map/all_to_all | solution.py:71
  43.8 3.0 %collective-permute-start.3 = (bf16[256,512]{1,0:T(8,128)(2,1)S(1)}, bf16[256,512]{1,0:T(8,128)(2,1)S(1)}, u32[]{:S(2)}, u32[]{:S(2)}) collective-permute-start(bf16[256,512]{1,0:T(8,128)(2,1)S(1)} %bitcast.27), channel_id=1, source_target_pairs={{0,1},{1,0},{2,3},{3,2},{4,5},{5,4},{6,7},{7,6},{8,9},{9,8},{10,11... | collective-permute-start | bytes 786440 | tf_op jit(solution)/shard_map/ppermute | solution.py:54
  46.8 1.2 collective-permute-done.3.other_ref
  47.9 0.7 copy-done.6
  48.6 5.2 %right_partial.3 = bf16[3584,512]{1,0:T(8,128)(2,1)} custom-call(s32[5]{0:T(128)S(1)} %stack.19.meta_ref, bf16[512,3584]{1,0:T(8,128)(2,1)} %get-tuple-element.48.b_ref, bf16[256,512]{1,0:T(8,128)(2,1)} %bitcast.28, bf16[256,512]{1,0:T(8,128)(2,1)} %copy-done.6), custom_call_target="tpu_custom_call" | custom-call | tf_op jit(solution)/shard_map/right_partial/pallas_call | solution.py:310
  53.8 0.0 reduce-scatter.11.cloned.1.call-start
  53.9 0.9 copy-done.5
  54.8 0.1 copy-done.7
  54.8 0.9 gram_share.3
  55.7 17.2 %all_to_all.80 = f32[16,40,128]{2,1,0:T(8,128)S(1)} all-to-all(f32[16,40,128]{2,1,0:T(8,128)S(1)} %bitcast.41), channel_id=1, replica_groups=mesh['fsdp'=16,'tp'=8] {'fsdp'}, dimensions={0} | all-to-all | bytes 655360 | tf_op jit(solution)/shard_map/all_to_all | solution.py:71
  72.9 12.9 %all_to_all.81 = f32[16,40,128]{2,1,0:T(8,128)S(1)} all-to-all(f32[16,40,128]{2,1,0:T(8,128)S(1)} %bitcast.38), channel_id=1, replica_groups=mesh['fsdp'=16,'tp'=8] {'fsdp'}, dimensions={0} | all-to-all | bytes 655360 | tf_op jit(solution)/shard_map/all_to_all | solution.py:71
  85.8 2.3 reduce-scatter.9.cloned.1.call-done
  88.1 1.0 collective-permute-start.4
  89.2 1.3 collective-permute-done.4.other_ref
  90.4 17.4 %inverse_factor.3 = (f32[512,512]{1,0:T(8,128)S(1)}, f32[1,1]{1,0:T(1,128)}) custom-call(s32[5]{0:T(128)S(1)} %stack.19.meta_ref, f32[640,128]{1,0:T(8,128)S(1)} %bitcast.34, f32[640,128]{1,0:T(8,128)S(1)} %collective-permute-done.4.other_ref), custom_call_target="tpu_custom_call" | custom-call | bytes 70000000 | tf_op jit(solution)/shard_map/inverse_factor/pallas_call | solution.py:393
  107.9 1.3 ortho_left.3
  109.2 0.0 reduce-scatter.11.cloned.1.call-done
  109.8 119.3 %conditional.1 = (bf16[224,512]{1,0:T(8,128)(2,1)S(1)}, bf16[512,512]{1,0:T(8,128)(2,1)S(1)}) conditional(s32[]{:T(128)} %bitcast.17, (f32[64,512]{1,0:T(8,128)S(1)}, s32[5]{0:T(128)S(1)}, bf16[512,3584]{1,0:T(8,128)(2,1)}) %tuple.22, (bf16[224,512]{1,0:T(8,128)(2,1)}, f32[512,512]{1,0:T(8,128)S(1)}, bf16[512,512]{1,0:T(8,128)(2,1)S(1)}) %tuple.23), branch_computations={%region_2.5_spmd, %region_5.6_spmd} | conditional | bytes 121052864 | solution.py:588
  109.9 0.0 reduce-scatter.5.cloned.1.call-start
  109.9 0.1 tile.0
  110.0 11.0 %all_to_all.75 = f32[4,64,512]{2,1,0:T(8,128)S(1)} all-to-all(f32[4,64,512]{2,1,0:T(8,128)S(1)} %tile.0), channel_id=1, replica_groups={{0,2,4,6},{1,3,5,7},{8,10,12,14},{9,11,13,15},{16,18,20,22},{17,19,21,2..., dimensions={0} | all-to-all | bytes 1048576 | tf_op jit(solution)/shard_map/cond/branch_0_fun/all_to_all | solution.py:71
  120.9 4.0 %collective-permute-start = (f32[256,512]{1,0:T(8,128)S(1)}, f32[256,512]{1,0:T(8,128)S(1)}, u32[]{:S(2)}, u32[]{:S(2)}) collective-permute-start(f32[256,512]{1,0:T(8,128)S(1)} %bitcast.19), channel_id=1, source_target_pairs={{0,1},{1,0},{2,3},{3,2},{4,5},{5,4},{6,7},{7,6},{8,9},{9,8},{10,11... | collective-permute-start | bytes 1572872 | tf_op jit(solution)/shard_map/cond/branch_0_fun/ppermute | solution.py:54
  125.0 1.5 collective-permute-done.other_ref
  126.5 0.8 copy-done.2
  127.3 8.3 %right_partial.2 = f32[3584,512]{1,0:T(8,128)} custom-call(s32[5]{0:T(128)S(1)} %get-tuple-element.12.meta_ref, bf16[512,3584]{1,0:T(8,128)(2,1)} %get-tuple-element.13.b_ref, f32[256,512]{1,0:T(8,128)} %bitcast.20, f32[256,512]{1,0:T(8,128)} %copy-done.2), custom_call_target="tpu_custom_call" | custom-call | tf_op jit(solution)/shard_map/cond/branch_0_fun/right_partial/pallas_call | solution.py:310
  135.6 0.0 reduce-scatter.7.cloned.1.call-start
  135.7 40.7 %reduce-scatter.5.cloned.1.call-done = f32[896,512]{1,0:T(8,128)} async-done(((f32[3584,512]{1,0:T(8,128)}), f32[896,512]{1,0:T(8,128)}) %reduce-scatter.5.cloned.1.call-update) | async-done | bytes 1835024 | tf_op jit(solution)/shard_map/cond/branch_0_fun/reduce_scatter | solution.py:87
  176.5 1.4 gram_share.2
  177.9 12.8 %all_to_all.76 = f32[16,40,128]{2,1,0:T(8,128)S(1)} all-to-all(f32[16,40,128]{2,1,0:T(8,128)S(1)} %bitcast.32), channel_id=1, replica_groups=mesh['fsdp'=16,'tp'=8] {'fsdp'}, dimensions={0} | all-to-all | bytes 655360 | tf_op jit(solution)/shard_map/cond/branch_0_fun/all_to_all | solution.py:71
  190.8 12.4 %all_to_all.77 = f32[16,40,128]{2,1,0:T(8,128)S(1)} all-to-all(f32[16,40,128]{2,1,0:T(8,128)S(1)} %bitcast.40), channel_id=1, replica_groups=mesh['fsdp'=16,'tp'=8] {'fsdp'}, dimensions={0} | all-to-all | bytes 655360 | tf_op jit(solution)/shard_map/cond/branch_0_fun/all_to_all | solution.py:71
  203.2 2.1 collective-permute-start.1
  205.3 1.3 collective-permute-done.1.other_ref
  206.6 17.7 %inverse_factor.2 = (f32[512,512]{1,0:T(8,128)S(1)}, f32[1,1]{1,0:T(1,128)}) custom-call(s32[5]{0:T(128)S(1)} %get-tuple-element.12.meta_ref, f32[640,128]{1,0:T(8,128)S(1)} %bitcast.36, f32[640,128]{1,0:T(8,128)S(1)} %collective-permute-done.1.other_ref), custom_call_target="tpu_custom_call" | custom-call | bytes 70000000 | tf_op jit(solution)/shard_map/cond/branch_0_fun/inverse_factor/pallas_call | solution.py:393
  224.2 2.4 ortho_left.2
  226.7 0.0 reduce-scatter.7.cloned.1.call-done.w_ref
  226.7 1.0 copy-done.8
  227.7 1.1 solve_rows.2
  229.1 0.1 tile.4
  229.2 11.8 %all_to_all.82 = bf16[4,224,512]{2,1,0:T(8,128)(2,1)S(1)} all-to-all(bf16[4,224,512]{2,1,0:T(8,128)(2,1)S(1)} %tile.4), channel_id=1, replica_groups={{0,32,64,96},{2,34,66,98},{4,36,68,100},{6,38,70,102},{8,40,72,104},{10..., dimensions={0} | all-to-all | bytes 1835008 | tf_op jit(solution)/shard_map/all_to_all | solution.py:71
  241.0 0.9 collective-permute-start.6
  241.8 0.6 collective-permute-start.5
  242.4 0.1 block_sums.1
  242.5 2.7 collective-permute-start.9
  245.2 0.4 collective-permute-start.8
  245.6 0.7 collective-permute-start.7
  246.3 3.0 %collective-permute-done.8 = f32[8,512]{1,0:T(8,128)S(1)} collective-permute-done((f32[8,512]{1,0:T(8,128)S(1)}, f32[8,512]{1,0:T(8,128)S(1)}, u32[]{:S(2)}, u32[]{:S(2)}) %collective-permute-start.8) | collective-permute-done | bytes 16416 | tf_op jit(solution)/shard_map/ppermute | solution.py:58
  249.3 0.5 collective-permute-done.7
  249.8 2.1 collective-permute-start.12
  252.0 0.7 collective-permute-start.10
  252.6 1.0 collective-permute-done.12
  253.7 2.4 collective-permute-done.11
  256.2 0.8 collective-permute-start.15
  257.0 0.7 collective-permute-start.14
  257.7 6.0 %collective-permute-start.13 = (f32[8,512]{1,0:T(8,128)S(1)}, f32[8,512]{1,0:T(8,128)S(1)}, u32[]{:S(2)}, u32[]{:S(2)}) collective-permute-start(f32[8,512]{1,0:T(8,128)S(1)} %add_add_fusion.sums_ref), channel_id=1, source_target_pairs={{0,1},{1,0},{2,3},{3,2},{4,5},{5,4},{6,7},{7,6},{8,9},{9,8},{10,11... | collective-permute-start | bytes 49160 | tf_op jit(solution)/shard_map/ppermute | solution.py:54
  263.7 0.8 collective-permute-done.13.swapped_ref
  264.5 6.7 %apply_three.1 = (bf16[512,3584]{1,0:T(8,128)(2,1)}, bf16[512,3584]{1,0:T(8,128)(2,1)}, bf16[512,512]{1,0:T(8,128)(2,1)S(1)}) custom-call(s32[5]{0:T(128)S(1)} %stack.19.meta_ref, bf16[512,3584]{1,0:T(8,128)(2,1)S(1)} %copy-done.9, bf16[512,512]{1,0:T(8,128)(2,1)S(1)} %get-tuple-element.64.q_ref, f32[8,512]{1,0:T(8,128)S(1)} %add_add_fusion.sums_ref, ...), custom_call_target="tpu_custom_call" | custom-call | tf_op jit(solution)/shard_map/apply_three/pallas_call | solution.py:491
  271.3 3.0 %apply_last.1 = (bf16[512,3584]{1,0:T(8,128)(2,1)}, bf16[512,3584]{1,0:T(8,128)(2,1)}) custom-call(s32[5]{0:T(128)S(1)} %stack.19.meta_ref, bf16[512,3584]{1,0:T(8,128)(2,1)S(1)} %copy-done.9, bf16[512,512]{1,0:T(8,128)(2,1)S(1)} %get-tuple-element.64.q_ref, ...), custom_call_target="tpu_custom_call", output_to_operand_aliasing={{0}: (6, {}), {1}: (7, {})} | custom-call | tf_op jit(solution)/shard_map/apply_last/pallas_call | solution.py:523
  (33 shorter events, 0.3 us)
Async XLA Ops:
  7.2 80.9 %reduce-scatter.9.cloned.1.call-start = ((), (), s32[]{:S(2)}) async-start(), calls=%async_computation.14 | async-start | bytes 4587520 | tf_op jit(solution)/shard_map/reduce_scatter | solution.py:87
  18.0 3.2 %collective-permute-start.2 = (f32[256,512]{1,0:T(8,128)}, f32[256,512]{1,0:T(8,128)S(1)}, u32[]{:S(2)}, u32[]{:S(2)}) collective-permute-start(f32[256,512]{1,0:T(8,128)} %get-tuple-element.50), channel_id=1, source_target_pairs={{0,1},{1,0},{2,3},{3,2},{4,5},{5,4},{6,7},{7,6},{8,9},{9,8},{10,11... | collective-permute-start | bytes 1572872 | tf_op jit(solution)/shard_map/ppermute | solution.py:54
  43.8 4.1 %copy-start.4 = (bf16[4,64,512]{2,1,0:T(8,128)(2,1)}, bf16[4,64,512]{2,1,0:T(8,128)(2,1)S(1)}, u32[]{:S(2)}) copy-start(bf16[4,64,512]{2,1,0:T(8,128)(2,1)S(1)} %all_to_all.79) | copy-start | bytes 786436
  43.8 4.1 %collective-permute-start.3 = (bf16[256,512]{1,0:T(8,128)(2,1)S(1)}, bf16[256,512]{1,0:T(8,128)(2,1)S(1)}, u32[]{:S(2)}, u32[]{:S(2)}) collective-permute-start(bf16[256,512]{1,0:T(8,128)(2,1)S(1)} %bitcast.27), channel_id=1, source_target_pairs={{0,1},{1,0},{2,3},{3,2},{4,5},{5,4},{6,7},{7,6},{8,9},{9,8},{10,11... | collective-permute-start | bytes 786440 | tf_op jit(solution)/shard_map/ppermute | solution.py:54
  47.9 0.7 copy-start.6
  53.8 0.9 copy-start.5
  53.8 1.0 copy-start.7
  53.8 55.3 %reduce-scatter.11.cloned.1.call-start = ((), (), s32[]{:S(2)}) async-start(), calls=%async_computation.15 | async-start | bytes 1146880 | tf_op jit(solution)/shard_map/reduce_scatter | solution.py:87
  88.1 2.3 collective-permute-start.4
  109.9 66.6 %reduce-scatter.5.cloned.1.call-start = ((), (), s32[]{:S(2)}) async-start(), calls=%async_computation.12 | async-start | bytes 9175040 | tf_op jit(solution)/shard_map/cond/branch_0_fun/reduce_scatter | solution.py:87
  120.9 5.6 %copy-start = (f32[4,64,512]{2,1,0:T(8,128)}, f32[4,64,512]{2,1,0:T(8,128)S(1)}, u32[]{:S(2)}) copy-start(f32[4,64,512]{2,1,0:T(8,128)S(1)} %all_to_all.75) | copy-start | bytes 1572868 | tf_op jit(solution)/shard_map/cond
  120.9 5.6 %collective-permute-start = (f32[256,512]{1,0:T(8,128)S(1)}, f32[256,512]{1,0:T(8,128)S(1)}, u32[]{:S(2)}, u32[]{:S(2)}) collective-permute-start(f32[256,512]{1,0:T(8,128)S(1)} %bitcast.19), channel_id=1, source_target_pairs={{0,1},{1,0},{2,3},{3,2},{4,5},{5,4},{6,7},{7,6},{8,9},{9,8},{10,11... | collective-permute-start | bytes 1572872 | tf_op jit(solution)/shard_map/cond/branch_0_fun/ppermute | solution.py:54
  126.5 0.8 copy-start.2
  135.6 40.8 %copy-start.1 = (f32[4,64,512]{2,1,0:T(8,128)S(1)}, f32[4,64,512]{2,1,0:T(8,128)}, u32[]{:S(2)}) copy-start(f32[4,64,512]{2,1,0:T(8,128)} %copy-done) | copy-start | bytes 1572868 | tf_op jit(solution)/shard_map/cond
  135.6 40.8 %copy-start.3 = (f32[256,512]{1,0:T(8,128)S(1)}, f32[256,512]{1,0:T(8,128)}, u32[]{:S(2)}) copy-start(f32[256,512]{1,0:T(8,128)} %copy-done.2) | copy-start | bytes 1572868 | tf_op jit(solution)/shard_map/cond
  135.6 91.1 %reduce-scatter.7.cloned.1.call-start = ((), (), s32[]{:S(2)}) async-start(), calls=%async_computation.13 | async-start | bytes 2293760 | tf_op jit(solution)/shard_map/cond/branch_0_fun/reduce_scatter | solution.py:87
  203.2 3.3 %collective-permute-start.1 = (f32[640,128]{1,0:T(8,128)S(1)}, f32[640,128]{1,0:T(8,128)S(1)}, u32[]{:S(2)}, u32[]{:S(2)}) collective-permute-start(f32[640,128]{1,0:T(8,128)S(1)} %bitcast.35), channel_id=1, source_target_pairs={{0,1},{1,0},{2,3},{3,2},{4,5},{5,4},{6,7},{7,6},{8,9},{9,8},{10,11... | collective-permute-start | bytes 983048 | tf_op jit(solution)/shard_map/cond/branch_0_fun/ppermute | solution.py:54
  226.7 1.0 copy-start.8
  229.1 35.4 %copy-start.9 = (bf16[512,3584]{1,0:T(8,128)(2,1)S(1)}, bf16[512,3584]{1,0:T(8,128)(2,1)}, u32[]{:S(2)}) copy-start(bf16[512,3584]{1,0:T(8,128)(2,1)} %get-tuple-element.48.b_ref) | copy-start | bytes 11010052
  241.0 15.1 %collective-permute-start.6 = (bf16[896,512]{1,0:T(8,128)(2,1)S(1)}, bf16[896,512]{1,0:T(8,128)(2,1)S(1)}, u32[]{:S(2)}, u32[]{:S(2)}) collective-permute-start(bf16[896,512]{1,0:T(8,128)(2,1)S(1)} %bitcast.23), channel_id=1, source_target_pairs={{0,24},{1,97},{2,26},{3,99},{4,28},{5,101},{6,30},{7,103},{8,0},{9... | collective-permute-start | bytes 2752520 | tf_op jit(solution)/shard_map/ppermute | solution.py:46
  241.8 14.2 %collective-permute-start.5 = (bf16[896,512]{1,0:T(8,128)(2,1)S(1)}, bf16[896,512]{1,0:T(8,128)(2,1)S(1)}, u32[]{:S(2)}, u32[]{:S(2)}) collective-permute-start(bf16[896,512]{1,0:T(8,128)(2,1)S(1)} %bitcast.24), channel_id=1, source_target_pairs={{0,8},{1,33},{2,10},{3,35},{4,12},{5,37},{6,14},{7,39},{8,16},{9,4... | collective-permute-start | bytes 2752520 | tf_op jit(solution)/shard_map/ppermute | solution.py:46
  242.5 3.8 %collective-permute-start.9 = (f32[8,512]{1,0:T(8,128)S(1)}, f32[8,512]{1,0:T(8,128)S(1)}, u32[]{:S(2)}, u32[]{:S(2)}) collective-permute-start(f32[8,512]{1,0:T(8,128)S(1)} %block_sums.1), channel_id=1, source_target_pairs={{0,6},{1,7},{2,0},{3,1},{4,2},{5,3},{6,4},{7,5},{8,14},{9,15},{10,... | collective-permute-start | bytes 49160 | tf_op jit(solution)/shard_map/ppermute | solution.py:58
  245.2 4.1 %collective-permute-start.8 = (f32[8,512]{1,0:T(8,128)S(1)}, f32[8,512]{1,0:T(8,128)S(1)}, u32[]{:S(2)}, u32[]{:S(2)}) collective-permute-start(f32[8,512]{1,0:T(8,128)S(1)} %block_sums.1), channel_id=1, source_target_pairs={{0,4},{1,5},{2,6},{3,7},{4,0},{5,1},{6,2},{7,3},{8,12},{9,13},{10,... | collective-permute-start | bytes 49160 | tf_op jit(solution)/shard_map/ppermute | solution.py:58
  245.6 4.2 %collective-permute-start.7 = (f32[8,512]{1,0:T(8,128)S(1)}, f32[8,512]{1,0:T(8,128)S(1)}, u32[]{:S(2)}, u32[]{:S(2)}) collective-permute-start(f32[8,512]{1,0:T(8,128)S(1)} %block_sums.1), channel_id=1, source_target_pairs={{0,2},{1,3},{2,4},{3,5},{4,6},{5,7},{6,0},{7,1},{8,10},{9,11},{10,... | collective-permute-start | bytes 49160 | tf_op jit(solution)/shard_map/ppermute | solution.py:58
  249.8 3.9 %collective-permute-start.12 = (f32[8,512]{1,0:T(8,128)S(1)}, f32[8,512]{1,0:T(8,128)S(1)}, u32[]{:S(2)}, u32[]{:S(2)}) collective-permute-start(f32[8,512]{1,0:T(8,128)S(1)} %add_add_fusion.1), channel_id=1, source_target_pairs={{0,24},{1,97},{2,26},{3,99},{4,28},{5,101},{6,30},{7,103},{8,0},{9... | collective-permute-start | bytes 49160 | tf_op jit(solution)/shard_map/ppermute | solution.py:46
  252.0 4.1 %collective-permute-start.11 = (f32[8,512]{1,0:T(8,128)S(1)}, f32[8,512]{1,0:T(8,128)S(1)}, u32[]{:S(2)}, u32[]{:S(2)}) collective-permute-start(f32[8,512]{1,0:T(8,128)S(1)} %add_add_fusion.1), channel_id=1, source_target_pairs={{0,16},{1,65},{2,18},{3,67},{4,20},{5,69},{6,22},{7,71},{8,24},{9,... | collective-permute-start | bytes 49160 | tf_op jit(solution)/shard_map/ppermute | solution.py:46
  252.0 4.1 %collective-permute-start.10 = (f32[8,512]{1,0:T(8,128)S(1)}, f32[8,512]{1,0:T(8,128)S(1)}, u32[]{:S(2)}, u32[]{:S(2)}) collective-permute-start(f32[8,512]{1,0:T(8,128)S(1)} %add_add_fusion.1), channel_id=1, source_target_pairs={{0,8},{1,33},{2,10},{3,35},{4,12},{5,37},{6,14},{7,39},{8,16},{9,4... | collective-permute-start | bytes 49160 | tf_op jit(solution)/shard_map/ppermute | solution.py:46
  256.2 15.1 %collective-permute-start.15 = (bf16[896,256]{1,0:T(8,128)(2,1)S(1)}, bf16[896,256]{1,0:T(8,128)(2,1)S(1)}, u32[]{:S(2)}, u32[]{:S(2)}) collective-permute-start(bf16[896,256]{1,0:T(8,128)(2,1)S(1)} %slice.7), channel_id=1, source_target_pairs={{0,24},{1,97},{2,26},{3,99},{4,28},{5,101},{6,30},{7,103},{8,0},{9... | collective-permute-start | bytes 1376264 | tf_op jit(solution)/shard_map/ppermute | solution.py:46
  257.0 14.3 %collective-permute-start.14 = (bf16[896,256]{1,0:T(8,128)(2,1)S(1)}, bf16[896,256]{1,0:T(8,128)(2,1)S(1)}, u32[]{:S(2)}, u32[]{:S(2)}) collective-permute-start(bf16[896,256]{1,0:T(8,128)(2,1)S(1)} %slice.6), channel_id=1, source_target_pairs={{0,8},{1,33},{2,10},{3,35},{4,12},{5,37},{6,14},{7,39},{8,16},{9,4... | collective-permute-start | bytes 1376264 | tf_op jit(solution)/shard_map/ppermute | solution.py:46
  257.7 6.8 %collective-permute-start.13 = (f32[8,512]{1,0:T(8,128)S(1)}, f32[8,512]{1,0:T(8,128)S(1)}, u32[]{:S(2)}, u32[]{:S(2)}) collective-permute-start(f32[8,512]{1,0:T(8,128)S(1)} %add_add_fusion.sums_ref), channel_id=1, source_target_pairs={{0,1},{1,0},{2,3},{3,2},{4,5},{5,4},{6,7},{7,6},{8,9},{9,8},{10,11... | collective-permute-start | bytes 49160 | tf_op jit(solution)/shard_map/ppermute | solution.py:54
Sparse Core Ops, SparseCore 0:
  54.0 34.0 reduce-scatter.8
  90.5 18.5 reduce-scatter.10
  135.8 40.6 reduce-scatter.4
  178.7 25.5 reduce-scatter.6

commit v8 on v7

--- a/solution.py
+++ b/solution.py
@@ -17,7 +17,8 @@
 PANEL = 64
 STRIP = 16
 VMEM_LIMIT = 48 * 1024 * 1024
-VMEM_MOST = 61 * 1024 * 1024
+VMEM_MOST = 57 * 1024 * 1024
+VMEM_RIGHT = 52 * 1024 * 1024
 F32, BF16 = jnp.float32, jnp.bfloat16
 AXES = ("fsdp", "tp")
 LOSS_MAX = 2.0
@@ -314,7 +315,7 @@
         out_specs=pl.BlockSpec((block, RANK), lambda r: (r, 0)),
         scratch_shapes=[pltpu.VMEM((RANK, terms * RANK), BF16)],
         out_shape=jax.ShapeDtypeStruct((cols, RANK), mine.dtype),
-        compiler_params=params(VMEM_MOST),
+        compiler_params=params(VMEM_RIGHT),
         name="right_partial",
     )(meta, blended, mine, other)
 

time: 281 us -> 277 us (0.986)
  no operation moved by 1% of the time
where the time goes in v8:
time: 277 us; the launch traced here: 276 us
  blocking collectives  98.5 us (36%)
  Pallas kernels  73.8 us (27%)
  waiting for transfers between devices  59 us (21%)
  starting transfers between devices  27.1 us (10%)
  between operations  15.2 us (5%)
    all_to_all x8, blocking collectives, exchange(): return lax.all_to_all(a, axis, 0, 0, axis_index_groups=groups, tiled=True)  98.5 us
    reduce_scatter x4, waiting for transfers between devices, scatter(): lax.psum_scatter(a, AXES, scatter_dimension=0, axis_index_groups=groups,...  44.3 us
    pallas_call x2, Pallas kernels, inverse_factor(): pl.pallas_call(inverse_kernel, out_shape=(jax.ShapeDtypeStruct((RANK, RAN...  34.9 us
    ppermute x6, starting transfers between devices, swap_cores(): return lax.ppermute(a, 'tp', [(i, i ^ 1) for i in range(8)])  16.9 us
    pallas_call x2, Pallas kernels, right_partial(): pl.pallas_call(right_kernel, grid=(steps,), in_specs=[smem_spec(), pl.Blo...  12.3 us
    pallas_call x1, Pallas kernels, left_partial(): pl.pallas_call(left_kernel, grid=(2,), out_shape=(jax.ShapeDtypeStruct((r...  9.67 us
    ppermute x6, waiting for transfers between devices, swap_cores(): return lax.ppermute(a, 'tp', [(i, i ^ 1) for i in range(8)])  7.8 us
    pallas_call x1, Pallas kernels, apply_three(): pl.pallas_call(apply_kernel, grid_spec=pltpu.PrefetchScalarGridSpec(num_s...  6.72 us
  transfers between devices with their start and end apart: 20, of which 12 were waited for; matrix products, arithmetic and copies ran while one was open for 0% of the time, Pallas kernels for 17%

profile of v8, /device:TPU:1, one launch (start us, length us, event | category | flops | bytes accessed | tf_op | source)
XLA Modules:
  0.0 276.3 jit_solution(13222669769705459129)
XLA Ops:
  7.2 0.0 reduce-scatter.9.cloned.1.call-start
  7.9 0.1 stack.19.meta_ref
  8.0 9.7 %left_partial.1 = (bf16[512,3584]{1,0:T(8,128)(2,1)S(1)}, f32[256,512]{1,0:T(8,128)}, f32[256,512]{1,0:T(8,128)}) custom-call(s32[5]{0:T(128)S(1)} %stack.19.meta_ref, bf16[512,3584]{1,0:T(8,128)(2,1)} %m_ref.1, bf16[512,3584]{1,0:T(8,128)(2,1)} %g_ref.1), custom_call_target="tpu_custom_call" | custom-call | tf_op jit(solution)/shard_map/left_partial/pallas_call | solution.py:236
  17.6 1.4 collective-permute-start.2
  19.1 1.7 collective-permute-done.2
  20.8 1.1 add.39
  21.9 13.5 %all_to_all.78 = f32[4,64,512]{2,1,0:T(8,128)S(1)} all-to-all(f32[4,64,512]{2,1,0:T(8,128)S(1)} %bitcast.43), channel_id=1, replica_groups={{0,2,4,6},{1,3,5,7},{8,10,12,14},{9,11,13,15},{16,18,20,22},{17,19,21,2..., dimensions={0} | all-to-all | bytes 1048576 | tf_op jit(solution)/shard_map/all_to_all | solution.py:72
  35.5 7.9 %all_to_all.79 = bf16[4,64,512]{2,1,0:T(8,128)(2,1)S(1)} all-to-all(bf16[4,64,512]{2,1,0:T(8,128)(2,1)S(1)} %bitcast.42), channel_id=1, replica_groups={{0,2,4,6},{1,3,5,7},{8,10,12,14},{9,11,13,15},{16,18,20,22},{17,19,21,2..., dimensions={0} | all-to-all | bytes 524288 | tf_op jit(solution)/shard_map/all_to_all | solution.py:72
  43.4 3.0 %collective-permute-start.3 = (bf16[256,512]{1,0:T(8,128)(2,1)S(1)}, bf16[256,512]{1,0:T(8,128)(2,1)S(1)}, u32[]{:S(2)}, u32[]{:S(2)}) collective-permute-start(bf16[256,512]{1,0:T(8,128)(2,1)S(1)} %bitcast.27), channel_id=1, source_target_pairs={{0,1},{1,0},{2,3},{3,2},{4,5},{5,4},{6,7},{7,6},{8,9},{9,8},{10,11... | collective-permute-start | bytes 786440 | tf_op jit(solution)/shard_map/ppermute | solution.py:55
  46.4 1.2 collective-permute-done.3.other_ref
  47.6 4.3 %right_partial.3 = bf16[3584,512]{1,0:T(8,128)(2,1)} custom-call(s32[5]{0:T(128)S(1)} %stack.19.meta_ref, bf16[512,3584]{1,0:T(8,128)(2,1)S(1)} %get-tuple-element.48.b_ref, bf16[256,512]{1,0:T(8,128)(2,1)S(1)} %bitcast.28, bf16[256,512]{1,0:T(8,128)(2,1)S(1)} %collective-permute-done.3.other_ref), custom_call_target="tpu_custom_call" | custom-call | tf_op jit(solution)/shard_map/right_partial/pallas_call | solution.py:311
  51.8 0.0 reduce-scatter.9.cloned.1.call-update
  51.8 0.0 reduce-scatter.11.cloned.1.call-start
  51.9 0.9 gram_share.3
  52.8 17.0 %all_to_all.80 = f32[16,40,128]{2,1,0:T(8,128)S(1)} all-to-all(f32[16,40,128]{2,1,0:T(8,128)S(1)} %bitcast.41), channel_id=1, replica_groups=mesh['fsdp'=16,'tp'=8] {'fsdp'}, dimensions={0} | all-to-all | bytes 655360 | tf_op jit(solution)/shard_map/all_to_all | solution.py:72
  69.8 12.9 %all_to_all.81 = f32[16,40,128]{2,1,0:T(8,128)S(1)} all-to-all(f32[16,40,128]{2,1,0:T(8,128)S(1)} %bitcast.38), channel_id=1, replica_groups=mesh['fsdp'=16,'tp'=8] {'fsdp'}, dimensions={0} | all-to-all | bytes 655360 | tf_op jit(solution)/shard_map/all_to_all | solution.py:72
  82.7 3.4 %reduce-scatter.9.cloned.1.call-done = bf16[896,512]{1,0:T(8,128)(2,1)} async-done(((bf16[3584,512]{1,0:T(8,128)(2,1)}), bf16[896,512]{1,0:T(8,128)(2,1)}) %reduce-scatter.9.cloned.1.call-update) | async-done | bytes 917520 | tf_op jit(solution)/shard_map/reduce_scatter | solution.py:88
  86.1 0.0 reduce-scatter.11.cloned.1.call-update
  86.1 0.8 collective-permute-start.4
  86.9 1.3 collective-permute-done.4.other_ref
  88.2 17.4 %inverse_factor.3 = (f32[512,512]{1,0:T(8,128)S(1)}, f32[1,1]{1,0:T(1,128)}) custom-call(s32[5]{0:T(128)S(1)} %stack.19.meta_ref, f32[640,128]{1,0:T(8,128)S(1)} %bitcast.34, f32[640,128]{1,0:T(8,128)S(1)} %collective-permute-done.4.other_ref), custom_call_target="tpu_custom_call" | custom-call | bytes 70000000 | tf_op jit(solution)/shard_map/inverse_factor/pallas_call | solution.py:394
  105.6 1.3 ortho_left.3
  106.9 0.0 reduce-scatter.11.cloned.1.call-done
  107.6 117.2 %conditional.1 = (bf16[224,512]{1,0:T(8,128)(2,1)S(1)}, bf16[512,512]{1,0:T(8,128)(2,1)S(1)}) conditional(s32[]{:T(128)} %bitcast.17, (f32[64,512]{1,0:T(8,128)S(1)}, s32[5]{0:T(128)S(1)}, bf16[512,3584]{1,0:T(8,128)(2,1)}) %tuple.35, (bf16[224,512]{1,0:T(8,128)(2,1)}, f32[512,512]{1,0:T(8,128)S(1)}, bf16[512,512]{1,0:T(8,128)(2,1)S(1)}) %tuple.23), branch_computations={%region_2.5_spmd, %region_5.6_spmd} | conditional | bytes 112664144 | solution.py:589
  107.6 0.0 reduce-scatter.5.cloned.1.call-start
  107.7 0.1 tile.0
  107.7 10.1 %all_to_all.75 = f32[4,64,512]{2,1,0:T(8,128)S(1)} all-to-all(f32[4,64,512]{2,1,0:T(8,128)S(1)} %tile.0), channel_id=1, replica_groups={{0,2,4,6},{1,3,5,7},{8,10,12,14},{9,11,13,15},{16,18,20,22},{17,19,21,2..., dimensions={0} | all-to-all | bytes 1048576 | tf_op jit(solution)/shard_map/cond/branch_0_fun/all_to_all | solution.py:72
  117.9 4.0 %collective-permute-start = (f32[256,512]{1,0:T(8,128)S(1)}, f32[256,512]{1,0:T(8,128)S(1)}, u32[]{:S(2)}, u32[]{:S(2)}) collective-permute-start(f32[256,512]{1,0:T(8,128)S(1)} %bitcast.19), channel_id=1, source_target_pairs={{0,1},{1,0},{2,3},{3,2},{4,5},{5,4},{6,7},{7,6},{8,9},{9,8},{10,11... | collective-permute-start | bytes 1572872 | tf_op jit(solution)/shard_map/cond/branch_0_fun/ppermute | solution.py:55
  121.9 1.5 collective-permute-done.other_ref
  123.4 8.0 %right_partial.2 = f32[3584,512]{1,0:T(8,128)} custom-call(s32[5]{0:T(128)S(1)} %get-tuple-element.12.meta_ref, bf16[512,3584]{1,0:T(8,128)(2,1)} %get-tuple-element.13.b_ref, f32[256,512]{1,0:T(8,128)S(1)} %bitcast.20, f32[256,512]{1,0:T(8,128)S(1)} %collective-permute-done.other_ref), custom_call_target="tpu_custom_call" | custom-call | tf_op jit(solution)/shard_map/cond/branch_0_fun/right_partial/pallas_call | solution.py:311
  131.4 0.0 reduce-scatter.5.cloned.1.call-update
  131.4 0.0 reduce-scatter.7.cloned.1.call-start
  131.5 40.9 %reduce-scatter.5.cloned.1.call-done = f32[896,512]{1,0:T(8,128)} async-done(((f32[3584,512]{1,0:T(8,128)}), f32[896,512]{1,0:T(8,128)}) %reduce-scatter.5.cloned.1.call-update) | async-done | bytes 1835024 | tf_op jit(solution)/shard_map/cond/branch_0_fun/reduce_scatter | solution.py:88
  172.4 0.0 reduce-scatter.7.cloned.1.call-update
  172.4 1.4 gram_share.2
  173.8 12.8 %all_to_all.76 = f32[16,40,128]{2,1,0:T(8,128)S(1)} all-to-all(f32[16,40,128]{2,1,0:T(8,128)S(1)} %bitcast.32), channel_id=1, replica_groups=mesh['fsdp'=16,'tp'=8] {'fsdp'}, dimensions={0} | all-to-all | bytes 655360 | tf_op jit(solution)/shard_map/cond/branch_0_fun/all_to_all | solution.py:72
  186.7 12.5 %all_to_all.77 = f32[16,40,128]{2,1,0:T(8,128)S(1)} all-to-all(f32[16,40,128]{2,1,0:T(8,128)S(1)} %bitcast.40), channel_id=1, replica_groups=mesh['fsdp'=16,'tp'=8] {'fsdp'}, dimensions={0} | all-to-all | bytes 655360 | tf_op jit(solution)/shard_map/cond/branch_0_fun/all_to_all | solution.py:72
  199.1 2.1 collective-permute-start.1
  201.2 1.3 collective-permute-done.1.other_ref
  202.5 17.4 %inverse_factor.2 = (f32[512,512]{1,0:T(8,128)S(1)}, f32[1,1]{1,0:T(1,128)}) custom-call(s32[5]{0:T(128)S(1)} %get-tuple-element.12.meta_ref, f32[640,128]{1,0:T(8,128)S(1)} %bitcast.36, f32[640,128]{1,0:T(8,128)S(1)} %collective-permute-done.1.other_ref), custom_call_target="tpu_custom_call" | custom-call | bytes 70000000 | tf_op jit(solution)/shard_map/cond/branch_0_fun/inverse_factor/pallas_call | solution.py:394
  219.9 2.4 ortho_left.2
  222.4 0.0 reduce-scatter.7.cloned.1.call-done.w_ref
  222.4 1.0 copy-done
  223.4 1.1 solve_rows.2
  224.8 0.1 tile.4
  224.8 11.7 %all_to_all.82 = bf16[4,224,512]{2,1,0:T(8,128)(2,1)S(1)} all-to-all(bf16[4,224,512]{2,1,0:T(8,128)(2,1)S(1)} %tile.4), channel_id=1, replica_groups={{0,32,64,96},{2,34,66,98},{4,36,68,100},{6,38,70,102},{8,40,72,104},{10..., dimensions={0} | all-to-all | bytes 1835008 | tf_op jit(solution)/shard_map/all_to_all | solution.py:72
  236.6 1.3 collective-permute-start.6
  237.8 0.2 collective-permute-start.5
  238.0 0.1 block_sums.1
  238.1 2.8 %collective-permute-start.9 = (f32[8,512]{1,0:T(8,128)S(1)}, f32[8,512]{1,0:T(8,128)S(1)}, u32[]{:S(2)}, u32[]{:S(2)}) collective-permute-start(f32[8,512]{1,0:T(8,128)S(1)} %block_sums.1), channel_id=1, source_target_pairs={{0,6},{1,7},{2,0},{3,1},{4,2},{5,3},{6,4},{7,5},{8,14},{9,15},{10,... | collective-permute-start | bytes 49160 | tf_op jit(solution)/shard_map/ppermute | solution.py:59
  240.9 0.6 collective-permute-start.8
  241.4 0.8 collective-permute-start.7
  242.2 2.8 %collective-permute-done.8 = f32[8,512]{1,0:T(8,128)S(1)} collective-permute-done((f32[8,512]{1,0:T(8,128)S(1)}, f32[8,512]{1,0:T(8,128)S(1)}, u32[]{:S(2)}, u32[]{:S(2)}) %collective-permute-start.8) | collective-permute-done | bytes 16416 | tf_op jit(solution)/shard_map/ppermute | solution.py:59
  245.0 0.6 collective-permute-done.7
  245.5 2.3 collective-permute-start.12
  247.8 0.7 collective-permute-start.10
  248.5 0.8 collective-permute-done.12
  249.3 2.6 collective-permute-done.11
  252.0 0.8 collective-permute-start.15
  252.8 0.7 collective-permute-start.14
  253.5 5.7 %collective-permute-start.13 = (f32[8,512]{1,0:T(8,128)S(1)}, f32[8,512]{1,0:T(8,128)S(1)}, u32[]{:S(2)}, u32[]{:S(2)}) collective-permute-start(f32[8,512]{1,0:T(8,128)S(1)} %add_add_fusion.sums_ref), channel_id=1, source_target_pairs={{0,1},{1,0},{2,3},{3,2},{4,5},{5,4},{6,7},{7,6},{8,9},{9,8},{10,11... | collective-permute-start | bytes 49160 | tf_op jit(solution)/shard_map/ppermute | solution.py:55
  259.2 0.8 collective-permute-done.13.swapped_ref
  260.1 6.7 %apply_three.1 = (bf16[512,3584]{1,0:T(8,128)(2,1)}, bf16[512,3584]{1,0:T(8,128)(2,1)}, bf16[512,512]{1,0:T(8,128)(2,1)S(1)}) custom-call(s32[5]{0:T(128)S(1)} %stack.19.meta_ref, bf16[512,3584]{1,0:T(8,128)(2,1)S(1)} %copy-done.2, bf16[512,512]{1,0:T(8,128)(2,1)S(1)} %get-tuple-element.64.q_ref, f32[8,512]{1,0:T(8,128)S(1)} %add_add_fusion.sums_ref, ...), custom_call_target="tpu_custom_call" | custom-call | tf_op jit(solution)/shard_map/apply_three/pallas_call | solution.py:492
  266.8 3.0 %apply_last.1 = (bf16[512,3584]{1,0:T(8,128)(2,1)}, bf16[512,3584]{1,0:T(8,128)(2,1)}) custom-call(s32[5]{0:T(128)S(1)} %stack.19.meta_ref, bf16[512,3584]{1,0:T(8,128)(2,1)S(1)} %copy-done.2, bf16[512,512]{1,0:T(8,128)(2,1)S(1)} %get-tuple-element.64.q_ref, ...), custom_call_target="tpu_custom_call", output_to_operand_aliasing={{0}: (6, {}), {1}: (7, {})} | custom-call | tf_op jit(solution)/shard_map/apply_last/pallas_call | solution.py:524
  (19 shorter events, 0.2 us)
Async XLA Ops:
  7.2 78.9 %reduce-scatter.9.cloned.1.call-start = ((), (), s32[]{:S(2)}) async-start(), calls=%async_computation.14 | async-start | bytes 4587520 | tf_op jit(solution)/shard_map/reduce_scatter | solution.py:88
  17.6 29.9 %copy-start.1 = (bf16[512,3584]{1,0:T(8,128)(2,1)}, bf16[512,3584]{1,0:T(8,128)(2,1)S(1)}, u32[]{:S(2)}) copy-start(bf16[512,3584]{1,0:T(8,128)(2,1)S(1)} %get-tuple-element.48.b_ref) | copy-start | bytes 11010052
  17.6 3.2 %collective-permute-start.2 = (f32[256,512]{1,0:T(8,128)}, f32[256,512]{1,0:T(8,128)S(1)}, u32[]{:S(2)}, u32[]{:S(2)}) collective-permute-start(f32[256,512]{1,0:T(8,128)} %get-tuple-element.50), channel_id=1, source_target_pairs={{0,1},{1,0},{2,3},{3,2},{4,5},{5,4},{6,7},{7,6},{8,9},{9,8},{10,11... | collective-permute-start | bytes 1572872 | tf_op jit(solution)/shard_map/ppermute | solution.py:55
  43.4 4.1 %collective-permute-start.3 = (bf16[256,512]{1,0:T(8,128)(2,1)S(1)}, bf16[256,512]{1,0:T(8,128)(2,1)S(1)}, u32[]{:S(2)}, u32[]{:S(2)}) collective-permute-start(bf16[256,512]{1,0:T(8,128)(2,1)S(1)} %bitcast.27), channel_id=1, source_target_pairs={{0,1},{1,0},{2,3},{3,2},{4,5},{5,4},{6,7},{7,6},{8,9},{9,8},{10,11... | collective-permute-start | bytes 786440 | tf_op jit(solution)/shard_map/ppermute | solution.py:55
  51.8 55.1 %reduce-scatter.11.cloned.1.call-start = ((), (), s32[]{:S(2)}) async-start(), calls=%async_computation.15 | async-start | bytes 1146880 | tf_op jit(solution)/shard_map/reduce_scatter | solution.py:88
  86.1 2.0 collective-permute-start.4
  107.6 64.7 %reduce-scatter.5.cloned.1.call-start = ((), (), s32[]{:S(2)}) async-start(), calls=%async_computation.12 | async-start | bytes 9175040 | tf_op jit(solution)/shard_map/cond/branch_0_fun/reduce_scatter | solution.py:88
  117.9 5.5 %collective-permute-start = (f32[256,512]{1,0:T(8,128)S(1)}, f32[256,512]{1,0:T(8,128)S(1)}, u32[]{:S(2)}, u32[]{:S(2)}) collective-permute-start(f32[256,512]{1,0:T(8,128)S(1)} %bitcast.19), channel_id=1, source_target_pairs={{0,1},{1,0},{2,3},{3,2},{4,5},{5,4},{6,7},{7,6},{8,9},{9,8},{10,11... | collective-permute-start | bytes 1572872 | tf_op jit(solution)/shard_map/cond/branch_0_fun/ppermute | solution.py:55
  131.4 91.0 %reduce-scatter.7.cloned.1.call-start = ((), (), s32[]{:S(2)}) async-start(), calls=%async_computation.13 | async-start | bytes 2293760 | tf_op jit(solution)/shard_map/cond/branch_0_fun/reduce_scatter | solution.py:88
  199.1 3.3 %collective-permute-start.1 = (f32[640,128]{1,0:T(8,128)S(1)}, f32[640,128]{1,0:T(8,128)S(1)}, u32[]{:S(2)}, u32[]{:S(2)}) collective-permute-start(f32[640,128]{1,0:T(8,128)S(1)} %bitcast.35), channel_id=1, source_target_pairs={{0,1},{1,0},{2,3},{3,2},{4,5},{5,4},{6,7},{7,6},{8,9},{9,8},{10,11... | collective-permute-start | bytes 983048 | tf_op jit(solution)/shard_map/cond/branch_0_fun/ppermute | solution.py:55
  222.4 1.0 copy-start
  224.8 35.3 %copy-start.2 = (bf16[512,3584]{1,0:T(8,128)(2,1)S(1)}, bf16[512,3584]{1,0:T(8,128)(2,1)}, u32[]{:S(2)}) copy-start(bf16[512,3584]{1,0:T(8,128)(2,1)} %copy-done.1) | copy-start | bytes 11010052
  236.6 15.4 %collective-permute-start.6 = (bf16[896,512]{1,0:T(8,128)(2,1)S(1)}, bf16[896,512]{1,0:T(8,128)(2,1)S(1)}, u32[]{:S(2)}, u32[]{:S(2)}) collective-permute-start(bf16[896,512]{1,0:T(8,128)(2,1)S(1)} %bitcast.23), channel_id=1, source_target_pairs={{0,24},{1,97},{2,26},{3,99},{4,28},{5,101},{6,30},{7,103},{8,0},{9... | collective-permute-start | bytes 2752520 | tf_op jit(solution)/shard_map/ppermute | solution.py:47
  237.8 14.1 %collective-permute-start.5 = (bf16[896,512]{1,0:T(8,128)(2,1)S(1)}, bf16[896,512]{1,0:T(8,128)(2,1)S(1)}, u32[]{:S(2)}, u32[]{:S(2)}) collective-permute-start(bf16[896,512]{1,0:T(8,128)(2,1)S(1)} %bitcast.24), channel_id=1, source_target_pairs={{0,8},{1,33},{2,10},{3,35},{4,12},{5,37},{6,14},{7,39},{8,16},{9,4... | collective-permute-start | bytes 2752520 | tf_op jit(solution)/shard_map/ppermute | solution.py:47
  238.1 4.1 %collective-permute-start.9 = (f32[8,512]{1,0:T(8,128)S(1)}, f32[8,512]{1,0:T(8,128)S(1)}, u32[]{:S(2)}, u32[]{:S(2)}) collective-permute-start(f32[8,512]{1,0:T(8,128)S(1)} %block_sums.1), channel_id=1, source_target_pairs={{0,6},{1,7},{2,0},{3,1},{4,2},{5,3},{6,4},{7,5},{8,14},{9,15},{10,... | collective-permute-start | bytes 49160 | tf_op jit(solution)/shard_map/ppermute | solution.py:59
  240.9 4.1 %collective-permute-start.8 = (f32[8,512]{1,0:T(8,128)S(1)}, f32[8,512]{1,0:T(8,128)S(1)}, u32[]{:S(2)}, u32[]{:S(2)}) collective-permute-start(f32[8,512]{1,0:T(8,128)S(1)} %block_sums.1), channel_id=1, source_target_pairs={{0,4},{1,5},{2,6},{3,7},{4,0},{5,1},{6,2},{7,3},{8,12},{9,13},{10,... | collective-permute-start | bytes 49160 | tf_op jit(solution)/shard_map/ppermute | solution.py:59
  241.4 4.1 %collective-permute-start.7 = (f32[8,512]{1,0:T(8,128)S(1)}, f32[8,512]{1,0:T(8,128)S(1)}, u32[]{:S(2)}, u32[]{:S(2)}) collective-permute-start(f32[8,512]{1,0:T(8,128)S(1)} %block_sums.1), channel_id=1, source_target_pairs={{0,2},{1,3},{2,4},{3,5},{4,6},{5,7},{6,0},{7,1},{8,10},{9,11},{10,... | collective-permute-start | bytes 49160 | tf_op jit(solution)/shard_map/ppermute | solution.py:59
  245.5 3.7 %collective-permute-start.12 = (f32[8,512]{1,0:T(8,128)S(1)}, f32[8,512]{1,0:T(8,128)S(1)}, u32[]{:S(2)}, u32[]{:S(2)}) collective-permute-start(f32[8,512]{1,0:T(8,128)S(1)} %add_add_fusion.1), channel_id=1, source_target_pairs={{0,24},{1,97},{2,26},{3,99},{4,28},{5,101},{6,30},{7,103},{8,0},{9... | collective-permute-start | bytes 49160 | tf_op jit(solution)/shard_map/ppermute | solution.py:47
  247.8 4.1 %collective-permute-start.11 = (f32[8,512]{1,0:T(8,128)S(1)}, f32[8,512]{1,0:T(8,128)S(1)}, u32[]{:S(2)}, u32[]{:S(2)}) collective-permute-start(f32[8,512]{1,0:T(8,128)S(1)} %add_add_fusion.1), channel_id=1, source_target_pairs={{0,16},{1,65},{2,18},{3,67},{4,20},{5,69},{6,22},{7,71},{8,24},{9,... | collective-permute-start | bytes 49160 | tf_op jit(solution)/shard_map/ppermute | solution.py:47
  247.8 4.1 %collective-permute-start.10 = (f32[8,512]{1,0:T(8,128)S(1)}, f32[8,512]{1,0:T(8,128)S(1)}, u32[]{:S(2)}, u32[]{:S(2)}) collective-permute-start(f32[8,512]{1,0:T(8,128)S(1)} %add_add_fusion.1), channel_id=1, source_target_pairs={{0,8},{1,33},{2,10},{3,35},{4,12},{5,37},{6,14},{7,39},{8,16},{9,4... | collective-permute-start | bytes 49160 | tf_op jit(solution)/shard_map/ppermute | solution.py:47
  252.0 14.8 %collective-permute-start.15 = (bf16[896,256]{1,0:T(8,128)(2,1)S(1)}, bf16[896,256]{1,0:T(8,128)(2,1)S(1)}, u32[]{:S(2)}, u32[]{:S(2)}) collective-permute-start(bf16[896,256]{1,0:T(8,128)(2,1)S(1)} %slice.7), channel_id=1, source_target_pairs={{0,24},{1,97},{2,26},{3,99},{4,28},{5,101},{6,30},{7,103},{8,0},{9... | collective-permute-start | bytes 1376264 | tf_op jit(solution)/shard_map/ppermute | solution.py:47
  252.8 14.0 %collective-permute-start.14 = (bf16[896,256]{1,0:T(8,128)(2,1)S(1)}, bf16[896,256]{1,0:T(8,128)(2,1)S(1)}, u32[]{:S(2)}, u32[]{:S(2)}) collective-permute-start(bf16[896,256]{1,0:T(8,128)(2,1)S(1)} %slice.6), channel_id=1, source_target_pairs={{0,8},{1,33},{2,10},{3,35},{4,12},{5,37},{6,14},{7,39},{8,16},{9,4... | collective-permute-start | bytes 1376264 | tf_op jit(solution)/shard_map/ppermute | solution.py:47
  253.5 6.5 %collective-permute-start.13 = (f32[8,512]{1,0:T(8,128)S(1)}, f32[8,512]{1,0:T(8,128)S(1)}, u32[]{:S(2)}, u32[]{:S(2)}) collective-permute-start(f32[8,512]{1,0:T(8,128)S(1)} %add_add_fusion.sums_ref), channel_id=1, source_target_pairs={{0,1},{1,0},{2,3},{3,2},{4,5},{5,4},{6,7},{7,6},{8,9},{9,8},{10,11... | collective-permute-start | bytes 49160 | tf_op jit(solution)/shard_map/ppermute | solution.py:55
Sparse Core Ops, SparseCore 0:
  52.0 34.0 reduce-scatter.8
  88.5 17.5 reduce-scatter.10
  131.5 40.7 reduce-scatter.4
  174.6 25.5 reduce-scatter.6

commit v9 on v8

--- a/solution.py
+++ b/solution.py
@@ -21,7 +21,7 @@
 VMEM_RIGHT = 52 * 1024 * 1024
 F32, BF16 = jnp.float32, jnp.bfloat16
 AXES = ("fsdp", "tp")
-LOSS_MAX = 2.0
+LOSS_MAX = 0.0
 
 
 def flat(y, x, z, core):

time: 277 us -> 277 us (level)
  transfers between devices with their start and end apart: 20 -> 20, of which waited for: 12 -> 13; matrix products, arithmetic and copies ran while one was open for 0% -> 0% of each run, Pallas kernels for 17% -> 17%
where the time goes in v9:
time: 277 us; the launch traced here: 276 us
  blocking collectives  98.4 us (36%)
  Pallas kernels  73.8 us (27%)
  waiting for transfers between devices  59.3 us (21%)
  starting transfers between devices  26.8 us (10%)
  between operations  15.2 us (5%)
    all_to_all x8, blocking collectives, exchange(): return lax.all_to_all(a, axis, 0, 0, axis_index_groups=groups, tiled=True)  98.4 us
    reduce_scatter x4, waiting for transfers between devices, scatter(): lax.psum_scatter(a, AXES, scatter_dimension=0, axis_index_groups=groups,...  44.4 us
    pallas_call x2, Pallas kernels, inverse_factor(): pl.pallas_call(inverse_kernel, out_shape=(jax.ShapeDtypeStruct((RANK, RAN...  34.9 us
    ppermute x6, starting transfers between devices, swap_cores(): return lax.ppermute(a, 'tp', [(i, i ^ 1) for i in range(8)])  17.1 us
    pallas_call x2, Pallas kernels, right_partial(): pl.pallas_call(right_kernel, grid=(steps,), in_specs=[smem_spec(), pl.Blo...  12.3 us
    pallas_call x1, Pallas kernels, left_partial(): pl.pallas_call(left_kernel, grid=(2,), out_shape=(jax.ShapeDtypeStruct((r...  9.68 us
    ppermute x6, waiting for transfers between devices, swap_cores(): return lax.ppermute(a, 'tp', [(i, i ^ 1) for i in range(8)])  7.8 us
    pallas_call x1, Pallas kernels, apply_three(): pl.pallas_call(apply_kernel, grid_spec=pltpu.PrefetchScalarGridSpec(num_s...  6.72 us
  transfers between devices with their start and end apart: 20, of which 13 were waited for; matrix products, arithmetic and copies ran while one was open for 0% of the time, Pallas kernels for 17%

profile of v9, /device:TPU:1, one launch (start us, length us, event | category | flops | bytes accessed | tf_op | source)
XLA Modules:
  0.0 276.3 jit_solution(782519211649523411)
XLA Ops:
  7.2 0.0 reduce-scatter.9.cloned.1.call-start
  7.9 0.1 stack.19.meta_ref
  8.0 9.7 %left_partial.1 = (bf16[512,3584]{1,0:T(8,128)(2,1)S(1)}, f32[256,512]{1,0:T(8,128)}, f32[256,512]{1,0:T(8,128)}) custom-call(s32[5]{0:T(128)S(1)} %stack.19.meta_ref, bf16[512,3584]{1,0:T(8,128)(2,1)} %m_ref.1, bf16[512,3584]{1,0:T(8,128)(2,1)} %g_ref.1), custom_call_target="tpu_custom_call" | custom-call | tf_op jit(solution)/shard_map/left_partial/pallas_call | solution.py:236
  17.7 1.4 collective-permute-start.2
  19.1 1.7 collective-permute-done.2
  20.8 1.1 add.39
  21.9 13.5 %all_to_all.78 = f32[4,64,512]{2,1,0:T(8,128)S(1)} all-to-all(f32[4,64,512]{2,1,0:T(8,128)S(1)} %bitcast.43), channel_id=1, replica_groups={{0,2,4,6},{1,3,5,7},{8,10,12,14},{9,11,13,15},{16,18,20,22},{17,19,21,2..., dimensions={0} | all-to-all | bytes 1048576 | tf_op jit(solution)/shard_map/all_to_all | solution.py:72
  35.5 7.9 %all_to_all.79 = bf16[4,64,512]{2,1,0:T(8,128)(2,1)S(1)} all-to-all(bf16[4,64,512]{2,1,0:T(8,128)(2,1)S(1)} %bitcast.42), channel_id=1, replica_groups={{0,2,4,6},{1,3,5,7},{8,10,12,14},{9,11,13,15},{16,18,20,22},{17,19,21,2..., dimensions={0} | all-to-all | bytes 524288 | tf_op jit(solution)/shard_map/all_to_all | solution.py:72
  43.4 3.0 %collective-permute-start.3 = (bf16[256,512]{1,0:T(8,128)(2,1)S(1)}, bf16[256,512]{1,0:T(8,128)(2,1)S(1)}, u32[]{:S(2)}, u32[]{:S(2)}) collective-permute-start(bf16[256,512]{1,0:T(8,128)(2,1)S(1)} %bitcast.27), channel_id=1, source_target_pairs={{0,1},{1,0},{2,3},{3,2},{4,5},{5,4},{6,7},{7,6},{8,9},{9,8},{10,11... | collective-permute-start | bytes 786440 | tf_op jit(solution)/shard_map/ppermute | solution.py:55
  46.4 1.2 collective-permute-done.3.other_ref
  47.6 4.3 %right_partial.3 = bf16[3584,512]{1,0:T(8,128)(2,1)} custom-call(s32[5]{0:T(128)S(1)} %stack.19.meta_ref, bf16[512,3584]{1,0:T(8,128)(2,1)S(1)} %get-tuple-element.48.b_ref, bf16[256,512]{1,0:T(8,128)(2,1)S(1)} %bitcast.28, bf16[256,512]{1,0:T(8,128)(2,1)S(1)} %collective-permute-done.3.other_ref), custom_call_target="tpu_custom_call" | custom-call | tf_op jit(solution)/shard_map/right_partial/pallas_call | solution.py:311
  51.8 0.0 reduce-scatter.11.cloned.1.call-start
  51.9 0.9 gram_share.3
  52.8 17.0 %all_to_all.80 = f32[16,40,128]{2,1,0:T(8,128)S(1)} all-to-all(f32[16,40,128]{2,1,0:T(8,128)S(1)} %bitcast.41), channel_id=1, replica_groups=mesh['fsdp'=16,'tp'=8] {'fsdp'}, dimensions={0} | all-to-all | bytes 655360 | tf_op jit(solution)/shard_map/all_to_all | solution.py:72
  69.8 12.9 %all_to_all.81 = f32[16,40,128]{2,1,0:T(8,128)S(1)} all-to-all(f32[16,40,128]{2,1,0:T(8,128)S(1)} %bitcast.38), channel_id=1, replica_groups=mesh['fsdp'=16,'tp'=8] {'fsdp'}, dimensions={0} | all-to-all | bytes 655360 | tf_op jit(solution)/shard_map/all_to_all | solution.py:72
  82.7 3.4 %reduce-scatter.9.cloned.1.call-done = bf16[896,512]{1,0:T(8,128)(2,1)} async-done(((bf16[3584,512]{1,0:T(8,128)(2,1)}), bf16[896,512]{1,0:T(8,128)(2,1)}) %reduce-scatter.9.cloned.1.call-update) | async-done | bytes 917520 | tf_op jit(solution)/shard_map/reduce_scatter | solution.py:88
  86.1 0.0 reduce-scatter.11.cloned.1.call-update
  86.1 0.8 collective-permute-start.4
  86.9 1.3 collective-permute-done.4.other_ref
  88.2 17.4 %inverse_factor.3 = (f32[512,512]{1,0:T(8,128)S(1)}, f32[1,1]{1,0:T(1,128)}) custom-call(s32[5]{0:T(128)S(1)} %stack.19.meta_ref, f32[640,128]{1,0:T(8,128)S(1)} %bitcast.34, f32[640,128]{1,0:T(8,128)S(1)} %collective-permute-done.4.other_ref), custom_call_target="tpu_custom_call" | custom-call | bytes 70000000 | tf_op jit(solution)/shard_map/inverse_factor/pallas_call | solution.py:394
  105.6 1.3 ortho_left.3
  106.9 0.0 reduce-scatter.11.cloned.1.call-done
  107.6 117.2 %conditional.1 = (bf16[224,512]{1,0:T(8,128)(2,1)S(1)}, bf16[512,512]{1,0:T(8,128)(2,1)S(1)}) conditional(s32[]{:T(128)} %bitcast.17, (f32[64,512]{1,0:T(8,128)S(1)}, s32[5]{0:T(128)S(1)}, bf16[512,3584]{1,0:T(8,128)(2,1)}) %tuple.35, (bf16[224,512]{1,0:T(8,128)(2,1)}, f32[512,512]{1,0:T(8,128)S(1)}, bf16[512,512]{1,0:T(8,128)(2,1)S(1)}) %tuple.23), branch_computations={%region_2.5_spmd, %region_5.6_spmd} | conditional | bytes 112664144 | solution.py:589
  107.6 0.0 reduce-scatter.5.cloned.1.call-start
  107.7 0.1 tile.0
  107.7 10.1 %all_to_all.75 = f32[4,64,512]{2,1,0:T(8,128)S(1)} all-to-all(f32[4,64,512]{2,1,0:T(8,128)S(1)} %tile.0), channel_id=1, replica_groups={{0,2,4,6},{1,3,5,7},{8,10,12,14},{9,11,13,15},{16,18,20,22},{17,19,21,2..., dimensions={0} | all-to-all | bytes 1048576 | tf_op jit(solution)/shard_map/cond/branch_0_fun/all_to_all | solution.py:72
  117.8 4.0 %collective-permute-start = (f32[256,512]{1,0:T(8,128)S(1)}, f32[256,512]{1,0:T(8,128)S(1)}, u32[]{:S(2)}, u32[]{:S(2)}) collective-permute-start(f32[256,512]{1,0:T(8,128)S(1)} %bitcast.19), channel_id=1, source_target_pairs={{0,1},{1,0},{2,3},{3,2},{4,5},{5,4},{6,7},{7,6},{8,9},{9,8},{10,11... | collective-permute-start | bytes 1572872 | tf_op jit(solution)/shard_map/cond/branch_0_fun/ppermute | solution.py:55
  121.8 1.5 collective-permute-done.other_ref
  123.4 8.0 %right_partial.2 = f32[3584,512]{1,0:T(8,128)} custom-call(s32[5]{0:T(128)S(1)} %get-tuple-element.12.meta_ref, bf16[512,3584]{1,0:T(8,128)(2,1)} %get-tuple-element.13.b_ref, f32[256,512]{1,0:T(8,128)S(1)} %bitcast.20, f32[256,512]{1,0:T(8,128)S(1)} %collective-permute-done.other_ref), custom_call_target="tpu_custom_call" | custom-call | tf_op jit(solution)/shard_map/cond/branch_0_fun/right_partial/pallas_call | solution.py:311
  131.4 0.0 reduce-scatter.5.cloned.1.call-update
  131.4 0.0 reduce-scatter.7.cloned.1.call-start
  131.4 40.9 %reduce-scatter.5.cloned.1.call-done = f32[896,512]{1,0:T(8,128)} async-done(((f32[3584,512]{1,0:T(8,128)}), f32[896,512]{1,0:T(8,128)}) %reduce-scatter.5.cloned.1.call-update) | async-done | bytes 1835024 | tf_op jit(solution)/shard_map/cond/branch_0_fun/reduce_scatter | solution.py:88
  172.4 1.4 gram_share.2
  173.8 12.8 %all_to_all.76 = f32[16,40,128]{2,1,0:T(8,128)S(1)} all-to-all(f32[16,40,128]{2,1,0:T(8,128)S(1)} %bitcast.32), channel_id=1, replica_groups=mesh['fsdp'=16,'tp'=8] {'fsdp'}, dimensions={0} | all-to-all | bytes 655360 | tf_op jit(solution)/shard_map/cond/branch_0_fun/all_to_all | solution.py:72
  186.7 12.5 %all_to_all.77 = f32[16,40,128]{2,1,0:T(8,128)S(1)} all-to-all(f32[16,40,128]{2,1,0:T(8,128)S(1)} %bitcast.40), channel_id=1, replica_groups=mesh['fsdp'=16,'tp'=8] {'fsdp'}, dimensions={0} | all-to-all | bytes 655360 | tf_op jit(solution)/shard_map/cond/branch_0_fun/all_to_all | solution.py:72
  199.1 2.1 collective-permute-start.1
  201.2 1.3 collective-permute-done.1.other_ref
  202.5 17.4 %inverse_factor.2 = (f32[512,512]{1,0:T(8,128)S(1)}, f32[1,1]{1,0:T(1,128)}) custom-call(s32[5]{0:T(128)S(1)} %get-tuple-element.12.meta_ref, f32[640,128]{1,0:T(8,128)S(1)} %bitcast.36, f32[640,128]{1,0:T(8,128)S(1)} %collective-permute-done.1.other_ref), custom_call_target="tpu_custom_call" | custom-call | bytes 70000000 | tf_op jit(solution)/shard_map/cond/branch_0_fun/inverse_factor/pallas_call | solution.py:394
  219.9 2.4 ortho_left.2
  222.4 0.0 reduce-scatter.7.cloned.1.call-done.w_ref
  222.4 1.0 copy-done
  223.4 1.1 solve_rows.2
  224.8 0.1 tile.4
  224.8 11.7 %all_to_all.82 = bf16[4,224,512]{2,1,0:T(8,128)(2,1)S(1)} all-to-all(bf16[4,224,512]{2,1,0:T(8,128)(2,1)S(1)} %tile.4), channel_id=1, replica_groups={{0,32,64,96},{2,34,66,98},{4,36,68,100},{6,38,70,102},{8,40,72,104},{10..., dimensions={0} | all-to-all | bytes 1835008 | tf_op jit(solution)/shard_map/all_to_all | solution.py:72
  236.6 1.3 collective-permute-start.6
  237.8 0.2 collective-permute-start.5
  238.0 0.1 block_sums.1
  238.1 2.8 %collective-permute-start.9 = (f32[8,512]{1,0:T(8,128)S(1)}, f32[8,512]{1,0:T(8,128)S(1)}, u32[]{:S(2)}, u32[]{:S(2)}) collective-permute-start(f32[8,512]{1,0:T(8,128)S(1)} %block_sums.1), channel_id=1, source_target_pairs={{0,6},{1,7},{2,0},{3,1},{4,2},{5,3},{6,4},{7,5},{8,14},{9,15},{10,... | collective-permute-start | bytes 49160 | tf_op jit(solution)/shard_map/ppermute | solution.py:59
  240.9 0.3 collective-permute-start.8
  241.2 0.7 collective-permute-start.7
  241.9 3.1 %collective-permute-done.8 = f32[8,512]{1,0:T(8,128)S(1)} collective-permute-done((f32[8,512]{1,0:T(8,128)S(1)}, f32[8,512]{1,0:T(8,128)S(1)}, u32[]{:S(2)}, u32[]{:S(2)}) %collective-permute-start.8) | collective-permute-done | bytes 16416 | tf_op jit(solution)/shard_map/ppermute | solution.py:59
  245.0 0.5 collective-permute-done.7
  245.5 2.1 collective-permute-start.12
  247.6 0.1 collective-permute-start.11
  247.6 0.6 collective-permute-start.10
  248.2 1.0 collective-permute-done.12
  249.3 2.4 collective-permute-done.11
  251.7 0.1 collective-permute-done.10
  251.8 0.7 collective-permute-start.15
  252.6 0.8 collective-permute-start.14
  253.4 5.9 %collective-permute-start.13 = (f32[8,512]{1,0:T(8,128)S(1)}, f32[8,512]{1,0:T(8,128)S(1)}, u32[]{:S(2)}, u32[]{:S(2)}) collective-permute-start(f32[8,512]{1,0:T(8,128)S(1)} %add_add_fusion.sums_ref), channel_id=1, source_target_pairs={{0,1},{1,0},{2,3},{3,2},{4,5},{5,4},{6,7},{7,6},{8,9},{9,8},{10,11... | collective-permute-start | bytes 49160 | tf_op jit(solution)/shard_map/ppermute | solution.py:55
  259.2 0.8 collective-permute-done.13.swapped_ref
  260.1 6.7 %apply_three.1 = (bf16[512,3584]{1,0:T(8,128)(2,1)}, bf16[512,3584]{1,0:T(8,128)(2,1)}, bf16[512,512]{1,0:T(8,128)(2,1)S(1)}) custom-call(s32[5]{0:T(128)S(1)} %stack.19.meta_ref, bf16[512,3584]{1,0:T(8,128)(2,1)S(1)} %copy-done.2, bf16[512,512]{1,0:T(8,128)(2,1)S(1)} %get-tuple-element.64.q_ref, f32[8,512]{1,0:T(8,128)S(1)} %add_add_fusion.sums_ref, ...), custom_call_target="tpu_custom_call" | custom-call | tf_op jit(solution)/shard_map/apply_three/pallas_call | solution.py:492
  266.8 3.0 %apply_last.1 = (bf16[512,3584]{1,0:T(8,128)(2,1)}, bf16[512,3584]{1,0:T(8,128)(2,1)}) custom-call(s32[5]{0:T(128)S(1)} %stack.19.meta_ref, bf16[512,3584]{1,0:T(8,128)(2,1)S(1)} %copy-done.2, bf16[512,512]{1,0:T(8,128)(2,1)S(1)} %get-tuple-element.64.q_ref, ...), custom_call_target="tpu_custom_call", output_to_operand_aliasing={{0}: (6, {}), {1}: (7, {})} | custom-call | tf_op jit(solution)/shard_map/apply_last/pallas_call | solution.py:524
  (19 shorter events, 0.3 us)
Async XLA Ops:
  7.2 78.9 %reduce-scatter.9.cloned.1.call-start = ((), (), s32[]{:S(2)}) async-start(), calls=%async_computation.14 | async-start | bytes 4587520 | tf_op jit(solution)/shard_map/reduce_scatter | solution.py:88
  17.6 29.9 %copy-start.1 = (bf16[512,3584]{1,0:T(8,128)(2,1)}, bf16[512,3584]{1,0:T(8,128)(2,1)S(1)}, u32[]{:S(2)}) copy-start(bf16[512,3584]{1,0:T(8,128)(2,1)S(1)} %get-tuple-element.48.b_ref) | copy-start | bytes 11010052
  17.7 3.2 %collective-permute-start.2 = (f32[256,512]{1,0:T(8,128)}, f32[256,512]{1,0:T(8,128)S(1)}, u32[]{:S(2)}, u32[]{:S(2)}) collective-permute-start(f32[256,512]{1,0:T(8,128)} %get-tuple-element.50), channel_id=1, source_target_pairs={{0,1},{1,0},{2,3},{3,2},{4,5},{5,4},{6,7},{7,6},{8,9},{9,8},{10,11... | collective-permute-start | bytes 1572872 | tf_op jit(solution)/shard_map/ppermute | solution.py:55
  43.4 4.1 %collective-permute-start.3 = (bf16[256,512]{1,0:T(8,128)(2,1)S(1)}, bf16[256,512]{1,0:T(8,128)(2,1)S(1)}, u32[]{:S(2)}, u32[]{:S(2)}) collective-permute-start(bf16[256,512]{1,0:T(8,128)(2,1)S(1)} %bitcast.27), channel_id=1, source_target_pairs={{0,1},{1,0},{2,3},{3,2},{4,5},{5,4},{6,7},{7,6},{8,9},{9,8},{10,11... | collective-permute-start | bytes 786440 | tf_op jit(solution)/shard_map/ppermute | solution.py:55
  51.8 55.1 %reduce-scatter.11.cloned.1.call-start = ((), (), s32[]{:S(2)}) async-start(), calls=%async_computation.15 | async-start | bytes 1146880 | tf_op jit(solution)/shard_map/reduce_scatter | solution.py:88
  86.1 2.0 collective-permute-start.4
  107.6 64.7 %reduce-scatter.5.cloned.1.call-start = ((), (), s32[]{:S(2)}) async-start(), calls=%async_computation.12 | async-start | bytes 9175040 | tf_op jit(solution)/shard_map/cond/branch_0_fun/reduce_scatter | solution.py:88
  117.8 5.6 %collective-permute-start = (f32[256,512]{1,0:T(8,128)S(1)}, f32[256,512]{1,0:T(8,128)S(1)}, u32[]{:S(2)}, u32[]{:S(2)}) collective-permute-start(f32[256,512]{1,0:T(8,128)S(1)} %bitcast.19), channel_id=1, source_target_pairs={{0,1},{1,0},{2,3},{3,2},{4,5},{5,4},{6,7},{7,6},{8,9},{9,8},{10,11... | collective-permute-start | bytes 1572872 | tf_op jit(solution)/shard_map/cond/branch_0_fun/ppermute | solution.py:55
  131.4 91.0 %reduce-scatter.7.cloned.1.call-start = ((), (), s32[]{:S(2)}) async-start(), calls=%async_computation.13 | async-start | bytes 2293760 | tf_op jit(solution)/shard_map/cond/branch_0_fun/reduce_scatter | solution.py:88
  199.1 3.3 %collective-permute-start.1 = (f32[640,128]{1,0:T(8,128)S(1)}, f32[640,128]{1,0:T(8,128)S(1)}, u32[]{:S(2)}, u32[]{:S(2)}) collective-permute-start(f32[640,128]{1,0:T(8,128)S(1)} %bitcast.35), channel_id=1, source_target_pairs={{0,1},{1,0},{2,3},{3,2},{4,5},{5,4},{6,7},{7,6},{8,9},{9,8},{10,11... | collective-permute-start | bytes 983048 | tf_op jit(solution)/shard_map/cond/branch_0_fun/ppermute | solution.py:55
  222.4 1.0 copy-start
  224.8 35.3 %copy-start.2 = (bf16[512,3584]{1,0:T(8,128)(2,1)S(1)}, bf16[512,3584]{1,0:T(8,128)(2,1)}, u32[]{:S(2)}) copy-start(bf16[512,3584]{1,0:T(8,128)(2,1)} %copy-done.1) | copy-start | bytes 11010052
  236.6 15.2 %collective-permute-start.6 = (bf16[896,512]{1,0:T(8,128)(2,1)S(1)}, bf16[896,512]{1,0:T(8,128)(2,1)S(1)}, u32[]{:S(2)}, u32[]{:S(2)}) collective-permute-start(bf16[896,512]{1,0:T(8,128)(2,1)S(1)} %bitcast.23), channel_id=1, source_target_pairs={{0,24},{1,97},{2,26},{3,99},{4,28},{5,101},{6,30},{7,103},{8,0},{9... | collective-permute-start | bytes 2752520 | tf_op jit(solution)/shard_map/ppermute | solution.py:47
  237.8 13.9 %collective-permute-start.5 = (bf16[896,512]{1,0:T(8,128)(2,1)S(1)}, bf16[896,512]{1,0:T(8,128)(2,1)S(1)}, u32[]{:S(2)}, u32[]{:S(2)}) collective-permute-start(bf16[896,512]{1,0:T(8,128)(2,1)S(1)} %bitcast.24), channel_id=1, source_target_pairs={{0,8},{1,33},{2,10},{3,35},{4,12},{5,37},{6,14},{7,39},{8,16},{9,4... | collective-permute-start | bytes 2752520 | tf_op jit(solution)/shard_map/ppermute | solution.py:47
  238.1 3.8 %collective-permute-start.9 = (f32[8,512]{1,0:T(8,128)S(1)}, f32[8,512]{1,0:T(8,128)S(1)}, u32[]{:S(2)}, u32[]{:S(2)}) collective-permute-start(f32[8,512]{1,0:T(8,128)S(1)} %block_sums.1), channel_id=1, source_target_pairs={{0,6},{1,7},{2,0},{3,1},{4,2},{5,3},{6,4},{7,5},{8,14},{9,15},{10,... | collective-permute-start | bytes 49160 | tf_op jit(solution)/shard_map/ppermute | solution.py:59
  240.9 4.1 %collective-permute-start.8 = (f32[8,512]{1,0:T(8,128)S(1)}, f32[8,512]{1,0:T(8,128)S(1)}, u32[]{:S(2)}, u32[]{:S(2)}) collective-permute-start(f32[8,512]{1,0:T(8,128)S(1)} %block_sums.1), channel_id=1, source_target_pairs={{0,4},{1,5},{2,6},{3,7},{4,0},{5,1},{6,2},{7,3},{8,12},{9,13},{10,... | collective-permute-start | bytes 49160 | tf_op jit(solution)/shard_map/ppermute | solution.py:59
  241.2 4.2 %collective-permute-start.7 = (f32[8,512]{1,0:T(8,128)S(1)}, f32[8,512]{1,0:T(8,128)S(1)}, u32[]{:S(2)}, u32[]{:S(2)}) collective-permute-start(f32[8,512]{1,0:T(8,128)S(1)} %block_sums.1), channel_id=1, source_target_pairs={{0,2},{1,3},{2,4},{3,5},{4,6},{5,7},{6,0},{7,1},{8,10},{9,11},{10,... | collective-permute-start | bytes 49160 | tf_op jit(solution)/shard_map/ppermute | solution.py:59
  245.5 3.8 %collective-permute-start.12 = (f32[8,512]{1,0:T(8,128)S(1)}, f32[8,512]{1,0:T(8,128)S(1)}, u32[]{:S(2)}, u32[]{:S(2)}) collective-permute-start(f32[8,512]{1,0:T(8,128)S(1)} %add_add_fusion.1), channel_id=1, source_target_pairs={{0,24},{1,97},{2,26},{3,99},{4,28},{5,101},{6,30},{7,103},{8,0},{9... | collective-permute-start | bytes 49160 | tf_op jit(solution)/shard_map/ppermute | solution.py:47
  247.6 4.1 %collective-permute-start.11 = (f32[8,512]{1,0:T(8,128)S(1)}, f32[8,512]{1,0:T(8,128)S(1)}, u32[]{:S(2)}, u32[]{:S(2)}) collective-permute-start(f32[8,512]{1,0:T(8,128)S(1)} %add_add_fusion.1), channel_id=1, source_target_pairs={{0,16},{1,65},{2,18},{3,67},{4,20},{5,69},{6,22},{7,71},{8,24},{9,... | collective-permute-start | bytes 49160 | tf_op jit(solution)/shard_map/ppermute | solution.py:47
  247.6 4.1 %collective-permute-start.10 = (f32[8,512]{1,0:T(8,128)S(1)}, f32[8,512]{1,0:T(8,128)S(1)}, u32[]{:S(2)}, u32[]{:S(2)}) collective-permute-start(f32[8,512]{1,0:T(8,128)S(1)} %add_add_fusion.1), channel_id=1, source_target_pairs={{0,8},{1,33},{2,10},{3,35},{4,12},{5,37},{6,14},{7,39},{8,16},{9,4... | collective-permute-start | bytes 49160 | tf_op jit(solution)/shard_map/ppermute | solution.py:47
  251.8 15.0 %collective-permute-start.15 = (bf16[896,256]{1,0:T(8,128)(2,1)S(1)}, bf16[896,256]{1,0:T(8,128)(2,1)S(1)}, u32[]{:S(2)}, u32[]{:S(2)}) collective-permute-start(bf16[896,256]{1,0:T(8,128)(2,1)S(1)} %slice.7), channel_id=1, source_target_pairs={{0,24},{1,97},{2,26},{3,99},{4,28},{5,101},{6,30},{7,103},{8,0},{9... | collective-permute-start | bytes 1376264 | tf_op jit(solution)/shard_map/ppermute | solution.py:47
  252.6 14.2 %collective-permute-start.14 = (bf16[896,256]{1,0:T(8,128)(2,1)S(1)}, bf16[896,256]{1,0:T(8,128)(2,1)S(1)}, u32[]{:S(2)}, u32[]{:S(2)}) collective-permute-start(bf16[896,256]{1,0:T(8,128)(2,1)S(1)} %slice.6), channel_id=1, source_target_pairs={{0,8},{1,33},{2,10},{3,35},{4,12},{5,37},{6,14},{7,39},{8,16},{9,4... | collective-permute-start | bytes 1376264 | tf_op jit(solution)/shard_map/ppermute | solution.py:47
  253.4 6.7 %collective-permute-start.13 = (f32[8,512]{1,0:T(8,128)S(1)}, f32[8,512]{1,0:T(8,128)S(1)}, u32[]{:S(2)}, u32[]{:S(2)}) collective-permute-start(f32[8,512]{1,0:T(8,128)S(1)} %add_add_fusion.sums_ref), channel_id=1, source_target_pairs={{0,1},{1,0},{2,3},{3,2},{4,5},{5,4},{6,7},{7,6},{8,9},{9,8},{10,11... | collective-permute-start | bytes 49160 | tf_op jit(solution)/shard_map/ppermute | solution.py:55
Sparse Core Ops, SparseCore 0:
  52.0 34.0 reduce-scatter.8
  88.5 17.5 reduce-scatter.10
  131.5 40.8 reduce-scatter.4
  174.6 25.5 reduce-scatter.6

commit v10 on v8

--- a/solution.py
+++ b/solution.py
@@ -478,7 +478,7 @@
 def apply_three(meta, blended, q, sums, rights):
     rows, cols = blended.shape
 
-    tiles = 2
+    tiles = 1
 
     def place(i, j, meta_ref):
         offset = jnp.where(i == 0, 0, jnp.where(i == 1, 3, 1))
@@ -513,7 +513,7 @@
 
 def apply_last(meta, blended, q, scaled, rights, outs):
     rows, cols = blended.shape
-    tiles = 2
+    tiles = 1
     here = pl.BlockSpec(
         (rows // tiles, cols // 4), lambda i, meta_ref: (i, (meta_ref[3] + 2) % 4)
     )

time: 277 us -> 276 us (level)
  no operation moved by 1% of the time
where the time goes in v10:
time: 276 us
  blocking collectives  98.5 us (36%)
  Pallas kernels  73.3 us (27%)
  waiting for transfers between devices  59.1 us (21%)
  starting transfers between devices  27 us (10%)
  between operations  15.2 us (6%)
    all_to_all x8, blocking collectives, exchange(): return lax.all_to_all(a, axis, 0, 0, axis_index_groups=groups, tiled=True)  98.5 us
    reduce_scatter x4, waiting for transfers between devices, scatter(): lax.psum_scatter(a, AXES, scatter_dimension=0, axis_index_groups=groups,...  44.3 us
    pallas_call x2, Pallas kernels, inverse_factor(): pl.pallas_call(inverse_kernel, out_shape=(jax.ShapeDtypeStruct((RANK, RAN...  34.9 us
    ppermute x6, starting transfers between devices, swap_cores(): return lax.ppermute(a, 'tp', [(i, i ^ 1) for i in range(8)])  16.9 us
    pallas_call x2, Pallas kernels, right_partial(): pl.pallas_call(right_kernel, grid=(steps,), in_specs=[smem_spec(), pl.Blo...  12.3 us
    pallas_call x1, Pallas kernels, left_partial(): pl.pallas_call(left_kernel, grid=(2,), out_shape=(jax.ShapeDtypeStruct((r...  9.67 us
    ppermute x6, waiting for transfers between devices, swap_cores(): return lax.ppermute(a, 'tp', [(i, i ^ 1) for i in range(8)])  7.8 us
    pallas_call x1, Pallas kernels, apply_three(): pl.pallas_call(apply_kernel, grid_spec=pltpu.PrefetchScalarGridSpec(num_s...  6.17 us
  transfers between devices with their start and end apart: 20, of which 12 were waited for; matrix products, arithmetic and copies ran while one was open for 0% of the time, Pallas kernels for 17%

profile of v10, /device:TPU:1, one launch (start us, length us, event | category | flops | bytes accessed | tf_op | source)
XLA Modules:
  0.0 275.7 jit_solution(2795911508688223771)
XLA Ops:
  7.2 0.0 reduce-scatter.9.cloned.1.call-start
  7.9 0.1 stack.19.meta_ref
  8.0 9.7 %left_partial.1 = (bf16[512,3584]{1,0:T(8,128)(2,1)S(1)}, f32[256,512]{1,0:T(8,128)}, f32[256,512]{1,0:T(8,128)}) custom-call(s32[5]{0:T(128)S(1)} %stack.19.meta_ref, bf16[512,3584]{1,0:T(8,128)(2,1)} %m_ref.1, bf16[512,3584]{1,0:T(8,128)(2,1)} %g_ref.1), custom_call_target="tpu_custom_call" | custom-call | tf_op jit(solution)/shard_map/left_partial/pallas_call | solution.py:236
  17.6 1.4 collective-permute-start.2
  19.1 1.7 collective-permute-done.2
  20.8 1.1 add.39
  21.9 13.5 %all_to_all.78 = f32[4,64,512]{2,1,0:T(8,128)S(1)} all-to-all(f32[4,64,512]{2,1,0:T(8,128)S(1)} %bitcast.43), channel_id=1, replica_groups={{0,2,4,6},{1,3,5,7},{8,10,12,14},{9,11,13,15},{16,18,20,22},{17,19,21,2..., dimensions={0} | all-to-all | bytes 1048576 | tf_op jit(solution)/shard_map/all_to_all | solution.py:72
  35.5 7.9 %all_to_all.79 = bf16[4,64,512]{2,1,0:T(8,128)(2,1)S(1)} all-to-all(bf16[4,64,512]{2,1,0:T(8,128)(2,1)S(1)} %bitcast.42), channel_id=1, replica_groups={{0,2,4,6},{1,3,5,7},{8,10,12,14},{9,11,13,15},{16,18,20,22},{17,19,21,2..., dimensions={0} | all-to-all | bytes 524288 | tf_op jit(solution)/shard_map/all_to_all | solution.py:72
  43.4 3.0 %collective-permute-start.3 = (bf16[256,512]{1,0:T(8,128)(2,1)S(1)}, bf16[256,512]{1,0:T(8,128)(2,1)S(1)}, u32[]{:S(2)}, u32[]{:S(2)}) collective-permute-start(bf16[256,512]{1,0:T(8,128)(2,1)S(1)} %bitcast.27), channel_id=1, source_target_pairs={{0,1},{1,0},{2,3},{3,2},{4,5},{5,4},{6,7},{7,6},{8,9},{9,8},{10,11... | collective-permute-start | bytes 786440 | tf_op jit(solution)/shard_map/ppermute | solution.py:55
  46.4 1.2 collective-permute-done.3.other_ref
  47.5 4.3 %right_partial.3 = bf16[3584,512]{1,0:T(8,128)(2,1)} custom-call(s32[5]{0:T(128)S(1)} %stack.19.meta_ref, bf16[512,3584]{1,0:T(8,128)(2,1)S(1)} %get-tuple-element.48.b_ref, bf16[256,512]{1,0:T(8,128)(2,1)S(1)} %bitcast.28, bf16[256,512]{1,0:T(8,128)(2,1)S(1)} %collective-permute-done.3.other_ref), custom_call_target="tpu_custom_call" | custom-call | tf_op jit(solution)/shard_map/right_partial/pallas_call | solution.py:311
  51.8 0.0 reduce-scatter.9.cloned.1.call-update
  51.8 0.0 reduce-scatter.11.cloned.1.call-start
  51.9 0.9 gram_share.3
  52.8 17.0 %all_to_all.80 = f32[16,40,128]{2,1,0:T(8,128)S(1)} all-to-all(f32[16,40,128]{2,1,0:T(8,128)S(1)} %bitcast.41), channel_id=1, replica_groups=mesh['fsdp'=16,'tp'=8] {'fsdp'}, dimensions={0} | all-to-all | bytes 655360 | tf_op jit(solution)/shard_map/all_to_all | solution.py:72
  69.8 12.9 %all_to_all.81 = f32[16,40,128]{2,1,0:T(8,128)S(1)} all-to-all(f32[16,40,128]{2,1,0:T(8,128)S(1)} %bitcast.38), channel_id=1, replica_groups=mesh['fsdp'=16,'tp'=8] {'fsdp'}, dimensions={0} | all-to-all | bytes 655360 | tf_op jit(solution)/shard_map/all_to_all | solution.py:72
  82.7 3.4 %reduce-scatter.9.cloned.1.call-done = bf16[896,512]{1,0:T(8,128)(2,1)} async-done(((bf16[3584,512]{1,0:T(8,128)(2,1)}), bf16[896,512]{1,0:T(8,128)(2,1)}) %reduce-scatter.9.cloned.1.call-update) | async-done | bytes 917520 | tf_op jit(solution)/shard_map/reduce_scatter | solution.py:88
  86.1 0.0 reduce-scatter.11.cloned.1.call-update
  86.1 0.8 collective-permute-start.4
  86.9 1.3 collective-permute-done.4.other_ref
  88.2 17.4 %inverse_factor.3 = (f32[512,512]{1,0:T(8,128)S(1)}, f32[1,1]{1,0:T(1,128)}) custom-call(s32[5]{0:T(128)S(1)} %stack.19.meta_ref, f32[640,128]{1,0:T(8,128)S(1)} %bitcast.34, f32[640,128]{1,0:T(8,128)S(1)} %collective-permute-done.4.other_ref), custom_call_target="tpu_custom_call" | custom-call | bytes 70000000 | tf_op jit(solution)/shard_map/inverse_factor/pallas_call | solution.py:394
  105.6 1.3 ortho_left.3
  106.9 0.0 reduce-scatter.11.cloned.1.call-done
  107.6 117.2 %conditional.1 = (bf16[224,512]{1,0:T(8,128)(2,1)S(1)}, bf16[512,512]{1,0:T(8,128)(2,1)S(1)}) conditional(s32[]{:T(128)} %bitcast.17, (f32[64,512]{1,0:T(8,128)S(1)}, s32[5]{0:T(128)S(1)}, bf16[512,3584]{1,0:T(8,128)(2,1)}) %tuple.35, (bf16[224,512]{1,0:T(8,128)(2,1)}, f32[512,512]{1,0:T(8,128)S(1)}, bf16[512,512]{1,0:T(8,128)(2,1)S(1)}) %tuple.23), branch_computations={%region_2.5_spmd, %region_5.6_spmd} | conditional | bytes 112664144 | solution.py:589
  107.6 0.0 reduce-scatter.5.cloned.1.call-start
  107.7 0.1 tile.0
  107.7 10.1 %all_to_all.75 = f32[4,64,512]{2,1,0:T(8,128)S(1)} all-to-all(f32[4,64,512]{2,1,0:T(8,128)S(1)} %tile.0), channel_id=1, replica_groups={{0,2,4,6},{1,3,5,7},{8,10,12,14},{9,11,13,15},{16,18,20,22},{17,19,21,2..., dimensions={0} | all-to-all | bytes 1048576 | tf_op jit(solution)/shard_map/cond/branch_0_fun/all_to_all | solution.py:72
  117.9 4.0 %collective-permute-start = (f32[256,512]{1,0:T(8,128)S(1)}, f32[256,512]{1,0:T(8,128)S(1)}, u32[]{:S(2)}, u32[]{:S(2)}) collective-permute-start(f32[256,512]{1,0:T(8,128)S(1)} %bitcast.19), channel_id=1, source_target_pairs={{0,1},{1,0},{2,3},{3,2},{4,5},{5,4},{6,7},{7,6},{8,9},{9,8},{10,11... | collective-permute-start | bytes 1572872 | tf_op jit(solution)/shard_map/cond/branch_0_fun/ppermute | solution.py:55
  121.8 1.5 collective-permute-done.other_ref
  123.4 8.0 %right_partial.2 = f32[3584,512]{1,0:T(8,128)} custom-call(s32[5]{0:T(128)S(1)} %get-tuple-element.12.meta_ref, bf16[512,3584]{1,0:T(8,128)(2,1)} %get-tuple-element.13.b_ref, f32[256,512]{1,0:T(8,128)S(1)} %bitcast.20, f32[256,512]{1,0:T(8,128)S(1)} %collective-permute-done.other_ref), custom_call_target="tpu_custom_call" | custom-call | tf_op jit(solution)/shard_map/cond/branch_0_fun/right_partial/pallas_call | solution.py:311
  131.4 0.0 reduce-scatter.5.cloned.1.call-update
  131.4 0.0 reduce-scatter.7.cloned.1.call-start
  131.5 40.9 %reduce-scatter.5.cloned.1.call-done = f32[896,512]{1,0:T(8,128)} async-done(((f32[3584,512]{1,0:T(8,128)}), f32[896,512]{1,0:T(8,128)}) %reduce-scatter.5.cloned.1.call-update) | async-done | bytes 1835024 | tf_op jit(solution)/shard_map/cond/branch_0_fun/reduce_scatter | solution.py:88
  172.4 0.0 reduce-scatter.7.cloned.1.call-update
  172.4 1.4 gram_share.2
  173.8 12.8 %all_to_all.76 = f32[16,40,128]{2,1,0:T(8,128)S(1)} all-to-all(f32[16,40,128]{2,1,0:T(8,128)S(1)} %bitcast.32), channel_id=1, replica_groups=mesh['fsdp'=16,'tp'=8] {'fsdp'}, dimensions={0} | all-to-all | bytes 655360 | tf_op jit(solution)/shard_map/cond/branch_0_fun/all_to_all | solution.py:72
  186.7 12.5 %all_to_all.77 = f32[16,40,128]{2,1,0:T(8,128)S(1)} all-to-all(f32[16,40,128]{2,1,0:T(8,128)S(1)} %bitcast.40), channel_id=1, replica_groups=mesh['fsdp'=16,'tp'=8] {'fsdp'}, dimensions={0} | all-to-all | bytes 655360 | tf_op jit(solution)/shard_map/cond/branch_0_fun/all_to_all | solution.py:72
  199.1 2.1 collective-permute-start.1
  201.2 1.3 collective-permute-done.1.other_ref
  202.5 17.4 %inverse_factor.2 = (f32[512,512]{1,0:T(8,128)S(1)}, f32[1,1]{1,0:T(1,128)}) custom-call(s32[5]{0:T(128)S(1)} %get-tuple-element.12.meta_ref, f32[640,128]{1,0:T(8,128)S(1)} %bitcast.36, f32[640,128]{1,0:T(8,128)S(1)} %collective-permute-done.1.other_ref), custom_call_target="tpu_custom_call" | custom-call | bytes 70000000 | tf_op jit(solution)/shard_map/cond/branch_0_fun/inverse_factor/pallas_call | solution.py:394
  219.9 2.4 ortho_left.2
  222.4 0.0 reduce-scatter.7.cloned.1.call-done.w_ref
  222.4 1.0 copy-done
  223.4 1.1 solve_rows.2
  224.8 0.1 tile.4
  224.8 11.7 %all_to_all.82 = bf16[4,224,512]{2,1,0:T(8,128)(2,1)S(1)} all-to-all(bf16[4,224,512]{2,1,0:T(8,128)(2,1)S(1)} %tile.4), channel_id=1, replica_groups={{0,32,64,96},{2,34,66,98},{4,36,68,100},{6,38,70,102},{8,40,72,104},{10..., dimensions={0} | all-to-all | bytes 1835008 | tf_op jit(solution)/shard_map/all_to_all | solution.py:72
  236.6 0.9 collective-permute-start.6
  237.4 0.6 collective-permute-start.5
  238.0 0.1 block_sums.1
  238.1 2.8 %collective-permute-start.9 = (f32[8,512]{1,0:T(8,128)S(1)}, f32[8,512]{1,0:T(8,128)S(1)}, u32[]{:S(2)}, u32[]{:S(2)}) collective-permute-start(f32[8,512]{1,0:T(8,128)S(1)} %block_sums.1), channel_id=1, source_target_pairs={{0,6},{1,7},{2,0},{3,1},{4,2},{5,3},{6,4},{7,5},{8,14},{9,15},{10,... | collective-permute-start | bytes 49160 | tf_op jit(solution)/shard_map/ppermute | solution.py:59
  240.9 0.6 collective-permute-start.8
  241.5 0.7 collective-permute-start.7
  242.2 2.8 %collective-permute-done.8 = f32[8,512]{1,0:T(8,128)S(1)} collective-permute-done((f32[8,512]{1,0:T(8,128)S(1)}, f32[8,512]{1,0:T(8,128)S(1)}, u32[]{:S(2)}, u32[]{:S(2)}) %collective-permute-start.8) | collective-permute-done | bytes 16416 | tf_op jit(solution)/shard_map/ppermute | solution.py:59
  245.0 0.6 collective-permute-done.7
  245.6 2.2 collective-permute-start.12
  247.8 0.7 collective-permute-start.10
  248.5 0.8 collective-permute-done.12
  249.3 2.6 collective-permute-done.11
  252.0 0.8 collective-permute-start.15
  252.8 0.7 collective-permute-start.14
  253.5 5.7 %collective-permute-start.13 = (f32[8,512]{1,0:T(8,128)S(1)}, f32[8,512]{1,0:T(8,128)S(1)}, u32[]{:S(2)}, u32[]{:S(2)}) collective-permute-start(f32[8,512]{1,0:T(8,128)S(1)} %add_add_fusion.sums_ref), channel_id=1, source_target_pairs={{0,1},{1,0},{2,3},{3,2},{4,5},{5,4},{6,7},{7,6},{8,9},{9,8},{10,11... | collective-permute-start | bytes 49160 | tf_op jit(solution)/shard_map/ppermute | solution.py:55
  259.2 0.8 collective-permute-done.13.swapped_ref
  260.1 6.2 %apply_three.1 = (bf16[512,3584]{1,0:T(8,128)(2,1)}, bf16[512,3584]{1,0:T(8,128)(2,1)}, bf16[512,512]{1,0:T(8,128)(2,1)S(1)}) custom-call(s32[5]{0:T(128)S(1)} %stack.19.meta_ref, bf16[512,3584]{1,0:T(8,128)(2,1)S(1)} %copy-done.2, bf16[512,512]{1,0:T(8,128)(2,1)S(1)} %get-tuple-element.64.q_ref, f32[8,512]{1,0:T(8,128)S(1)} %add_add_fusion.sums_ref, ...), custom_call_target="tpu_custom_call" | custom-call | tf_op jit(solution)/shard_map/apply_three/pallas_call | solution.py:492
  266.2 3.0 %apply_last.1 = (bf16[512,3584]{1,0:T(8,128)(2,1)}, bf16[512,3584]{1,0:T(8,128)(2,1)}) custom-call(s32[5]{0:T(128)S(1)} %stack.19.meta_ref, bf16[512,3584]{1,0:T(8,128)(2,1)S(1)} %copy-done.2, bf16[512,512]{1,0:T(8,128)(2,1)S(1)} %get-tuple-element.64.q_ref, ...), custom_call_target="tpu_custom_call", output_to_operand_aliasing={{0}: (6, {}), {1}: (7, {})} | custom-call | tf_op jit(solution)/shard_map/apply_last/pallas_call | solution.py:524
  (19 shorter events, 0.2 us)
Async XLA Ops:
  7.2 78.9 %reduce-scatter.9.cloned.1.call-start = ((), (), s32[]{:S(2)}) async-start(), calls=%async_computation.14 | async-start | bytes 4587520 | tf_op jit(solution)/shard_map/reduce_scatter | solution.py:88
  17.6 29.9 %copy-start.1 = (bf16[512,3584]{1,0:T(8,128)(2,1)}, bf16[512,3584]{1,0:T(8,128)(2,1)S(1)}, u32[]{:S(2)}) copy-start(bf16[512,3584]{1,0:T(8,128)(2,1)S(1)} %get-tuple-element.48.b_ref) | copy-start | bytes 11010052
  17.6 3.2 %collective-permute-start.2 = (f32[256,512]{1,0:T(8,128)}, f32[256,512]{1,0:T(8,128)S(1)}, u32[]{:S(2)}, u32[]{:S(2)}) collective-permute-start(f32[256,512]{1,0:T(8,128)} %get-tuple-element.50), channel_id=1, source_target_pairs={{0,1},{1,0},{2,3},{3,2},{4,5},{5,4},{6,7},{7,6},{8,9},{9,8},{10,11... | collective-permute-start | bytes 1572872 | tf_op jit(solution)/shard_map/ppermute | solution.py:55
  43.4 4.1 %collective-permute-start.3 = (bf16[256,512]{1,0:T(8,128)(2,1)S(1)}, bf16[256,512]{1,0:T(8,128)(2,1)S(1)}, u32[]{:S(2)}, u32[]{:S(2)}) collective-permute-start(bf16[256,512]{1,0:T(8,128)(2,1)S(1)} %bitcast.27), channel_id=1, source_target_pairs={{0,1},{1,0},{2,3},{3,2},{4,5},{5,4},{6,7},{7,6},{8,9},{9,8},{10,11... | collective-permute-start | bytes 786440 | tf_op jit(solution)/shard_map/ppermute | solution.py:55
  51.8 55.1 %reduce-scatter.11.cloned.1.call-start = ((), (), s32[]{:S(2)}) async-start(), calls=%async_computation.15 | async-start | bytes 1146880 | tf_op jit(solution)/shard_map/reduce_scatter | solution.py:88
  86.1 2.0 collective-permute-start.4
  107.6 64.7 %reduce-scatter.5.cloned.1.call-start = ((), (), s32[]{:S(2)}) async-start(), calls=%async_computation.12 | async-start | bytes 9175040 | tf_op jit(solution)/shard_map/cond/branch_0_fun/reduce_scatter | solution.py:88
  117.9 5.5 %collective-permute-start = (f32[256,512]{1,0:T(8,128)S(1)}, f32[256,512]{1,0:T(8,128)S(1)}, u32[]{:S(2)}, u32[]{:S(2)}) collective-permute-start(f32[256,512]{1,0:T(8,128)S(1)} %bitcast.19), channel_id=1, source_target_pairs={{0,1},{1,0},{2,3},{3,2},{4,5},{5,4},{6,7},{7,6},{8,9},{9,8},{10,11... | collective-permute-start | bytes 1572872 | tf_op jit(solution)/shard_map/cond/branch_0_fun/ppermute | solution.py:55
  131.4 91.0 %reduce-scatter.7.cloned.1.call-start = ((), (), s32[]{:S(2)}) async-start(), calls=%async_computation.13 | async-start | bytes 2293760 | tf_op jit(solution)/shard_map/cond/branch_0_fun/reduce_scatter | solution.py:88
  199.1 3.3 %collective-permute-start.1 = (f32[640,128]{1,0:T(8,128)S(1)}, f32[640,128]{1,0:T(8,128)S(1)}, u32[]{:S(2)}, u32[]{:S(2)}) collective-permute-start(f32[640,128]{1,0:T(8,128)S(1)} %bitcast.35), channel_id=1, source_target_pairs={{0,1},{1,0},{2,3},{3,2},{4,5},{5,4},{6,7},{7,6},{8,9},{9,8},{10,11... | collective-permute-start | bytes 983048 | tf_op jit(solution)/shard_map/cond/branch_0_fun/ppermute | solution.py:55
  222.4 1.0 copy-start
  224.8 35.3 %copy-start.2 = (bf16[512,3584]{1,0:T(8,128)(2,1)S(1)}, bf16[512,3584]{1,0:T(8,128)(2,1)}, u32[]{:S(2)}) copy-start(bf16[512,3584]{1,0:T(8,128)(2,1)} %copy-done.1) | copy-start | bytes 11010052
  236.6 15.4 %collective-permute-start.6 = (bf16[896,512]{1,0:T(8,128)(2,1)S(1)}, bf16[896,512]{1,0:T(8,128)(2,1)S(1)}, u32[]{:S(2)}, u32[]{:S(2)}) collective-permute-start(bf16[896,512]{1,0:T(8,128)(2,1)S(1)} %bitcast.23), channel_id=1, source_target_pairs={{0,24},{1,97},{2,26},{3,99},{4,28},{5,101},{6,30},{7,103},{8,0},{9... | collective-permute-start | bytes 2752520 | tf_op jit(solution)/shard_map/ppermute | solution.py:47
  237.4 14.5 %collective-permute-start.5 = (bf16[896,512]{1,0:T(8,128)(2,1)S(1)}, bf16[896,512]{1,0:T(8,128)(2,1)S(1)}, u32[]{:S(2)}, u32[]{:S(2)}) collective-permute-start(bf16[896,512]{1,0:T(8,128)(2,1)S(1)} %bitcast.24), channel_id=1, source_target_pairs={{0,8},{1,33},{2,10},{3,35},{4,12},{5,37},{6,14},{7,39},{8,16},{9,4... | collective-permute-start | bytes 2752520 | tf_op jit(solution)/shard_map/ppermute | solution.py:47
  238.1 4.1 %collective-permute-start.9 = (f32[8,512]{1,0:T(8,128)S(1)}, f32[8,512]{1,0:T(8,128)S(1)}, u32[]{:S(2)}, u32[]{:S(2)}) collective-permute-start(f32[8,512]{1,0:T(8,128)S(1)} %block_sums.1), channel_id=1, source_target_pairs={{0,6},{1,7},{2,0},{3,1},{4,2},{5,3},{6,4},{7,5},{8,14},{9,15},{10,... | collective-permute-start | bytes 49160 | tf_op jit(solution)/shard_map/ppermute | solution.py:59
  240.9 4.1 %collective-permute-start.8 = (f32[8,512]{1,0:T(8,128)S(1)}, f32[8,512]{1,0:T(8,128)S(1)}, u32[]{:S(2)}, u32[]{:S(2)}) collective-permute-start(f32[8,512]{1,0:T(8,128)S(1)} %block_sums.1), channel_id=1, source_target_pairs={{0,4},{1,5},{2,6},{3,7},{4,0},{5,1},{6,2},{7,3},{8,12},{9,13},{10,... | collective-permute-start | bytes 49160 | tf_op jit(solution)/shard_map/ppermute | solution.py:59
  241.5 4.1 %collective-permute-start.7 = (f32[8,512]{1,0:T(8,128)S(1)}, f32[8,512]{1,0:T(8,128)S(1)}, u32[]{:S(2)}, u32[]{:S(2)}) collective-permute-start(f32[8,512]{1,0:T(8,128)S(1)} %block_sums.1), channel_id=1, source_target_pairs={{0,2},{1,3},{2,4},{3,5},{4,6},{5,7},{6,0},{7,1},{8,10},{9,11},{10,... | collective-permute-start | bytes 49160 | tf_op jit(solution)/shard_map/ppermute | solution.py:59
  245.6 3.6 %collective-permute-start.12 = (f32[8,512]{1,0:T(8,128)S(1)}, f32[8,512]{1,0:T(8,128)S(1)}, u32[]{:S(2)}, u32[]{:S(2)}) collective-permute-start(f32[8,512]{1,0:T(8,128)S(1)} %add_add_fusion.1), channel_id=1, source_target_pairs={{0,24},{1,97},{2,26},{3,99},{4,28},{5,101},{6,30},{7,103},{8,0},{9... | collective-permute-start | bytes 49160 | tf_op jit(solution)/shard_map/ppermute | solution.py:47
  247.8 4.1 %collective-permute-start.11 = (f32[8,512]{1,0:T(8,128)S(1)}, f32[8,512]{1,0:T(8,128)S(1)}, u32[]{:S(2)}, u32[]{:S(2)}) collective-permute-start(f32[8,512]{1,0:T(8,128)S(1)} %add_add_fusion.1), channel_id=1, source_target_pairs={{0,16},{1,65},{2,18},{3,67},{4,20},{5,69},{6,22},{7,71},{8,24},{9,... | collective-permute-start | bytes 49160 | tf_op jit(solution)/shard_map/ppermute | solution.py:47
  247.8 4.1 %collective-permute-start.10 = (f32[8,512]{1,0:T(8,128)S(1)}, f32[8,512]{1,0:T(8,128)S(1)}, u32[]{:S(2)}, u32[]{:S(2)}) collective-permute-start(f32[8,512]{1,0:T(8,128)S(1)} %add_add_fusion.1), channel_id=1, source_target_pairs={{0,8},{1,33},{2,10},{3,35},{4,12},{5,37},{6,14},{7,39},{8,16},{9,4... | collective-permute-start | bytes 49160 | tf_op jit(solution)/shard_map/ppermute | solution.py:47
  252.0 14.2 %collective-permute-start.15 = (bf16[896,256]{1,0:T(8,128)(2,1)S(1)}, bf16[896,256]{1,0:T(8,128)(2,1)S(1)}, u32[]{:S(2)}, u32[]{:S(2)}) collective-permute-start(bf16[896,256]{1,0:T(8,128)(2,1)S(1)} %slice.7), channel_id=1, source_target_pairs={{0,24},{1,97},{2,26},{3,99},{4,28},{5,101},{6,30},{7,103},{8,0},{9... | collective-permute-start | bytes 1376264 | tf_op jit(solution)/shard_map/ppermute | solution.py:47
  252.8 13.4 %collective-permute-start.14 = (bf16[896,256]{1,0:T(8,128)(2,1)S(1)}, bf16[896,256]{1,0:T(8,128)(2,1)S(1)}, u32[]{:S(2)}, u32[]{:S(2)}) collective-permute-start(bf16[896,256]{1,0:T(8,128)(2,1)S(1)} %slice.6), channel_id=1, source_target_pairs={{0,8},{1,33},{2,10},{3,35},{4,12},{5,37},{6,14},{7,39},{8,16},{9,4... | collective-permute-start | bytes 1376264 | tf_op jit(solution)/shard_map/ppermute | solution.py:47
  253.5 6.5 %collective-permute-start.13 = (f32[8,512]{1,0:T(8,128)S(1)}, f32[8,512]{1,0:T(8,128)S(1)}, u32[]{:S(2)}, u32[]{:S(2)}) collective-permute-start(f32[8,512]{1,0:T(8,128)S(1)} %add_add_fusion.sums_ref), channel_id=1, source_target_pairs={{0,1},{1,0},{2,3},{3,2},{4,5},{5,4},{6,7},{7,6},{8,9},{9,8},{10,11... | collective-permute-start | bytes 49160 | tf_op jit(solution)/shard_map/ppermute | solution.py:55
Sparse Core Ops, SparseCore 0:
  52.0 34.0 reduce-scatter.8
  88.5 17.5 reduce-scatter.10
  131.5 40.7 reduce-scatter.4
  174.6 25.5 reduce-scatter.6

commit v11 on v10

--- a/solution.py
+++ b/solution.py
@@ -577,7 +577,7 @@
 
     mine = exchange(rounded, "tp", Z_GROUPS)
     other = swap_cores(mine)
-    w = right_partial(meta, blended, mine, other, 2)
+    w = right_partial(meta, blended, mine, other, 4)
     mine, other, w = lax.optimization_barrier((mine, other, w))
     w = scatter(w, FIRST_GROUPS)
     gram = gram_sum(mine, other)

time: 276 us -> 277 us (level)
  transfers between devices with their start and end apart: 20 -> 20, of which waited for: 12 -> 13; matrix products, arithmetic and copies ran while one was open for 0% -> 0% of each run, Pallas kernels for 17% -> 17%
where the time goes in v11:
time: 277 us; the launch traced here: 276 us
  blocking collectives  98.6 us (36%)
  Pallas kernels  73.6 us (27%)
  waiting for transfers between devices  59.2 us (21%)
  starting transfers between devices  26.8 us (10%)
  between operations  15.2 us (5%)
    all_to_all x8, blocking collectives, exchange(): return lax.all_to_all(a, axis, 0, 0, axis_index_groups=groups, tiled=True)  98.6 us
    reduce_scatter x4, waiting for transfers between devices, scatter(): lax.psum_scatter(a, AXES, scatter_dimension=0, axis_index_groups=groups,...  44.3 us
    pallas_call x2, Pallas kernels, inverse_factor(): pl.pallas_call(inverse_kernel, out_shape=(jax.ShapeDtypeStruct((RANK, RAN...  34.9 us
    ppermute x6, starting transfers between devices, swap_cores(): return lax.ppermute(a, 'tp', [(i, i ^ 1) for i in range(8)])  17.1 us
    pallas_call x2, Pallas kernels, right_partial(): pl.pallas_call(right_kernel, grid=(steps,), in_specs=[smem_spec(), pl.Blo...  12.6 us
    pallas_call x1, Pallas kernels, left_partial(): pl.pallas_call(left_kernel, grid=(2,), out_shape=(jax.ShapeDtypeStruct((r...  9.66 us
    ppermute x6, waiting for transfers between devices, swap_cores(): return lax.ppermute(a, 'tp', [(i, i ^ 1) for i in range(8)])  7.8 us
    pallas_call x1, Pallas kernels, apply_three(): pl.pallas_call(apply_kernel, grid_spec=pltpu.PrefetchScalarGridSpec(num_s...  6.17 us
  transfers between devices with their start and end apart: 20, of which 13 were waited for; matrix products, arithmetic and copies ran while one was open for 0% of the time, Pallas kernels for 17%

profile of v11, /device:TPU:1, one launch (start us, length us, event | category | flops | bytes accessed | tf_op | source)
XLA Modules:
  0.0 276.1 jit_solution(17707582036952066578)
XLA Ops:
  7.2 0.0 reduce-scatter.9.cloned.1.call-start
  7.9 0.1 stack.19.meta_ref
  8.0 9.7 %left_partial.1 = (bf16[512,3584]{1,0:T(8,128)(2,1)S(1)}, f32[256,512]{1,0:T(8,128)}, f32[256,512]{1,0:T(8,128)}) custom-call(s32[5]{0:T(128)S(1)} %stack.19.meta_ref, bf16[512,3584]{1,0:T(8,128)(2,1)} %m_ref.1, bf16[512,3584]{1,0:T(8,128)(2,1)} %g_ref.1), custom_call_target="tpu_custom_call" | custom-call | tf_op jit(solution)/shard_map/left_partial/pallas_call | solution.py:236
  17.6 1.4 collective-permute-start.2
  19.1 1.7 collective-permute-done.2
  20.8 1.1 add.39
  21.9 13.5 %all_to_all.78 = f32[4,64,512]{2,1,0:T(8,128)S(1)} all-to-all(f32[4,64,512]{2,1,0:T(8,128)S(1)} %bitcast.43), channel_id=1, replica_groups={{0,2,4,6},{1,3,5,7},{8,10,12,14},{9,11,13,15},{16,18,20,22},{17,19,21,2..., dimensions={0} | all-to-all | bytes 1048576 | tf_op jit(solution)/shard_map/all_to_all | solution.py:72
  35.5 7.9 %all_to_all.79 = bf16[4,64,512]{2,1,0:T(8,128)(2,1)S(1)} all-to-all(bf16[4,64,512]{2,1,0:T(8,128)(2,1)S(1)} %bitcast.42), channel_id=1, replica_groups={{0,2,4,6},{1,3,5,7},{8,10,12,14},{9,11,13,15},{16,18,20,22},{17,19,21,2..., dimensions={0} | all-to-all | bytes 524288 | tf_op jit(solution)/shard_map/all_to_all | solution.py:72
  43.4 3.0 %collective-permute-start.3 = (bf16[256,512]{1,0:T(8,128)(2,1)S(1)}, bf16[256,512]{1,0:T(8,128)(2,1)S(1)}, u32[]{:S(2)}, u32[]{:S(2)}) collective-permute-start(bf16[256,512]{1,0:T(8,128)(2,1)S(1)} %bitcast.27), channel_id=1, source_target_pairs={{0,1},{1,0},{2,3},{3,2},{4,5},{5,4},{6,7},{7,6},{8,9},{9,8},{10,11... | collective-permute-start | bytes 786440 | tf_op jit(solution)/shard_map/ppermute | solution.py:55
  46.4 1.2 collective-permute-done.3.other_ref
  47.6 4.6 %right_partial.3 = bf16[3584,512]{1,0:T(8,128)(2,1)} custom-call(s32[5]{0:T(128)S(1)} %stack.19.meta_ref, bf16[512,3584]{1,0:T(8,128)(2,1)S(1)} %get-tuple-element.48.b_ref, bf16[256,512]{1,0:T(8,128)(2,1)S(1)} %bitcast.28, bf16[256,512]{1,0:T(8,128)(2,1)S(1)} %collective-permute-done.3.other_ref), custom_call_target="tpu_custom_call" | custom-call | tf_op jit(solution)/shard_map/right_partial/pallas_call | solution.py:311
  52.2 0.0 reduce-scatter.9.cloned.1.call-update
  52.2 0.0 reduce-scatter.11.cloned.1.call-start
  52.3 0.9 gram_share.3
  53.1 17.0 %all_to_all.80 = f32[16,40,128]{2,1,0:T(8,128)S(1)} all-to-all(f32[16,40,128]{2,1,0:T(8,128)S(1)} %bitcast.41), channel_id=1, replica_groups=mesh['fsdp'=16,'tp'=8] {'fsdp'}, dimensions={0} | all-to-all | bytes 655360 | tf_op jit(solution)/shard_map/all_to_all | solution.py:72
  70.2 12.9 %all_to_all.81 = f32[16,40,128]{2,1,0:T(8,128)S(1)} all-to-all(f32[16,40,128]{2,1,0:T(8,128)S(1)} %bitcast.38), channel_id=1, replica_groups=mesh['fsdp'=16,'tp'=8] {'fsdp'}, dimensions={0} | all-to-all | bytes 655360 | tf_op jit(solution)/shard_map/all_to_all | solution.py:72
  83.1 3.4 %reduce-scatter.9.cloned.1.call-done = bf16[896,512]{1,0:T(8,128)(2,1)} async-done(((bf16[3584,512]{1,0:T(8,128)(2,1)}), bf16[896,512]{1,0:T(8,128)(2,1)}) %reduce-scatter.9.cloned.1.call-update) | async-done | bytes 917520 | tf_op jit(solution)/shard_map/reduce_scatter | solution.py:88
  86.5 0.0 reduce-scatter.11.cloned.1.call-update
  86.5 0.8 collective-permute-start.4
  87.3 1.3 collective-permute-done.4.other_ref
  88.6 17.4 %inverse_factor.3 = (f32[512,512]{1,0:T(8,128)S(1)}, f32[1,1]{1,0:T(1,128)}) custom-call(s32[5]{0:T(128)S(1)} %stack.19.meta_ref, f32[640,128]{1,0:T(8,128)S(1)} %bitcast.34, f32[640,128]{1,0:T(8,128)S(1)} %collective-permute-done.4.other_ref), custom_call_target="tpu_custom_call" | custom-call | bytes 70000000 | tf_op jit(solution)/shard_map/inverse_factor/pallas_call | solution.py:394
  106.0 1.3 ortho_left.3
  107.3 0.0 reduce-scatter.11.cloned.1.call-done
  108.0 117.1 %conditional.1 = (bf16[224,512]{1,0:T(8,128)(2,1)S(1)}, bf16[512,512]{1,0:T(8,128)(2,1)S(1)}) conditional(s32[]{:T(128)} %bitcast.17, (f32[64,512]{1,0:T(8,128)S(1)}, s32[5]{0:T(128)S(1)}, bf16[512,3584]{1,0:T(8,128)(2,1)}) %tuple.35, (bf16[224,512]{1,0:T(8,128)(2,1)}, f32[512,512]{1,0:T(8,128)S(1)}, bf16[512,512]{1,0:T(8,128)(2,1)S(1)}) %tuple.23), branch_computations={%region_2.5_spmd, %region_5.6_spmd} | conditional | bytes 112664144 | solution.py:589
  108.0 0.0 reduce-scatter.5.cloned.1.call-start
  108.0 0.1 tile.0
  108.1 10.1 %all_to_all.75 = f32[4,64,512]{2,1,0:T(8,128)S(1)} all-to-all(f32[4,64,512]{2,1,0:T(8,128)S(1)} %tile.0), channel_id=1, replica_groups={{0,2,4,6},{1,3,5,7},{8,10,12,14},{9,11,13,15},{16,18,20,22},{17,19,21,2..., dimensions={0} | all-to-all | bytes 1048576 | tf_op jit(solution)/shard_map/cond/branch_0_fun/all_to_all | solution.py:72
  118.3 4.0 %collective-permute-start = (f32[256,512]{1,0:T(8,128)S(1)}, f32[256,512]{1,0:T(8,128)S(1)}, u32[]{:S(2)}, u32[]{:S(2)}) collective-permute-start(f32[256,512]{1,0:T(8,128)S(1)} %bitcast.19), channel_id=1, source_target_pairs={{0,1},{1,0},{2,3},{3,2},{4,5},{5,4},{6,7},{7,6},{8,9},{9,8},{10,11... | collective-permute-start | bytes 1572872 | tf_op jit(solution)/shard_map/cond/branch_0_fun/ppermute | solution.py:55
  122.2 1.5 collective-permute-done.other_ref
  123.7 8.0 %right_partial.2 = f32[3584,512]{1,0:T(8,128)} custom-call(s32[5]{0:T(128)S(1)} %get-tuple-element.12.meta_ref, bf16[512,3584]{1,0:T(8,128)(2,1)} %get-tuple-element.13.b_ref, f32[256,512]{1,0:T(8,128)S(1)} %bitcast.20, f32[256,512]{1,0:T(8,128)S(1)} %collective-permute-done.other_ref), custom_call_target="tpu_custom_call" | custom-call | tf_op jit(solution)/shard_map/cond/branch_0_fun/right_partial/pallas_call | solution.py:311
  131.8 0.0 reduce-scatter.7.cloned.1.call-start
  131.8 40.9 %reduce-scatter.5.cloned.1.call-done = f32[896,512]{1,0:T(8,128)} async-done(((f32[3584,512]{1,0:T(8,128)}), f32[896,512]{1,0:T(8,128)}) %reduce-scatter.5.cloned.1.call-update) | async-done | bytes 1835024 | tf_op jit(solution)/shard_map/cond/branch_0_fun/reduce_scatter | solution.py:88
  172.7 1.4 gram_share.2
  174.2 12.8 %all_to_all.76 = f32[16,40,128]{2,1,0:T(8,128)S(1)} all-to-all(f32[16,40,128]{2,1,0:T(8,128)S(1)} %bitcast.32), channel_id=1, replica_groups=mesh['fsdp'=16,'tp'=8] {'fsdp'}, dimensions={0} | all-to-all | bytes 655360 | tf_op jit(solution)/shard_map/cond/branch_0_fun/all_to_all | solution.py:72
  187.0 12.5 %all_to_all.77 = f32[16,40,128]{2,1,0:T(8,128)S(1)} all-to-all(f32[16,40,128]{2,1,0:T(8,128)S(1)} %bitcast.40), channel_id=1, replica_groups=mesh['fsdp'=16,'tp'=8] {'fsdp'}, dimensions={0} | all-to-all | bytes 655360 | tf_op jit(solution)/shard_map/cond/branch_0_fun/all_to_all | solution.py:72
  199.5 2.1 collective-permute-start.1
  201.6 1.3 collective-permute-done.1.other_ref
  202.8 17.4 %inverse_factor.2 = (f32[512,512]{1,0:T(8,128)S(1)}, f32[1,1]{1,0:T(1,128)}) custom-call(s32[5]{0:T(128)S(1)} %get-tuple-element.12.meta_ref, f32[640,128]{1,0:T(8,128)S(1)} %bitcast.36, f32[640,128]{1,0:T(8,128)S(1)} %collective-permute-done.1.other_ref), custom_call_target="tpu_custom_call" | custom-call | bytes 70000000 | tf_op jit(solution)/shard_map/cond/branch_0_fun/inverse_factor/pallas_call | solution.py:394
  220.3 2.4 ortho_left.2
  222.7 0.0 reduce-scatter.7.cloned.1.call-done.w_ref
  222.8 1.0 copy-done
  223.8 1.1 solve_rows.2
  225.1 0.1 tile.4
  225.2 11.8 %all_to_all.82 = bf16[4,224,512]{2,1,0:T(8,128)(2,1)S(1)} all-to-all(bf16[4,224,512]{2,1,0:T(8,128)(2,1)S(1)} %tile.4), channel_id=1, replica_groups={{0,32,64,96},{2,34,66,98},{4,36,68,100},{6,38,70,102},{8,40,72,104},{10..., dimensions={0} | all-to-all | bytes 1835008 | tf_op jit(solution)/shard_map/all_to_all | solution.py:72
  237.0 0.9 collective-permute-start.6
  237.9 0.6 collective-permute-start.5
  238.5 0.1 block_sums.1
  238.5 2.7 collective-permute-start.9
  241.3 0.3 collective-permute-start.8
  241.6 0.7 collective-permute-start.7
  242.3 3.1 %collective-permute-done.8 = f32[8,512]{1,0:T(8,128)S(1)} collective-permute-done((f32[8,512]{1,0:T(8,128)S(1)}, f32[8,512]{1,0:T(8,128)S(1)}, u32[]{:S(2)}, u32[]{:S(2)}) %collective-permute-start.8) | collective-permute-done | bytes 16416 | tf_op jit(solution)/shard_map/ppermute | solution.py:59
  245.4 0.5 collective-permute-done.7
  245.8 2.1 collective-permute-start.12
  247.9 0.1 collective-permute-start.11
  248.0 0.6 collective-permute-start.10
  248.6 1.1 collective-permute-done.12
  249.7 2.3 collective-permute-done.11
  252.0 0.1 collective-permute-done.10
  252.2 0.8 collective-permute-start.15
  252.9 0.8 collective-permute-start.14
  253.7 5.9 %collective-permute-start.13 = (f32[8,512]{1,0:T(8,128)S(1)}, f32[8,512]{1,0:T(8,128)S(1)}, u32[]{:S(2)}, u32[]{:S(2)}) collective-permute-start(f32[8,512]{1,0:T(8,128)S(1)} %add_add_fusion.sums_ref), channel_id=1, source_target_pairs={{0,1},{1,0},{2,3},{3,2},{4,5},{5,4},{6,7},{7,6},{8,9},{9,8},{10,11... | collective-permute-start | bytes 49160 | tf_op jit(solution)/shard_map/ppermute | solution.py:55
  259.6 0.8 collective-permute-done.13.swapped_ref
  260.5 6.2 %apply_three.1 = (bf16[512,3584]{1,0:T(8,128)(2,1)}, bf16[512,3584]{1,0:T(8,128)(2,1)}, bf16[512,512]{1,0:T(8,128)(2,1)S(1)}) custom-call(s32[5]{0:T(128)S(1)} %stack.19.meta_ref, bf16[512,3584]{1,0:T(8,128)(2,1)S(1)} %copy-done.2, bf16[512,512]{1,0:T(8,128)(2,1)S(1)} %get-tuple-element.64.q_ref, f32[8,512]{1,0:T(8,128)S(1)} %add_add_fusion.sums_ref, ...), custom_call_target="tpu_custom_call" | custom-call | tf_op jit(solution)/shard_map/apply_three/pallas_call | solution.py:492
  266.6 3.0 %apply_last.1 = (bf16[512,3584]{1,0:T(8,128)(2,1)}, bf16[512,3584]{1,0:T(8,128)(2,1)}) custom-call(s32[5]{0:T(128)S(1)} %stack.19.meta_ref, bf16[512,3584]{1,0:T(8,128)(2,1)S(1)} %copy-done.2, bf16[512,512]{1,0:T(8,128)(2,1)S(1)} %get-tuple-element.64.q_ref, ...), custom_call_target="tpu_custom_call", output_to_operand_aliasing={{0}: (6, {}), {1}: (7, {})} | custom-call | tf_op jit(solution)/shard_map/apply_last/pallas_call | solution.py:524
  (19 shorter events, 0.3 us)
Async XLA Ops:
  7.2 79.3 %reduce-scatter.9.cloned.1.call-start = ((), (), s32[]{:S(2)}) async-start(), calls=%async_computation.14 | async-start | bytes 4587520 | tf_op jit(solution)/shard_map/reduce_scatter | solution.py:88
  17.6 29.9 %copy-start.1 = (bf16[512,3584]{1,0:T(8,128)(2,1)}, bf16[512,3584]{1,0:T(8,128)(2,1)S(1)}, u32[]{:S(2)}) copy-start(bf16[512,3584]{1,0:T(8,128)(2,1)S(1)} %get-tuple-element.48.b_ref) | copy-start | bytes 11010052
  17.6 3.2 %collective-permute-start.2 = (f32[256,512]{1,0:T(8,128)}, f32[256,512]{1,0:T(8,128)S(1)}, u32[]{:S(2)}, u32[]{:S(2)}) collective-permute-start(f32[256,512]{1,0:T(8,128)} %get-tuple-element.50), channel_id=1, source_target_pairs={{0,1},{1,0},{2,3},{3,2},{4,5},{5,4},{6,7},{7,6},{8,9},{9,8},{10,11... | collective-permute-start | bytes 1572872 | tf_op jit(solution)/shard_map/ppermute | solution.py:55
  43.4 4.1 %collective-permute-start.3 = (bf16[256,512]{1,0:T(8,128)(2,1)S(1)}, bf16[256,512]{1,0:T(8,128)(2,1)S(1)}, u32[]{:S(2)}, u32[]{:S(2)}) collective-permute-start(bf16[256,512]{1,0:T(8,128)(2,1)S(1)} %bitcast.27), channel_id=1, source_target_pairs={{0,1},{1,0},{2,3},{3,2},{4,5},{5,4},{6,7},{7,6},{8,9},{9,8},{10,11... | collective-permute-start | bytes 786440 | tf_op jit(solution)/shard_map/ppermute | solution.py:55
  52.2 55.1 %reduce-scatter.11.cloned.1.call-start = ((), (), s32[]{:S(2)}) async-start(), calls=%async_computation.15 | async-start | bytes 1146880 | tf_op jit(solution)/shard_map/reduce_scatter | solution.py:88
  86.5 2.1 collective-permute-start.4
  108.0 64.7 %reduce-scatter.5.cloned.1.call-start = ((), (), s32[]{:S(2)}) async-start(), calls=%async_computation.12 | async-start | bytes 9175040 | tf_op jit(solution)/shard_map/cond/branch_0_fun/reduce_scatter | solution.py:88
  118.3 5.5 %collective-permute-start = (f32[256,512]{1,0:T(8,128)S(1)}, f32[256,512]{1,0:T(8,128)S(1)}, u32[]{:S(2)}, u32[]{:S(2)}) collective-permute-start(f32[256,512]{1,0:T(8,128)S(1)} %bitcast.19), channel_id=1, source_target_pairs={{0,1},{1,0},{2,3},{3,2},{4,5},{5,4},{6,7},{7,6},{8,9},{9,8},{10,11... | collective-permute-start | bytes 1572872 | tf_op jit(solution)/shard_map/cond/branch_0_fun/ppermute | solution.py:55
  131.8 91.0 %reduce-scatter.7.cloned.1.call-start = ((), (), s32[]{:S(2)}) async-start(), calls=%async_computation.13 | async-start | bytes 2293760 | tf_op jit(solution)/shard_map/cond/branch_0_fun/reduce_scatter | solution.py:88
  199.5 3.3 %collective-permute-start.1 = (f32[640,128]{1,0:T(8,128)S(1)}, f32[640,128]{1,0:T(8,128)S(1)}, u32[]{:S(2)}, u32[]{:S(2)}) collective-permute-start(f32[640,128]{1,0:T(8,128)S(1)} %bitcast.35), channel_id=1, source_target_pairs={{0,1},{1,0},{2,3},{3,2},{4,5},{5,4},{6,7},{7,6},{8,9},{9,8},{10,11... | collective-permute-start | bytes 983048 | tf_op jit(solution)/shard_map/cond/branch_0_fun/ppermute | solution.py:55
  222.8 1.0 copy-start
  225.1 35.3 %copy-start.2 = (bf16[512,3584]{1,0:T(8,128)(2,1)S(1)}, bf16[512,3584]{1,0:T(8,128)(2,1)}, u32[]{:S(2)}) copy-start(bf16[512,3584]{1,0:T(8,128)(2,1)} %copy-done.1) | copy-start | bytes 11010052
  237.0 15.1 %collective-permute-start.6 = (bf16[896,512]{1,0:T(8,128)(2,1)S(1)}, bf16[896,512]{1,0:T(8,128)(2,1)S(1)}, u32[]{:S(2)}, u32[]{:S(2)}) collective-permute-start(bf16[896,512]{1,0:T(8,128)(2,1)S(1)} %bitcast.23), channel_id=1, source_target_pairs={{0,24},{1,97},{2,26},{3,99},{4,28},{5,101},{6,30},{7,103},{8,0},{9... | collective-permute-start | bytes 2752520 | tf_op jit(solution)/shard_map/ppermute | solution.py:47
  237.9 14.2 %collective-permute-start.5 = (bf16[896,512]{1,0:T(8,128)(2,1)S(1)}, bf16[896,512]{1,0:T(8,128)(2,1)S(1)}, u32[]{:S(2)}, u32[]{:S(2)}) collective-permute-start(bf16[896,512]{1,0:T(8,128)(2,1)S(1)} %bitcast.24), channel_id=1, source_target_pairs={{0,8},{1,33},{2,10},{3,35},{4,12},{5,37},{6,14},{7,39},{8,16},{9,4... | collective-permute-start | bytes 2752520 | tf_op jit(solution)/shard_map/ppermute | solution.py:47
  238.5 3.8 %collective-permute-start.9 = (f32[8,512]{1,0:T(8,128)S(1)}, f32[8,512]{1,0:T(8,128)S(1)}, u32[]{:S(2)}, u32[]{:S(2)}) collective-permute-start(f32[8,512]{1,0:T(8,128)S(1)} %block_sums.1), channel_id=1, source_target_pairs={{0,6},{1,7},{2,0},{3,1},{4,2},{5,3},{6,4},{7,5},{8,14},{9,15},{10,... | collective-permute-start | bytes 49160 | tf_op jit(solution)/shard_map/ppermute | solution.py:59
  241.3 4.1 %collective-permute-start.8 = (f32[8,512]{1,0:T(8,128)S(1)}, f32[8,512]{1,0:T(8,128)S(1)}, u32[]{:S(2)}, u32[]{:S(2)}) collective-permute-start(f32[8,512]{1,0:T(8,128)S(1)} %block_sums.1), channel_id=1, source_target_pairs={{0,4},{1,5},{2,6},{3,7},{4,0},{5,1},{6,2},{7,3},{8,12},{9,13},{10,... | collective-permute-start | bytes 49160 | tf_op jit(solution)/shard_map/ppermute | solution.py:59
  241.6 4.2 %collective-permute-start.7 = (f32[8,512]{1,0:T(8,128)S(1)}, f32[8,512]{1,0:T(8,128)S(1)}, u32[]{:S(2)}, u32[]{:S(2)}) collective-permute-start(f32[8,512]{1,0:T(8,128)S(1)} %block_sums.1), channel_id=1, source_target_pairs={{0,2},{1,3},{2,4},{3,5},{4,6},{5,7},{6,0},{7,1},{8,10},{9,11},{10,... | collective-permute-start | bytes 49160 | tf_op jit(solution)/shard_map/ppermute | solution.py:59
  245.8 3.9 %collective-permute-start.12 = (f32[8,512]{1,0:T(8,128)S(1)}, f32[8,512]{1,0:T(8,128)S(1)}, u32[]{:S(2)}, u32[]{:S(2)}) collective-permute-start(f32[8,512]{1,0:T(8,128)S(1)} %add_add_fusion.1), channel_id=1, source_target_pairs={{0,24},{1,97},{2,26},{3,99},{4,28},{5,101},{6,30},{7,103},{8,0},{9... | collective-permute-start | bytes 49160 | tf_op jit(solution)/shard_map/ppermute | solution.py:47
  247.9 4.1 %collective-permute-start.11 = (f32[8,512]{1,0:T(8,128)S(1)}, f32[8,512]{1,0:T(8,128)S(1)}, u32[]{:S(2)}, u32[]{:S(2)}) collective-permute-start(f32[8,512]{1,0:T(8,128)S(1)} %add_add_fusion.1), channel_id=1, source_target_pairs={{0,16},{1,65},{2,18},{3,67},{4,20},{5,69},{6,22},{7,71},{8,24},{9,... | collective-permute-start | bytes 49160 | tf_op jit(solution)/shard_map/ppermute | solution.py:47
  248.0 4.1 %collective-permute-start.10 = (f32[8,512]{1,0:T(8,128)S(1)}, f32[8,512]{1,0:T(8,128)S(1)}, u32[]{:S(2)}, u32[]{:S(2)}) collective-permute-start(f32[8,512]{1,0:T(8,128)S(1)} %add_add_fusion.1), channel_id=1, source_target_pairs={{0,8},{1,33},{2,10},{3,35},{4,12},{5,37},{6,14},{7,39},{8,16},{9,4... | collective-permute-start | bytes 49160 | tf_op jit(solution)/shard_map/ppermute | solution.py:47
  252.2 14.5 %collective-permute-start.15 = (bf16[896,256]{1,0:T(8,128)(2,1)S(1)}, bf16[896,256]{1,0:T(8,128)(2,1)S(1)}, u32[]{:S(2)}, u32[]{:S(2)}) collective-permute-start(bf16[896,256]{1,0:T(8,128)(2,1)S(1)} %slice.7), channel_id=1, source_target_pairs={{0,24},{1,97},{2,26},{3,99},{4,28},{5,101},{6,30},{7,103},{8,0},{9... | collective-permute-start | bytes 1376264 | tf_op jit(solution)/shard_map/ppermute | solution.py:47
  252.9 13.7 %collective-permute-start.14 = (bf16[896,256]{1,0:T(8,128)(2,1)S(1)}, bf16[896,256]{1,0:T(8,128)(2,1)S(1)}, u32[]{:S(2)}, u32[]{:S(2)}) collective-permute-start(bf16[896,256]{1,0:T(8,128)(2,1)S(1)} %slice.6), channel_id=1, source_target_pairs={{0,8},{1,33},{2,10},{3,35},{4,12},{5,37},{6,14},{7,39},{8,16},{9,4... | collective-permute-start | bytes 1376264 | tf_op jit(solution)/shard_map/ppermute | solution.py:47
  253.7 6.7 %collective-permute-start.13 = (f32[8,512]{1,0:T(8,128)S(1)}, f32[8,512]{1,0:T(8,128)S(1)}, u32[]{:S(2)}, u32[]{:S(2)}) collective-permute-start(f32[8,512]{1,0:T(8,128)S(1)} %add_add_fusion.sums_ref), channel_id=1, source_target_pairs={{0,1},{1,0},{2,3},{3,2},{4,5},{5,4},{6,7},{7,6},{8,9},{9,8},{10,11... | collective-permute-start | bytes 49160 | tf_op jit(solution)/shard_map/ppermute | solution.py:55
Sparse Core Ops, SparseCore 0:
  52.3 34.0 reduce-scatter.8
  88.9 17.6 reduce-scatter.10
  131.9 40.7 reduce-scatter.4
  175.0 25.5 reduce-scatter.6
